TPU v7x, 32 devices: a whole 2x2x4 slice. The times are simulated.
32 devices in a mesh: gx: 4 (over z), gy: 4 (over y, core), gz: 2 (over x).
Axes of the slice: x: 2, y: 2, z: 4, core: 2. Of those that a mesh axis runs over, the one named last changes fastest.
Arguments:
- hidden_atoms: float32 [256, 256], P(('gx', 'gy', 'gz')), may hold values from -6 to 6
- edge_states: float32 [7680, 512], P(('gx', 'gy', 'gz')), may hold values from -6 to 6
- edge_vectors: float32 [3, 7680], P(None, ('gx', 'gy', 'gz')), may hold values from -11 to 11, as said below
- atom_tags: int32 [256], P(('gx', 'gy', 'gz')), may hold values from 0 to 2
- send_list: int32 [128], P(('gx', 'gy', 'gz')), may hold values from 0 to 7, as said below
- sources: int32 [7680], P(('gx', 'gy', 'gz')), may hold values from 0 to 115, as said below
- trip_slots: int32 [7680, 8], P(('gx', 'gy', 'gz')), may hold values from 0 to 29
- triplet_mask: int32 [7680, 8], P(('gx', 'gy', 'gz')), may hold values 0 or 1
- quad_slots: int32 [7680, 8], P(('gx', 'gy', 'gz')), may hold values from 0 to 29
- quad_mask: int32 [7680, 8], P(('gx', 'gy', 'gz')), may hold values 0 or 1
- edge_mask: int32 [7680], P(('gx', 'gy', 'gz')), may hold values 0 or 1
- w_inputs: bfloat16 [2, 512, 512], replicated, may hold values from -0.25 to 0.25
- w_radial: bfloat16 [5, 128, 512], replicated, may hold values from -0.5 to 0.5
- w_trip_down: bfloat16 [512, 64], replicated, may hold values from -0.25 to 0.25
- triplet_bilinear_weight: bfloat16 [1024, 64], replicated, may hold values from -0.75 to 0.75
- w_trip_up: bfloat16 [64, 512], replicated, may hold values from -0.75 to 0.75
- w_quad_down: bfloat16 [512, 32], replicated, may hold values from -0.25 to 0.25
- w_quad_bil: bfloat16 [1024, 32], replicated, may hold values from -1 to 1
- w_quad_up: bfloat16 [32, 512], replicated, may hold values from -1 to 1
- w_atom_edge: bfloat16 [2, 256, 512], replicated, may hold values from -0.375 to 0.375
- w_residual: bfloat16 [2, 512, 512], replicated, may hold values from -0.25 to 0.25
- w_edge_atom: bfloat16 [2, 512, 256], replicated, may hold values from -0.25 to 0.25
- w_atom_dense: bfloat16 [4, 256, 256], replicated, may hold values from -0.375 to 0.375
- tag_table: bfloat16 [3, 256], replicated, may hold values from -4 to 4
- cot_atoms: float32 [256, 256], P(('gx', 'gy', 'gz')), may hold values from -6 to 6
- cot_edges: float32 [7680, 512], P(('gx', 'gy', 'gz')), may hold values from -6 to 6
- cot_energy: float32 [256, 256], P(('gx', 'gy', 'gz')), may hold values from -6 to 6
Outputs:
- atoms_out: float32 [256, 256], P(('gx', 'gy', 'gz'))
- edges_out: float32 [7680, 512], P(('gx', 'gy', 'gz'))
- energy_out: float32 [256, 256], P(('gx', 'gy', 'gz'))
- grad_atoms: float32 [256, 256], P(('gx', 'gy', 'gz'))
- grad_edges: float32 [7680, 512], P(('gx', 'gy', 'gz'))
- grad_inputs: float32 [2, 512, 512], replicated
- grad_radial: float32 [5, 128, 512], replicated
- grad_trip_down: float32 [512, 64], replicated
- grad_trip_bil: float32 [1024, 64], replicated
- grad_trip_up: float32 [64, 512], replicated
- grad_quad_down: float32 [512, 32], replicated
- grad_quad_bil: float32 [1024, 32], replicated
- grad_quad_up: float32 [32, 512], replicated
- grad_atom_edge: float32 [2, 256, 512], replicated
- grad_residual: float32 [2, 512, 512], replicated
- grad_edge_atom: float32 [2, 512, 256], replicated
- grad_atom_dense: float32 [4, 256, 256], replicated
- grad_tag_table: float32 [3, 256], replicated
Inputs may be any that keep to these rules, and one draw needn't show every extreme that they name: `edge_vectors`: each column's length lies between 2 and 11. `send_list`: the 4 entries of one device are distinct local atom numbers. `sources`: A value under 8 is a local atom other than the edge's target; a value 8 + b * 4 + r names border atom r of the neighbour at offset (b // 9 - 1, (b // 3) % 3 - 1, b % 3 - 1), never offset (0, 0, 0) and never beyond either end of gz.
All inputs are finite; a program needn't handle non-finite values. No bound on the sum of `triplet_mask` or of `quad_mask` or of `edge_mask` on one device may be relied on, other than what follows from the above.
Results may differ from a plain program's by a relative error of at most 0.0009.
Values sent between devices are 32-bit elements; how exact they have to be, the bound alone decides.
No kernel may reach another device: no remote copies, remote signals or barrier semaphores. Data moves between devices by JAX's collectives and lax.ppermute only.
A program may use at most 128 MiB of HBM per device.

v0:
```python
import math

import jax
import jax.numpy as jnp
from jax import lax
from jax.sharding import PartitionSpec as P

HIGHEST = lax.Precision.HIGHEST
cutoff_radius = 12.0
root_half = 0.7071067811865476


def with_halo(x, sides, width):
    for axis, dim in sides:
        devices, length = (lax.axis_size(axis), x.shape[dim])
        up = [(i, (i + 1) % devices) for i in range(devices)]
        down = [(j, i) for i, j in up]
        last = lax.slice_in_dim(x, length - width, length, axis=dim)
        first = lax.slice_in_dim(x, 0, width, axis=dim)
        before = lax.ppermute(last, axis, up)
        after = lax.ppermute(first, axis, down)
        x = jnp.concatenate([before, x, after], axis=dim)
    return x


def from_behind(value, axis, steps):
    count = lax.axis_size(axis)
    pairs = [(source, (source + steps) % count) for source in range(count)]
    return lax.ppermute(value, axis, pairs)


def passed_along(x, axis, by):
    devices = lax.axis_size(axis)
    pairs = [(i, i + by) for i in range(devices) if 0 <= i + by < devices]
    return lax.ppermute(x, axis, pairs)


def scaled_silu(values):
    return jax.nn.silu(values) / 0.6


def matmul(left, right):
    return jnp.dot(left, right, precision=HIGHEST, preferred_element_type=jnp.float32)


def envelope(scaled):
    return 1.0 - 28.0 * scaled**6 + 48.0 * scaled**7 - 21.0 * scaled**8


def radial_basis(lengths, count):
    scaled = lengths / cutoff_radius
    orders = jnp.arange(1, count + 1).astype(jnp.float32)
    return (
        envelope(scaled)[:, None]
        * jnp.sin(math.pi * scaled[:, None] * orders[None, :])
        / scaled[:, None]
    )


def legendre_terms(cosine, count):
    terms = [jnp.ones_like(cosine), cosine]
    for degree in range(1, count - 1):
        terms.append(
            ((2 * degree + 1) * cosine * terms[degree] - degree * terms[degree - 1]) / (degree + 1)
        )
    return jnp.stack(terms[:count], axis=-1)


def spherical_basis(cosine, lengths, count):
    poly = legendre_terms(cosine, count // 2)
    scaled = lengths / cutoff_radius
    shaped = envelope(scaled)
    first = shaped * jnp.sin(math.pi * scaled) / scaled
    second = shaped * jnp.sin(2.0 * math.pi * scaled) / scaled
    return jnp.concatenate([poly * first[..., None], poly * second[..., None]], axis=-1)


def per_device(
    hidden_atoms,
    edge_states,
    edge_vectors,
    atom_tags,
    send_list,
    sources,
    trip_slots,
    triplet_mask,
    quad_slots,
    quad_mask,
    edge_mask,
    w_inputs,
    w_radial,
    w_trip_down,
    triplet_bilinear_weight,
    w_trip_up,
    w_quad_down,
    w_quad_bil,
    w_quad_up,
    w_atom_edge,
    w_residual,
    w_edge_atom,
    w_atom_dense,
    tag_table,
    cot_atoms,
    cot_edges,
    cot_energy,
):
    weights = tuple(
        (
            weight.astype(jnp.float32)
            for weight in (
                w_inputs,
                w_radial,
                w_trip_down,
                triplet_bilinear_weight,
                w_trip_up,
                w_quad_down,
                w_quad_bil,
                w_quad_up,
                w_atom_edge,
                w_residual,
                w_edge_atom,
                w_atom_dense,
                tag_table,
            )
        )
    )
    atom_count = hidden_atoms.shape[0]
    edge_count = edge_states.shape[0]
    slot_count = edge_count // atom_count
    send_count = send_list.shape[0]
    atom_width = hidden_atoms.shape[1]
    edge_width = edge_states.shape[1]
    trip_width = w_trip_down.shape[1]
    quad_width = w_quad_down.shape[1]
    radial_count = w_radial.shape[1]
    angle_count = triplet_bilinear_weight.shape[0] // trip_width
    sphere_count = w_quad_bil.shape[0] // quad_width
    trip_count = trip_slots.shape[1]
    quad_count = quad_slots.shape[1]
    block_rows = 27 * send_count
    vectors = edge_vectors.T
    local_lengths = jnp.sqrt(jnp.sum(vectors * vectors, axis=1))
    radial = radial_basis(local_lengths, radial_count)
    onehot = (atom_tags[:, None] == jnp.arange(3)[None, :]).astype(jnp.float32)
    live_edges = edge_mask.astype(jnp.float32)
    send_edges = (send_list[:, None] * slot_count + jnp.arange(slot_count)[None, :]).reshape(-1)

    def local_start(atoms_in, edges_in, params):
        tagged = atoms_in + matmul(onehot, params[12])
        trip_start = scaled_silu(matmul(edges_in, params[0][0])) * matmul(radial, params[1][0])
        trip_down = scaled_silu(matmul(trip_start, params[2])) * live_edges[:, None]
        quad_start = scaled_silu(matmul(edges_in, params[0][1])) * matmul(radial, params[1][1])
        quad_down = scaled_silu(matmul(quad_start, params[5])) * live_edges[:, None]
        return (tagged, trip_down, quad_down)

    (tagged, trip_down, quad_down), pull_start = jax.vjp(
        local_start, hidden_atoms, edge_states, weights
    )
    payload = jnp.concatenate(
        [
            tagged[send_list],
            trip_down[send_edges].reshape(send_count, slot_count * trip_width),
            quad_down[send_edges].reshape(send_count, slot_count * quad_width),
            vectors[send_edges].reshape(send_count, slot_count * 3),
        ],
        axis=1,
    )
    border = with_halo(payload[None, None, None], (("gx", 0), ("gy", 1), ("gz", 2)), 1)
    border = border.reshape(block_rows, -1)
    col_quad = atom_width + slot_count * trip_width
    col_vector = col_quad + slot_count * quad_width
    tagged_halo = border[:, :atom_width]
    trip_halo = border[:, atom_width:col_quad].reshape(block_rows * slot_count, trip_width)
    quad_halo = border[:, col_quad:col_vector].reshape(block_rows * slot_count, quad_width)
    vector_halo = border[:, col_vector:].reshape(block_rows * slot_count, 3)
    vector_table = jnp.concatenate([vectors, vector_halo], axis=0)
    length_table = jnp.sqrt(jnp.sum(vector_table * vector_table, axis=1))
    safe_lengths = jnp.where(length_table > 0.0, length_table, 1.0)
    unit_table = vector_table / safe_lengths[:, None]
    unit_local = unit_table[:edge_count]
    first_edge = jnp.where(
        sources < atom_count, sources * slot_count, edge_count + (sources - atom_count) * slot_count
    )
    trip_index = first_edge[:, None] + trip_slots
    quad_index = first_edge[:, None] + quad_slots
    triplet_cosine = -jnp.sum(unit_local[:, None, :] * unit_table[trip_index], axis=-1)
    triplet_basis = legendre_terms(triplet_cosine, angle_count) * triplet_mask[..., None].astype(
        jnp.float32
    )
    cos_quad = -jnp.sum(unit_local[:, None, :] * unit_table[quad_index], axis=-1)
    quad_basis = spherical_basis(cos_quad, safe_lengths[quad_index], sphere_count) * quad_mask[
        ..., None
    ].astype(jnp.float32)
    targets = jnp.arange(edge_count) // slot_count

    def local_finish(
        tagged_in, edges_in, trip_in, quad_in, tagged_out, trip_out_rows, quad_out_rows, params
    ):
        (
            p_inputs,
            p_radial,
            p_trip_down,
            p_trip_bil,
            p_trip_up,
            p_quad_down,
            p_quad_bil,
            p_quad_up,
            p_atom_edge,
            p_residual,
            p_edge_atom,
            p_atom_dense,
            p_tags,
        ) = params
        trip_table = jnp.concatenate([trip_in, trip_out_rows], axis=0)
        quad_table = jnp.concatenate([quad_in, quad_out_rows], axis=0)
        tagged_table = jnp.concatenate([tagged_in, tagged_out], axis=0)
        trip_sum = jnp.einsum(
            "ejc,ejf->ecf", triplet_basis, trip_table[trip_index], precision=HIGHEST
        )
        trip_sum = trip_sum.reshape(edge_count, -1) / math.sqrt(trip_count)
        trip_msg = scaled_silu(matmul(scaled_silu(matmul(trip_sum, p_trip_bil)), p_trip_up))
        quad_sum = jnp.einsum("ejc,ejf->ecf", quad_basis, quad_table[quad_index], precision=HIGHEST)
        quad_sum = quad_sum.reshape(edge_count, -1) / math.sqrt(quad_count)
        quad_msg = scaled_silu(matmul(scaled_silu(matmul(quad_sum, p_quad_bil)), p_quad_up))
        atom_msg = scaled_silu(
            matmul(tagged_table, p_atom_edge[0])[sources]
            + matmul(tagged_in, p_atom_edge[1])[targets]
        )
        atom_msg = atom_msg * matmul(radial, p_radial[2])
        merged = (edges_in + trip_msg + quad_msg + atom_msg) * 0.5
        edges_new = (
            merged + scaled_silu(matmul(scaled_silu(matmul(merged, p_residual[0])), p_residual[1]))
        ) * root_half
        weighted = edges_new * live_edges[:, None]
        gathered = jnp.sum(
            (weighted * matmul(radial, p_radial[3])).reshape(-1, slot_count, edge_width), axis=1
        ) / math.sqrt(slot_count)
        updated = (tagged_in + scaled_silu(matmul(gathered, p_edge_atom[0]))) * root_half
        atoms_new = (
            updated
            + scaled_silu(matmul(scaled_silu(matmul(updated, p_atom_dense[0])), p_atom_dense[1]))
        ) * root_half
        summary = jnp.sum(
            (weighted * matmul(radial, p_radial[4])).reshape(-1, slot_count, edge_width), axis=1
        ) / math.sqrt(slot_count)
        energy_new = scaled_silu(
            matmul(
                scaled_silu(matmul(summary, p_edge_atom[1]) + matmul(atoms_new, p_atom_dense[2])),
                p_atom_dense[3],
            )
        )
        return (atoms_new, edges_new, energy_new)

    outputs, pull_finish = jax.vjp(
        local_finish,
        tagged,
        edge_states,
        trip_down,
        quad_down,
        tagged_halo,
        trip_halo,
        quad_halo,
        weights,
    )
    (
        grad_tagged,
        grad_edges_late,
        grad_trip,
        grad_quad,
        grad_tagged_halo,
        grad_trip_halo,
        grad_quad_halo,
        grad_late,
    ) = pull_finish((cot_atoms, cot_edges, cot_energy))
    back = jnp.concatenate(
        [
            grad_tagged_halo,
            grad_trip_halo.reshape(block_rows, slot_count * trip_width),
            grad_quad_halo.reshape(block_rows, slot_count * quad_width),
        ],
        axis=1,
    )
    back = back.reshape(3, 3, 3, send_count, -1)
    returned = jnp.zeros(back.shape[3:], jnp.float32)
    for step_x in range(3):
        for step_y in range(3):
            for step_z in range(3):
                piece = back[step_x, step_y, step_z]
                if step_x != 1:
                    piece = from_behind(piece, "gx", step_x - 1)
                if step_y != 1:
                    piece = from_behind(piece, "gy", step_y - 1)
                if step_z != 1:
                    piece = passed_along(piece, "gz", step_z - 1)
                returned = returned + piece
    grad_tagged = grad_tagged.at[send_list].add(returned[:, :atom_width])
    grad_trip = grad_trip.at[send_edges].add(
        returned[:, atom_width:col_quad].reshape(send_count * slot_count, trip_width)
    )
    grad_quad = grad_quad.at[send_edges].add(
        returned[:, col_quad:].reshape(send_count * slot_count, quad_width)
    )
    grad_atoms, grad_edges_early, grad_early = pull_start((grad_tagged, grad_trip, grad_quad))
    partial_grads = tuple((late + early for late, early in zip(grad_late, grad_early)))
    summed = lax.psum(partial_grads, ("gx", "gy", "gz"))
    return (
        outputs[0],
        outputs[1],
        outputs[2],
        grad_atoms,
        grad_edges_late + grad_edges_early,
        summed[0],
        summed[1],
        summed[2],
        summed[3],
        summed[4],
        summed[5],
        summed[6],
        summed[7],
        summed[8],
        summed[9],
        summed[10],
        summed[11],
        summed[12],
    )


def solution(mesh):
    placed = (
        P(("gx", "gy", "gz"), None),
        P(("gx", "gy", "gz"), None),
        P(None, ("gx", "gy", "gz")),
        P(("gx", "gy", "gz")),
        P(("gx", "gy", "gz")),
        P(("gx", "gy", "gz")),
        P(("gx", "gy", "gz"), None),
        P(("gx", "gy", "gz"), None),
        P(("gx", "gy", "gz"), None),
        P(("gx", "gy", "gz"), None),
        P(("gx", "gy", "gz")),
        P(),
        P(),
        P(),
        P(),
        P(),
        P(),
        P(),
        P(),
        P(),
        P(),
        P(),
        P(),
        P(),
        P(("gx", "gy", "gz"), None),
        P(("gx", "gy", "gz"), None),
        P(("gx", "gy", "gz"), None),
    )
    return jax.shard_map(
        per_device,
        mesh=mesh,
        in_specs=placed,
        out_specs=(
            P(("gx", "gy", "gz"), None),
            P(("gx", "gy", "gz"), None),
            P(("gx", "gy", "gz"), None),
            P(("gx", "gy", "gz"), None),
            P(("gx", "gy", "gz"), None),
            P(),
            P(),
            P(),
            P(),
            P(),
            P(),
            P(),
            P(),
            P(),
            P(),
            P(),
            P(),
            P(),
        ),
        check_vma=False,
    )
```

profile of v0, /device:TPU:0, one launch (start us, length us, event | category | flops | bytes accessed | tf_op | source)
XLA Modules:
  0.0 588.9 jit_solution(18259935676668890362)
XLA Ops:
  7.4 1.8 fusion.19
  9.2 1.8 fusion.22
  13.4 2.5 fusion.120
  17.9 2.6 fusion.121
  23.3 5.0 collective-permute-start.1
  30.1 4.1 collective-permute-done
  38.9 1.9 collective-permute-done.2
  43.7 2.5 fusion.95
  46.2 8.6 %collective-permute-done.5 = f32[3,3,1,4,3226]{4,3,2,1,0:T(4,128)S(1)} collective-permute-done((f32[3,3,1,4,3226]{4,3,2,1,0:T(4,128)S(1)}, f32[3,3,1,4,3226]{4,3,2,1,0:T(4,128)S(1)}, u32[]{:S(2)}, u32[]{:S(2)}) %collective-permute-start.5) | collective-permute-done | bytes 464576 | tf_op jit(solution)/shard_map/ppermute | solution.py:21
  54.8 9.4 %collective-permute-done.4 = f32[3,3,1,4,3226]{4,3,2,1,0:T(4,128)S(1)} collective-permute-done((f32[3,3,1,4,3226]{4,3,2,1,0:T(4,128)S(1)}, f32[3,3,1,4,3226]{4,3,2,1,0:T(4,128)S(1)}, u32[]{:S(2)}, u32[]{:S(2)}) %collective-permute-start.4) | collective-permute-done | bytes 464576 | tf_op jit(solution)/shard_map/ppermute | solution.py:20
  65.7 1.9 reshape.780
  71.7 2.0 fusion
  73.7 10.4 %gather_fusion.7 = f32[1920]{0:T(1024)S(1)} fusion(f32[3480]{0:T(1024)S(1)} %compare_select_fusion, s32[2048]{0:T(1024)S(1)} %get-tuple-element.192), kind=kCustom, calls=%fused_computation.7 | custom fusion | bytes 23040 | tf_op jit(solution)/shard_map/gather | solution.py:191
  84.1 3.5 gather_fusion.6
  88.9 2.7 reshape.782
  91.5 2.8 pad_maximum_fusion.1
  94.3 4.5 gather_fusion.4
  98.8 6.0 %gather_fusion.5 = f32[1920,64]{1,0:T(8,128)} fusion(f32[3480,64]{1,0:T(8,128)} %pad_maximum_fusion.1, s32[2048]{0:T(1024)S(1)} %get-tuple-element.193), kind=kCustom, calls=%fused_computation.5 | custom fusion | bytes 990720 | tf_op jit(solution)/shard_map/jvp()/gather | solution.py:218
  107.6 6.1 %gather_fusion.8 = f32[1920,32]{1,0:T(8,128)} fusion(f32[3480,32]{1,0:T(8,128)} %pad_maximum_fusion.2, s32[2048]{0:T(1024)S(1)} %get-tuple-element.192), kind=kCustom, calls=%fused_computation.8 | custom fusion | bytes 499200 | tf_op jit(solution)/shard_map/jvp()/gather | solution.py:222
  117.8 5.7 convolution_multiply_fusion.1
  123.6 2.4 copy.140
  126.0 8.8 %convolution_multiply_fusion = f32[240,32,32]{2,1,0:T(8,128)} fusion(f32[240,8,32]{2,1,0:T(8,128)S(1)} %copy.151, f32[1920,32]{1,0:T(8,128)} %gather_fusion.8), kind=kOutput, calls=%fused_computation.22 | convolution fusion | flops 23838720 | bytes 1474560 | tf_op jit(solution)/shard_map/jvp(ejc,ejf->ecf)/dot_general | solution.py:222
  134.8 3.7 copy.152
  138.6 2.0 gather_fusion.9
  145.6 2.9 multiply_multiply_fusion.4
  148.5 1.9 reshape.785
  150.4 2.6 broadcast_multiply_fusion
  172.9 1.9 reshape.787
  174.7 2.7 convolution_bitcast_fusion.13
  180.4 2.4 convolution_bitcast_fusion.3
  182.8 2.1 fusion.33
  188.0 2.1 convolution_bitcast_fusion.2
  190.0 1.9 fusion.299
  195.8 2.5 scatter_custom_fusion.1
  200.8 2.5 copy.155
  203.3 2.7 convolution_bitcast_fusion.1
  206.0 12.3 %scatter_custom_fusion.2 = f32[3480,64]{1,0:T(8,128)S(1)} fusion(s32[1920]{0:T(1024)} %copy-done.100, f32[1920,64]{1,0:T(8,128)} %convolution_bitcast_fusion.1, f32[]{:T(128)} %constant.196.clone.1), kind=kCustom, calls=%fused_computation.77 | custom fusion | flops 122880 | bytes 891392 | tf_op jit(solution)/shard_map/transpose(jvp())/scatter-add | solution.py:218
  219.7 3.0 concatenate.47
  224.7 4.5 copy.158
  229.3 5.7 convolution_bitcast_fusion
  234.9 13.1 %scatter_custom_fusion.3 = f32[3480,32]{1,0:T(8,128)} fusion(s32[1920]{0:T(1024)} %copy-done.99, f32[1920,32]{1,0:T(8,128)} %convolution_bitcast_fusion, f32[]{:T(128)} %constant.196.clone.1), kind=kCustom, calls=%fused_computation.75 | custom fusion | flops 61440 | bytes 445952 | tf_op jit(solution)/shard_map/transpose(jvp())/scatter-add | solution.py:222
  248.1 2.7 split.27
  250.8 2.8 concatenate.48
  256.6 2.0 slice_bitcast_fusion.25
  258.7 1.8 convolution_bitcast_fusion.12
  262.1 3.2 collective-permute-start.17
  269.3 3.2 collective-permute-start.9
  274.6 3.7 collective-permute-start.50
  281.4 3.5 collective-permute-start.42
  286.8 3.2 scatter_custom_fusion
  290.0 3.4 collective-permute-start.33
  298.5 3.6 collective-permute-start.24
  304.2 4.5 collective-permute-start.18
  312.9 1.9 collective-permute-done.15
  314.8 2.8 collective-permute-start.51
  321.9 4.3 collective-permute-start.38
  327.5 4.5 collective-permute-start.31
  336.5 4.5 collective-permute-start.13
  344.3 4.5 collective-permute-start.46
  350.2 4.5 collective-permute-start.26
  374.4 40.3 %psum.103 = f32[3,256]{1,0:T(4,128)} all-reduce(f32[3,256]{1,0:T(4,128)S(1)} %fusion.232), channel_id=1, replica_groups=mesh['gx'=4,'gy'=4,'gz'=2] {'gx','gy','gz'}, use_global_device_ids=true, to_apply=%region_25.26 | all-reduce | flops 768 | bytes 6144 | tf_op jit(solution)/shard_map/psum | solution.py:305
  414.7 2.1 fusion.17
  418.4 150.0 %all-reduce.20.cloned.1.call-done = (f32[2,512,512]{1,2,0:T(8,128)}, f32[5,128,512]{2,1,0:T(8,128)}, f32[512,64]{0,1:T(8,128)}, f32[1024,64]{0,1:T(8,128)}, f32[...) async-done(((f32[2,512,512]{1,2,0:T(8,128)}, ...) | async-done | bytes 9437200 | tf_op jit(solution)/shard_map/psum | solution.py:305
  568.3 3.0 copy.161
  (635 shorter events, 142.3 us)
Async XLA Ops:
  7.2 133.4 %copy-start = (bf16[1024,64]{0,1:T(8,128)(2,1)S(1)}, bf16[1024,64]{0,1:T(8,128)(2,1)}, u32[]{:S(2)}) copy-start(bf16[1024,64]{0,1:T(8,128)(2,1)} %param.41) | copy-start | bytes 393220
  7.2 561.1 %all-reduce.20.cloned.1.call-start = ((), (), s32[]{:S(2)}) async-start(), calls=%async_computation | async-start | bytes 18874368 | tf_op jit(solution)/shard_map/psum | solution.py:305
  23.3 6.8 %collective-permute-start.1 = (f32[1,1,1,4,3226]{4,3,2,1,0:T(4,128)S(1)}, f32[1,1,1,4,3226]{4,3,2,1,0:T(4,128)S(1)}, u32[]{:S(2)}, u32[]{:S(2)}) collective-permute-start(f32[1,1,1,4,3226]{4,3,2,1,0:T(4,128)S(1)} %bitcast.666), channel_id=1, source_target_pairs={{8,0},{16,8},{24,16},{0,24},{9,1},{17,9},{25,17},{1,25},{10,2},{18... | collective-permute-start | bytes 154856 | tf_op jit(solution)/shard_map/ppermute | solution.py:21
  28.3 5.9 %collective-permute-start = (f32[1,1,1,4,3226]{4,3,2,1,0:T(4,128)S(1)}, f32[1,1,1,4,3226]{4,3,2,1,0:T(4,128)S(1)}, u32[]{:S(2)}, u32[]{:S(2)}) collective-permute-start(f32[1,1,1,4,3226]{4,3,2,1,0:T(4,128)S(1)} %bitcast.667), channel_id=1, source_target_pairs={{0,8},{8,16},{16,24},{24,0},{1,9},{9,17},{17,25},{25,1},{2,10},{10... | collective-permute-start | bytes 154856 | tf_op jit(solution)/shard_map/ppermute | solution.py:20
  34.3 4.6 collective-permute-start.3
  34.4 6.5 %collective-permute-start.2 = (f32[3,1,1,4,3226]{4,3,2,1,0:T(4,128)S(1)}, f32[3,1,1,4,3226]{4,3,2,1,0:T(4,128)S(1)}, u32[]{:S(2)}, u32[]{:S(2)}) collective-permute-start(f32[3,1,1,4,3226]{4,3,2,1,0:T(4,128)S(1)} %pad_maximum_fusion.5), channel_id=1, source_target_pairs={{0,2},{2,4},{4,6},{6,0},{1,3},{3,5},{5,7},{7,1},{8,10},{10,12},{12... | collective-permute-start | bytes 464552 | tf_op jit(solution)/shard_map/ppermute | solution.py:20
  40.9 13.9 %collective-permute-start.5 = (f32[3,3,1,4,3226]{4,3,2,1,0:T(4,128)S(1)}, f32[3,3,1,4,3226]{4,3,2,1,0:T(4,128)S(1)}, u32[]{:S(2)}, u32[]{:S(2)}) collective-permute-start(f32[3,3,1,4,3226]{4,3,2,1,0:T(4,128)S(1)} %pad_maximum_fusion.4), channel_id=1, source_target_pairs={{1,0},{0,1},{3,2},{2,3},{5,4},{4,5},{7,6},{6,7},{9,8},{8,9},{11,10... | collective-permute-start | bytes 1393640 | tf_op jit(solution)/shard_map/ppermute | solution.py:21
  42.5 21.7 %collective-permute-start.4 = (f32[3,3,1,4,3226]{4,3,2,1,0:T(4,128)S(1)}, f32[3,3,1,4,3226]{4,3,2,1,0:T(4,128)S(1)}, u32[]{:S(2)}, u32[]{:S(2)}) collective-permute-start(f32[3,3,1,4,3226]{4,3,2,1,0:T(4,128)S(1)} %pad_maximum_fusion.4), channel_id=1, source_target_pairs={{0,1},{1,0},{2,3},{3,2},{4,5},{5,4},{6,7},{7,6},{8,9},{9,8},{10,11... | collective-permute-start | bytes 1393640 | tf_op jit(solution)/shard_map/ppermute | solution.py:20
  218.3 137.5 %copy-start.7 = (f32[3480,64]{1,0:T(8,128)}, f32[3480,64]{1,0:T(8,128)S(1)}, u32[]{:S(2)}) copy-start(f32[3480,64]{1,0:T(8,128)S(1)} %scatter_custom_fusion.2) | copy-start | bytes 2672644
  260.4 7.2 %collective-permute-start.6 = (f32[4,3136]{1,0:T(4,128)S(1)}, f32[4,3136]{1,0:T(4,128)S(1)}, u32[]{:S(2)}, u32[]{:S(2)}) collective-permute-start(f32[4,3136]{1,0:T(4,128)S(1)} %get-tuple-element.145), channel_id=1, source_target_pairs={{0,24},{8,0},{16,8},{24,16},{1,25},{9,1},{17,9},{25,17},{2,26},{10... | collective-permute-start | bytes 150536 | tf_op jit(solution)/shard_map/ppermute | solution.py:29
  260.4 7.2 %collective-permute-start.22 = (f32[4,3136]{1,0:T(4,128)S(1)}, f32[4,3136]{1,0:T(4,128)S(1)}, u32[]{:S(2)}, u32[]{:S(2)}) collective-permute-start(f32[4,3136]{1,0:T(4,128)S(1)} %get-tuple-element.146), channel_id=1, source_target_pairs={{0,24},{8,0},{16,8},{24,16},{1,25},{9,1},{17,9},{25,17},{2,26},{10... | collective-permute-start | bytes 150536 | tf_op jit(solution)/shard_map/ppermute | solution.py:29
  260.5 8.8 %collective-permute-start.19 = (f32[4,3136]{1,0:T(4,128)S(1)}, f32[4,3136]{1,0:T(4,128)S(1)}, u32[]{:S(2)}, u32[]{:S(2)}) collective-permute-start(f32[4,3136]{1,0:T(4,128)S(1)} %get-tuple-element.147), channel_id=1, source_target_pairs={{0,24},{8,0},{16,8},{24,16},{1,25},{9,1},{17,9},{25,17},{2,26},{10... | collective-permute-start | bytes 150536 | tf_op jit(solution)/shard_map/ppermute | solution.py:29
  262.1 10.4 %collective-permute-start.17 = (f32[4,3136]{1,0:T(4,128)S(1)}, f32[4,3136]{1,0:T(4,128)S(1)}, u32[]{:S(2)}, u32[]{:S(2)}) collective-permute-start(f32[4,3136]{1,0:T(4,128)S(1)} %get-tuple-element.148), channel_id=1, source_target_pairs={{0,24},{8,0},{16,8},{24,16},{1,25},{9,1},{17,9},{25,17},{2,26},{10... | collective-permute-start | bytes 150536 | tf_op jit(solution)/shard_map/ppermute | solution.py:29
  265.4 7.9 %collective-permute-start.16 = (f32[4,3136]{1,0:T(4,128)S(1)}, f32[4,3136]{1,0:T(4,128)S(1)}, u32[]{:S(2)}, u32[]{:S(2)}) collective-permute-start(f32[4,3136]{1,0:T(4,128)S(1)} %get-tuple-element.149), channel_id=1, source_target_pairs={{0,24},{8,0},{16,8},{24,16},{1,25},{9,1},{17,9},{25,17},{2,26},{10... | collective-permute-start | bytes 150536 | tf_op jit(solution)/shard_map/ppermute | solution.py:29
  267.6 5.8 collective-permute-start.14
  267.7 6.9 %collective-permute-start.11 = (f32[4,3136]{1,0:T(4,128)S(1)}, f32[4,3136]{1,0:T(4,128)S(1)}, u32[]{:S(2)}, u32[]{:S(2)}) collective-permute-start(f32[4,3136]{1,0:T(4,128)S(1)} %get-tuple-element.151), channel_id=1, source_target_pairs={{0,24},{8,0},{16,8},{24,16},{1,25},{9,1},{17,9},{25,17},{2,26},{10... | collective-permute-start | bytes 150536 | tf_op jit(solution)/shard_map/ppermute | solution.py:29
  269.3 9.0 %collective-permute-start.9 = (f32[4,3136]{1,0:T(4,128)S(1)}, f32[4,3136]{1,0:T(4,128)S(1)}, u32[]{:S(2)}, u32[]{:S(2)}) collective-permute-start(f32[4,3136]{1,0:T(4,128)S(1)} %get-tuple-element.126), channel_id=1, source_target_pairs={{0,24},{8,0},{16,8},{24,16},{1,25},{9,1},{17,9},{25,17},{2,26},{10... | collective-permute-start | bytes 150536 | tf_op jit(solution)/shard_map/ppermute | solution.py:29
  272.6 6.0 %collective-permute-start.57 = (f32[4,3136]{1,0:T(4,128)S(1)}, f32[4,3136]{1,0:T(4,128)S(1)}, u32[]{:S(2)}, u32[]{:S(2)}) collective-permute-start(f32[4,3136]{1,0:T(4,128)S(1)} %get-tuple-element.127), channel_id=1, source_target_pairs={{0,8},{8,16},{16,24},{24,0},{1,9},{9,17},{17,25},{25,1},{2,10},{10... | collective-permute-start | bytes 150536 | tf_op jit(solution)/shard_map/ppermute | solution.py:29
  273.3 6.9 %collective-permute-start.55 = (f32[4,3136]{1,0:T(4,128)S(1)}, f32[4,3136]{1,0:T(4,128)S(1)}, u32[]{:S(2)}, u32[]{:S(2)}) collective-permute-start(f32[4,3136]{1,0:T(4,128)S(1)} %get-tuple-element.128), channel_id=1, source_target_pairs={{0,8},{8,16},{16,24},{24,0},{1,9},{9,17},{17,25},{25,1},{2,10},{10... | collective-permute-start | bytes 150536 | tf_op jit(solution)/shard_map/ppermute | solution.py:29
  273.4 8.0 %collective-permute-start.52 = (f32[4,3136]{1,0:T(4,128)S(1)}, f32[4,3136]{1,0:T(4,128)S(1)}, u32[]{:S(2)}, u32[]{:S(2)}) collective-permute-start(f32[4,3136]{1,0:T(4,128)S(1)} %get-tuple-element.129), channel_id=1, source_target_pairs={{0,8},{8,16},{16,24},{24,0},{1,9},{9,17},{17,25},{25,1},{2,10},{10... | collective-permute-start | bytes 150536 | tf_op jit(solution)/shard_map/ppermute | solution.py:29
  274.6 10.4 %collective-permute-start.50 = (f32[4,3136]{1,0:T(4,128)S(1)}, f32[4,3136]{1,0:T(4,128)S(1)}, u32[]{:S(2)}, u32[]{:S(2)}) collective-permute-start(f32[4,3136]{1,0:T(4,128)S(1)} %get-tuple-element.130), channel_id=1, source_target_pairs={{0,8},{8,16},{16,24},{24,0},{1,9},{9,17},{17,25},{25,1},{2,10},{10... | collective-permute-start | bytes 150536 | tf_op jit(solution)/shard_map/ppermute | solution.py:29
  278.3 6.9 %collective-permute-start.49 = (f32[4,3136]{1,0:T(4,128)S(1)}, f32[4,3136]{1,0:T(4,128)S(1)}, u32[]{:S(2)}, u32[]{:S(2)}) collective-permute-start(f32[4,3136]{1,0:T(4,128)S(1)} %get-tuple-element.131), channel_id=1, source_target_pairs={{0,8},{8,16},{16,24},{24,0},{1,9},{9,17},{17,25},{25,1},{2,10},{10... | collective-permute-start | bytes 150536 | tf_op jit(solution)/shard_map/ppermute | solution.py:29
  279.2 6.3 %collective-permute-start.47 = (f32[4,3136]{1,0:T(4,128)S(1)}, f32[4,3136]{1,0:T(4,128)S(1)}, u32[]{:S(2)}, u32[]{:S(2)}) collective-permute-start(f32[4,3136]{1,0:T(4,128)S(1)} %get-tuple-element.132), channel_id=1, source_target_pairs={{0,8},{8,16},{16,24},{24,0},{1,9},{9,17},{17,25},{25,1},{2,10},{10... | collective-permute-start | bytes 150536 | tf_op jit(solution)/shard_map/ppermute | solution.py:29
  280.2 9.7 %collective-permute-start.44 = (f32[4,3136]{1,0:T(4,128)}, f32[4,3136]{1,0:T(4,128)}, u32[]{:S(2)}, u32[]{:S(2)}) collective-permute-start(f32[4,3136]{1,0:T(4,128)} %get-tuple-element.133), channel_id=1, source_target_pairs={{0,8},{8,16},{16,24},{24,0},{1,9},{9,17},{17,25},{25,1},{2,10},{10... | collective-permute-start | bytes 150536 | tf_op jit(solution)/shard_map/ppermute | solution.py:29
  281.4 8.6 %collective-permute-start.42 = (f32[4,3136]{1,0:T(4,128)}, f32[4,3136]{1,0:T(4,128)}, u32[]{:S(2)}, u32[]{:S(2)}) collective-permute-start(f32[4,3136]{1,0:T(4,128)} %get-tuple-element.134), channel_id=1, source_target_pairs={{0,8},{8,16},{16,24},{24,0},{1,9},{9,17},{17,25},{25,1},{2,10},{10... | collective-permute-start | bytes 150536 | tf_op jit(solution)/shard_map/ppermute | solution.py:29
  285.0 8.5 %collective-permute-start.39 = (f32[4,3136]{1,0:T(4,128)}, f32[4,3136]{1,0:T(4,128)}, u32[]{:S(2)}, u32[]{:S(2)}) collective-permute-start(f32[4,3136]{1,0:T(4,128)} %get-tuple-element.135), channel_id=1, source_target_pairs={{0,8},{8,16},{16,24},{24,0},{1,9},{9,17},{17,25},{25,1},{2,10},{10... | collective-permute-start | bytes 150536 | tf_op jit(solution)/shard_map/ppermute | solution.py:29
  285.2 9.6 %collective-permute-start.37 = (f32[4,3136]{1,0:T(4,128)}, f32[4,3136]{1,0:T(4,128)}, u32[]{:S(2)}, u32[]{:S(2)}) collective-permute-start(f32[4,3136]{1,0:T(4,128)} %get-tuple-element.136), channel_id=1, source_target_pairs={{0,2},{2,4},{4,6},{6,0},{1,3},{3,5},{5,7},{7,1},{8,10},{10,12},{12... | collective-permute-start | bytes 150536 | tf_op jit(solution)/shard_map/ppermute | solution.py:29
  285.5 10.7 %collective-permute-start.36 = (f32[4,3136]{1,0:T(4,128)}, f32[4,3136]{1,0:T(4,128)S(1)}, u32[]{:S(2)}, u32[]{:S(2)}) collective-permute-start(f32[4,3136]{1,0:T(4,128)} %get-tuple-element.137), channel_id=1, source_target_pairs={{0,2},{2,4},{4,6},{6,0},{1,3},{3,5},{5,7},{7,1},{8,10},{10,12},{12... | collective-permute-start | bytes 150536 | tf_op jit(solution)/shard_map/ppermute | solution.py:29
  286.8 54.3 %copy-start.93 = (f32[8,256]{1,0:T(8,128)S(1)}, f32[8,256]{1,0:T(8,128)}, u32[]{:S(2)}) copy-start(f32[8,256]{1,0:T(8,128)} %copy-done.92) | copy-start | bytes 24580
  290.0 7.5 %collective-permute-start.34 = (f32[4,3136]{1,0:T(4,128)}, f32[4,3136]{1,0:T(4,128)S(1)}, u32[]{:S(2)}, u32[]{:S(2)}) collective-permute-start(f32[4,3136]{1,0:T(4,128)} %get-tuple-element.138), channel_id=1, source_target_pairs={{0,2},{2,4},{4,6},{6,0},{1,3},{3,5},{5,7},{7,1},{8,10},{10,12},{12... | collective-permute-start | bytes 150536 | tf_op jit(solution)/shard_map/ppermute | solution.py:29
  290.0 8.5 %collective-permute-start.33 = (f32[4,3136]{1,0:T(4,128)S(1)}, f32[4,3136]{1,0:T(4,128)S(1)}, u32[]{:S(2)}, u32[]{:S(2)}) collective-permute-start(f32[4,3136]{1,0:T(4,128)S(1)} %copy-done.90), channel_id=1, source_target_pairs={{0,1},{2,3},{4,5},{6,7},{8,9},{10,11},{12,13},{14,15},{16,17},{18,... | collective-permute-start | bytes 150536 | tf_op jit(solution)/shard_map/ppermute | solution.py:35
  293.4 8.7 %collective-permute-start.32 = (f32[4,3136]{1,0:T(4,128)S(1)}, f32[4,3136]{1,0:T(4,128)S(1)}, u32[]{:S(2)}, u32[]{:S(2)}) collective-permute-start(f32[4,3136]{1,0:T(4,128)S(1)} %copy-done.89), channel_id=1, source_target_pairs={{1,0},{3,2},{5,4},{7,6},{9,8},{11,10},{13,12},{15,14},{17,16},{19,... | collective-permute-start | bytes 150536 | tf_op jit(solution)/shard_map/ppermute | solution.py:35
  294.8 7.4 %collective-permute-start.30 = (f32[4,3136]{1,0:T(4,128)S(1)}, f32[4,3136]{1,0:T(4,128)S(1)}, u32[]{:S(2)}, u32[]{:S(2)}) collective-permute-start(f32[4,3136]{1,0:T(4,128)S(1)} %copy-done.88), channel_id=1, source_target_pairs={{0,6},{2,0},{4,2},{6,4},{1,7},{3,1},{5,3},{7,5},{8,14},{10,8},{12,... | collective-permute-start | bytes 150536 | tf_op jit(solution)/shard_map/ppermute | solution.py:29
  296.3 6.4 %collective-permute-start.29 = (f32[4,3136]{1,0:T(4,128)S(1)}, f32[4,3136]{1,0:T(4,128)S(1)}, u32[]{:S(2)}, u32[]{:S(2)}) collective-permute-start(f32[4,3136]{1,0:T(4,128)S(1)} %copy-done.87), channel_id=1, source_target_pairs={{0,6},{2,0},{4,2},{6,4},{1,7},{3,1},{5,3},{7,5},{8,14},{10,8},{12,... | collective-permute-start | bytes 150536 | tf_op jit(solution)/shard_map/ppermute | solution.py:29
  297.5 6.7 %collective-permute-start.27 = (f32[4,3136]{1,0:T(4,128)S(1)}, f32[4,3136]{1,0:T(4,128)S(1)}, u32[]{:S(2)}, u32[]{:S(2)}) collective-permute-start(f32[4,3136]{1,0:T(4,128)S(1)} %get-tuple-element.143), channel_id=1, source_target_pairs={{0,6},{2,0},{4,2},{6,4},{1,7},{3,1},{5,3},{7,5},{8,14},{10,8},{12,... | collective-permute-start | bytes 150536 | tf_op jit(solution)/shard_map/ppermute | solution.py:29
  298.5 10.2 %collective-permute-start.24 = (f32[4,3136]{1,0:T(4,128)S(1)}, f32[4,3136]{1,0:T(4,128)S(1)}, u32[]{:S(2)}, u32[]{:S(2)}) collective-permute-start(f32[4,3136]{1,0:T(4,128)S(1)} %get-tuple-element.144), channel_id=1, source_target_pairs={{0,24},{8,0},{16,8},{24,16},{1,25},{9,1},{17,9},{25,17},{2,26},{10... | collective-permute-start | bytes 150536 | tf_op jit(solution)/shard_map/ppermute | solution.py:29
  302.1 7.9 %collective-permute-start.7 = (f32[4,3136]{1,0:T(4,128)}, f32[4,3136]{1,0:T(4,128)S(1)}, u32[]{:S(2)}, u32[]{:S(2)}) collective-permute-start(f32[4,3136]{1,0:T(4,128)} %copy-done.154), channel_id=1, source_target_pairs={{0,6},{2,0},{4,2},{6,4},{1,7},{3,1},{5,3},{7,5},{8,14},{10,8},{12,... | collective-permute-start | bytes 150536 | tf_op jit(solution)/shard_map/ppermute | solution.py:29
  302.1 8.7 %collective-permute-start.23 = (f32[4,3136]{1,0:T(4,128)}, f32[4,3136]{1,0:T(4,128)S(1)}, u32[]{:S(2)}, u32[]{:S(2)}) collective-permute-start(f32[4,3136]{1,0:T(4,128)} %copy-done.153), channel_id=1, source_target_pairs={{0,2},{2,4},{4,6},{6,0},{1,3},{3,5},{5,7},{7,1},{8,10},{10,12},{12... | collective-permute-start | bytes 150536 | tf_op jit(solution)/shard_map/ppermute | solution.py:29
  302.7 8.5 %collective-permute-start.20 = (f32[4,3136]{1,0:T(4,128)}, f32[4,3136]{1,0:T(4,128)S(1)}, u32[]{:S(2)}, u32[]{:S(2)}) collective-permute-start(f32[4,3136]{1,0:T(4,128)} %copy-done.143), channel_id=1, source_target_pairs={{0,2},{2,4},{4,6},{6,0},{1,3},{3,5},{5,7},{7,1},{8,10},{10,12},{12... | collective-permute-start | bytes 150536 | tf_op jit(solution)/shard_map/ppermute | solution.py:29
  304.2 7.6 %collective-permute-start.18 = (f32[4,3136]{1,0:T(4,128)S(1)}, f32[4,3136]{1,0:T(4,128)S(1)}, u32[]{:S(2)}, u32[]{:S(2)}) collective-permute-start(f32[4,3136]{1,0:T(4,128)S(1)} %copy-done.142), channel_id=1, source_target_pairs={{0,1},{2,3},{4,5},{6,7},{8,9},{10,11},{12,13},{14,15},{16,17},{18,... | collective-permute-start | bytes 150536 | tf_op jit(solution)/shard_map/ppermute | solution.py:35
  308.7 6.0 %collective-permute-start.15 = (f32[4,3136]{1,0:T(4,128)S(1)}, f32[4,3136]{1,0:T(4,128)S(1)}, u32[]{:S(2)}, u32[]{:S(2)}) collective-permute-start(f32[4,3136]{1,0:T(4,128)S(1)} %copy-done.145), channel_id=1, source_target_pairs={{1,0},{3,2},{5,4},{7,6},{9,8},{11,10},{13,12},{15,14},{17,16},{19,... | collective-permute-start | bytes 150536 | tf_op jit(solution)/shard_map/ppermute | solution.py:35
  310.0 4.7 collective-permute-start.12
  310.8 6.7 %collective-permute-start.10 = (f32[4,3136]{1,0:T(4,128)}, f32[4,3136]{1,0:T(4,128)S(1)}, u32[]{:S(2)}, u32[]{:S(2)}) collective-permute-start(f32[4,3136]{1,0:T(4,128)} %copy-done.151), channel_id=1, source_target_pairs={{0,6},{2,0},{4,2},{6,4},{1,7},{3,1},{5,3},{7,5},{8,14},{10,8},{12,... | collective-permute-start | bytes 150536 | tf_op jit(solution)/shard_map/ppermute | solution.py:29
  311.2 7.7 %collective-permute-start.58 = (f32[4,3136]{1,0:T(4,128)}, f32[4,3136]{1,0:T(4,128)S(1)}, u32[]{:S(2)}, u32[]{:S(2)}) collective-permute-start(f32[4,3136]{1,0:T(4,128)} %copy-done.152), channel_id=1, source_target_pairs={{0,2},{2,4},{4,6},{6,0},{1,3},{3,5},{5,7},{7,1},{8,10},{10,12},{12... | collective-permute-start | bytes 150536 | tf_op jit(solution)/shard_map/ppermute | solution.py:29
  311.8 8.9 %collective-permute-start.56 = (f32[4,3136]{1,0:T(4,128)S(1)}, f32[4,3136]{1,0:T(4,128)S(1)}, u32[]{:S(2)}, u32[]{:S(2)}) collective-permute-start(f32[4,3136]{1,0:T(4,128)S(1)} %collective-permute-done.55), channel_id=1, source_target_pairs={{0,2},{2,4},{4,6},{6,0},{1,3},{3,5},{5,7},{7,1},{8,10},{10,12},{12... | collective-permute-start | bytes 150536 | tf_op jit(solution)/shard_map/ppermute | solution.py:29
  314.7 6.1 %collective-permute-start.53 = (f32[4,3136]{1,0:T(4,128)S(1)}, f32[4,3136]{1,0:T(4,128)S(1)}, u32[]{:S(2)}, u32[]{:S(2)}) collective-permute-start(f32[4,3136]{1,0:T(4,128)S(1)} %copy-done.147), channel_id=1, source_target_pairs={{0,2},{2,4},{4,6},{6,0},{1,3},{3,5},{5,7},{7,1},{8,10},{10,12},{12... | collective-permute-start | bytes 150536 | tf_op jit(solution)/shard_map/ppermute | solution.py:29
  314.8 7.1 %collective-permute-start.51 = (f32[4,3136]{1,0:T(4,128)S(1)}, f32[4,3136]{1,0:T(4,128)S(1)}, u32[]{:S(2)}, u32[]{:S(2)}) collective-permute-start(f32[4,3136]{1,0:T(4,128)S(1)} %copy-done.149), channel_id=1, source_target_pairs={{0,1},{2,3},{4,5},{6,7},{8,9},{10,11},{12,13},{14,15},{16,17},{18,... | collective-permute-start | bytes 150536 | tf_op jit(solution)/shard_map/ppermute | solution.py:35
  317.5 8.6 %collective-permute-start.48 = (f32[4,3136]{1,0:T(4,128)S(1)}, f32[4,3136]{1,0:T(4,128)S(1)}, u32[]{:S(2)}, u32[]{:S(2)}) collective-permute-start(f32[4,3136]{1,0:T(4,128)S(1)} %copy-done.156), channel_id=1, source_target_pairs={{1,0},{3,2},{5,4},{7,6},{9,8},{11,10},{13,12},{15,14},{17,16},{19,... | collective-permute-start | bytes 150536 | tf_op jit(solution)/shard_map/ppermute | solution.py:35
  318.9 8.6 %collective-permute-start.45 = (f32[4,3136]{1,0:T(4,128)}, f32[4,3136]{1,0:T(4,128)S(1)}, u32[]{:S(2)}, u32[]{:S(2)}) collective-permute-start(f32[4,3136]{1,0:T(4,128)} %collective-permute-done.44), channel_id=1, source_target_pairs={{0,6},{2,0},{4,2},{6,4},{1,7},{3,1},{5,3},{7,5},{8,14},{10,8},{12,... | collective-permute-start | bytes 150536 | tf_op jit(solution)/shard_map/ppermute | solution.py:29
  320.8 11.7 %collective-permute-start.43 = (f32[4,3136]{1,0:T(4,128)}, f32[4,3136]{1,0:T(4,128)S(1)}, u32[]{:S(2)}, u32[]{:S(2)}) collective-permute-start(f32[4,3136]{1,0:T(4,128)} %collective-permute-done.42), channel_id=1, source_target_pairs={{0,6},{2,0},{4,2},{6,4},{1,7},{3,1},{5,3},{7,5},{8,14},{10,8},{12,... | collective-permute-start | bytes 150536 | tf_op jit(solution)/shard_map/ppermute | solution.py:29
  320.9 12.9 %collective-permute-start.40 = (f32[4,3136]{1,0:T(4,128)}, f32[4,3136]{1,0:T(4,128)S(1)}, u32[]{:S(2)}, u32[]{:S(2)}) collective-permute-start(f32[4,3136]{1,0:T(4,128)} %collective-permute-done.39), channel_id=1, source_target_pairs={{0,6},{2,0},{4,2},{6,4},{1,7},{3,1},{5,3},{7,5},{8,14},{10,8},{12,... | collective-permute-start | bytes 150536 | tf_op jit(solution)/shard_map/ppermute | solution.py:29
  321.9 12.0 %collective-permute-start.38 = (f32[4,3136]{1,0:T(4,128)}, f32[4,3136]{1,0:T(4,128)S(1)}, u32[]{:S(2)}, u32[]{:S(2)}) collective-permute-start(f32[4,3136]{1,0:T(4,128)} %collective-permute-done.37), channel_id=1, source_target_pairs={{0,1},{2,3},{4,5},{6,7},{8,9},{10,11},{12,13},{14,15},{16,17},{18,... | collective-permute-start | bytes 150536 | tf_op jit(solution)/shard_map/ppermute | solution.py:35
  326.2 9.0 %collective-permute-start.35 = (f32[4,3136]{1,0:T(4,128)S(1)}, f32[4,3136]{1,0:T(4,128)S(1)}, u32[]{:S(2)}, u32[]{:S(2)}) collective-permute-start(f32[4,3136]{1,0:T(4,128)S(1)} %collective-permute-done.34), channel_id=1, source_target_pairs={{1,0},{3,2},{5,4},{7,6},{9,8},{11,10},{13,12},{15,14},{17,16},{19,... | collective-permute-start | bytes 150536 | tf_op jit(solution)/shard_map/ppermute | solution.py:35
  327.5 9.0 %collective-permute-start.31 = (f32[4,3136]{1,0:T(4,128)S(1)}, f32[4,3136]{1,0:T(4,128)S(1)}, u32[]{:S(2)}, u32[]{:S(2)}) collective-permute-start(f32[4,3136]{1,0:T(4,128)S(1)} %collective-permute-done.30), channel_id=1, source_target_pairs={{0,1},{2,3},{4,5},{6,7},{8,9},{10,11},{12,13},{14,15},{16,17},{18,... | collective-permute-start | bytes 150536 | tf_op jit(solution)/shard_map/ppermute | solution.py:35
  332.5 9.0 %collective-permute-start.28 = (f32[4,3136]{1,0:T(4,128)S(1)}, f32[4,3136]{1,0:T(4,128)S(1)}, u32[]{:S(2)}, u32[]{:S(2)}) collective-permute-start(f32[4,3136]{1,0:T(4,128)S(1)} %collective-permute-done.27), channel_id=1, source_target_pairs={{1,0},{3,2},{5,4},{7,6},{9,8},{11,10},{13,12},{15,14},{17,16},{19,... | collective-permute-start | bytes 150536 | tf_op jit(solution)/shard_map/ppermute | solution.py:35
  333.8 9.2 %collective-permute-start.25 = (f32[4,3136]{1,0:T(4,128)S(1)}, f32[4,3136]{1,0:T(4,128)S(1)}, u32[]{:S(2)}, u32[]{:S(2)}) collective-permute-start(f32[4,3136]{1,0:T(4,128)S(1)} %collective-permute-done.24), channel_id=1, source_target_pairs={{0,2},{2,4},{4,6},{6,0},{1,3},{3,5},{5,7},{7,1},{8,10},{10,12},{12... | collective-permute-start | bytes 150536 | tf_op jit(solution)/shard_map/ppermute | solution.py:29
  333.9 10.4 %collective-permute-start.8 = (f32[4,3136]{1,0:T(4,128)S(1)}, f32[4,3136]{1,0:T(4,128)S(1)}, u32[]{:S(2)}, u32[]{:S(2)}) collective-permute-start(f32[4,3136]{1,0:T(4,128)S(1)} %collective-permute-done.7), channel_id=1, source_target_pairs={{1,0},{3,2},{5,4},{7,6},{9,8},{11,10},{13,12},{15,14},{17,16},{19,... | collective-permute-start | bytes 150536 | tf_op jit(solution)/shard_map/ppermute | solution.py:35
  335.2 13.7 %collective-permute-start.21 = (f32[4,3136]{1,0:T(4,128)S(1)}, f32[4,3136]{1,0:T(4,128)S(1)}, u32[]{:S(2)}, u32[]{:S(2)}) collective-permute-start(f32[4,3136]{1,0:T(4,128)S(1)} %collective-permute-done.20), channel_id=1, source_target_pairs={{1,0},{3,2},{5,4},{7,6},{9,8},{11,10},{13,12},{15,14},{17,16},{19,... | collective-permute-start | bytes 150536 | tf_op jit(solution)/shard_map/ppermute | solution.py:35
  336.5 13.7 %collective-permute-start.13 = (f32[4,3136]{1,0:T(4,128)S(1)}, f32[4,3136]{1,0:T(4,128)S(1)}, u32[]{:S(2)}, u32[]{:S(2)}) collective-permute-start(f32[4,3136]{1,0:T(4,128)S(1)} %collective-permute-done.12), channel_id=1, source_target_pairs={{0,1},{2,3},{4,5},{6,7},{8,9},{10,11},{12,13},{14,15},{16,17},{18,... | collective-permute-start | bytes 150536 | tf_op jit(solution)/shard_map/ppermute | solution.py:35
  341.6 14.3 %collective-permute-start.59 = (f32[4,3136]{1,0:T(4,128)S(1)}, f32[4,3136]{1,0:T(4,128)S(1)}, u32[]{:S(2)}, u32[]{:S(2)}) collective-permute-start(f32[4,3136]{1,0:T(4,128)S(1)} %collective-permute-done.58), channel_id=1, source_target_pairs={{0,1},{2,3},{4,5},{6,7},{8,9},{10,11},{12,13},{14,15},{16,17},{18,... | collective-permute-start | bytes 150536 | tf_op jit(solution)/shard_map/ppermute | solution.py:35
  343.0 12.8 %collective-permute-start.54 = (f32[4,3136]{1,0:T(4,128)S(1)}, f32[4,3136]{1,0:T(4,128)S(1)}, u32[]{:S(2)}, u32[]{:S(2)}) collective-permute-start(f32[4,3136]{1,0:T(4,128)S(1)} %collective-permute-done.53), channel_id=1, source_target_pairs={{1,0},{3,2},{5,4},{7,6},{9,8},{11,10},{13,12},{15,14},{17,16},{19,... | collective-permute-start | bytes 150536 | tf_op jit(solution)/shard_map/ppermute | solution.py:35
  344.3 11.5 %collective-permute-start.46 = (f32[4,3136]{1,0:T(4,128)S(1)}, f32[4,3136]{1,0:T(4,128)S(1)}, u32[]{:S(2)}, u32[]{:S(2)}) collective-permute-start(f32[4,3136]{1,0:T(4,128)S(1)} %collective-permute-done.45), channel_id=1, source_target_pairs={{0,1},{2,3},{4,5},{6,7},{8,9},{10,11},{12,13},{14,15},{16,17},{18,... | collective-permute-start | bytes 150536 | tf_op jit(solution)/shard_map/ppermute | solution.py:35
  348.9 7.0 %collective-permute-start.41 = (f32[4,3136]{1,0:T(4,128)S(1)}, f32[4,3136]{1,0:T(4,128)S(1)}, u32[]{:S(2)}, u32[]{:S(2)}) collective-permute-start(f32[4,3136]{1,0:T(4,128)S(1)} %collective-permute-done.40), channel_id=1, source_target_pairs={{1,0},{3,2},{5,4},{7,6},{9,8},{11,10},{13,12},{15,14},{17,16},{19,... | collective-permute-start | bytes 150536 | tf_op jit(solution)/shard_map/ppermute | solution.py:35
  350.2 6.3 %collective-permute-start.26 = (f32[4,3136]{1,0:T(4,128)S(1)}, f32[4,3136]{1,0:T(4,128)S(1)}, u32[]{:S(2)}, u32[]{:S(2)}) collective-permute-start(f32[4,3136]{1,0:T(4,128)S(1)} %collective-permute-done.25), channel_id=1, source_target_pairs={{0,1},{2,3},{4,5},{6,7},{8,9},{10,11},{12,13},{14,15},{16,17},{18,... | collective-permute-start | bytes 150536 | tf_op jit(solution)/shard_map/ppermute | solution.py:35
  (169 other events, 1389.5 us)
Sparse Core Ops, SparseCore 0:
  371.5 196.8 all-reduce.19
where the time goes:
time: 596 us; the launch traced here: 589 us
  waiting for transfers between devices  179 us (30%)
  local copies, waits for them, and re-layouts  109 us (18%)
  matrix products  97 us (16%)
  starting transfers between devices  86.7 us (15%)
  other arithmetic  60.3 us (10%)
  blocking collectives  40.3 us (7%)
  between operations  17 us (3%)
    psum x1, waiting for transfers between devices, per_device(): summed = lax.psum(partial_grads, ('gx', 'gy', 'gz'))  150 us
    dot_general x66, matrix products, matmul(): jnp.dot(left, right, precision=HIGHEST, preferred_element_type=jnp.float32)  74.1 us
    ppermute x18, starting transfers between devices, passed_along(): return lax.ppermute(x, axis, pairs)  46.2 us
    psum x1, blocking collectives, per_device(): summed = lax.psum(partial_grads, ('gx', 'gy', 'gz'))  40.3 us
    ppermute x36, starting transfers between devices, from_behind(): return lax.ppermute(value, axis, pairs)  32.8 us
    unnamed x355, local copies, waits for them, and re-layouts  23.2 us
    ppermute x3, waiting for transfers between devices, with_halo(): before = lax.ppermute(last, axis, up)  15.5 us
    dot_general x2, matrix products, local_finish(): jnp.einsum('ejc,ejf->ecf', quad_basis, quad_table[quad_index], precision=...  14.5 us
  transfers between devices with their start and end apart: 61, of which 10 were waited for; matrix products, arithmetic and copies ran while one was open for 4% of the time, Pallas kernels for 0%

commit v1 on v0

v1 whole, which is shorter than its diff:
```python
import functools
import math

import jax
import jax.numpy as jnp
from jax import lax
from jax.experimental import pallas as pl
from jax.experimental.pallas import tpu as pltpu
from jax.sharding import Mesh
from jax.sharding import PartitionSpec as P

BF = jnp.bfloat16
F32 = jnp.float32
ROWS = ("gx", "gyh", "gyl", "gz")
GY = ("gyh", "gyl")
ATOMS, SEND, SLOTS, EDGES = 8, 4, 30, 240
ATOM_W, EDGE_W, TRIP_W, QUAD_W, RADIAL = 256, 512, 64, 32, 128
ANGLES, PICKS = 16, 8
PAIRS = 17
BLOCK = 16
BLOCKS = EDGES // BLOCK
root_half = 0.7071067811865476
NN = (((1,), (0,)), ((), ()))
NT = (((1,), (1,)), ((), ()))
TN = (((0,), (0,)), ((), ()))


def shifted(value, axis, steps, wrap):
    count = lax.axis_size(axis)
    pairs = [(i, (i + steps) % count) for i in range(count) if wrap or 0 <= i + steps < count]
    return lax.ppermute(value, axis, pairs)


def planes_of(value):
    if lax.axis_size("gz") == 2:
        other = lax.ppermute(value, "gz", [(0, 1), (1, 0)])
        top = lax.axis_index("gz") == 1
        return jnp.stack([jnp.where(top, other, value), jnp.where(top, value, other)])
    return jnp.stack([shifted(value, "gz", 1, False), value, shifted(value, "gz", -1, False)])


def with_halo(value):
    value = planes_of(value)
    value = jnp.concatenate([shifted(value, "gx", 1, True), value, shifted(value, "gx", -1, True)])
    return shifted(value, GY, 1, True), value, shifted(value, GY, -1, True)


def bits_of(axis):
    count = lax.axis_size(axis)
    return [(axis, b) for b in range(count.bit_length() - 1)]


def swap(value, axis, bit):
    count = lax.axis_size(axis)
    return lax.ppermute(value, axis, [(i, i ^ (1 << bit)) for i in range(count)])


def bit_value(axis, bit):
    return (lax.axis_index(axis) >> bit) & 1


def part(arrays, at, size):
    total = lax.dynamic_slice_in_dim(arrays[0], at, size)
    for x in arrays[1:]:
        total = total + lax.dynamic_slice_in_dim(x, at, size)
    return total


class Chain:
    def __init__(self):
        self.last = None

    def after(self, values):
        if self.last is not None:
            self.last, values = lax.optimization_barrier((self.last, values))
        return values

    def step(self, value):
        self.last = value
        return value


def halved(chain, arrays, axis, bit):
    arrays = chain.after(arrays)
    half = arrays[0].shape[0] // 2
    one = bit_value(axis, bit)
    send = chain.step(part(arrays, (1 - one) * half, half))
    got = swap(send, axis, bit)
    send, arrays = lax.optimization_barrier((send, arrays))
    return [part(arrays, one * half, half), got]


def joined_halves(value, other, axis, bit):
    one = bit_value(axis, bit) == 1
    return jnp.concatenate([jnp.where(one, other, value), jnp.where(one, value, other)])


def reduction(chain, first, second):
    across, along = bits_of("gz"), bits_of("gyh")
    lanes = [first, second]
    for plan in ((across, along), (along, across)):
        for i in range(2):
            for axis, bit in plan[i]:
                lanes[i] = halved(chain, lanes[i], axis, bit)
        yield
    sizes = [x[0].shape[0] for x in lanes]
    joint = [jnp.concatenate(pair) for pair in zip(*chain.after(lanes))]
    for axis, bit in bits_of("gx"):
        joint = halved(chain, joint, axis, bit)
        yield
    joint = chain.after(joint)
    value = chain.step(sum(joint[1:], joint[0]))
    for axis, bit in bits_of("gx")[::-1]:
        other = swap(value, axis, bit)
        yield
        value, other = chain.after((value, other))
        value = chain.step(joined_halves(value, other, axis, bit))
    values = [value[: sizes[0]], value[sizes[0] :]]
    for plan in ((along, across), (across, along)):
        for turn in range(max(len(across), len(along))):
            others = [None, None]
            for i in range(2):
                if turn < len(plan[i]):
                    others[i] = swap(values[i], *plan[i][::-1][turn])
            yield
            for i in range(2):
                if turn < len(plan[i]):
                    values[i], others[i] = chain.after((values[i], others[i]))
                    values[i] = chain.step(joined_halves(values[i], others[i], *plan[i][::-1][turn]))
    others = [swap(x, "gyl", 0) for x in values]
    yield
    values, others = chain.after((values, others))
    return [(value, chain.step(other)) for value, other in zip(values, others)]


def iota(shape, dim):
    return lax.broadcasted_iota(jnp.int32, shape, dim)


def dot(left, right, dims=NN):
    return lax.dot_general(left, right, dims, preferred_element_type=F32)


def halves(x):
    high = x.astype(BF)
    return high, (x - high.astype(F32)).astype(BF)


def stacked(x):
    high, low = halves(x)
    if x.shape[0] % 16 == 0:
        return jnp.concatenate([high, low], axis=0)
    return jnp.concatenate([high.astype(F32), low.astype(F32)], axis=0).astype(BF)


def folded(x):
    half = x.shape[0] // 2
    return x[:half] + x[half:]


def times(x, weight, dims=NN):
    return folded(dot(stacked(x), weight, dims))


def side_by_side(x):
    return jnp.concatenate(halves(x), axis=1)


def side_sum(x):
    half = x.shape[1] // 2
    return x[:, :half] + x[:, half:]


def weight_grad(x, y):
    x_high, x_low = halves(x)
    y_high, y_low = halves(y)
    left, right = [x_high, x_high, x_low], [y_high, y_low, y_high]
    if x.shape[0] % 16 == 0:
        return dot(jnp.concatenate(left, axis=0), jnp.concatenate(right, axis=0), TN)
    left = jnp.concatenate([p.astype(F32) for p in left], axis=0).astype(BF)
    right = jnp.concatenate([p.astype(F32) for p in right], axis=0).astype(BF)
    return dot(left, right, TN)


def onehot(hit):
    return jnp.where(hit, 1.0, 0.0).astype(BF)


def sigmoid(v):
    return 1.0 / (1.0 + jnp.exp(-v))


def act(v):
    return v * sigmoid(v) * (1.0 / 0.6)


def act_and_slope(v):
    s = sigmoid(v)
    return v * s * (1.0 / 0.6), s * (1.0 + v * (1.0 - s)) * (1.0 / 0.6)


def sin_pi(t):
    n = jnp.floor(t + 0.5)
    r = t - n
    odd = n - 2.0 * jnp.floor(n * 0.5)
    q = r * r
    total = jnp.zeros_like(r)
    for k in range(6, -1, -1):
        total = total * q + (-1.0) ** k * math.pi ** (2 * k + 1) / math.factorial(2 * k + 1)
    return total * r * (1.0 - 2.0 * odd)


def to_column(row):
    n = row.shape[1]
    same = iota((n, n), 0) == iota((n, n), 1)
    return jnp.sum(jnp.where(same, row, jnp.zeros_like(row)), axis=1, keepdims=True)


def send_column(send, rows):
    shape = (rows, SEND)
    hit = (iota(shape, 0) & (SEND - 1)) == iota(shape, 1)
    return jnp.sum(jnp.where(hit, send, 0), axis=1, keepdims=True)


def send_lanes(send):
    shape = (8, 128)
    hit = iota(shape, 0) == (iota(shape, 1) & (SEND - 1))
    return jnp.sum(jnp.where(hit, send_column(send, 8), 0), axis=0, keepdims=True)


def paid(row, send):
    edge = send * SLOTS + 2 * (row >> 3) + ((row >> 2) & 1)
    return jnp.where(row < 120, edge, -1)


def atom_of(edge):
    total = jnp.zeros_like(edge)
    for a in range(1, ATOMS):
        total = total + jnp.where(edge >= a * SLOTS, 1, 0)
    return total


def radial_of(length):
    x = length / 12.0
    x2 = x * x
    x4 = x2 * x2
    envelope = 1.0 - 28.0 * (x4 * x2) + 48.0 * (x4 * x2 * x) - 21.0 * (x4 * x4)
    orders = (iota((1, RADIAL), 1) + 1).astype(F32)
    return envelope * sin_pi(x * orders) / x


def geometry(unit):
    own = atom_of(iota((8, EDGES), 1)) == iota((8, EDGES), 0)
    edge = iota((EDGES, 128), 0)
    slot = edge - atom_of(edge) * SLOTS
    total = jnp.zeros((24, 128), F32)
    for k in range(3):
        x = jnp.where(own, unit[k : k + 1, :], 0.0)
        high = x.astype(BF).astype(F32)
        mid = (x - high).astype(BF).astype(F32)
        parts = jnp.concatenate([high, mid, x - high - mid], axis=0).astype(BF)
        total = total + dot(parts, onehot(iota((EDGES, 128), 1) == slot + 32 * k))
    return total[0:8] + total[8:16] + total[16:24]


def local_rows(index):
    return (index & 7) * SLOTS + 2 * (index >> 4) + ((index >> 3) & 1)


def start_kernel(
    edge, vec, mask, hidden, tag_row, send_row, table, w_in, w_rad, w_trip, w_quad,
    payload, local, tagged, pre, downs, rads, radial_out, columns,
):
    vectors = vec[...]
    length = jnp.sqrt(jnp.sum(vectors * vectors, axis=0, keepdims=True))
    unit = vectors / length
    geo = geometry(unit)
    live = to_column(jnp.where(mask[...] > 0, 1.0, 0.0))
    parts = [live] + [to_column(unit[k : k + 1, :]) for k in range(3)]
    columns[...] = jnp.concatenate(parts + [jnp.zeros((EDGES, 124), F32)], axis=1)
    send = send_column(send_row[...], 8)
    pay = paid(iota((128, 1), 0), send_column(send_row[...], 128))
    tags = to_column(tag_row[...])
    radial = radial_of(to_column(length))
    radial_out[...] = radial
    split = stacked(radial)
    for k in range(5):
        rads[k] = folded(dot(split, w_rad[k]))
    split = stacked(edge[...])
    pre[0] = folded(dot(split, w_in[0]))
    pre[1] = folded(dot(split, w_in[1]))
    trip_pre = times(act(pre[0]) * rads[0], w_trip[...], NT)
    quad_pre = times(act(pre[1]) * rads[1], w_quad[...], NT)
    downs[...] = jnp.concatenate([trip_pre, quad_pre, jnp.zeros((EDGES, 32), F32)], axis=1)
    trip = act(trip_pre) * live
    quad = act(quad_pre) * live
    rows = jnp.concatenate([trip, quad * radial[:, 0:1], quad * radial[:, 1:2]], axis=1)
    rows = side_by_side(rows)
    shape = (EDGES, EDGES)
    place = onehot(local_rows(iota(shape, 0)) == iota(shape, 1))
    local[0:15] = side_sum(dot(place, rows)).reshape(15, 16, 128)
    place = onehot(pay == iota((128, EDGES), 1))
    payload[0:16] = side_sum(dot(place, rows)).reshape(16, 8, 128)
    tag = hidden[...]
    for t in range(3):
        tag = tag + jnp.where(tags == t, table[t : t + 1, :].astype(F32), 0.0)
    tagged[...] = tag
    local[15] = jnp.concatenate([tag[:, :128], tag[:, 128:]], axis=0)
    local[16] = jnp.concatenate([geo, jnp.zeros((8, 128), F32)], axis=0)
    both = jnp.concatenate([tag, geo], axis=1)
    sent = jnp.zeros((8, 384), F32)
    for a in range(ATOMS):
        sent = sent + jnp.where(send == a, both[a : a + 1, :], 0.0)
    payload[15] = jnp.where(iota((8, 128), 0) < 4, sent[:, :128], sent[:, 128:256])
    payload[16] = sent[:, 256:]


def split_cores(core, whole, keep, send):
    half = whole.shape[0] // 2
    upper = core[0] == 1
    low, high = whole[:half], whole[half:]
    keep[...] = jnp.where(upper, high, low)
    send[...] = jnp.where(upper, low, high)


def segments(shape, edge_dim, atom_dim):
    edge, atom = iota(shape, edge_dim), iota(shape, atom_dim) & 7
    return onehot((edge >= atom * SLOTS) & (edge < atom * SLOTS + SLOTS))


def legendre(cosine):
    before, now = jnp.ones_like(cosine), cosine
    yield before
    yield now
    for k in range(1, ANGLES - 1):
        before, now = now, ((2 * k + 1) / (k + 1)) * cosine * now - (k / (k + 1)) * before
        yield now


def main_kernel(
    halo_before, halo_here, halo_after, local, tagged, edge, columns, rads, radial,
    src_cols, slots, marks,
    trip_bil, trip_up, quad_bil, quad_up, w_ae, w_res, w_ea, w_ad,
    cot_atoms, cot_edges, cot_energy, core,
    atoms_out, edges_out, energy_out, grad_edges, grad_tag,
    cosines, grad_sums, grad_src, keep, send, grad_rads, atom_rows, quad_up_grad,
    table, sums, weight, kept, cos_table, first,
):
    live = columns[:, 0:1]
    halos = (halo_before, halo_here, halo_after)
    group = halo_here.shape[0] * 8
    depth = 3 * group + 16
    lanes = iota((EDGES, depth), 1)
    place = jnp.concatenate(
        [onehot(src_cols[:, 0:1] == lanes), onehot(src_cols[:, 1:2] == lanes)], axis=0
    )

    def rows_at(p):
        parts = [h[:, p].reshape(group, 128) for h in halos]
        return jnp.concatenate(parts + [local[p]], axis=0)

    def gather_pair(p, carry):
        got = dot(place, side_by_side(rows_at(p))).astype(BF)
        table[2 * p] = got[:EDGES]
        table[2 * p + 1] = got[EDGES:]
        return carry

    lax.fori_loop(0, 16, gather_pair, 0)

    rows = rows_at(16)
    high, low = halves(rows)
    rest = (rows - high.astype(F32) - low.astype(F32)).astype(BF)
    got = dot(place[:EDGES], jnp.concatenate([high, low, rest], axis=1))
    got = got[:, :128] + got[:, 128:256] + got[:, 256:]
    cos_table[...] = -(
        columns[:, 1:2] * got
        + columns[:, 2:3] * pltpu.roll(got, 96, 1)
        + columns[:, 3:4] * pltpu.roll(got, 64, 1)
    )

    for k in range(ANGLES):
        top = trip_bil[:, k * 64 : k * 64 + 64].astype(F32)
        top = jnp.concatenate([top, jnp.zeros((64, 64), F32)], axis=1)
        low_left = quad_bil[:, k * 32 : k * 32 + 32].astype(F32)
        low_right = quad_bil[:, 512 + k * 32 : 544 + k * 32].astype(F32)
        bottom = jnp.concatenate([jnp.zeros((32, 64), F32), low_left, low_right], axis=1)
        piece = jnp.concatenate([top, bottom, jnp.zeros((32, 128), F32)], axis=0)
        weight[:, k * 128 : (k + 1) * 128] = piece.astype(BF)

    trip_lanes = iota((128, 128), 1) < TRIP_W
    scale = 1.0 / math.sqrt(PICKS)

    def basis_block(b, carry):
        at = pl.multiple_of(b * BLOCK, BLOCK)
        own = pl.ds(at, BLOCK)
        wide = iota((BLOCK, 512), 1)
        mark = marks[own, :]
        hits = [jnp.where(mark[:, t : t + 1] == wide, 1.0, 0.0) for t in range(2 * PICKS)]
        hits = jnp.concatenate(hits, axis=0).astype(BF)
        got = side_sum(dot(hits, table[:, own, :].reshape(512, 256)))
        picked = jnp.where(trip_lanes, got[:128], got[128:]) * scale
        picked = picked.reshape(PICKS, BLOCK, 128)
        cos_here = cos_table[own, :]
        slot = slots[own, :]
        low_lanes = iota((BLOCK, 128), 1) < TRIP_W
        for h in range(2):
            rows = slice(8 * h, 8 * h + 8)
            cos = []
            for j in range(PICKS):
                index = jnp.where(
                    low_lanes[rows], slot[rows, j : j + 1], slot[rows, PICKS + j : PICKS + j + 1]
                )
                cos.append(jnp.take_along_axis(cos_here[rows], index, axis=1))
            cos = jnp.stack(cos)
            cosines[2 * b + h] = cos
            values = picked[:, rows]
            for k, poly in enumerate(legendre(cos)):
                sums[pl.ds(pl.multiple_of(at + 8 * h, 8), 8), k * 128 : (k + 1) * 128] = jnp.sum(
                    poly * values, axis=0
                )
        return carry

    lax.fori_loop(0, BLOCKS, basis_block, 0)

    down = times(sums[...], weight[...], NT)
    down_act, down_slope = act_and_slope(down)
    trip_h, quad_h = down_act[:, :64], down_act[:, 64:96]
    trip_pre = times(trip_h, trip_up[...])
    quad_pre = times(quad_h, quad_up[...])
    src = jnp.concatenate(
        [side_sum(table[30].astype(F32)), side_sum(table[31].astype(F32))], axis=1
    )
    target = times(tagged[...], w_ae[1])
    spread = segments((EDGES, 16), 0, 1)
    gathers = segments((8, EDGES), 1, 0)

    def to_edges(x):
        return dot(spread, stacked(x))

    def to_atoms(x):
        return side_sum(dot(gathers, side_by_side(x)))

    atom_pre = times(src, w_ae[0]) + to_edges(target)
    atom_act, atom_slope = act_and_slope(atom_pre)
    trip_act, trip_slope = act_and_slope(trip_pre)
    quad_act, quad_slope = act_and_slope(quad_pre)
    merged = (edge[...] + trip_act + quad_act + atom_act * rads[2]) * 0.5
    kept[0] = merged
    first_act, first_slope = act_and_slope(times(merged, w_res[0]))
    kept[1] = first_act
    second_act, second_slope = act_and_slope(times(first_act, w_res[1]))
    new_edges = (merged + second_act) * root_half
    edges_out[...] = new_edges
    weighted = new_edges * live
    root_slots = 1.0 / math.sqrt(SLOTS)
    gathered = to_atoms(weighted * rads[3]) * root_slots
    summary = to_atoms(weighted * rads[4]) * root_slots
    gate_act, gate_slope = act_and_slope(times(gathered, w_ea[0]))
    updated = (tagged[...] + gate_act) * root_half
    a0_act, a0_slope = act_and_slope(times(updated, w_ad[0]))
    a1_act, a1_slope = act_and_slope(times(a0_act, w_ad[1]))
    new_atoms = (updated + a1_act) * root_half
    atoms_out[...] = new_atoms
    e_act, e_slope = act_and_slope(times(summary, w_ea[1]) + times(new_atoms, w_ad[2]))
    out_act, out_slope = act_and_slope(times(e_act, w_ad[3]))
    energy_out[...] = out_act

    d_out = cot_energy[...] * out_slope
    d_e = times(d_out, w_ad[3], NT) * e_slope
    d_summary = times(d_e, w_ea[1], NT)
    d_atoms = (cot_atoms[...] + times(d_e, w_ad[2], NT)) * root_half
    d_a1 = d_atoms * a1_slope
    d_a0 = times(d_a1, w_ad[1], NT) * a0_slope
    d_updated = (d_atoms + times(d_a0, w_ad[0], NT)) * root_half
    d_gate = d_updated * gate_slope
    d_gathered = times(d_gate, w_ea[0], NT)

    d_gathered = to_edges(d_gathered * root_slots)
    d_summary = to_edges(d_summary * root_slots)
    grad_rads[1] = weighted * d_gathered
    grad_rads[2] = weighted * d_summary
    d_new = cot_edges[...] + live * (d_gathered * rads[3] + d_summary * rads[4])
    d_new = d_new * root_half
    d_second = d_new * second_slope
    kept[3] = d_second
    d_first = times(d_second, w_res[1], NT) * first_slope
    kept[2] = d_first
    d_merged = (d_new + times(d_first, w_res[0], NT)) * 0.5
    grad_edges[...] = d_merged
    grad_rads[0] = d_merged * atom_act
    d_atom = d_merged * rads[2] * atom_slope
    kept[4] = d_atom
    d_trip = d_merged * trip_slope
    d_quad = d_merged * quad_slope
    d_target = to_atoms(d_atom)
    grad_tag[...] = d_updated + times(d_target, w_ae[1], NT)
    d_down = jnp.concatenate(
        [times(d_trip, trip_up[...], NT), times(d_quad, quad_up[...], NT), jnp.zeros((EDGES, 32), F32)],
        axis=1,
    )
    d_down = d_down * down_slope
    grad_src[...] = times(d_atom, w_ae[0], NT)

    first[0:512] = weight_grad(kept[0], kept[2])
    first[512:768] = weight_grad(src, kept[4])
    first[896:1408] = weight_grad(kept[1], kept[3])
    first[1408:1664] = weight_grad(tagged[...], d_target)
    bil = weight_grad(d_down, sums[...])
    for m in range(8):
        tile = [bil[0:64, k * 128 : k * 128 + 64] for k in (2 * m, 2 * m + 1)]
        row = 768 + 64 * (m // 4)
        first[row : row + 64, (m % 4) * 128 : (m % 4 + 1) * 128] = jnp.concatenate(tile, axis=1)
    for half in range(2):
        for m in range(4):
            at = 64 + 32 * half
            tile = [bil[64:96, k * 128 + at : k * 128 + at + 32] for k in range(4 * m, 4 * m + 4)]
            row = 1728 + 32 * half
            first[row : row + 32, m * 128 : (m + 1) * 128] = jnp.concatenate(tile, axis=1)
    first[1664:1728] = weight_grad(down_act, d_trip)[:64]
    quad_up_grad[...] = weight_grad(down_act, d_quad)[64:96]
    atom_rows[...] = jnp.concatenate(
        [gathered, summary, updated, a0_act, new_atoms, e_act, d_a0, d_a1, d_e, d_out, d_gate], axis=1
    )
    split_cores(core, first, keep, send)
    grad_sums[...] = times(d_down, weight[...])


def late_kernel(grad_rads, radial, atom_rows, quad_up_grad, core, keep, send, second):
    atoms = atom_rows[...]
    gathered, summary = atoms[:, :512], atoms[:, 512:1024]
    updated, a0_act, new_atoms, e_act, d_a0, d_a1, d_e, d_out, d_gate = [
        atoms[:, at : at + 256] for at in range(1024, 3328, 256)
    ]
    second[0:512, 0:256] = weight_grad(gathered, d_gate)
    second[0:512, 256:512] = weight_grad(summary, d_e)
    second[512:768, 0:256] = weight_grad(updated, d_a0)
    second[512:768, 256:512] = weight_grad(a0_act, d_a1)
    second[768:1024, 0:256] = weight_grad(new_atoms, d_e)
    second[768:1024, 256:512] = weight_grad(e_act, d_out)
    for k in range(3):
        second[1024 + 128 * k : 1152 + 128 * k] = weight_grad(radial[...], grad_rads[k])
    second[1408:1440] = quad_up_grad[...]
    second[1440:1536] = jnp.zeros((96, 512), F32)
    split_cores(core, second, keep, send)


def scatter_kernel(
    cosines, sums, grad_src, src_rows, mark_rows,
    back_before, back_here, back_after, back_local,
    table,
):
    group = back_here.shape[0] * 8
    depth = 3 * group + 16
    trip_lanes = iota((128, 128), 1) < TRIP_W
    scale = 1.0 / math.sqrt(PICKS)

    def basis_back(b, carry):
        at = pl.multiple_of(b * BLOCK, BLOCK)
        own = pl.ds(at, BLOCK)
        parts = []
        for h in range(2):
            total = jnp.zeros((PICKS, 8, 128), F32)
            for k, poly in enumerate(legendre(cosines[2 * b + h])):
                total = total + poly * sums[pl.ds(pl.multiple_of(at + 8 * h, 8), 8), k * 128 : (k + 1) * 128]
            parts.append(total * scale)
        grad = jnp.concatenate(parts, axis=1).reshape(128, 128)
        grad = jnp.concatenate(
            [jnp.where(trip_lanes, grad, 0.0), jnp.where(trip_lanes, 0.0, grad)], axis=0
        )
        hits = onehot(mark_rows[b] == iota((512, 256), 0))
        got = side_by_side(side_sum(dot(hits, side_by_side(grad))))
        table[:, own, :] = got.reshape(32, BLOCK, 256)
        return carry

    lax.fori_loop(0, BLOCKS, basis_back, 0)
    table[30] = side_by_side(grad_src[:, :128])
    table[31] = side_by_side(grad_src[:, 128:])
    rows = iota((depth, EDGES), 0)
    place_even = onehot(src_rows[0:1, :] == rows)
    place_odd = onehot(src_rows[1:2, :] == rows)

    def scatter_pair(p, carry):
        got = side_sum(dot(place_even, table[2 * p]) + dot(place_odd, table[2 * p + 1]))
        for i, back in enumerate((back_before, back_here, back_after)):
            back[:, p] = got[i * group : (i + 1) * group].reshape(group // 8, 8, 128)
        back_local[p] = got[3 * group :]
        return carry

    lax.fori_loop(0, 16, scatter_pair, 0)


def finish_kernel(
    back_local, returned, grad_late, tag_late, edge, radial, columns, pre, downs, rads, tag_row, send_row,
    w_in, w_trip, w_quad, core,
    grad_atoms, grad_edges, keep_first, send_first, keep_second, send_second,
    first, second,
):
    shape = (EDGES, 256)
    lane = iota(shape, 1)
    place = onehot((local_rows(lane) == iota(shape, 0)) & (lane < EDGES))
    rows = dot(place, side_by_side(back_local[...].reshape(256, 128)))
    pay = paid(iota((1, 128), 1), send_lanes(send_row[...]))
    place = onehot(pay == iota((EDGES, 128), 0))
    send = send_column(send_row[...], 8)
    tags = to_column(tag_row[...])
    rows = side_sum(rows + dot(place, side_by_side(returned[...].reshape(128, 128))))
    back = returned[15]
    tag = tag_late[...] + jnp.concatenate([back_local[15, 0:8], back_local[15, 8:16]], axis=1)
    atom = iota((8, 1), 0)
    for r in range(SEND):
        piece = jnp.concatenate([back[r : r + 1], back[4 + r : 5 + r]], axis=1)
        tag = tag + jnp.where(send[r : r + 1, :] == atom, piece, 0.0)
    grad_atoms[...] = tag
    table = [
        jnp.sum(jnp.where(tags == t, tag, 0.0), axis=0, keepdims=True) for t in range(3)
    ]
    table = jnp.concatenate(table + [jnp.zeros((29, ATOM_W), F32)], axis=0)
    d_trip = rows[:, :64]
    d_quad = rows[:, 64:96] * radial[:, 0:1] + rows[:, 96:128] * radial[:, 1:2]
    total = grad_late[...]
    for k, (d_row, down, weight, out) in enumerate(
        ((d_trip, slice(0, 64), w_trip, first), (d_quad, slice(64, 96), w_quad, second))
    ):
        d_down = d_row * columns[:, 0:1] * act_and_slope(downs[:, down])[1]
        value, slope = act_and_slope(pre[k])
        d_start = times(d_down, weight[...])
        d_pre = d_start * rads[k] * slope
        total = total + times(d_pre, w_in[k], NT)
        out[0:512] = weight_grad(edge[...], d_pre)
        out[512:640] = weight_grad(radial[...], d_start * value)
        down_grad = weight_grad(d_down, value * rads[k])
        if k == 0:
            out[640:704] = down_grad
            out[704:768] = jnp.zeros((64, 512), F32)
        else:
            out[640:672] = down_grad
            out[672:704, 0:256] = table
            out[672:704, 256:512] = jnp.zeros((32, 256), F32)
            out[704:768] = jnp.zeros((64, 512), F32)
    grad_edges[...] = total
    split_cores(core, first, keep_first, send_first)
    split_cores(core, second, keep_second, send_second)


def call(kernel, outs, args, scratch=(), micros=1):
    flops = int(micros * 1.15e9)
    return pl.pallas_call(
        kernel,
        out_shape=[jax.ShapeDtypeStruct(shape, F32) for shape in outs],
        in_specs=[pl.BlockSpec(memory_space=pltpu.SMEM if x.ndim == 1 else pltpu.VMEM) for x in args],
        out_specs=[pl.BlockSpec(memory_space=pltpu.VMEM)] * len(outs),
        scratch_shapes=list(scratch),
        compiler_params=pltpu.CompilerParams(vmem_limit_bytes=56 * 1024 * 1024),
        cost_estimate=pl.CostEstimate(flops=flops, bytes_accessed=4 << 20, transcendentals=0),
    )(*args)


def per_device(
    hidden_atoms,
    edge_states,
    edge_vectors,
    atom_tags,
    send_list,
    sources,
    trip_slots,
    triplet_mask,
    quad_slots,
    quad_mask,
    edge_mask,
    w_inputs,
    w_radial,
    w_trip_down,
    triplet_bilinear_weight,
    w_trip_up,
    w_quad_down,
    w_quad_bil,
    w_quad_up,
    w_atom_edge,
    w_residual,
    w_edge_atom,
    w_atom_dense,
    tag_table,
    cot_atoms,
    cot_edges,
    cot_energy,
):
    planes = 2 if lax.axis_size("gz") == 2 else 3
    group = 3 * planes

    offset = jnp.maximum(sources - ATOMS, 0)
    block, border = offset // SEND, offset % SEND
    step_x, step_y, step_z = block // 9, block // 3 % 3, block % 3
    if planes == 2:
        step_z = jnp.clip(step_z - 1 + lax.axis_index("gz"), 0, 1)
    block = (step_y * 3 + step_x) * planes + step_z
    inside = sources < ATOMS
    even = jnp.where(inside, 3 * group * 8 + sources, block * 8 + border)
    src = jnp.stack([even, even + jnp.where(inside, ATOMS, SEND)])
    slots = jnp.concatenate([trip_slots, quad_slots], axis=1)
    masks = jnp.concatenate([triplet_mask, quad_mask], axis=1)
    marks = jnp.where(masks > 0, slots * BLOCK + (jnp.arange(EDGES) % BLOCK)[:, None], -1)
    mark_rows = marks.reshape(BLOCKS, BLOCK, 2 * PICKS).transpose(0, 2, 1)
    mark_rows = mark_rows.reshape(BLOCKS, 1, 2 * PICKS * BLOCK)
    trip_down_t, quad_down_t = w_trip_down.T, w_quad_down.T

    tag_row, send_row = atom_tags[None, :], send_list[None, :]
    payload, local, tagged, pre, downs, rads, radial, columns = call(
        start_kernel,
        [(PAIRS, 8, 128), (PAIRS, 16, 128), (8, 256), (2, EDGES, 512), (EDGES, 128), (5, EDGES, 512)]
        + [(EDGES, 128)] * 2,
        [edge_states, edge_vectors, edge_mask[None, :], hidden_atoms, tag_row, send_row, tag_table,
         w_inputs, w_radial, trip_down_t, quad_down_t],
        micros=5,
    )
    core = bit_value("gyl", 0)[None]
    before, here, after = with_halo(payload)
    (
        atoms_out, edges_out, energy_out, grad_edges, grad_tag,
        cosines, grad_sums, grad_src, keep_a, send_a, grad_rads, atom_rows, quad_up_grad,
    ) = call(
        main_kernel,
        [(8, 256), (EDGES, 512), (8, 256), (EDGES, 512), (8, 256)]
        + [(2 * BLOCKS, PICKS, 8, 128), (EDGES, 2048), (EDGES, 256), (896, 512), (896, 512)]
        + [(3, EDGES, 512), (8, 3328), (32, 512)],
        [before, here, after, local, tagged, edge_states, columns, rads, radial,
         src.T, slots, marks,
         triplet_bilinear_weight.T, w_trip_up, w_quad_bil.T, w_quad_up, w_atom_edge, w_residual,
         w_edge_atom, w_atom_dense, cot_atoms, cot_edges, cot_energy, core],
        scratch=[
            pltpu.VMEM((32, EDGES, 256), BF),
            pltpu.VMEM((EDGES, 2048), F32),
            pltpu.VMEM((128, 2048), BF),
            pltpu.VMEM((5, EDGES, 512), F32),
            pltpu.VMEM((EDGES, 128), F32),
            pltpu.VMEM((1792, 512), F32),
        ],
        micros=26,
    )
    chain = Chain()
    got_a = swap(send_a, "gyl", 0)
    keep_b, send_b = call(
        late_kernel,
        [(768, 512)] * 2,
        [grad_rads, radial, atom_rows, quad_up_grad, core],
        scratch=[pltpu.VMEM((1536, 512), F32)],
        micros=4,
    )
    late = reduction(chain, [keep_a, got_a], [keep_b, swap(send_b, "gyl", 0)])
    next(late)
    grad_sums = chain.after(grad_sums)
    back_before, back_here, back_after, back_local = call(
        scatter_kernel,
        [(group, 16, 8, 128)] * 3 + [(16, 16, 128)],
        [cosines, grad_sums, grad_src, src, mark_rows],
        scratch=[pltpu.VMEM((32, EDGES, 256), BF)],
        micros=13,
    )
    got = shifted(back_before, GY, -1, True), shifted(back_after, GY, 1, True)
    chain.step(back_local)
    next(late)
    got, value = chain.after((got, back_here))
    value = chain.step(value + got[0] + got[1])
    first_plane, middle, last_plane = value[:planes], value[planes : 2 * planes], value[2 * planes :]
    got = shifted(first_plane, "gx", -1, True), shifted(last_plane, "gx", 1, True)
    got, middle = chain.after((got, middle))
    value = chain.step(middle + got[0] + got[1])
    next(late)
    if planes == 2:
        top = lax.axis_index("gz") == 1
        mine = jnp.where(top, value[1], value[0])
        theirs = jnp.where(top, value[0], value[1])
        returned = mine + lax.ppermute(theirs, "gz", [(0, 1), (1, 0)])
    else:
        returned = value[1] + shifted(value[0], "gz", -1, False) + shifted(value[2], "gz", 1, False)
    grad_atoms, grad_edges, keep_c, send_c, keep_d, send_d = call(
        finish_kernel,
        [(8, 256), (EDGES, 512)] + [(384, 512)] * 4,
        [back_local, returned, grad_edges, grad_tag, edge_states, radial, columns, pre, downs, rads,
         tag_row, send_row, w_inputs, trip_down_t, quad_down_t, core],
        scratch=[pltpu.VMEM((768, 512), F32)] * 2,
        micros=7,
    )
    got_c, got_d = swap(send_c, "gyl", 0), swap(send_d, "gyl", 0)
    early = reduction(chain, [keep_c, got_c], [keep_d, got_d])
    chain.step(keep_c)
    running = {"L": late, "E": early}
    done = {}

    def resume(name):
        if name in done:
            return
        try:
            next(running[name])
        except StopIteration as end:
            done[name] = end.value

    for name in "LELEELELEELEELEEL":
        resume(name)
    while len(done) < 2:
        resume("E")
        resume("L")
    upper = bit_value("gyl", 0) == 1

    def both(name, i):
        mine, other = done[name][i]
        return jnp.where(upper, other, mine), jnp.where(upper, mine, other)

    (a_low, a_high), (b_low, b_high) = both("L", 0), both("L", 1)
    (c_low, c_high), (d_low, d_high) = both("E", 0), both("E", 1)

    def pair(x, width):
        return jnp.stack([x[:, :width], x[:, width:]])

    def joined(x):
        half = x.shape[0] // 2
        return jnp.concatenate([x[:half], x[half:]], axis=1)

    grad_radial = [c_high[128:256], d_high[128:256]] + [
        b_high[256 + 128 * k : 384 + 128 * k] for k in range(3)
    ]
    grad_inputs = jnp.concatenate([c_low, c_high[:128], d_low, d_high[:128]])
    return (
        atoms_out,
        edges_out,
        energy_out,
        grad_atoms,
        grad_edges,
        grad_inputs.reshape(2, 512, 512),
        jnp.stack(grad_radial),
        c_high[256:320].T,
        joined(a_low[768:896]).T,
        a_high[768:832],
        d_high[256:288].T,
        joined(a_high[832:896]).T,
        b_high[640:672],
        jnp.stack([a_low[512:768], a_high[512:768]]),
        jnp.stack([a_low[:512], a_high[:512]]),
        pair(b_low[:512], 256),
        jnp.concatenate([pair(b_low[512:768], 256), pair(b_high[:256], 256)]),
        d_high[288:291, :256],
    )


def solution(mesh):
    size = dict(mesh.shape)
    inner = Mesh(mesh.devices.reshape(size["gx"], size["gy"] // 2, 2, size["gz"]), ROWS)
    flat, columns, vector, whole = P(ROWS, None), P(None, ROWS), P(ROWS), P()
    placed = [flat, flat, columns] + [vector] * 3 + [flat] * 4 + [vector] + [whole] * 13 + [flat] * 3
    return jax.shard_map(
        per_device,
        mesh=inner,
        in_specs=tuple(placed),
        out_specs=tuple([flat] * 5 + [whole] * 13),
        check_vma=False,
    )
```

time: 596 us -> 260 us (0.44); the launches traced: 589 us -> 259 us
  local copies, waits for them, and re-layouts: 109 us -> 7.43 us
  matrix products: 97 us -> 0 us
  waiting for transfers between devices: 179 us -> 122 us
  Pallas kernels: 0 us -> 54.6 us
  starting transfers between devices: 86.7 us -> 37.5 us
  blocking collectives: 40.3 us -> 0 us
  other arithmetic: 60.3 us -> 36.1 us
  between operations: 17 us -> 1.44 us
    psum x1 -> x0, waiting for transfers between devices: 150 us -> none  [per_device(): summed = lax.psum(partial_grads, ('gx', 'gy', 'gz'))]
    dot_general x70 -> x0, matrix products: 97 us -> none  [the longest x66 74.1 us: matmul(): jnp.dot(left, right, precision=HIGHEST, preferred_element_type=jnp.float32)]
    ppermute x60 -> x42, waiting for transfers between devices: 28.7 us -> 122 us  [the longest x32 93.7 us: swap(): return lax.ppermute(value, axis, [(i, i ^ 1 << bit) for i in range(count)])]
    pallas_call x0 -> x5, Pallas kernels: none -> 54.6 us  [call(): pl.pallas_call(kernel, out_shape=[jax.ShapeDtypeStruct(shape, F32) for sh...]
    ppermute x60 -> x42, starting transfers between devices: 86.7 us -> 37.5 us  [the longest x32 23.8 us: swap(): return lax.ppermute(value, axis, [(i, i ^ 1 << bit) for i in range(count)])]
    psum x1 -> x0, blocking collectives: 40.3 us -> none  [per_device(): summed = lax.psum(partial_grads, ('gx', 'gy', 'gz'))]
    gather x11 -> x0, local copies, waits for them, and re-layouts: 36.7 us -> none  [the longest x1 10.4 us: per_device(): safe_lengths[quad_index]]
    scatter-add x7 -> x0, other arithmetic: 34.5 us -> none  [the longest x1 13.1 us: local_finish(): quad_table[quad_index]]
  transfers between devices with their start and end apart: 61 -> 42, of which waited for: 10 -> 28; matrix products, arithmetic and copies ran while one was open for 4% -> 12% of each run, Pallas kernels for 0% -> 9%
where the time goes in v1:
time: 260 us; the launch traced here: 259 us
  waiting for transfers between devices  122 us (47%)
  Pallas kernels  54.6 us (21%)
  starting transfers between devices  37.5 us (14%)
  other arithmetic  36.1 us (14%)
  local copies, waits for them, and re-layouts  7.43 us (3%)
    ppermute x32, waiting for transfers between devices, swap(): return lax.ppermute(value, axis, [(i, i ^ 1 << bit) for i in range(count)])  93.7 us
    pallas_call x5, Pallas kernels, call(): pl.pallas_call(kernel, out_shape=[jax.ShapeDtypeStruct(shape, F32) for sh...  54.6 us
    ppermute x32, starting transfers between devices, swap(): return lax.ppermute(value, axis, [(i, i ^ 1 << bit) for i in range(count)])  23.8 us
    ppermute x8, waiting for transfers between devices, shifted(): return lax.ppermute(value, axis, pairs)  23.1 us
    add x24, other arithmetic, part(): total = total + lax.dynamic_slice_in_dim(x, at, size)  15.8 us
    ppermute x8, starting transfers between devices, shifted(): return lax.ppermute(value, axis, pairs)  9.27 us
    select_n x4, other arithmetic, both(): return (jnp.where(upper, other, mine), jnp.where(upper, mine, other))  5.39 us
  transfers between devices with their start and end apart: 42, of which 28 were waited for; matrix products, arithmetic and copies ran while one was open for 12% of the time, Pallas kernels for 9%

profile of v1, /device:TPU:0, one launch (start us, length us, event | category | flops | bytes accessed | tf_op | source)
XLA Modules:
  0.0 259.5 jit_solution(12260654635013051121)
XLA Ops:
  0.7 4.7 %shard_map.394 = (f32[17,8,128]{2,1,0:T(8,128)}, f32[17,16,128]{2,1,0:T(8,128)}, f32[8,256]{1,0:T(8,128)}, f32[2,240,512]{2,1,0:T(8,128)}, f32[240,128]{1,0:T(8,...) custom-call(f32[240,512]{1,0:T(8,128)} %edge.5, f32[3,240]{1,0:T(4,128)} %vec.1, ...), custom_call_target="tpu_custom_call" | custom-call | flops 5750000128 | bytes 4194304 | tf_op jit(solution)/shard_map/pallas_call | solution.py:647
  5.4 3.0 %collective-permute-start = (f32[17,8,128]{2,1,0:T(8,128)}, f32[17,8,128]{2,1,0:T(8,128)S(1)}, u32[]{:S(2)}, u32[]{:S(2)}) collective-permute-start(f32[17,8,128]{2,1,0:T(8,128)} %get-tuple-element.148), channel_id=1, source_target_pairs={{0,1},{1,0},{2,3},{3,2},{4,5},{5,4},{6,7},{7,6},{8,9},{9,8},{10,11... | collective-permute-start | bytes 208904 | tf_op jit(solution)/shard_map/ppermute | solution.py:36
  9.2 1.7 collective-permute-done
  11.8 4.2 %collective-permute-start.2 = (f32[2,17,8,128]{3,2,1,0:T(8,128)S(1)}, f32[2,17,8,128]{3,2,1,0:T(8,128)S(1)}, u32[]{:S(2)}, u32[]{:S(2)}) collective-permute-start(f32[2,17,8,128]{3,2,1,0:T(8,128)S(1)} %pad_maximum_fusion.21), channel_id=1, source_target_pairs={{0,24},{8,0},{16,8},{24,16},{1,25},{9,1},{17,9},{25,17},{2,26},{10... | collective-permute-start | bytes 417800 | tf_op jit(solution)/shard_map/ppermute | solution.py:31
  16.0 3.3 %collective-permute-done.2 = f32[2,17,8,128]{3,2,1,0:T(8,128)S(1)} collective-permute-done((f32[2,17,8,128]{3,2,1,0:T(8,128)S(1)}, f32[2,17,8,128]{3,2,1,0:T(8,128)S(1)}, u32[]{:S(2)}, u32[]{:S(2)}) %collective-permute-start.2) | collective-permute-done | bytes 139296 | tf_op jit(solution)/shard_map/ppermute | solution.py:31
  19.2 3.6 %collective-permute-done.1 = f32[2,17,8,128]{3,2,1,0:T(8,128)S(1)} collective-permute-done((f32[2,17,8,128]{3,2,1,0:T(8,128)S(1)}, f32[2,17,8,128]{3,2,1,0:T(8,128)S(1)}, u32[]{:S(2)}, u32[]{:S(2)}) %collective-permute-start.1) | collective-permute-done | bytes 139296 | tf_op jit(solution)/shard_map/ppermute | solution.py:31
  25.7 6.0 %collective-permute-done.4.halo_after = f32[6,17,8,128]{3,2,1,0:T(8,128)S(1)} collective-permute-done((f32[6,17,8,128]{3,2,1,0:T(8,128)S(1)}, f32[6,17,8,128]{3,2,1,0:T(8,128)S(1)}, u32[]{:S(2)}, u32[]{:S(2)}) %collective-permute-start.4) | collective-permute-done | bytes 417824 | tf_op jit(solution)/shard_map/ppermute | solution.py:31
  31.8 3.2 %collective-permute-done.3.halo_before = f32[6,17,8,128]{3,2,1,0:T(8,128)S(1)} collective-permute-done((f32[6,17,8,128]{3,2,1,0:T(8,128)S(1)}, f32[6,17,8,128]{3,2,1,0:T(8,128)S(1)}, u32[]{:S(2)}, u32[]{:S(2)}) %collective-permute-start.3) | collective-permute-done | bytes 417824 | tf_op jit(solution)/shard_map/ppermute | solution.py:31
  35.7 25.7 %shard_map.395 = (f32[8,256]{1,0:T(8,128)}, f32[240,512]{1,0:T(8,128)}, f32[8,256]{1,0:T(8,128)}, f32[240,512]{1,0:T(8,128)}, f32[8,256]{1,0:T(8,128)}, /*index=...) custom-call(f32[6,17,8,128]{3,2,1,0:T(8,128)} %copy-done.15, ...), custom_call_target="tpu_custom_call" | custom-call | flops 29899999232 | bytes 4194304 | tf_op jit(solution)/shard_map/pallas_call | solution.py:647
  61.6 4.2 %shard_map.396 = (f32[768,512]{1,0:T(8,128)}, f32[768,512]{1,0:T(8,128)}) custom-call(f32[3,240,512]{2,1,0:T(8,128)} %get-tuple-element.160.grad_rads, f32[240,128]{1,0:T(8,128)} %get-tuple-element.153.radial, f32[8,3328]{1,0:T(8,128)} %get-tuple-element.161.atom_rows, f32[32,512]{1,0:T(8,128)} %get-tuple-element.162.quad_up_grad, s32[1]{0:T(128)} %bitcast.12.core), custom_call_target="tpu_custom_call" | custom-call | flops 4600000000 | bytes 4194304 | tf_op jit(solution)/shard_map/pallas_call | solution.py:647
  67.3 1.4 dynamic-slice_add_fusion.1
  68.7 1.6 collective-permute-start.7
  70.3 1.3 dynamic-slice_add_fusion.3
  72.1 13.3 %shard_map.397 = (f32[6,16,8,128]{3,2,1,0:T(8,128)}, f32[6,16,8,128]{3,2,1,0:T(8,128)}, f32[6,16,8,128]{3,2,1,0:T(8,128)}, f32[16,16,128]{2,1,0:T(8,128)}) custom-call(f32[30,8,8,128]{3,2,1,0:T(8,128)} %get-tuple-element.157.cosines, f32[240,2048]{1,0:T(8,128)} %get-tuple-element.168.sums, f32[240,256]{1,0:T(8,128)} %get-tuple-element.169.grad_src, ...), custom_call_target="tpu_custom_call" | custom-call | flops 14949999616 | bytes 4194304 | tf_op jit(solution)/shard_map/pallas_call | solution.py:647
  86.0 1.3 dynamic-slice_add_fusion.2
  87.3 1.4 dynamic-slice_add_fusion
  88.7 2.4 collective-permute-done.7
  91.2 1.0 collective-permute-done.8
  92.1 1.1 dynamic-slice_add_fusion.13
  93.2 4.1 %collective-permute-done.9 = f32[6,16,8,128]{3,2,1,0:T(8,128)S(1)} collective-permute-done((f32[6,16,8,128]{3,2,1,0:T(8,128)}, f32[6,16,8,128]{3,2,1,0:T(8,128)S(1)}, u32[]{:S(2)}, u32[]{:S(2)}) %collective-permute-start.9) | collective-permute-done | bytes 393248 | tf_op jit(solution)/shard_map/ppermute | solution.py:31
  98.6 3.4 %collective-permute-start.11 = (f32[2,16,8,128]{3,2,1,0:T(8,128)S(1)}, f32[2,16,8,128]{3,2,1,0:T(8,128)}, u32[]{:S(2)}, u32[]{:S(2)}) collective-permute-start(f32[2,16,8,128]{3,2,1,0:T(8,128)S(1)} %get-tuple-element.322), channel_id=1, source_target_pairs={{0,24},{8,0},{16,8},{24,16},{1,25},{9,1},{17,9},{25,17},{2,26},{10... | collective-permute-start | bytes 393224 | tf_op jit(solution)/shard_map/ppermute | solution.py:31
  102.9 1.7 collective-permute-start.15
  104.6 1.1 dynamic-slice_add_fusion.4
  106.5 1.3 collective-permute-done.11
  108.8 1.4 collective-permute-start.13
  110.2 1.1 dynamic-slice_add_fusion.12
  111.3 3.8 %collective-permute-done.13 = f32[16,8,128]{2,1,0:T(8,128)S(1)} collective-permute-done((f32[16,8,128]{2,1,0:T(8,128)S(1)}, f32[16,8,128]{2,1,0:T(8,128)S(1)}, u32[]{:S(2)}, u32[]{:S(2)}) %collective-permute-start.13) | collective-permute-done | bytes 65568 | tf_op jit(solution)/shard_map/ppermute | solution.py:772
  115.8 6.8 %shard_map.398 = (f32[8,256]{1,0:T(8,128)}, f32[240,512]{1,0:T(8,128)}, f32[384,512]{1,0:T(8,128)}, f32[384,512]{1,0:T(8,128)}, f32[384,512]{1,0:T(8,128)}, /*index=5*/f32[384,512]{1,0:T(8,128)}) custom-call(f32[16,16,128]{2,1,0:T(8,128)} %get-tuple-element.170.back_local, f32[16,8,128]{2,1,0:T(8,128)} %bitcast_add_fusion.returned, ...), custom_call_target="tpu_custom_call" | custom-call | flops 8049999872 | bytes 4194304 | tf_op jit(solution)/shard_map/pallas_call | solution.py:647
  124.1 12.0 %collective-permute-done.16 = f32[208,512]{1,0:T(8,128)} collective-permute-done((f32[208,512]{1,0:T(8,128)}, f32[208,512]{1,0:T(8,128)}, u32[]{:S(2)}, u32[]{:S(2)}) %collective-permute-start.16) | collective-permute-done | bytes 426016 | tf_op jit(solution)/shard_map/ppermute | solution.py:55
  137.3 1.1 dynamic-slice_add_fusion.11
  138.3 1.5 collective-permute-start.20
  139.8 1.1 dynamic-slice_add_fusion.10
  140.9 1.5 collective-permute-start.21
  143.4 1.1 dynamic-slice_add_fusion.9
  144.4 1.1 dynamic-slice_add_fusion.8
  145.5 3.5 %collective-permute-done.19 = f32[104,512]{1,0:T(8,128)S(1)} collective-permute-done((f32[104,512]{1,0:T(8,128)S(1)}, f32[104,512]{1,0:T(8,128)S(1)}, u32[]{:S(2)}, u32[]{:S(2)}) %collective-permute-start.19) | collective-permute-done | bytes 213024 | tf_op jit(solution)/shard_map/ppermute | solution.py:55
  149.2 1.6 collective-permute-done.21
  151.6 1.6 collective-permute-start.22
  153.2 3.4 %collective-permute-done.23 = f32[96,512]{1,0:T(8,128)S(1)} collective-permute-done((f32[96,512]{1,0:T(8,128)S(1)}, f32[96,512]{1,0:T(8,128)S(1)}, u32[]{:S(2)}, u32[]{:S(2)}) %collective-permute-start.23) | collective-permute-done | bytes 196640 | tf_op jit(solution)/shard_map/ppermute | solution.py:55
  157.4 1.2 collective-permute-done.24
  158.7 2.0 collective-permute-start.25
  160.7 13.9 %collective-permute-done.25 = f32[96,512]{1,0:T(8,128)S(1)} collective-permute-done((f32[96,512]{1,0:T(8,128)S(1)}, f32[96,512]{1,0:T(8,128)S(1)}, u32[]{:S(2)}, u32[]{:S(2)}) %collective-permute-start.25) | collective-permute-done | bytes 196640 | tf_op jit(solution)/shard_map/ppermute | solution.py:55
  174.9 1.6 collective-permute-start.29
  176.5 5.1 %collective-permute-done.27 = f32[48,512]{1,0:T(8,128)S(1)} collective-permute-done((f32[48,512]{1,0:T(8,128)S(1)}, f32[48,512]{1,0:T(8,128)S(1)}, u32[]{:S(2)}, u32[]{:S(2)}) %collective-permute-start.27) | collective-permute-done | bytes 98336 | tf_op jit(solution)/shard_map/ppermute | solution.py:55
  181.7 6.0 %collective-permute-done.28 = f32[48,512]{1,0:T(8,128)S(1)} collective-permute-done((f32[48,512]{1,0:T(8,128)S(1)}, f32[48,512]{1,0:T(8,128)S(1)}, u32[]{:S(2)}, u32[]{:S(2)}) %collective-permute-start.28) | collective-permute-done | bytes 98336 | tf_op jit(solution)/shard_map/ppermute | solution.py:55
  187.8 1.5 collective-permute-start.30
  189.5 8.9 %collective-permute-done.30 = f32[192,512]{1,0:T(8,128)S(1)} collective-permute-done((f32[192,512]{1,0:T(8,128)S(1)}, f32[192,512]{1,0:T(8,128)S(1)}, u32[]{:S(2)}, u32[]{:S(2)}) %collective-permute-start.30) | collective-permute-done | bytes 393248 | tf_op jit(solution)/shard_map/ppermute | solution.py:55
  198.6 1.6 collective-permute-start.32
  200.2 1.4 collective-permute-start.34
  202.7 3.7 %collective-permute-done.32 = f32[96,512]{1,0:T(8,128)S(1)} collective-permute-done((f32[96,512]{1,0:T(8,128)S(1)}, f32[96,512]{1,0:T(8,128)S(1)}, u32[]{:S(2)}, u32[]{:S(2)}) %collective-permute-start.32) | collective-permute-done | bytes 196640 | tf_op jit(solution)/shard_map/ppermute | solution.py:55
  206.5 1.5 collective-permute-start.36
  208.0 19.7 %collective-permute-done.33 = f32[96,512]{1,0:T(8,128)S(1)} collective-permute-done((f32[96,512]{1,0:T(8,128)S(1)}, f32[96,512]{1,0:T(8,128)S(1)}, u32[]{:S(2)}, u32[]{:S(2)}) %collective-permute-start.33) | collective-permute-done | bytes 196640 | tf_op jit(solution)/shard_map/ppermute | solution.py:55
  229.0 4.4 %collective-permute-done.36 = f32[192,512]{1,0:T(8,128)S(1)} collective-permute-done((f32[192,512]{1,0:T(8,128)S(1)}, f32[192,512]{1,0:T(8,128)S(1)}, u32[]{:S(2)}, u32[]{:S(2)}) %collective-permute-start.36) | collective-permute-done | bytes 393248 | tf_op jit(solution)/shard_map/ppermute | solution.py:55
  234.4 1.2 collective-permute-done.37
  237.7 1.6 collective-permute-done.39
  239.3 3.4 %collective-permute-done.38 = f32[384,512]{1,0:T(8,128)} collective-permute-done((f32[384,512]{1,0:T(8,128)}, f32[384,512]{1,0:T(8,128)}, u32[]{:S(2)}, u32[]{:S(2)}) %collective-permute-start.38) | collective-permute-done | bytes 786464 | tf_op jit(solution)/shard_map/ppermute | solution.py:55
  242.6 1.5 broadcast_select_fusion.9
  244.8 1.5 broadcast_select_fusion.11
  246.4 1.5 pad_maximum_fusion
  250.3 1.9 broadcast_select_fusion
  254.8 1.5 pad_maximum_fusion.1
  256.3 1.0 pad_maximum_fusion.4
  257.4 1.0 pad_maximum_fusion.5
  258.4 1.0 pad_maximum_fusion.6
  (170 shorter events, 30.0 us)
Async XLA Ops:
  0.7 7.7 %copy-start.13 = (s32[240]{0:T(256)S(1)}, s32[240]{0:T(256)}, u32[]{:S(2)}) copy-start(s32[240]{0:T(256)} %param.32) | copy-start | bytes 2884
  0.7 7.7 %copy-start.9 = (s32[240,8]{0,1:T(8,128)S(1)}, s32[240,8]{0,1:T(8,128)}, u32[]{:S(2)}) copy-start(s32[240,8]{0,1:T(8,128)} %param.33) | copy-start | bytes 23044
  0.7 7.8 %copy-start.11 = (s32[240,8]{0,1:T(8,128)S(1)}, s32[240,8]{0,1:T(8,128)}, u32[]{:S(2)}) copy-start(s32[240,8]{0,1:T(8,128)} %param.35) | copy-start | bytes 23044
  5.3 18.1 %copy-start.10 = (s32[240,8]{0,1:T(8,128)S(1)}, s32[240,8]{0,1:T(8,128)}, u32[]{:S(2)}) copy-start(s32[240,8]{0,1:T(8,128)} %param.34) | copy-start | bytes 23044
  5.4 18.1 %copy-start.12 = (s32[240,8]{0,1:T(8,128)S(1)}, s32[240,8]{0,1:T(8,128)}, u32[]{:S(2)}) copy-start(s32[240,8]{0,1:T(8,128)} %param.36) | copy-start | bytes 23044
  5.4 5.5 %collective-permute-start = (f32[17,8,128]{2,1,0:T(8,128)}, f32[17,8,128]{2,1,0:T(8,128)S(1)}, u32[]{:S(2)}, u32[]{:S(2)}) collective-permute-start(f32[17,8,128]{2,1,0:T(8,128)} %get-tuple-element.148), channel_id=1, source_target_pairs={{0,1},{1,0},{2,3},{3,2},{4,5},{5,4},{6,7},{7,6},{8,9},{9,8},{10,11... | collective-permute-start | bytes 208904 | tf_op jit(solution)/shard_map/ppermute | solution.py:36
  11.8 7.5 %collective-permute-start.2 = (f32[2,17,8,128]{3,2,1,0:T(8,128)S(1)}, f32[2,17,8,128]{3,2,1,0:T(8,128)S(1)}, u32[]{:S(2)}, u32[]{:S(2)}) collective-permute-start(f32[2,17,8,128]{3,2,1,0:T(8,128)S(1)} %pad_maximum_fusion.21), channel_id=1, source_target_pairs={{0,24},{8,0},{16,8},{24,16},{1,25},{9,1},{17,9},{25,17},{2,26},{10... | collective-permute-start | bytes 417800 | tf_op jit(solution)/shard_map/ppermute | solution.py:31
  16.0 6.9 %collective-permute-start.1 = (f32[2,17,8,128]{3,2,1,0:T(8,128)S(1)}, f32[2,17,8,128]{3,2,1,0:T(8,128)S(1)}, u32[]{:S(2)}, u32[]{:S(2)}) collective-permute-start(f32[2,17,8,128]{3,2,1,0:T(8,128)S(1)} %pad_maximum_fusion.21), channel_id=1, source_target_pairs={{0,8},{8,16},{16,24},{24,0},{1,9},{9,17},{17,25},{25,1},{2,10},{10... | collective-permute-start | bytes 417800 | tf_op jit(solution)/shard_map/ppermute | solution.py:31
  22.9 12.1 %copy-start.6 = (f32[6,17,8,128]{3,2,1,0:T(8,128)}, f32[6,17,8,128]{3,2,1,0:T(8,128)S(1)}, u32[]{:S(2)}) copy-start(f32[6,17,8,128]{3,2,1,0:T(8,128)S(1)} %pad_maximum_fusion.15.halo_here) | copy-start | bytes 1253380
  22.9 8.9 %collective-permute-start.4 = (f32[6,17,8,128]{3,2,1,0:T(8,128)S(1)}, f32[6,17,8,128]{3,2,1,0:T(8,128)S(1)}, u32[]{:S(2)}, u32[]{:S(2)}) collective-permute-start(f32[6,17,8,128]{3,2,1,0:T(8,128)S(1)} %pad_maximum_fusion.15.halo_here), channel_id=1, source_target_pairs={{0,6},{2,0},{4,2},{6,4},{1,7},{3,1},{5,3},{7,5},{8,14},{10,8},{12,... | collective-permute-start | bytes 1253384 | tf_op jit(solution)/shard_map/ppermute | solution.py:31
  22.9 12.0 %collective-permute-start.3 = (f32[6,17,8,128]{3,2,1,0:T(8,128)S(1)}, f32[6,17,8,128]{3,2,1,0:T(8,128)S(1)}, u32[]{:S(2)}, u32[]{:S(2)}) collective-permute-start(f32[6,17,8,128]{3,2,1,0:T(8,128)S(1)} %pad_maximum_fusion.15.halo_here), channel_id=1, source_target_pairs={{0,2},{2,4},{4,6},{6,0},{1,3},{3,5},{5,7},{7,1},{8,10},{10,12},{12... | collective-permute-start | bytes 1253384 | tf_op jit(solution)/shard_map/ppermute | solution.py:31
  31.8 3.2 %copy-start.14 = (f32[6,17,8,128]{3,2,1,0:T(8,128)}, f32[6,17,8,128]{3,2,1,0:T(8,128)S(1)}, u32[]{:S(2)}) copy-start(f32[6,17,8,128]{3,2,1,0:T(8,128)S(1)} %collective-permute-done.4.halo_after) | copy-start | bytes 1253380
  34.9 0.8 copy-start.15
  61.4 5.9 %collective-permute-start.5 = (f32[896,512]{1,0:T(8,128)}, f32[896,512]{1,0:T(8,128)}, u32[]{:S(2)}, u32[]{:S(2)}) collective-permute-start(f32[896,512]{1,0:T(8,128)} %get-tuple-element.159), channel_id=1, source_target_pairs={{0,2},{2,0},{1,3},{3,1},{4,6},{6,4},{5,7},{7,5},{8,10},{10,8},{9,1... | collective-permute-start | bytes 5505032 | tf_op jit(solution)/shard_map/ppermute | solution.py:55
  61.6 5.8 %copy-start = (f32[896,512]{1,0:T(8,128)S(1)}, f32[896,512]{1,0:T(8,128)}, u32[]{:S(2)}) copy-start(f32[896,512]{1,0:T(8,128)} %get-tuple-element.171) | copy-start | bytes 5505028
  65.7 4.5 %collective-permute-start.6 = (f32[768,512]{1,0:T(8,128)}, f32[768,512]{1,0:T(8,128)}, u32[]{:S(2)}, u32[]{:S(2)}) collective-permute-start(f32[768,512]{1,0:T(8,128)} %get-tuple-element.164), channel_id=1, source_target_pairs={{0,2},{2,0},{1,3},{3,1},{4,6},{6,4},{5,7},{7,5},{8,10},{10,8},{9,1... | collective-permute-start | bytes 4718600 | tf_op jit(solution)/shard_map/ppermute | solution.py:55
  66.5 3.7 %copy-start.1 = (f32[768,512]{1,0:T(8,128)S(1)}, f32[768,512]{1,0:T(8,128)}, u32[]{:S(2)}) copy-start(f32[768,512]{1,0:T(8,128)} %get-tuple-element.175) | copy-start | bytes 4718596
  68.7 22.4 %collective-permute-start.7 = (f32[448,512]{1,0:T(8,128)S(1)}, f32[448,512]{1,0:T(8,128)S(1)}, u32[]{:S(2)}, u32[]{:S(2)}) collective-permute-start(f32[448,512]{1,0:T(8,128)S(1)} %dynamic-slice_add_fusion.1), channel_id=1, source_target_pairs={{0,1},{1,0},{2,3},{3,2},{4,5},{5,4},{6,7},{7,6},{8,9},{9,8},{10,11... | collective-permute-start | bytes 2752520 | tf_op jit(solution)/shard_map/ppermute | solution.py:55
  71.5 20.6 %collective-permute-start.8 = (f32[384,512]{1,0:T(8,128)S(1)}, f32[384,512]{1,0:T(8,128)}, u32[]{:S(2)}, u32[]{:S(2)}) collective-permute-start(f32[384,512]{1,0:T(8,128)S(1)} %dynamic-slice_add_fusion.3), channel_id=1, source_target_pairs={{0,4},{4,0},{1,5},{5,1},{2,6},{6,2},{3,7},{7,3},{8,12},{12,8},{9,1... | collective-permute-start | bytes 2359304 | tf_op jit(solution)/shard_map/ppermute | solution.py:55
  72.1 13.9 %copy-start.2 = (f32[768,512]{1,0:T(8,128)S(1)}, f32[768,512]{1,0:T(8,128)}, u32[]{:S(2)}) copy-start(f32[768,512]{1,0:T(8,128)} %get-tuple-element.175) | copy-start | bytes 4718596
  85.4 12.0 %collective-permute-start.9 = (f32[6,16,8,128]{3,2,1,0:T(8,128)}, f32[6,16,8,128]{3,2,1,0:T(8,128)S(1)}, u32[]{:S(2)}, u32[]{:S(2)}) collective-permute-start(f32[6,16,8,128]{3,2,1,0:T(8,128)} %get-tuple-element.179), channel_id=1, source_target_pairs={{0,6},{2,0},{4,2},{6,4},{1,7},{3,1},{5,3},{7,5},{8,14},{10,8},{12,... | collective-permute-start | bytes 1179656 | tf_op jit(solution)/shard_map/ppermute | solution.py:31
  86.0 12.1 %collective-permute-start.10 = (f32[6,16,8,128]{3,2,1,0:T(8,128)}, f32[6,16,8,128]{3,2,1,0:T(8,128)S(1)}, u32[]{:S(2)}, u32[]{:S(2)}) collective-permute-start(f32[6,16,8,128]{3,2,1,0:T(8,128)} %get-tuple-element.180), channel_id=1, source_target_pairs={{0,2},{2,4},{4,6},{6,0},{1,3},{3,5},{5,7},{7,1},{8,10},{10,12},{12... | collective-permute-start | bytes 1179656 | tf_op jit(solution)/shard_map/ppermute | solution.py:31
  88.7 9.4 %copy-start.7 = (f32[6,16,8,128]{3,2,1,0:T(8,128)S(1)}, f32[6,16,8,128]{3,2,1,0:T(8,128)}, u32[]{:S(2)}) copy-start(f32[6,16,8,128]{3,2,1,0:T(8,128)} %get-tuple-element.182) | copy-start | bytes 1179652
  91.1 7.1 %copy-start.3 = (f32[448,512]{1,0:T(8,128)}, f32[448,512]{1,0:T(8,128)S(1)}, u32[]{:S(2)}) copy-start(f32[448,512]{1,0:T(8,128)S(1)} %collective-permute-done.7) | copy-start | bytes 2752516
  98.2 8.3 %collective-permute-start.12 = (f32[2,16,8,128]{3,2,1,0:T(8,128)S(1)}, f32[2,16,8,128]{3,2,1,0:T(8,128)S(1)}, u32[]{:S(2)}, u32[]{:S(2)}) collective-permute-start(f32[2,16,8,128]{3,2,1,0:T(8,128)S(1)} %get-tuple-element.321), channel_id=1, source_target_pairs={{0,8},{8,16},{16,24},{24,0},{1,9},{9,17},{17,25},{25,1},{2,10},{10... | collective-permute-start | bytes 393224 | tf_op jit(solution)/shard_map/ppermute | solution.py:31
  98.6 9.2 %collective-permute-start.11 = (f32[2,16,8,128]{3,2,1,0:T(8,128)S(1)}, f32[2,16,8,128]{3,2,1,0:T(8,128)}, u32[]{:S(2)}, u32[]{:S(2)}) collective-permute-start(f32[2,16,8,128]{3,2,1,0:T(8,128)S(1)} %get-tuple-element.322), channel_id=1, source_target_pairs={{0,24},{8,0},{16,8},{24,16},{1,25},{9,1},{17,9},{25,17},{2,26},{10... | collective-permute-start | bytes 393224 | tf_op jit(solution)/shard_map/ppermute | solution.py:31
  102.1 21.0 %collective-permute-start.14 = (f32[224,512]{1,0:T(8,128)S(1)}, f32[224,512]{1,0:T(8,128)S(1)}, u32[]{:S(2)}, u32[]{:S(2)}) collective-permute-start(f32[224,512]{1,0:T(8,128)S(1)} %dynamic-slice_add_fusion.5), channel_id=1, source_target_pairs={{0,4},{4,0},{1,5},{5,1},{2,6},{6,2},{3,7},{7,3},{8,12},{12,8},{9,1... | collective-permute-start | bytes 1376264 | tf_op jit(solution)/shard_map/ppermute | solution.py:55
  102.9 20.2 %collective-permute-start.15 = (f32[192,512]{1,0:T(8,128)S(1)}, f32[192,512]{1,0:T(8,128)S(1)}, u32[]{:S(2)}, u32[]{:S(2)}) collective-permute-start(f32[192,512]{1,0:T(8,128)S(1)} %dynamic-slice_add_fusion.13), channel_id=1, source_target_pairs={{0,1},{1,0},{2,3},{3,2},{4,5},{5,4},{6,7},{7,6},{8,9},{9,8},{10,11... | collective-permute-start | bytes 1179656 | tf_op jit(solution)/shard_map/ppermute | solution.py:55
  108.8 6.3 %collective-permute-start.13 = (f32[16,8,128]{2,1,0:T(8,128)S(1)}, f32[16,8,128]{2,1,0:T(8,128)S(1)}, u32[]{:S(2)}, u32[]{:S(2)}) collective-permute-start(f32[16,8,128]{2,1,0:T(8,128)S(1)} %select_bitcast_fusion.2), channel_id=1, source_target_pairs={{0,1},{1,0},{2,3},{3,2},{4,5},{5,4},{6,7},{7,6},{8,9},{9,8},{10,11... | collective-permute-start | bytes 196616 | tf_op jit(solution)/shard_map/ppermute | solution.py:772
  122.6 14.7 %collective-permute-start.17 = (f32[384,512]{1,0:T(8,128)}, f32[384,512]{1,0:T(8,128)}, u32[]{:S(2)}, u32[]{:S(2)}) collective-permute-start(f32[384,512]{1,0:T(8,128)} %get-tuple-element.209), channel_id=1, source_target_pairs={{0,2},{2,0},{1,3},{3,1},{4,6},{6,4},{5,7},{7,5},{8,10},{10,8},{9,1... | collective-permute-start | bytes 2359304 | tf_op jit(solution)/shard_map/ppermute | solution.py:55
  122.6 17.2 %collective-permute-start.18 = (f32[384,512]{1,0:T(8,128)}, f32[384,512]{1,0:T(8,128)}, u32[]{:S(2)}, u32[]{:S(2)}) collective-permute-start(f32[384,512]{1,0:T(8,128)} %get-tuple-element.213), channel_id=1, source_target_pairs={{0,2},{2,0},{1,3},{3,1},{4,6},{6,4},{5,7},{7,5},{8,10},{10,8},{9,1... | collective-permute-start | bytes 2359304 | tf_op jit(solution)/shard_map/ppermute | solution.py:55
  123.2 14.0 %copy-start.5 = (f32[384,512]{1,0:T(8,128)S(1)}, f32[384,512]{1,0:T(8,128)}, u32[]{:S(2)}) copy-start(f32[384,512]{1,0:T(8,128)} %get-tuple-element.220) | copy-start | bytes 2359300
  124.0 12.1 %collective-permute-start.16 = (f32[208,512]{1,0:T(8,128)}, f32[208,512]{1,0:T(8,128)}, u32[]{:S(2)}, u32[]{:S(2)}) collective-permute-start(f32[208,512]{1,0:T(8,128)} %dynamic-slice_add_fusion.7), channel_id=1, source_target_pairs={{0,8},{8,0},{16,24},{24,16},{1,9},{9,1},{17,25},{25,17},{2,10},{10... | collective-permute-start | bytes 1277960 | tf_op jit(solution)/shard_map/ppermute | solution.py:55
  124.1 15.8 %copy-start.4 = (f32[384,512]{1,0:T(8,128)S(1)}, f32[384,512]{1,0:T(8,128)}, u32[]{:S(2)}) copy-start(f32[384,512]{1,0:T(8,128)} %get-tuple-element.224) | copy-start | bytes 2359300
  137.1 11.9 %collective-permute-start.19 = (f32[104,512]{1,0:T(8,128)S(1)}, f32[104,512]{1,0:T(8,128)S(1)}, u32[]{:S(2)}, u32[]{:S(2)}) collective-permute-start(f32[104,512]{1,0:T(8,128)S(1)} %dynamic-slice_add_fusion.15), channel_id=1, source_target_pairs={{0,16},{8,24},{16,0},{24,8},{1,17},{9,25},{17,1},{25,9},{2,18},{10... | collective-permute-start | bytes 638984 | tf_op jit(solution)/shard_map/ppermute | solution.py:55
  138.3 10.9 %collective-permute-start.20 = (f32[192,512]{1,0:T(8,128)S(1)}, f32[192,512]{1,0:T(8,128)S(1)}, u32[]{:S(2)}, u32[]{:S(2)}) collective-permute-start(f32[192,512]{1,0:T(8,128)S(1)} %dynamic-slice_add_fusion.11), channel_id=1, source_target_pairs={{0,1},{1,0},{2,3},{3,2},{4,5},{5,4},{6,7},{7,6},{8,9},{9,8},{10,11... | collective-permute-start | bytes 1179656 | tf_op jit(solution)/shard_map/ppermute | solution.py:55
  140.9 10.0 %collective-permute-start.21 = (f32[192,512]{1,0:T(8,128)S(1)}, f32[192,512]{1,0:T(8,128)S(1)}, u32[]{:S(2)}, u32[]{:S(2)}) collective-permute-start(f32[192,512]{1,0:T(8,128)S(1)} %dynamic-slice_add_fusion.10), channel_id=1, source_target_pairs={{0,4},{4,0},{1,5},{5,1},{2,6},{6,2},{3,7},{7,3},{8,12},{12,8},{9,1... | collective-permute-start | bytes 1179656 | tf_op jit(solution)/shard_map/ppermute | solution.py:55
  149.1 9.5 %collective-permute-start.24 = (f32[104,512]{1,0:T(8,128)S(1)}, f32[104,512]{1,0:T(8,128)S(1)}, u32[]{:S(2)}, u32[]{:S(2)}) collective-permute-start(f32[104,512]{1,0:T(8,128)S(1)} %add.302), channel_id=1, source_target_pairs={{0,16},{8,24},{16,0},{24,8},{1,17},{9,25},{17,1},{25,9},{2,18},{10... | collective-permute-start | bytes 638984 | tf_op jit(solution)/shard_map/ppermute | solution.py:55
  150.9 5.7 %collective-permute-start.23 = (f32[96,512]{1,0:T(8,128)S(1)}, f32[96,512]{1,0:T(8,128)S(1)}, u32[]{:S(2)}, u32[]{:S(2)}) collective-permute-start(f32[96,512]{1,0:T(8,128)S(1)} %dynamic-slice_add_fusion.20), channel_id=1, source_target_pairs={{0,1},{1,0},{2,3},{3,2},{4,5},{5,4},{6,7},{7,6},{8,9},{9,8},{10,11... | collective-permute-start | bytes 589832 | tf_op jit(solution)/shard_map/ppermute | solution.py:55
  151.6 5.7 %collective-permute-start.22 = (f32[96,512]{1,0:T(8,128)S(1)}, f32[96,512]{1,0:T(8,128)S(1)}, u32[]{:S(2)}, u32[]{:S(2)}) collective-permute-start(f32[96,512]{1,0:T(8,128)S(1)} %dynamic-slice_add_fusion.21), channel_id=1, source_target_pairs={{0,4},{4,0},{1,5},{5,1},{2,6},{6,2},{3,7},{7,3},{8,12},{12,8},{9,1... | collective-permute-start | bytes 589832 | tf_op jit(solution)/shard_map/ppermute | solution.py:55
  158.6 16.1 %collective-permute-start.26 = (f32[208,512]{1,0:T(8,128)S(1)}, f32[208,512]{1,0:T(8,128)S(1)}, u32[]{:S(2)}, u32[]{:S(2)}) collective-permute-start(f32[208,512]{1,0:T(8,128)S(1)} %pad_maximum_fusion.14), channel_id=1, source_target_pairs={{0,8},{8,0},{16,24},{24,16},{1,9},{9,1},{17,25},{25,17},{2,10},{10... | collective-permute-start | bytes 1277960 | tf_op jit(solution)/shard_map/ppermute | solution.py:55
  158.7 15.9 %collective-permute-start.25 = (f32[96,512]{1,0:T(8,128)S(1)}, f32[96,512]{1,0:T(8,128)S(1)}, u32[]{:S(2)}, u32[]{:S(2)}) collective-permute-start(f32[96,512]{1,0:T(8,128)S(1)} %dynamic-slice_add_fusion.17), channel_id=1, source_target_pairs={{0,8},{8,0},{16,24},{24,16},{1,9},{9,1},{17,25},{25,17},{2,10},{10... | collective-permute-start | bytes 589832 | tf_op jit(solution)/shard_map/ppermute | solution.py:55
  174.7 6.9 %collective-permute-start.27 = (f32[48,512]{1,0:T(8,128)S(1)}, f32[48,512]{1,0:T(8,128)S(1)}, u32[]{:S(2)}, u32[]{:S(2)}) collective-permute-start(f32[48,512]{1,0:T(8,128)S(1)} %dynamic-slice_add_fusion.23), channel_id=1, source_target_pairs={{0,16},{8,24},{16,0},{24,8},{1,17},{9,25},{17,1},{25,9},{2,18},{10... | collective-permute-start | bytes 294920 | tf_op jit(solution)/shard_map/ppermute | solution.py:55
  174.9 14.4 %collective-permute-start.29 = (f32[224,512]{1,0:T(8,128)S(1)}, f32[224,512]{1,0:T(8,128)S(1)}, u32[]{:S(2)}, u32[]{:S(2)}) collective-permute-start(f32[224,512]{1,0:T(8,128)S(1)} %fusion), channel_id=1, source_target_pairs={{0,4},{4,0},{1,5},{5,1},{2,6},{6,2},{3,7},{7,3},{8,12},{12,8},{9,1... | collective-permute-start | bytes 1376264 | tf_op jit(solution)/shard_map/ppermute | solution.py:55
  181.6 6.0 %collective-permute-start.28 = (f32[48,512]{1,0:T(8,128)S(1)}, f32[48,512]{1,0:T(8,128)S(1)}, u32[]{:S(2)}, u32[]{:S(2)}) collective-permute-start(f32[48,512]{1,0:T(8,128)S(1)} %add.322), channel_id=1, source_target_pairs={{0,16},{8,24},{16,0},{24,8},{1,17},{9,25},{17,1},{25,9},{2,18},{10... | collective-permute-start | bytes 294920 | tf_op jit(solution)/shard_map/ppermute | solution.py:55
  187.7 10.8 %collective-permute-start.31 = (f32[96,512]{1,0:T(8,128)S(1)}, f32[96,512]{1,0:T(8,128)S(1)}, u32[]{:S(2)}, u32[]{:S(2)}) collective-permute-start(f32[96,512]{1,0:T(8,128)S(1)} %pad_maximum_fusion.20), channel_id=1, source_target_pairs={{0,8},{8,0},{16,24},{24,16},{1,9},{9,1},{17,25},{25,17},{2,10},{10... | collective-permute-start | bytes 589832 | tf_op jit(solution)/shard_map/ppermute | solution.py:55
  187.8 10.6 %collective-permute-start.30 = (f32[192,512]{1,0:T(8,128)S(1)}, f32[192,512]{1,0:T(8,128)S(1)}, u32[]{:S(2)}, u32[]{:S(2)}) collective-permute-start(f32[192,512]{1,0:T(8,128)S(1)} %slice.156), channel_id=1, source_target_pairs={{0,1},{1,0},{2,3},{3,2},{4,5},{5,4},{6,7},{7,6},{8,9},{9,8},{10,11... | collective-permute-start | bytes 1179656 | tf_op jit(solution)/shard_map/ppermute | solution.py:55
  198.6 7.8 %collective-permute-start.32 = (f32[96,512]{1,0:T(8,128)S(1)}, f32[96,512]{1,0:T(8,128)S(1)}, u32[]{:S(2)}, u32[]{:S(2)}) collective-permute-start(f32[96,512]{1,0:T(8,128)S(1)} %get-tuple-element.259), channel_id=1, source_target_pairs={{0,4},{4,0},{1,5},{5,1},{2,6},{6,2},{3,7},{7,3},{8,12},{12,8},{9,1... | collective-permute-start | bytes 589832 | tf_op jit(solution)/shard_map/ppermute | solution.py:55
  200.2 28.1 %collective-permute-start.34 = (f32[448,512]{1,0:T(8,128)S(1)}, f32[448,512]{1,0:T(8,128)S(1)}, u32[]{:S(2)}, u32[]{:S(2)}) collective-permute-start(f32[448,512]{1,0:T(8,128)S(1)} %pad_maximum_fusion.8), channel_id=1, source_target_pairs={{0,1},{1,0},{2,3},{3,2},{4,5},{5,4},{6,7},{7,6},{8,9},{9,8},{10,11... | collective-permute-start | bytes 2752520 | tf_op jit(solution)/shard_map/ppermute | solution.py:55
  201.6 27.1 %collective-permute-start.35 = (f32[384,512]{1,0:T(8,128)S(1)}, f32[384,512]{1,0:T(8,128)S(1)}, u32[]{:S(2)}, u32[]{:S(2)}) collective-permute-start(f32[384,512]{1,0:T(8,128)S(1)} %pad_maximum_fusion.11), channel_id=1, source_target_pairs={{0,4},{4,0},{1,5},{5,1},{2,6},{6,2},{3,7},{7,3},{8,12},{12,8},{9,1... | collective-permute-start | bytes 2359304 | tf_op jit(solution)/shard_map/ppermute | solution.py:55
  202.1 25.6 %collective-permute-start.33 = (f32[96,512]{1,0:T(8,128)S(1)}, f32[96,512]{1,0:T(8,128)S(1)}, u32[]{:S(2)}, u32[]{:S(2)}) collective-permute-start(f32[96,512]{1,0:T(8,128)S(1)} %get-tuple-element.261), channel_id=1, source_target_pairs={{0,1},{1,0},{2,3},{3,2},{4,5},{5,4},{6,7},{7,6},{8,9},{9,8},{10,11... | collective-permute-start | bytes 589832 | tf_op jit(solution)/shard_map/ppermute | solution.py:55
  206.5 26.9 %collective-permute-start.36 = (f32[192,512]{1,0:T(8,128)S(1)}, f32[192,512]{1,0:T(8,128)S(1)}, u32[]{:S(2)}, u32[]{:S(2)}) collective-permute-start(f32[192,512]{1,0:T(8,128)S(1)} %pad_maximum_fusion.18), channel_id=1, source_target_pairs={{0,1},{1,0},{2,3},{3,2},{4,5},{5,4},{6,7},{7,6},{8,9},{9,8},{10,11... | collective-permute-start | bytes 1179656 | tf_op jit(solution)/shard_map/ppermute | solution.py:55
  227.8 7.8 %collective-permute-start.37 = (f32[192,512]{1,0:T(8,128)S(1)}, f32[192,512]{1,0:T(8,128)S(1)}, u32[]{:S(2)}, u32[]{:S(2)}) collective-permute-start(f32[192,512]{1,0:T(8,128)S(1)} %pad_maximum_fusion.19), channel_id=1, source_target_pairs={{0,4},{4,0},{1,5},{5,1},{2,6},{6,2},{3,7},{7,3},{8,12},{12,8},{9,1... | collective-permute-start | bytes 1179656 | tf_op jit(solution)/shard_map/ppermute | solution.py:55
  236.6 2.6 %collective-permute-start.39 = (f32[384,512]{1,0:T(8,128)}, f32[384,512]{1,0:T(8,128)}, u32[]{:S(2)}, u32[]{:S(2)}) collective-permute-start(f32[384,512]{1,0:T(8,128)} %pad_maximum_fusion.13), channel_id=1, source_target_pairs={{0,2},{2,0},{1,3},{3,1},{4,6},{6,4},{5,7},{7,5},{8,10},{10,8},{9,1... | collective-permute-start | bytes 2359304 | tf_op jit(solution)/shard_map/ppermute | solution.py:55
  236.6 6.0 %collective-permute-start.38 = (f32[384,512]{1,0:T(8,128)}, f32[384,512]{1,0:T(8,128)}, u32[]{:S(2)}, u32[]{:S(2)}) collective-permute-start(f32[384,512]{1,0:T(8,128)} %pad_maximum_fusion.12), channel_id=1, source_target_pairs={{0,2},{2,0},{1,3},{3,1},{4,6},{6,4},{5,7},{7,5},{8,10},{10,8},{9,1... | collective-permute-start | bytes 2359304 | tf_op jit(solution)/shard_map/ppermute | solution.py:55
  237.1 12.1 %collective-permute-start.40 = (f32[896,512]{1,0:T(8,128)S(1)}, f32[896,512]{1,0:T(8,128)}, u32[]{:S(2)}, u32[]{:S(2)}) collective-permute-start(f32[896,512]{1,0:T(8,128)S(1)} %pad_maximum_fusion.2), channel_id=1, source_target_pairs={{0,2},{2,0},{1,3},{3,1},{4,6},{6,4},{5,7},{7,5},{8,10},{10,8},{9,1... | collective-permute-start | bytes 5505032 | tf_op jit(solution)/shard_map/ppermute | solution.py:55
  237.1 12.1 %collective-permute-start.41 = (f32[768,512]{1,0:T(8,128)S(1)}, f32[768,512]{1,0:T(8,128)S(1)}, u32[]{:S(2)}, u32[]{:S(2)}) collective-permute-start(f32[768,512]{1,0:T(8,128)S(1)} %pad_maximum_fusion.3), channel_id=1, source_target_pairs={{0,2},{2,0},{1,3},{3,1},{4,6},{6,4},{5,7},{7,5},{8,10},{10,8},{9,1... | collective-permute-start | bytes 4718600 | tf_op jit(solution)/shard_map/ppermute | solution.py:55
  253.4 2.9 %copy-start.8 = (f32[5,128,512]{2,1,0:T(8,128)}, f32[5,128,512]{2,1,0:T(8,128)S(1)}, u32[]{:S(2)}) copy-start(f32[5,128,512]{2,1,0:T(8,128)S(1)} %fusion.1) | copy-start | bytes 3932164

commit v2 on v1

--- a/solution.py
+++ b/solution.py
@@ -80,14 +80,17 @@
         return value
 
 
-def halved(chain, arrays, axis, bit):
+def halved(chain, arrays, axis, bit, tight=False):
     arrays = chain.after(arrays)
     half = arrays[0].shape[0] // 2
     one = bit_value(axis, bit)
     send = chain.step(part(arrays, (1 - one) * half, half))
     got = swap(send, axis, bit)
     send, arrays = lax.optimization_barrier((send, arrays))
-    return [part(arrays, one * half, half), got]
+    keep = part(arrays, one * half, half)
+    if tight:
+        chain.step((send, keep))
+    return [keep, got]
 
 
 def joined_halves(value, other, axis, bit):
@@ -95,18 +98,18 @@
     return jnp.concatenate([jnp.where(one, other, value), jnp.where(one, value, other)])
 
 
-def reduction(chain, first, second):
+def reduction(chain, first, second, tight=False):
     across, along = bits_of("gz"), bits_of("gyh")
     lanes = [first, second]
-    for plan in ((across, along), (along, across)):
+    for turn, plan in enumerate(((across, along), (along, across))):
         for i in range(2):
             for axis, bit in plan[i]:
-                lanes[i] = halved(chain, lanes[i], axis, bit)
+                lanes[i] = halved(chain, lanes[i], axis, bit, tight and turn == 1)
         yield
     sizes = [x[0].shape[0] for x in lanes]
     joint = [jnp.concatenate(pair) for pair in zip(*chain.after(lanes))]
     for axis, bit in bits_of("gx"):
-        joint = halved(chain, joint, axis, bit)
+        joint = halved(chain, joint, axis, bit, tight)
         yield
     joint = chain.after(joint)
     value = chain.step(sum(joint[1:], joint[0]))
@@ -642,6 +645,53 @@
     split_cores(core, second, keep_second, send_second)
 
 
+def late_outputs(
+    a_mine, a_other, b_mine, b_other, core,
+    res, ae, trip_bil, trip_up, quad_bil, quad_up, rad, ea, ad,
+):
+    upper = core[0] == 1
+
+    def rows(mine, other, at, size):
+        half = mine.shape[0]
+        where = slice(at % half, at % half + size)
+        if at < half:
+            return jnp.where(upper, other[where], mine[where])
+        return jnp.where(upper, mine[where], other[where])
+
+    a = lambda at, size: rows(a_mine, a_other, at, size)
+    b = lambda at, size: rows(b_mine, b_other, at, size)
+    for k in range(2):
+        res[k] = a(896 * k, 512)
+        ae[k] = a(896 * k + 512, 256)
+        trip_bil[:, 512 * k : 512 * k + 512] = a(768 + 64 * k, 64)
+        quad_bil[:, 512 * k : 512 * k + 512] = a(1728 + 32 * k, 32)
+    trip_up[...] = a(1664, 64)
+    quad_up[...] = b(1408, 32)
+    for k in range(3):
+        rad[k] = b(1024 + 128 * k, 128)
+    both = b(0, 512)
+    ea[0], ea[1] = both[:, :256], both[:, 256:]
+    both = b(512, 256)
+    ad[0], ad[1] = both[:, :256], both[:, 256:]
+    both = b(768, 256)
+    ad[2], ad[3] = both[:, :256], both[:, 256:]
+
+
+def early_outputs(c_mine, c_other, d_mine, d_other, late_rad, core, inputs, rad, trip_down, quad_down, tags):
+    upper = core[0] == 1
+    for k, (mine, other) in enumerate(((c_mine, c_other), (d_mine, d_other))):
+        inputs[k, 0:384] = jnp.where(upper, other[...], mine[...])
+        high = jnp.where(upper, mine[...], other[...])
+        inputs[k, 384:512] = high[:128]
+        rad[k] = high[128:256]
+        if k == 0:
+            trip_down[...] = high[256:320]
+        else:
+            quad_down[...] = high[256:288]
+            tags[...] = high[288:291, :256]
+    rad[2:5] = late_rad[...]
+
+
 def call(kernel, outs, args, scratch=(), micros=1):
     flops = int(micros * 1.15e9)
     return pl.pallas_call(
@@ -651,7 +701,7 @@
         out_specs=[pl.BlockSpec(memory_space=pltpu.VMEM)] * len(outs),
         scratch_shapes=list(scratch),
         compiler_params=pltpu.CompilerParams(vmem_limit_bytes=56 * 1024 * 1024),
-        cost_estimate=pl.CostEstimate(flops=flops, bytes_accessed=4 << 20, transcendentals=0),
+        cost_estimate=pl.CostEstimate(flops=flops, bytes_accessed=1 << 10, transcendentals=0),
     )(*args)
 
 
@@ -745,7 +795,7 @@
         scratch=[pltpu.VMEM((1536, 512), F32)],
         micros=4,
     )
-    late = reduction(chain, [keep_a, got_a], [keep_b, swap(send_b, "gyl", 0)])
+    late = reduction(chain, [keep_a, got_a], [keep_b, swap(send_b, "gyl", 0)], True)
     next(late)
     grad_sums = chain.after(grad_sums)
     back_before, back_here, back_after, back_local = call(
@@ -772,6 +822,7 @@
         returned = mine + lax.ppermute(theirs, "gz", [(0, 1), (1, 0)])
     else:
         returned = value[1] + shifted(value[0], "gz", -1, False) + shifted(value[2], "gz", 1, False)
+    returned = chain.after(returned)
     grad_atoms, grad_edges, keep_c, send_c, keep_d, send_d = call(
         finish_kernel,
         [(8, 256), (EDGES, 512)] + [(384, 512)] * 4,
@@ -780,9 +831,10 @@
         scratch=[pltpu.VMEM((768, 512), F32)] * 2,
         micros=7,
     )
+    next(late)
+    send_c, send_d = chain.after((send_c, send_d))
     got_c, got_d = swap(send_c, "gyl", 0), swap(send_d, "gyl", 0)
     early = reduction(chain, [keep_c, got_c], [keep_d, got_d])
-    chain.step(keep_c)
     running = {"L": late, "E": early}
     done = {}
 
@@ -794,50 +846,47 @@
         except StopIteration as end:
             done[name] = end.value
 
-    for name in "LELEELELEELEELEEL":
+    for name in "ELEELELEELEELEL":
         resume(name)
-    while len(done) < 2:
+    while "L" not in done:
+        resume("L")
+    (a_mine, a_other), (b_mine, b_other) = done["L"]
+    g_res, g_ae, g_trip_bil, g_trip_up, g_quad_bil, g_quad_up, g_rad, g_ea, g_ad = call(
+        late_outputs,
+        [(2, 512, 512), (2, 256, 512), (64, 1024), (64, 512), (32, 1024), (32, 512), (3, 128, 512)]
+        + [(2, 512, 256), (4, 256, 256)],
+        [a_mine, a_other, b_mine, b_other, core],
+        micros=5,
+    )
+    chain.step(g_rad)
+    while "E" not in done:
         resume("E")
-        resume("L")
-    upper = bit_value("gyl", 0) == 1
-
-    def both(name, i):
-        mine, other = done[name][i]
-        return jnp.where(upper, other, mine), jnp.where(upper, mine, other)
-
-    (a_low, a_high), (b_low, b_high) = both("L", 0), both("L", 1)
-    (c_low, c_high), (d_low, d_high) = both("E", 0), both("E", 1)
-
-    def pair(x, width):
-        return jnp.stack([x[:, :width], x[:, width:]])
-
-    def joined(x):
-        half = x.shape[0] // 2
-        return jnp.concatenate([x[:half], x[half:]], axis=1)
-
-    grad_radial = [c_high[128:256], d_high[128:256]] + [
-        b_high[256 + 128 * k : 384 + 128 * k] for k in range(3)
-    ]
-    grad_inputs = jnp.concatenate([c_low, c_high[:128], d_low, d_high[:128]])
+    (c_mine, c_other), (d_mine, d_other) = done["E"]
+    g_inputs, g_rad, g_trip_down, g_quad_down, g_tags = call(
+        early_outputs,
+        [(2, 512, 512), (5, 128, 512), (64, 512), (32, 512), (3, 256)],
+        [c_mine, c_other, d_mine, d_other, g_rad, core],
+        micros=3,
+    )
     return (
         atoms_out,
         edges_out,
         energy_out,
         grad_atoms,
         grad_edges,
-        grad_inputs.reshape(2, 512, 512),
-        jnp.stack(grad_radial),
-        c_high[256:320].T,
-        joined(a_low[768:896]).T,
-        a_high[768:832],
-        d_high[256:288].T,
-        joined(a_high[832:896]).T,
-        b_high[640:672],
-        jnp.stack([a_low[512:768], a_high[512:768]]),
-        jnp.stack([a_low[:512], a_high[:512]]),
-        pair(b_low[:512], 256),
-        jnp.concatenate([pair(b_low[512:768], 256), pair(b_high[:256], 256)]),
-        d_high[288:291, :256],
+        g_inputs,
+        g_rad,
+        g_trip_down.T,
+        g_trip_bil.T,
+        g_trip_up,
+        g_quad_down.T,
+        g_quad_bil.T,
+        g_quad_up,
+        g_ae,
+        g_res,
+        g_ea,
+        g_ad,
+        g_tags,
     )
 
 

time: 260 us -> 243 us (0.935)
  other arithmetic: 36.1 us -> 18.1 us
  waiting for transfers between devices: 122 us -> 105 us
  Pallas kernels: 54.6 us -> 64.4 us
  starting transfers between devices: 37.5 us -> 44.3 us
    ppermute x32, waiting for transfers between devices: 93.7 us -> 74.7 us  [swap(): return lax.ppermute(value, axis, [(i, i ^ 1 << bit) for i in range(count)])]
    pallas_call x5 -> x7, Pallas kernels: 54.6 us -> 64.4 us  [call(): pl.pallas_call(kernel, out_shape=[jax.ShapeDtypeStruct(shape, F32) for sh...]
    ppermute x32, starting transfers between devices: 23.8 us -> 30.1 us  [swap(): return lax.ppermute(value, axis, [(i, i ^ 1 << bit) for i in range(count)])]
    select_n x4 -> x0, other arithmetic: 5.39 us -> none  [both(): return (jnp.where(upper, other, mine), jnp.where(upper, mine, other))]
    unnamed x37 -> x43, local copies, waits for them, and re-layouts: 0.9 us -> 5.14 us
    another operation x3 -> x0, other arithmetic: 3.56 us -> none  [the longest x1 1.49 us: per_device(): jnp.stack([a_low[:512], a_high[:512]])]
    add x24, other arithmetic: 15.8 us -> 12.5 us  [part(): total = total + lax.dynamic_slice_in_dim(x, at, size)]
  transfers between devices with their start and end apart: 42 -> 42, of which waited for: 28 -> 26; matrix products, arithmetic and copies ran while one was open for 12% -> 9% of each run, Pallas kernels for 9% -> 12%
where the time goes in v2:
time: 243 us; the launch traced here: 242 us
  waiting for transfers between devices  105 us (43%)
  Pallas kernels  64.4 us (27%)
  starting transfers between devices  44.3 us (18%)
  other arithmetic  18.1 us (7%)
  local copies, waits for them, and re-layouts  9.31 us (4%)
    ppermute x32, waiting for transfers between devices, swap(): return lax.ppermute(value, axis, [(i, i ^ 1 << bit) for i in range(count)])  74.7 us
    pallas_call x7, Pallas kernels, call(): pl.pallas_call(kernel, out_shape=[jax.ShapeDtypeStruct(shape, F32) for sh...  64.4 us
    ppermute x32, starting transfers between devices, swap(): return lax.ppermute(value, axis, [(i, i ^ 1 << bit) for i in range(count)])  30.1 us
    ppermute x8, waiting for transfers between devices, shifted(): return lax.ppermute(value, axis, pairs)  24 us
    add x24, other arithmetic, part(): total = total + lax.dynamic_slice_in_dim(x, at, size)  12.5 us
    ppermute x8, starting transfers between devices, shifted(): return lax.ppermute(value, axis, pairs)  10.6 us
    unnamed x43, local copies, waits for them, and re-layouts  5.14 us
  transfers between devices with their start and end apart: 42, of which 26 were waited for; matrix products, arithmetic and copies ran while one was open for 9% of the time, Pallas kernels for 12%

profile of v2, /device:TPU:0, one launch (start us, length us, event | category | flops | bytes accessed | tf_op | source)
XLA Modules:
  0.0 242.5 jit_solution(16780951813169820513)
XLA Ops:
  0.7 4.7 %shard_map.394 = (f32[17,8,128]{2,1,0:T(8,128)}, f32[17,16,128]{2,1,0:T(8,128)}, f32[8,256]{1,0:T(8,128)}, f32[2,240,512]{2,1,0:T(8,128)}, f32[240,128]{1,0:T(8,...) custom-call(f32[240,512]{1,0:T(8,128)} %edge.5, f32[3,240]{1,0:T(4,128)} %vec.1, ...), custom_call_target="tpu_custom_call" | custom-call | flops 5750000128 | bytes 1024 | tf_op jit(solution)/shard_map/pallas_call | solution.py:697
  5.4 3.0 %collective-permute-start = (f32[17,8,128]{2,1,0:T(8,128)}, f32[17,8,128]{2,1,0:T(8,128)S(1)}, u32[]{:S(2)}, u32[]{:S(2)}) collective-permute-start(f32[17,8,128]{2,1,0:T(8,128)} %get-tuple-element.165), channel_id=1, source_target_pairs={{0,1},{1,0},{2,3},{3,2},{4,5},{5,4},{6,7},{7,6},{8,9},{9,8},{10,11... | collective-permute-start | bytes 208904 | tf_op jit(solution)/shard_map/ppermute | solution.py:36
  9.2 1.6 collective-permute-done
  10.9 0.9 select_bitcast_fusion.1
  11.8 2.2 collective-permute-start.1
  13.9 2.1 collective-permute-start.2
  16.0 4.1 %collective-permute-done.1 = f32[2,17,8,128]{3,2,1,0:T(8,128)S(1)} collective-permute-done((f32[2,17,8,128]{3,2,1,0:T(8,128)S(1)}, f32[2,17,8,128]{3,2,1,0:T(8,128)S(1)}, u32[]{:S(2)}, u32[]{:S(2)}) %collective-permute-start.1) | collective-permute-done | bytes 139296 | tf_op jit(solution)/shard_map/ppermute | solution.py:31
  21.0 1.7 collective-permute-start.4
  25.1 6.0 %collective-permute-done.3.halo_before = f32[6,17,8,128]{3,2,1,0:T(8,128)S(1)} collective-permute-done((f32[6,17,8,128]{3,2,1,0:T(8,128)S(1)}, f32[6,17,8,128]{3,2,1,0:T(8,128)S(1)}, u32[]{:S(2)}, u32[]{:S(2)}) %collective-permute-start.3) | collective-permute-done | bytes 417824 | tf_op jit(solution)/shard_map/ppermute | solution.py:31
  31.1 0.9 collective-permute-done.4.halo_after
  32.7 25.7 %shard_map.395 = (f32[8,256]{1,0:T(8,128)}, f32[240,512]{1,0:T(8,128)}, f32[8,256]{1,0:T(8,128)}, f32[240,512]{1,0:T(8,128)}, f32[8,256]{1,0:T(8,128)}, /*index=...) custom-call(f32[6,17,8,128]{3,2,1,0:T(8,128)} %copy-done.19, ...), custom_call_target="tpu_custom_call" | custom-call | flops 29899999232 | bytes 1024 | tf_op jit(solution)/shard_map/pallas_call | solution.py:697
  58.5 0.9 collective-permute-start.5
  59.3 4.2 %shard_map.396 = (f32[768,512]{1,0:T(8,128)}, f32[768,512]{1,0:T(8,128)}) custom-call(f32[3,240,512]{2,1,0:T(8,128)} %get-tuple-element.177.grad_rads, f32[240,128]{1,0:T(8,128)} %get-tuple-element.170.radial, f32[8,3328]{1,0:T(8,128)} %get-tuple-element.178.atom_rows, f32[32,512]{1,0:T(8,128)} %get-tuple-element.179.quad_up_grad, s32[1]{0:T(128)} %bitcast.12.core), custom_call_target="tpu_custom_call" | custom-call | flops 4600000000 | bytes 1024 | tf_op jit(solution)/shard_map/pallas_call | solution.py:697
  65.1 0.9 fusion.3
  66.8 1.4 dynamic-slice_add_fusion.1
  68.2 1.6 collective-permute-start.7
  69.7 1.3 dynamic-slice_add_fusion.3
  71.0 1.6 collective-permute-start.8
  72.6 13.2 %shard_map.397 = (f32[6,16,8,128]{3,2,1,0:T(8,128)}, f32[6,16,8,128]{3,2,1,0:T(8,128)}, f32[6,16,8,128]{3,2,1,0:T(8,128)}, f32[16,16,128]{2,1,0:T(8,128)}) custom-call(f32[30,8,8,128]{3,2,1,0:T(8,128)} %get-tuple-element.174.cosines, f32[240,2048]{1,0:T(8,128)} %get-tuple-element.185.sums, f32[240,256]{1,0:T(8,128)} %get-tuple-element.186.grad_src, ...), custom_call_target="tpu_custom_call" | custom-call | flops 14949999616 | bytes 1024 | tf_op jit(solution)/shard_map/pallas_call | solution.py:697
  85.8 1.7 collective-permute-start.9
  87.5 1.3 dynamic-slice_add_fusion.2
  88.8 1.4 dynamic-slice_add_fusion
  91.6 6.8 %collective-permute-done.10 = f32[6,16,8,128]{3,2,1,0:T(8,128)S(1)} collective-permute-done((f32[6,16,8,128]{3,2,1,0:T(8,128)}, f32[6,16,8,128]{3,2,1,0:T(8,128)S(1)}, u32[]{:S(2)}, u32[]{:S(2)}) %collective-permute-start.10) | collective-permute-done | bytes 393248 | tf_op jit(solution)/shard_map/ppermute | solution.py:31
  98.5 2.8 %collective-permute-start.11 = (f32[2,16,8,128]{3,2,1,0:T(8,128)S(1)}, f32[2,16,8,128]{3,2,1,0:T(8,128)S(1)}, u32[]{:S(2)}, u32[]{:S(2)}) collective-permute-start(f32[2,16,8,128]{3,2,1,0:T(8,128)S(1)} %get-tuple-element.338), channel_id=1, source_target_pairs={{0,24},{8,0},{16,8},{24,16},{1,25},{9,1},{17,9},{25,17},{2,26},{10... | collective-permute-start | bytes 393224 | tf_op jit(solution)/shard_map/ppermute | solution.py:31
  101.9 1.5 collective-permute-start.13
  103.4 1.8 collective-permute-done.11
  105.2 3.6 %collective-permute-done.12 = f32[2,16,8,128]{3,2,1,0:T(8,128)S(1)} collective-permute-done((f32[2,16,8,128]{3,2,1,0:T(8,128)S(1)}, f32[2,16,8,128]{3,2,1,0:T(8,128)S(1)}, u32[]{:S(2)}, u32[]{:S(2)}) %collective-permute-start.12) | collective-permute-done | bytes 131104 | tf_op jit(solution)/shard_map/ppermute | solution.py:31
  109.5 4.6 %collective-permute-done.15 = f32[16,8,128]{2,1,0:T(8,128)S(1)} collective-permute-done((f32[16,8,128]{2,1,0:T(8,128)S(1)}, f32[16,8,128]{2,1,0:T(8,128)S(1)}, u32[]{:S(2)}, u32[]{:S(2)}) %collective-permute-start.15) | collective-permute-done | bytes 65568 | tf_op jit(solution)/shard_map/ppermute | solution.py:822
  115.5 6.8 %shard_map.398 = (f32[8,256]{1,0:T(8,128)}, f32[240,512]{1,0:T(8,128)}, f32[384,512]{1,0:T(8,128)}, f32[384,512]{1,0:T(8,128)}, f32[384,512]{1,0:T(8,128)}, /*index=5*/f32[384,512]{1,0:T(8,128)}) custom-call(f32[16,16,128]{2,1,0:T(8,128)} %get-tuple-element.187.back_local, f32[16,8,128]{2,1,0:T(8,128)} %bitcast_add_fusion.returned, ...), custom_call_target="tpu_custom_call" | custom-call | flops 8049999872 | bytes 1024 | tf_op jit(solution)/shard_map/pallas_call | solution.py:697
  122.4 3.8 %collective-permute-done.16 = f32[208,512]{1,0:T(8,128)S(1)} collective-permute-done((f32[208,512]{1,0:T(8,128)S(1)}, f32[208,512]{1,0:T(8,128)S(1)}, u32[]{:S(2)}, u32[]{:S(2)}) %collective-permute-start.16) | collective-permute-done | bytes 426016 | tf_op jit(solution)/shard_map/ppermute | solution.py:55
  126.8 2.0 collective-permute-start.19
  129.1 1.8 dynamic-slice_add_fusion.11
  131.7 1.8 dynamic-slice_add_fusion.10
  133.5 1.6 collective-permute-start.21
  135.1 4.4 %collective-permute-done.19 = f32[104,512]{1,0:T(8,128)S(1)} collective-permute-done((f32[104,512]{1,0:T(8,128)S(1)}, f32[104,512]{1,0:T(8,128)S(1)}, u32[]{:S(2)}, u32[]{:S(2)}) %collective-permute-start.19) | collective-permute-done | bytes 213024 | tf_op jit(solution)/shard_map/ppermute | solution.py:55
  139.7 1.1 dynamic-slice_add_fusion.8
  140.8 1.5 collective-permute-done.20
  142.3 2.4 collective-permute-done.21
  144.7 1.0 dynamic-slice_add_fusion.20
  145.7 1.3 collective-permute-start.23
  147.0 1.6 collective-permute-start.22
  148.5 1.0 dynamic-slice_add_fusion.18
  149.5 2.0 collective-permute-done.23
  151.5 1.1 collective-permute-done.22
  152.8 1.2 collective-permute-start.26
  154.0 0.9 collective-permute-start.25
  155.0 11.9 %collective-permute-done.25 = f32[96,512]{1,0:T(8,128)S(1)} collective-permute-done((f32[96,512]{1,0:T(8,128)S(1)}, f32[96,512]{1,0:T(8,128)S(1)}, u32[]{:S(2)}, u32[]{:S(2)}) %collective-permute-start.25) | collective-permute-done | bytes 196640 | tf_op jit(solution)/shard_map/ppermute | solution.py:55
  166.8 2.3 collective-permute-start.27
  169.3 1.6 collective-permute-start.29
  170.9 4.0 %collective-permute-done.27 = f32[48,512]{1,0:T(8,128)S(1)} collective-permute-done((f32[48,512]{1,0:T(8,128)S(1)}, f32[48,512]{1,0:T(8,128)S(1)}, u32[]{:S(2)}, u32[]{:S(2)}) %collective-permute-start.27) | collective-permute-done | bytes 98336 | tf_op jit(solution)/shard_map/ppermute | solution.py:55
  175.8 5.3 %collective-permute-done.28 = f32[48,512]{1,0:T(8,128)S(1)} collective-permute-done((f32[48,512]{1,0:T(8,128)S(1)}, f32[48,512]{1,0:T(8,128)S(1)}, u32[]{:S(2)}, u32[]{:S(2)}) %collective-permute-start.28) | collective-permute-done | bytes 98336 | tf_op jit(solution)/shard_map/ppermute | solution.py:55
  181.1 1.8 collective-permute-start.31
  182.9 0.8 collective-permute-start.30
  183.9 10.9 %collective-permute-done.30 = f32[192,512]{1,0:T(8,128)S(1)} collective-permute-done((f32[192,512]{1,0:T(8,128)S(1)}, f32[192,512]{1,0:T(8,128)S(1)}, u32[]{:S(2)}, u32[]{:S(2)}) %collective-permute-start.30) | collective-permute-done | bytes 393248 | tf_op jit(solution)/shard_map/ppermute | solution.py:55
  195.0 1.8 collective-permute-start.32
  197.8 1.2 collective-permute-start.33
  199.1 1.6 collective-permute-done.32
  200.8 13.8 %collective-permute-done.33 = f32[96,512]{1,0:T(8,128)S(1)} collective-permute-done((f32[96,512]{1,0:T(8,128)S(1)}, f32[96,512]{1,0:T(8,128)S(1)}, u32[]{:S(2)}, u32[]{:S(2)}) %collective-permute-start.33) | collective-permute-done | bytes 196640 | tf_op jit(solution)/shard_map/ppermute | solution.py:55
  217.7 10.1 %collective-permute-done.36 = f32[192,512]{1,0:T(8,128)S(1)} collective-permute-done((f32[192,512]{1,0:T(8,128)S(1)}, f32[192,512]{1,0:T(8,128)S(1)}, u32[]{:S(2)}, u32[]{:S(2)}) %collective-permute-start.36) | collective-permute-done | bytes 393248 | tf_op jit(solution)/shard_map/ppermute | solution.py:55
  229.1 1.2 copy-done.16
  230.2 1.2 copy-done.15
  231.4 5.9 %shard_map.399 = (f32[2,512,512]{2,1,0:T(8,128)}, f32[2,256,512]{2,1,0:T(8,128)}, f32[64,1024]{1,0:T(8,128)}, f32[64,512]{1,0:T(8,128)}, f32[32,1024]{1,0:T(8,12...) custom-call(f32[896,512]{1,0:T(8,128)} %copy-done, ...), custom_call_target="tpu_custom_call" | custom-call | flops 5750000128 | bytes 1024 | tf_op jit(solution)/shard_map/pallas_call | solution.py:697
  237.3 0.9 copy-done.17
  238.5 4.0 %shard_map.400 = (f32[2,512,512]{2,1,0:T(8,128)}, f32[5,128,512]{2,1,0:T(8,128)}, f32[64,512]{1,0:T(8,128)}, f32[32,512]{1,0:T(8,128)}, f32[3,256]{1,0:T(4,128)}) custom-call(f32[384,512]{1,0:T(8,128)} %copy-done.4, f32[384,512]{1,0:T(8,128)} %copy-done.18, f32[384,512]{1,0:T(8,128)} %copy-done.5, f32[384,512]{1,0:T(8,128)} %copy-done.17, ...), custom_call_target="tpu_custom_call" | custom-call | flops 3449999872 | bytes 1024 | tf_op jit(solution)/shard_map/pallas_call | solution.py:697
  (150 shorter events, 20.3 us)
Async XLA Ops:
  0.7 7.7 %copy-start.14 = (s32[240]{0:T(256)S(1)}, s32[240]{0:T(256)}, u32[]{:S(2)}) copy-start(s32[240]{0:T(256)} %param.32) | copy-start | bytes 2884
  0.7 7.7 %copy-start.12 = (s32[240,8]{0,1:T(8,128)S(1)}, s32[240,8]{0,1:T(8,128)}, u32[]{:S(2)}) copy-start(s32[240,8]{0,1:T(8,128)} %param.33) | copy-start | bytes 23044
  0.7 7.8 %copy-start.13 = (s32[240,8]{0,1:T(8,128)S(1)}, s32[240,8]{0,1:T(8,128)}, u32[]{:S(2)}) copy-start(s32[240,8]{0,1:T(8,128)} %param.35) | copy-start | bytes 23044
  5.3 18.9 %copy-start.10 = (s32[240,8]{0,1:T(8,128)S(1)}, s32[240,8]{0,1:T(8,128)}, u32[]{:S(2)}) copy-start(s32[240,8]{0,1:T(8,128)} %param.34) | copy-start | bytes 23044
  5.4 18.9 %copy-start.11 = (s32[240,8]{0,1:T(8,128)S(1)}, s32[240,8]{0,1:T(8,128)}, u32[]{:S(2)}) copy-start(s32[240,8]{0,1:T(8,128)} %param.36) | copy-start | bytes 23044
  5.4 5.5 %collective-permute-start = (f32[17,8,128]{2,1,0:T(8,128)}, f32[17,8,128]{2,1,0:T(8,128)S(1)}, u32[]{:S(2)}, u32[]{:S(2)}) collective-permute-start(f32[17,8,128]{2,1,0:T(8,128)} %get-tuple-element.165), channel_id=1, source_target_pairs={{0,1},{1,0},{2,3},{3,2},{4,5},{5,4},{6,7},{7,6},{8,9},{9,8},{10,11... | collective-permute-start | bytes 208904 | tf_op jit(solution)/shard_map/ppermute | solution.py:36
  11.8 8.4 %collective-permute-start.1 = (f32[2,17,8,128]{3,2,1,0:T(8,128)S(1)}, f32[2,17,8,128]{3,2,1,0:T(8,128)S(1)}, u32[]{:S(2)}, u32[]{:S(2)}) collective-permute-start(f32[2,17,8,128]{3,2,1,0:T(8,128)S(1)} %pad_maximum_fusion.16), channel_id=1, source_target_pairs={{0,8},{8,16},{16,24},{24,0},{1,9},{9,17},{17,25},{25,1},{2,10},{10... | collective-permute-start | bytes 417800 | tf_op jit(solution)/shard_map/ppermute | solution.py:31
  13.9 7.0 %collective-permute-start.2 = (f32[2,17,8,128]{3,2,1,0:T(8,128)S(1)}, f32[2,17,8,128]{3,2,1,0:T(8,128)S(1)}, u32[]{:S(2)}, u32[]{:S(2)}) collective-permute-start(f32[2,17,8,128]{3,2,1,0:T(8,128)S(1)} %pad_maximum_fusion.16), channel_id=1, source_target_pairs={{0,24},{8,0},{16,8},{24,16},{1,25},{9,1},{17,9},{25,17},{2,26},{10... | collective-permute-start | bytes 417800 | tf_op jit(solution)/shard_map/ppermute | solution.py:31
  21.0 11.0 %copy-start.8 = (f32[6,17,8,128]{3,2,1,0:T(8,128)}, f32[6,17,8,128]{3,2,1,0:T(8,128)S(1)}, u32[]{:S(2)}) copy-start(f32[6,17,8,128]{3,2,1,0:T(8,128)S(1)} %pad_maximum_fusion.10.halo_here) | copy-start | bytes 1253380
  21.0 10.1 %collective-permute-start.3 = (f32[6,17,8,128]{3,2,1,0:T(8,128)S(1)}, f32[6,17,8,128]{3,2,1,0:T(8,128)S(1)}, u32[]{:S(2)}, u32[]{:S(2)}) collective-permute-start(f32[6,17,8,128]{3,2,1,0:T(8,128)S(1)} %pad_maximum_fusion.10.halo_here), channel_id=1, source_target_pairs={{0,2},{2,4},{4,6},{6,0},{1,3},{3,5},{5,7},{7,1},{8,10},{10,12},{12... | collective-permute-start | bytes 1253384 | tf_op jit(solution)/shard_map/ppermute | solution.py:31
  21.0 11.0 %collective-permute-start.4 = (f32[6,17,8,128]{3,2,1,0:T(8,128)S(1)}, f32[6,17,8,128]{3,2,1,0:T(8,128)S(1)}, u32[]{:S(2)}, u32[]{:S(2)}) collective-permute-start(f32[6,17,8,128]{3,2,1,0:T(8,128)S(1)} %pad_maximum_fusion.10.halo_here), channel_id=1, source_target_pairs={{0,6},{2,0},{4,2},{6,4},{1,7},{3,1},{5,3},{7,5},{8,14},{10,8},{12,... | collective-permute-start | bytes 1253384 | tf_op jit(solution)/shard_map/ppermute | solution.py:31
  31.1 0.9 copy-start.19
  32.0 0.8 copy-start.20
  58.5 8.3 %collective-permute-start.5 = (f32[896,512]{1,0:T(8,128)}, f32[896,512]{1,0:T(8,128)}, u32[]{:S(2)}, u32[]{:S(2)}) collective-permute-start(f32[896,512]{1,0:T(8,128)} %get-tuple-element.176), channel_id=1, source_target_pairs={{0,2},{2,0},{1,3},{3,1},{4,6},{6,4},{5,7},{7,5},{8,10},{10,8},{9,1... | collective-permute-start | bytes 5505032 | tf_op jit(solution)/shard_map/ppermute | solution.py:55
  59.3 7.5 %copy-start.1 = (f32[896,512]{1,0:T(8,128)S(1)}, f32[896,512]{1,0:T(8,128)}, u32[]{:S(2)}) copy-start(f32[896,512]{1,0:T(8,128)} %get-tuple-element.188) | copy-start | bytes 5505028
  63.5 6.2 %collective-permute-start.6 = (f32[768,512]{1,0:T(8,128)}, f32[768,512]{1,0:T(8,128)}, u32[]{:S(2)}, u32[]{:S(2)}) collective-permute-start(f32[768,512]{1,0:T(8,128)} %get-tuple-element.181), channel_id=1, source_target_pairs={{0,2},{2,0},{1,3},{3,1},{4,6},{6,4},{5,7},{7,5},{8,10},{10,8},{9,1... | collective-permute-start | bytes 4718600 | tf_op jit(solution)/shard_map/ppermute | solution.py:55
  64.4 5.3 %copy-start.2 = (f32[768,512]{1,0:T(8,128)S(1)}, f32[768,512]{1,0:T(8,128)}, u32[]{:S(2)}) copy-start(f32[768,512]{1,0:T(8,128)} %get-tuple-element.194) | copy-start | bytes 4718596
  68.2 22.8 %collective-permute-start.7 = (f32[448,512]{1,0:T(8,128)S(1)}, f32[448,512]{1,0:T(8,128)S(1)}, u32[]{:S(2)}, u32[]{:S(2)}) collective-permute-start(f32[448,512]{1,0:T(8,128)S(1)} %dynamic-slice_add_fusion.1), channel_id=1, source_target_pairs={{0,1},{1,0},{2,3},{3,2},{4,5},{5,4},{6,7},{7,6},{8,9},{9,8},{10,11... | collective-permute-start | bytes 2752520 | tf_op jit(solution)/shard_map/ppermute | solution.py:55
  71.0 20.4 %collective-permute-start.8 = (f32[384,512]{1,0:T(8,128)S(1)}, f32[384,512]{1,0:T(8,128)S(1)}, u32[]{:S(2)}, u32[]{:S(2)}) collective-permute-start(f32[384,512]{1,0:T(8,128)S(1)} %dynamic-slice_add_fusion.3), channel_id=1, source_target_pairs={{0,4},{4,0},{1,5},{5,1},{2,6},{6,2},{3,7},{7,3},{8,12},{12,8},{9,1... | collective-permute-start | bytes 2359304 | tf_op jit(solution)/shard_map/ppermute | solution.py:55
  85.8 12.6 %collective-permute-start.10 = (f32[6,16,8,128]{3,2,1,0:T(8,128)}, f32[6,16,8,128]{3,2,1,0:T(8,128)S(1)}, u32[]{:S(2)}, u32[]{:S(2)}) collective-permute-start(f32[6,16,8,128]{3,2,1,0:T(8,128)} %get-tuple-element.201), channel_id=1, source_target_pairs={{0,2},{2,4},{4,6},{6,0},{1,3},{3,5},{5,7},{7,1},{8,10},{10,12},{12... | collective-permute-start | bytes 1179656 | tf_op jit(solution)/shard_map/ppermute | solution.py:31
  85.8 12.6 %collective-permute-start.9 = (f32[6,16,8,128]{3,2,1,0:T(8,128)}, f32[6,16,8,128]{3,2,1,0:T(8,128)S(1)}, u32[]{:S(2)}, u32[]{:S(2)}) collective-permute-start(f32[6,16,8,128]{3,2,1,0:T(8,128)} %get-tuple-element.200), channel_id=1, source_target_pairs={{0,6},{2,0},{4,2},{6,4},{1,7},{3,1},{5,3},{7,5},{8,14},{10,8},{12,... | collective-permute-start | bytes 1179656 | tf_op jit(solution)/shard_map/ppermute | solution.py:31
  91.0 7.4 %copy-start.9 = (f32[6,16,8,128]{3,2,1,0:T(8,128)S(1)}, f32[6,16,8,128]{3,2,1,0:T(8,128)}, u32[]{:S(2)}) copy-start(f32[6,16,8,128]{3,2,1,0:T(8,128)} %get-tuple-element.203) | copy-start | bytes 1179652
  98.5 6.7 %collective-permute-start.11 = (f32[2,16,8,128]{3,2,1,0:T(8,128)S(1)}, f32[2,16,8,128]{3,2,1,0:T(8,128)S(1)}, u32[]{:S(2)}, u32[]{:S(2)}) collective-permute-start(f32[2,16,8,128]{3,2,1,0:T(8,128)S(1)} %get-tuple-element.338), channel_id=1, source_target_pairs={{0,24},{8,0},{16,8},{24,16},{1,25},{9,1},{17,9},{25,17},{2,26},{10... | collective-permute-start | bytes 393224 | tf_op jit(solution)/shard_map/ppermute | solution.py:31
  101.4 7.5 %collective-permute-start.12 = (f32[2,16,8,128]{3,2,1,0:T(8,128)S(1)}, f32[2,16,8,128]{3,2,1,0:T(8,128)S(1)}, u32[]{:S(2)}, u32[]{:S(2)}) collective-permute-start(f32[2,16,8,128]{3,2,1,0:T(8,128)S(1)} %get-tuple-element.337), channel_id=1, source_target_pairs={{0,8},{8,16},{16,24},{24,0},{1,9},{9,17},{17,25},{25,1},{2,10},{10... | collective-permute-start | bytes 393224 | tf_op jit(solution)/shard_map/ppermute | solution.py:31
  101.4 13.3 %collective-permute-start.14 = (f32[192,512]{1,0:T(8,128)S(1)}, f32[192,512]{1,0:T(8,128)S(1)}, u32[]{:S(2)}, u32[]{:S(2)}) collective-permute-start(f32[192,512]{1,0:T(8,128)S(1)} %dynamic-slice_add_fusion.13), channel_id=1, source_target_pairs={{0,1},{1,0},{2,3},{3,2},{4,5},{5,4},{6,7},{7,6},{8,9},{9,8},{10,11... | collective-permute-start | bytes 1179656 | tf_op jit(solution)/shard_map/ppermute | solution.py:55
  101.9 12.8 %collective-permute-start.13 = (f32[224,512]{1,0:T(8,128)S(1)}, f32[224,512]{1,0:T(8,128)S(1)}, u32[]{:S(2)}, u32[]{:S(2)}) collective-permute-start(f32[224,512]{1,0:T(8,128)S(1)} %dynamic-slice_add_fusion.5), channel_id=1, source_target_pairs={{0,4},{4,0},{1,5},{5,1},{2,6},{6,2},{3,7},{7,3},{8,12},{12,8},{9,1... | collective-permute-start | bytes 1376264 | tf_op jit(solution)/shard_map/ppermute | solution.py:55
  108.9 5.2 %collective-permute-start.15 = (f32[16,8,128]{2,1,0:T(8,128)S(1)}, f32[16,8,128]{2,1,0:T(8,128)S(1)}, u32[]{:S(2)}, u32[]{:S(2)}) collective-permute-start(f32[16,8,128]{2,1,0:T(8,128)S(1)} %select_bitcast_fusion.2), channel_id=1, source_target_pairs={{0,1},{1,0},{2,3},{3,2},{4,5},{5,4},{6,7},{7,6},{8,9},{9,8},{10,11... | collective-permute-start | bytes 196616 | tf_op jit(solution)/shard_map/ppermute | solution.py:822
  114.9 11.2 %collective-permute-start.16 = (f32[208,512]{1,0:T(8,128)S(1)}, f32[208,512]{1,0:T(8,128)S(1)}, u32[]{:S(2)}, u32[]{:S(2)}) collective-permute-start(f32[208,512]{1,0:T(8,128)S(1)} %dynamic-slice_add_fusion.7), channel_id=1, source_target_pairs={{0,8},{8,0},{16,24},{24,16},{1,9},{9,1},{17,25},{25,17},{2,10},{10... | collective-permute-start | bytes 1277960 | tf_op jit(solution)/shard_map/ppermute | solution.py:55
  122.3 9.4 %copy-start.6 = (f32[384,512]{1,0:T(8,128)S(1)}, f32[384,512]{1,0:T(8,128)}, u32[]{:S(2)}) copy-start(f32[384,512]{1,0:T(8,128)} %get-tuple-element.244) | copy-start | bytes 2359300
  126.2 13.4 %copy-start.7 = (f32[384,512]{1,0:T(8,128)S(1)}, f32[384,512]{1,0:T(8,128)}, u32[]{:S(2)}) copy-start(f32[384,512]{1,0:T(8,128)} %get-tuple-element.240) | copy-start | bytes 2359300
  126.2 2.9 %collective-permute-start.17 = (f32[384,512]{1,0:T(8,128)}, f32[384,512]{1,0:T(8,128)S(1)}, u32[]{:S(2)}, u32[]{:S(2)}) collective-permute-start(f32[384,512]{1,0:T(8,128)} %get-tuple-element.231), channel_id=1, source_target_pairs={{0,2},{2,0},{1,3},{3,1},{4,6},{6,4},{5,7},{7,5},{8,10},{10,8},{9,1... | collective-permute-start | bytes 2359304 | tf_op jit(solution)/shard_map/ppermute | solution.py:55
  126.3 5.4 %collective-permute-start.18 = (f32[384,512]{1,0:T(8,128)}, f32[384,512]{1,0:T(8,128)}, u32[]{:S(2)}, u32[]{:S(2)}) collective-permute-start(f32[384,512]{1,0:T(8,128)} %get-tuple-element.235), channel_id=1, source_target_pairs={{0,2},{2,0},{1,3},{3,1},{4,6},{6,4},{5,7},{7,5},{8,10},{10,8},{9,1... | collective-permute-start | bytes 2359304 | tf_op jit(solution)/shard_map/ppermute | solution.py:55
  126.8 12.7 %collective-permute-start.19 = (f32[104,512]{1,0:T(8,128)S(1)}, f32[104,512]{1,0:T(8,128)S(1)}, u32[]{:S(2)}, u32[]{:S(2)}) collective-permute-start(f32[104,512]{1,0:T(8,128)S(1)} %dynamic-slice_add_fusion.15), channel_id=1, source_target_pairs={{0,16},{8,24},{16,0},{24,8},{1,17},{9,25},{17,1},{25,9},{2,18},{10... | collective-permute-start | bytes 638984 | tf_op jit(solution)/shard_map/ppermute | solution.py:55
  130.9 11.4 %collective-permute-start.20 = (f32[192,512]{1,0:T(8,128)}, f32[192,512]{1,0:T(8,128)S(1)}, u32[]{:S(2)}, u32[]{:S(2)}) collective-permute-start(f32[192,512]{1,0:T(8,128)} %dynamic-slice_add_fusion.11), channel_id=1, source_target_pairs={{0,1},{1,0},{2,3},{3,2},{4,5},{5,4},{6,7},{7,6},{8,9},{9,8},{10,11... | collective-permute-start | bytes 1179656 | tf_op jit(solution)/shard_map/ppermute | solution.py:55
  133.5 11.2 %collective-permute-start.21 = (f32[192,512]{1,0:T(8,128)}, f32[192,512]{1,0:T(8,128)}, u32[]{:S(2)}, u32[]{:S(2)}) collective-permute-start(f32[192,512]{1,0:T(8,128)} %dynamic-slice_add_fusion.10), channel_id=1, source_target_pairs={{0,4},{4,0},{1,5},{5,1},{2,6},{6,2},{3,7},{7,3},{8,12},{12,8},{9,1... | collective-permute-start | bytes 1179656 | tf_op jit(solution)/shard_map/ppermute | solution.py:55
  139.5 13.2 %collective-permute-start.24 = (f32[104,512]{1,0:T(8,128)S(1)}, f32[104,512]{1,0:T(8,128)S(1)}, u32[]{:S(2)}, u32[]{:S(2)}) collective-permute-start(f32[104,512]{1,0:T(8,128)S(1)} %add.302), channel_id=1, source_target_pairs={{0,16},{8,24},{16,0},{24,8},{1,17},{9,25},{17,1},{25,9},{2,18},{10... | collective-permute-start | bytes 638984 | tf_op jit(solution)/shard_map/ppermute | solution.py:55
  145.7 5.9 %collective-permute-start.23 = (f32[96,512]{1,0:T(8,128)S(1)}, f32[96,512]{1,0:T(8,128)S(1)}, u32[]{:S(2)}, u32[]{:S(2)}) collective-permute-start(f32[96,512]{1,0:T(8,128)S(1)} %dynamic-slice_add_fusion.20), channel_id=1, source_target_pairs={{0,1},{1,0},{2,3},{3,2},{4,5},{5,4},{6,7},{7,6},{8,9},{9,8},{10,11... | collective-permute-start | bytes 589832 | tf_op jit(solution)/shard_map/ppermute | solution.py:55
  147.0 5.7 %collective-permute-start.22 = (f32[96,512]{1,0:T(8,128)S(1)}, f32[96,512]{1,0:T(8,128)S(1)}, u32[]{:S(2)}, u32[]{:S(2)}) collective-permute-start(f32[96,512]{1,0:T(8,128)S(1)} %dynamic-slice_add_fusion.21), channel_id=1, source_target_pairs={{0,4},{4,0},{1,5},{5,1},{2,6},{6,2},{3,7},{7,3},{8,12},{12,8},{9,1... | collective-permute-start | bytes 589832 | tf_op jit(solution)/shard_map/ppermute | solution.py:55
  152.8 16.3 %collective-permute-start.26 = (f32[208,512]{1,0:T(8,128)S(1)}, f32[208,512]{1,0:T(8,128)S(1)}, u32[]{:S(2)}, u32[]{:S(2)}) collective-permute-start(f32[208,512]{1,0:T(8,128)S(1)} %pad_maximum_fusion.9), channel_id=1, source_target_pairs={{0,8},{8,0},{16,24},{24,16},{1,9},{9,1},{17,25},{25,17},{2,10},{10... | collective-permute-start | bytes 1277960 | tf_op jit(solution)/shard_map/ppermute | solution.py:55
  154.0 12.8 %collective-permute-start.25 = (f32[96,512]{1,0:T(8,128)S(1)}, f32[96,512]{1,0:T(8,128)S(1)}, u32[]{:S(2)}, u32[]{:S(2)}) collective-permute-start(f32[96,512]{1,0:T(8,128)S(1)} %dynamic-slice_add_fusion.17), channel_id=1, source_target_pairs={{0,8},{8,0},{16,24},{24,16},{1,9},{9,1},{17,25},{25,17},{2,10},{10... | collective-permute-start | bytes 589832 | tf_op jit(solution)/shard_map/ppermute | solution.py:55
  166.8 8.1 %collective-permute-start.27 = (f32[48,512]{1,0:T(8,128)S(1)}, f32[48,512]{1,0:T(8,128)S(1)}, u32[]{:S(2)}, u32[]{:S(2)}) collective-permute-start(f32[48,512]{1,0:T(8,128)S(1)} %dynamic-slice_add_fusion.23), channel_id=1, source_target_pairs={{0,16},{8,24},{16,0},{24,8},{1,17},{9,25},{17,1},{25,9},{2,18},{10... | collective-permute-start | bytes 294920 | tf_op jit(solution)/shard_map/ppermute | solution.py:55
  169.3 14.4 %collective-permute-start.29 = (f32[224,512]{1,0:T(8,128)S(1)}, f32[224,512]{1,0:T(8,128)S(1)}, u32[]{:S(2)}, u32[]{:S(2)}) collective-permute-start(f32[224,512]{1,0:T(8,128)S(1)} %fusion), channel_id=1, source_target_pairs={{0,4},{4,0},{1,5},{5,1},{2,6},{6,2},{3,7},{7,3},{8,12},{12,8},{9,1... | collective-permute-start | bytes 1376264 | tf_op jit(solution)/shard_map/ppermute | solution.py:55
  175.0 6.1 %collective-permute-start.28 = (f32[48,512]{1,0:T(8,128)S(1)}, f32[48,512]{1,0:T(8,128)S(1)}, u32[]{:S(2)}, u32[]{:S(2)}) collective-permute-start(f32[48,512]{1,0:T(8,128)S(1)} %add.322), channel_id=1, source_target_pairs={{0,16},{8,24},{16,0},{24,8},{1,17},{9,25},{17,1},{25,9},{2,18},{10... | collective-permute-start | bytes 294920 | tf_op jit(solution)/shard_map/ppermute | solution.py:55
  181.1 13.8 %collective-permute-start.31 = (f32[96,512]{1,0:T(8,128)S(1)}, f32[96,512]{1,0:T(8,128)S(1)}, u32[]{:S(2)}, u32[]{:S(2)}) collective-permute-start(f32[96,512]{1,0:T(8,128)S(1)} %pad_maximum_fusion.15), channel_id=1, source_target_pairs={{0,8},{8,0},{16,24},{24,16},{1,9},{9,1},{17,25},{25,17},{2,10},{10... | collective-permute-start | bytes 589832 | tf_op jit(solution)/shard_map/ppermute | solution.py:55
  182.9 11.9 %collective-permute-start.30 = (f32[192,512]{1,0:T(8,128)S(1)}, f32[192,512]{1,0:T(8,128)S(1)}, u32[]{:S(2)}, u32[]{:S(2)}) collective-permute-start(f32[192,512]{1,0:T(8,128)S(1)} %slice.37), channel_id=1, source_target_pairs={{0,1},{1,0},{2,3},{3,2},{4,5},{5,4},{6,7},{7,6},{8,9},{9,8},{10,11... | collective-permute-start | bytes 1179656 | tf_op jit(solution)/shard_map/ppermute | solution.py:55
  195.0 5.7 %collective-permute-start.32 = (f32[96,512]{1,0:T(8,128)S(1)}, f32[96,512]{1,0:T(8,128)S(1)}, u32[]{:S(2)}, u32[]{:S(2)}) collective-permute-start(f32[96,512]{1,0:T(8,128)S(1)} %get-tuple-element.279), channel_id=1, source_target_pairs={{0,4},{4,0},{1,5},{5,1},{2,6},{6,2},{3,7},{7,3},{8,12},{12,8},{9,1... | collective-permute-start | bytes 589832 | tf_op jit(solution)/shard_map/ppermute | solution.py:55
  196.7 17.9 %collective-permute-start.34 = (f32[448,512]{1,0:T(8,128)S(1)}, f32[448,512]{1,0:T(8,128)S(1)}, u32[]{:S(2)}, u32[]{:S(2)}) collective-permute-start(f32[448,512]{1,0:T(8,128)S(1)} %pad_maximum_fusion.3), channel_id=1, source_target_pairs={{0,1},{1,0},{2,3},{3,2},{4,5},{5,4},{6,7},{7,6},{8,9},{9,8},{10,11... | collective-permute-start | bytes 2752520 | tf_op jit(solution)/shard_map/ppermute | solution.py:55
  197.5 17.6 %collective-permute-start.35 = (f32[384,512]{1,0:T(8,128)S(1)}, f32[384,512]{1,0:T(8,128)S(1)}, u32[]{:S(2)}, u32[]{:S(2)}) collective-permute-start(f32[384,512]{1,0:T(8,128)S(1)} %pad_maximum_fusion.6), channel_id=1, source_target_pairs={{0,4},{4,0},{1,5},{5,1},{2,6},{6,2},{3,7},{7,3},{8,12},{12,8},{9,1... | collective-permute-start | bytes 2359304 | tf_op jit(solution)/shard_map/ppermute | solution.py:55
  197.8 16.8 %collective-permute-start.33 = (f32[96,512]{1,0:T(8,128)S(1)}, f32[96,512]{1,0:T(8,128)S(1)}, u32[]{:S(2)}, u32[]{:S(2)}) collective-permute-start(f32[96,512]{1,0:T(8,128)S(1)} %get-tuple-element.281), channel_id=1, source_target_pairs={{0,1},{1,0},{2,3},{3,2},{4,5},{5,4},{6,7},{7,6},{8,9},{9,8},{10,11... | collective-permute-start | bytes 589832 | tf_op jit(solution)/shard_map/ppermute | solution.py:55
  215.1 1.2 copy-start
  215.1 14.0 %collective-permute-start.38 = (f32[896,512]{1,0:T(8,128)S(1)}, f32[896,512]{1,0:T(8,128)S(1)}, u32[]{:S(2)}, u32[]{:S(2)}) collective-permute-start(f32[896,512]{1,0:T(8,128)S(1)} %pad_maximum_fusion.a_mine), channel_id=1, source_target_pairs={{0,2},{2,0},{1,3},{3,1},{4,6},{6,4},{5,7},{7,5},{8,10},{10,8},{9,1... | collective-permute-start | bytes 5505032 | tf_op jit(solution)/shard_map/ppermute | solution.py:55
  216.3 12.1 %copy-start.3 = (f32[768,512]{1,0:T(8,128)}, f32[768,512]{1,0:T(8,128)S(1)}, u32[]{:S(2)}) copy-start(f32[768,512]{1,0:T(8,128)S(1)} %pad_maximum_fusion.1.b_mine) | copy-start | bytes 4718596
  216.3 12.8 %collective-permute-start.39 = (f32[768,512]{1,0:T(8,128)S(1)}, f32[768,512]{1,0:T(8,128)S(1)}, u32[]{:S(2)}, u32[]{:S(2)}) collective-permute-start(f32[768,512]{1,0:T(8,128)S(1)} %pad_maximum_fusion.1.b_mine), channel_id=1, source_target_pairs={{0,2},{2,0},{1,3},{3,1},{4,6},{6,4},{5,7},{7,5},{8,10},{10,8},{9,1... | collective-permute-start | bytes 4718600 | tf_op jit(solution)/shard_map/ppermute | solution.py:55
  216.3 11.5 %collective-permute-start.36 = (f32[192,512]{1,0:T(8,128)S(1)}, f32[192,512]{1,0:T(8,128)S(1)}, u32[]{:S(2)}, u32[]{:S(2)}) collective-permute-start(f32[192,512]{1,0:T(8,128)S(1)} %pad_maximum_fusion.13), channel_id=1, source_target_pairs={{0,1},{1,0},{2,3},{3,2},{4,5},{5,4},{6,7},{7,6},{8,9},{9,8},{10,11... | collective-permute-start | bytes 1179656 | tf_op jit(solution)/shard_map/ppermute | solution.py:55
  217.1 11.2 %collective-permute-start.37 = (f32[192,512]{1,0:T(8,128)S(1)}, f32[192,512]{1,0:T(8,128)S(1)}, u32[]{:S(2)}, u32[]{:S(2)}) collective-permute-start(f32[192,512]{1,0:T(8,128)S(1)} %pad_maximum_fusion.14), channel_id=1, source_target_pairs={{0,4},{4,0},{1,5},{5,1},{2,6},{6,2},{3,7},{7,3},{8,12},{12,8},{9,1... | collective-permute-start | bytes 1179656 | tf_op jit(solution)/shard_map/ppermute | solution.py:55
  227.9 9.4 %copy-start.4 = (f32[384,512]{1,0:T(8,128)}, f32[384,512]{1,0:T(8,128)S(1)}, u32[]{:S(2)}) copy-start(f32[384,512]{1,0:T(8,128)S(1)} %pad_maximum_fusion.7.c_mine) | copy-start | bytes 2359300
  228.5 8.8 %copy-start.5 = (f32[384,512]{1,0:T(8,128)}, f32[384,512]{1,0:T(8,128)S(1)}, u32[]{:S(2)}) copy-start(f32[384,512]{1,0:T(8,128)S(1)} %pad_maximum_fusion.8.d_mine) | copy-start | bytes 2359300
  228.5 8.8 %collective-permute-start.41 = (f32[384,512]{1,0:T(8,128)S(1)}, f32[384,512]{1,0:T(8,128)S(1)}, u32[]{:S(2)}, u32[]{:S(2)}) collective-permute-start(f32[384,512]{1,0:T(8,128)S(1)} %pad_maximum_fusion.8.d_mine), channel_id=1, source_target_pairs={{0,2},{2,0},{1,3},{3,1},{4,6},{6,4},{5,7},{7,5},{8,10},{10,8},{9,1... | collective-permute-start | bytes 2359304 | tf_op jit(solution)/shard_map/ppermute | solution.py:55
  228.5 8.8 %collective-permute-start.40 = (f32[384,512]{1,0:T(8,128)S(1)}, f32[384,512]{1,0:T(8,128)S(1)}, u32[]{:S(2)}, u32[]{:S(2)}) collective-permute-start(f32[384,512]{1,0:T(8,128)S(1)} %pad_maximum_fusion.7.c_mine), channel_id=1, source_target_pairs={{0,2},{2,0},{1,3},{3,1},{4,6},{6,4},{5,7},{7,5},{8,10},{10,8},{9,1... | collective-permute-start | bytes 2359304 | tf_op jit(solution)/shard_map/ppermute | solution.py:55
  229.1 1.2 copy-start.16
  230.2 1.2 copy-start.15
  237.3 0.9 copy-start.17
  237.3 1.2 copy-start.18

commit v3 on v2

--- a/solution.py
+++ b/solution.py
@@ -331,13 +331,30 @@
     return onehot((edge >= atom * SLOTS) & (edge < atom * SLOTS + SLOTS))
 
 
-def legendre(cosine):
+def lead(k):
+    return math.comb(2 * k, k) / 2.0**k
+
+
+def ratio(k):
+    return k * k / (4.0 * k * k - 1.0)
+
+
+def monic(cosine):
     before, now = jnp.ones_like(cosine), cosine
     yield before
     yield now
     for k in range(1, ANGLES - 1):
-        before, now = now, ((2 * k + 1) / (k + 1)) * cosine * now - (k / (k + 1)) * before
+        before, now = now, cosine * now - ratio(k) * before
         yield now
+
+
+def looped(count, step, body):
+    def turn(t, carry):
+        for i in range(step):
+            body(t * step + i)
+        return carry
+
+    lax.fori_loop(0, count // step, turn, 0)
 
 
 def main_kernel(
@@ -362,13 +379,12 @@
         parts = [h[:, p].reshape(group, 128) for h in halos]
         return jnp.concatenate(parts + [local[p]], axis=0)
 
-    def gather_pair(p, carry):
+    def gather_pair(p):
         got = dot(place, side_by_side(rows_at(p))).astype(BF)
         table[2 * p] = got[:EDGES]
         table[2 * p + 1] = got[EDGES:]
-        return carry
-
-    lax.fori_loop(0, 16, gather_pair, 0)
+
+    looped(16, 4, gather_pair)
 
     rows = rows_at(16)
     high, low = halves(rows)
@@ -393,7 +409,7 @@
     trip_lanes = iota((128, 128), 1) < TRIP_W
     scale = 1.0 / math.sqrt(PICKS)
 
-    def basis_block(b, carry):
+    def basis_block(b):
         at = pl.multiple_of(b * BLOCK, BLOCK)
         own = pl.ds(at, BLOCK)
         wide = iota((BLOCK, 512), 1)
@@ -401,7 +417,7 @@
         hits = [jnp.where(mark[:, t : t + 1] == wide, 1.0, 0.0) for t in range(2 * PICKS)]
         hits = jnp.concatenate(hits, axis=0).astype(BF)
         got = side_sum(dot(hits, table[:, own, :].reshape(512, 256)))
-        picked = jnp.where(trip_lanes, got[:128], got[128:]) * scale
+        picked = jnp.where(trip_lanes, got[:128], got[128:])
         picked = picked.reshape(PICKS, BLOCK, 128)
         cos_here = cos_table[own, :]
         slot = slots[own, :]
@@ -417,13 +433,11 @@
             cos = jnp.stack(cos)
             cosines[2 * b + h] = cos
             values = picked[:, rows]
-            for k, poly in enumerate(legendre(cos)):
-                sums[pl.ds(pl.multiple_of(at + 8 * h, 8), 8), k * 128 : (k + 1) * 128] = jnp.sum(
-                    poly * values, axis=0
-                )
-        return carry
-
-    lax.fori_loop(0, BLOCKS, basis_block, 0)
+            for k, poly in enumerate(monic(cos)):
+                total = jnp.sum(poly * values, axis=0) * (lead(k) * scale)
+                sums[pl.ds(pl.multiple_of(at + 8 * h, 8), 8), k * 128 : (k + 1) * 128] = total
+
+    looped(BLOCKS, 3, basis_block)
 
     down = times(sums[...], weight[...], NT)
     down_act, down_slope = act_and_slope(down)
@@ -557,15 +571,23 @@
     trip_lanes = iota((128, 128), 1) < TRIP_W
     scale = 1.0 / math.sqrt(PICKS)
 
-    def basis_back(b, carry):
+    def basis_back(b):
         at = pl.multiple_of(b * BLOCK, BLOCK)
         own = pl.ds(at, BLOCK)
         parts = []
         for h in range(2):
-            total = jnp.zeros((PICKS, 8, 128), F32)
-            for k, poly in enumerate(legendre(cosines[2 * b + h])):
-                total = total + poly * sums[pl.ds(pl.multiple_of(at + 8 * h, 8), 8), k * 128 : (k + 1) * 128]
-            parts.append(total * scale)
+            cos = cosines[2 * b + h]
+            own_rows = pl.ds(pl.multiple_of(at + 8 * h, 8), 8)
+            after = total = None
+            for k in range(ANGLES - 1, -1, -1):
+                term = sums[own_rows, k * 128 : (k + 1) * 128] * (lead(k) * scale)
+                if total is None:
+                    after, total = None, jnp.broadcast_to(term, cos.shape)
+                elif after is None:
+                    after, total = total, term + cos * total
+                else:
+                    after, total = total, term + cos * total - ratio(k + 1) * after
+            parts.append(total)
         grad = jnp.concatenate(parts, axis=1).reshape(128, 128)
         grad = jnp.concatenate(
             [jnp.where(trip_lanes, grad, 0.0), jnp.where(trip_lanes, 0.0, grad)], axis=0
@@ -573,23 +595,21 @@
         hits = onehot(mark_rows[b] == iota((512, 256), 0))
         got = side_by_side(side_sum(dot(hits, side_by_side(grad))))
         table[:, own, :] = got.reshape(32, BLOCK, 256)
-        return carry
-
-    lax.fori_loop(0, BLOCKS, basis_back, 0)
+
+    looped(BLOCKS, 3, basis_back)
     table[30] = side_by_side(grad_src[:, :128])
     table[31] = side_by_side(grad_src[:, 128:])
     rows = iota((depth, EDGES), 0)
     place_even = onehot(src_rows[0:1, :] == rows)
     place_odd = onehot(src_rows[1:2, :] == rows)
 
-    def scatter_pair(p, carry):
+    def scatter_pair(p):
         got = side_sum(dot(place_even, table[2 * p]) + dot(place_odd, table[2 * p + 1]))
         for i, back in enumerate((back_before, back_here, back_after)):
             back[:, p] = got[i * group : (i + 1) * group].reshape(group // 8, 8, 128)
         back_local[p] = got[3 * group :]
-        return carry
-
-    lax.fori_loop(0, 16, scatter_pair, 0)
+
+    looped(16, 4, scatter_pair)
 
 
 def finish_kernel(
@@ -846,7 +866,7 @@
         except StopIteration as end:
             done[name] = end.value
 
-    for name in "ELEELELEELEELEL":
+    for name in "ELELELEELEELE":
         resume(name)
     while "L" not in done:
         resume("L")

time: 243 us -> 238 us (0.979)
  starting transfers between devices: 44.3 us -> 35.2 us
  waiting for transfers between devices: 105 us -> 112 us
  Pallas kernels: 64.4 us -> 60.1 us
    ppermute x32, starting transfers between devices: 30.1 us -> 22.4 us  [swap(): return lax.ppermute(value, axis, [(i, i ^ 1 << bit) for i in range(count)])]
    pallas_call x7, Pallas kernels: 64.4 us -> 60.1 us  [call(): pl.pallas_call(kernel, out_shape=[jax.ShapeDtypeStruct(shape, F32) for sh...]
    ppermute x32, waiting for transfers between devices: 74.7 us -> 77.7 us  [swap(): return lax.ppermute(value, axis, [(i, i ^ 1 << bit) for i in range(count)])]
  transfers between devices with their start and end apart: 42 -> 42, of which waited for: 26 -> 28; matrix products, arithmetic and copies ran while one was open for 9% -> 9% of each run, Pallas kernels for 12% -> 11%
where the time goes in v3:
time: 238 us
  waiting for transfers between devices  112 us (47%)
  Pallas kernels  60.1 us (25%)
  starting transfers between devices  35.2 us (15%)
  other arithmetic  19.6 us (8%)
  local copies, waits for them, and re-layouts  9.08 us (4%)
    ppermute x32, waiting for transfers between devices, swap(): return lax.ppermute(value, axis, [(i, i ^ 1 << bit) for i in range(count)])  77.7 us
    pallas_call x7, Pallas kernels, call(): pl.pallas_call(kernel, out_shape=[jax.ShapeDtypeStruct(shape, F32) for sh...  60.1 us
    ppermute x8, waiting for transfers between devices, shifted(): return lax.ppermute(value, axis, pairs)  26.1 us
    ppermute x32, starting transfers between devices, swap(): return lax.ppermute(value, axis, [(i, i ^ 1 << bit) for i in range(count)])  22.4 us
    add x24, other arithmetic, part(): total = total + lax.dynamic_slice_in_dim(x, at, size)  13.1 us
    ppermute x8, starting transfers between devices, shifted(): return lax.ppermute(value, axis, pairs)  9.26 us
    ppermute x1, waiting for transfers between devices, per_device(): returned = mine + lax.ppermute(theirs, 'gz', [(0, 1), (1, 0)])  6.9 us
    unnamed x43, local copies, waits for them, and re-layouts  4.91 us
  transfers between devices with their start and end apart: 42, of which 28 were waited for; matrix products, arithmetic and copies ran while one was open for 9% of the time, Pallas kernels for 11%

profile of v3, /device:TPU:0, one launch (start us, length us, event | category | flops | bytes accessed | tf_op | source)
XLA Modules:
  0.0 237.6 jit_solution(3308257120143775313)
XLA Ops:
  0.7 4.6 %shard_map.394 = (f32[17,8,128]{2,1,0:T(8,128)}, f32[17,16,128]{2,1,0:T(8,128)}, f32[8,256]{1,0:T(8,128)}, f32[2,240,512]{2,1,0:T(8,128)}, f32[240,128]{1,0:T(8,...) custom-call(f32[240,512]{1,0:T(8,128)} %edge.5, f32[3,240]{1,0:T(4,128)} %vec.1, ...), custom_call_target="tpu_custom_call" | custom-call | flops 5750000128 | bytes 1024 | tf_op jit(solution)/shard_map/pallas_call | solution.py:717
  5.4 3.0 %collective-permute-start = (f32[17,8,128]{2,1,0:T(8,128)}, f32[17,8,128]{2,1,0:T(8,128)S(1)}, u32[]{:S(2)}, u32[]{:S(2)}) collective-permute-start(f32[17,8,128]{2,1,0:T(8,128)} %get-tuple-element.165), channel_id=1, source_target_pairs={{0,1},{1,0},{2,3},{3,2},{4,5},{5,4},{6,7},{7,6},{8,9},{9,8},{10,11... | collective-permute-start | bytes 208904 | tf_op jit(solution)/shard_map/ppermute | solution.py:36
  8.4 0.8 copy.71.slots
  9.2 1.6 collective-permute-done
  10.9 0.9 select_bitcast_fusion.1
  11.8 4.2 %collective-permute-start.2 = (f32[2,17,8,128]{3,2,1,0:T(8,128)S(1)}, f32[2,17,8,128]{3,2,1,0:T(8,128)S(1)}, u32[]{:S(2)}, u32[]{:S(2)}) collective-permute-start(f32[2,17,8,128]{3,2,1,0:T(8,128)S(1)} %pad_maximum_fusion.16), channel_id=1, source_target_pairs={{0,24},{8,0},{16,8},{24,16},{1,25},{9,1},{17,9},{25,17},{2,26},{10... | collective-permute-start | bytes 417800 | tf_op jit(solution)/shard_map/ppermute | solution.py:31
  16.0 3.3 %collective-permute-done.2 = f32[2,17,8,128]{3,2,1,0:T(8,128)S(1)} collective-permute-done((f32[2,17,8,128]{3,2,1,0:T(8,128)S(1)}, f32[2,17,8,128]{3,2,1,0:T(8,128)S(1)}, u32[]{:S(2)}, u32[]{:S(2)}) %collective-permute-start.2) | collective-permute-done | bytes 139296 | tf_op jit(solution)/shard_map/ppermute | solution.py:31
  19.2 3.6 %collective-permute-done.1 = f32[2,17,8,128]{3,2,1,0:T(8,128)S(1)} collective-permute-done((f32[2,17,8,128]{3,2,1,0:T(8,128)S(1)}, f32[2,17,8,128]{3,2,1,0:T(8,128)S(1)}, u32[]{:S(2)}, u32[]{:S(2)}) %collective-permute-start.1) | collective-permute-done | bytes 139296 | tf_op jit(solution)/shard_map/ppermute | solution.py:31
  24.3 0.8 copy.70.src_cols
  25.7 6.0 %collective-permute-done.4.halo_after = f32[6,17,8,128]{3,2,1,0:T(8,128)S(1)} collective-permute-done((f32[6,17,8,128]{3,2,1,0:T(8,128)S(1)}, f32[6,17,8,128]{3,2,1,0:T(8,128)S(1)}, u32[]{:S(2)}, u32[]{:S(2)}) %collective-permute-start.4) | collective-permute-done | bytes 417824 | tf_op jit(solution)/shard_map/ppermute | solution.py:31
  31.8 3.2 %collective-permute-done.3.halo_before = f32[6,17,8,128]{3,2,1,0:T(8,128)S(1)} collective-permute-done((f32[6,17,8,128]{3,2,1,0:T(8,128)S(1)}, f32[6,17,8,128]{3,2,1,0:T(8,128)S(1)}, u32[]{:S(2)}, u32[]{:S(2)}) %collective-permute-start.3) | collective-permute-done | bytes 417824 | tf_op jit(solution)/shard_map/ppermute | solution.py:31
  34.9 0.7 copy-done.20
  35.7 25.9 %shard_map.395 = (f32[8,256]{1,0:T(8,128)}, f32[240,512]{1,0:T(8,128)}, f32[8,256]{1,0:T(8,128)}, f32[240,512]{1,0:T(8,128)}, f32[8,256]{1,0:T(8,128)}, /*index=...) custom-call(f32[6,17,8,128]{3,2,1,0:T(8,128)} %copy-done.20, ...), custom_call_target="tpu_custom_call" | custom-call | flops 29899999232 | bytes 1024 | tf_op jit(solution)/shard_map/pallas_call | solution.py:717
  61.7 4.2 %shard_map.396 = (f32[768,512]{1,0:T(8,128)}, f32[768,512]{1,0:T(8,128)}) custom-call(f32[3,240,512]{2,1,0:T(8,128)} %get-tuple-element.177.grad_rads, f32[240,128]{1,0:T(8,128)} %get-tuple-element.170.radial, f32[8,3328]{1,0:T(8,128)} %get-tuple-element.178.atom_rows, f32[32,512]{1,0:T(8,128)} %get-tuple-element.179.quad_up_grad, s32[1]{0:T(128)} %bitcast.12.core), custom_call_target="tpu_custom_call" | custom-call | flops 4600000000 | bytes 1024 | tf_op jit(solution)/shard_map/pallas_call | solution.py:717
  67.9 0.9 fusion.3
  69.6 1.4 dynamic-slice_add_fusion.1
  71.0 1.6 collective-permute-start.7
  72.5 1.3 dynamic-slice_add_fusion.3
  74.4 8.7 %shard_map.397 = (f32[6,16,8,128]{3,2,1,0:T(8,128)}, f32[6,16,8,128]{3,2,1,0:T(8,128)}, f32[6,16,8,128]{3,2,1,0:T(8,128)}, f32[16,16,128]{2,1,0:T(8,128)}) custom-call(f32[30,8,8,128]{3,2,1,0:T(8,128)} %get-tuple-element.174.cosines, f32[240,2048]{1,0:T(8,128)} %get-tuple-element.185.sums, f32[240,256]{1,0:T(8,128)} %get-tuple-element.186.grad_src, ...), custom_call_target="tpu_custom_call" | custom-call | flops 14949999616 | bytes 1024 | tf_op jit(solution)/shard_map/pallas_call | solution.py:717
  83.7 1.3 dynamic-slice_add_fusion.2
  85.0 1.4 dynamic-slice_add_fusion
  86.3 7.0 %collective-permute-done.7 = f32[448,512]{1,0:T(8,128)S(1)} collective-permute-done((f32[448,512]{1,0:T(8,128)S(1)}, f32[448,512]{1,0:T(8,128)S(1)}, u32[]{:S(2)}, u32[]{:S(2)}) %collective-permute-start.7) | collective-permute-done | bytes 917536 | tf_op jit(solution)/shard_map/ppermute | solution.py:55
  93.5 0.8 collective-permute-done.8
  94.4 5.2 %collective-permute-done.9 = f32[6,16,8,128]{3,2,1,0:T(8,128)S(1)} collective-permute-done((f32[6,16,8,128]{3,2,1,0:T(8,128)}, f32[6,16,8,128]{3,2,1,0:T(8,128)S(1)}, u32[]{:S(2)}, u32[]{:S(2)}) %collective-permute-start.9) | collective-permute-done | bytes 393248 | tf_op jit(solution)/shard_map/ppermute | solution.py:31
  100.9 3.4 %collective-permute-start.11 = (f32[2,16,8,128]{3,2,1,0:T(8,128)S(1)}, f32[2,16,8,128]{3,2,1,0:T(8,128)S(1)}, u32[]{:S(2)}, u32[]{:S(2)}) collective-permute-start(f32[2,16,8,128]{3,2,1,0:T(8,128)S(1)} %get-tuple-element.338), channel_id=1, source_target_pairs={{0,24},{8,0},{16,8},{24,16},{1,25},{9,1},{17,9},{25,17},{2,26},{10... | collective-permute-start | bytes 393224 | tf_op jit(solution)/shard_map/ppermute | solution.py:31
  104.3 0.9 collective-permute-start.13
  105.7 3.0 %collective-permute-done.12 = f32[2,16,8,128]{3,2,1,0:T(8,128)S(1)} collective-permute-done((f32[2,16,8,128]{3,2,1,0:T(8,128)S(1)}, f32[2,16,8,128]{3,2,1,0:T(8,128)S(1)}, u32[]{:S(2)}, u32[]{:S(2)}) %collective-permute-start.12) | collective-permute-done | bytes 131104 | tf_op jit(solution)/shard_map/ppermute | solution.py:31
  108.7 1.1 collective-permute-done.11
  110.5 6.9 %collective-permute-done.15 = f32[16,8,128]{2,1,0:T(8,128)S(1)} collective-permute-done((f32[16,8,128]{2,1,0:T(8,128)S(1)}, f32[16,8,128]{2,1,0:T(8,128)S(1)}, u32[]{:S(2)}, u32[]{:S(2)}) %collective-permute-start.15) | collective-permute-done | bytes 65568 | tf_op jit(solution)/shard_map/ppermute | solution.py:842
  118.4 6.8 %shard_map.398 = (f32[8,256]{1,0:T(8,128)}, f32[240,512]{1,0:T(8,128)}, f32[384,512]{1,0:T(8,128)}, f32[384,512]{1,0:T(8,128)}, f32[384,512]{1,0:T(8,128)}, /*index=5*/f32[384,512]{1,0:T(8,128)}) custom-call(f32[16,16,128]{2,1,0:T(8,128)} %get-tuple-element.187.back_local, f32[16,8,128]{2,1,0:T(8,128)} %bitcast_add_fusion.returned, ...), custom_call_target="tpu_custom_call" | custom-call | flops 8049999872 | bytes 1024 | tf_op jit(solution)/shard_map/pallas_call | solution.py:717
  125.2 3.7 %collective-permute-done.16 = f32[208,512]{1,0:T(8,128)S(1)} collective-permute-done((f32[208,512]{1,0:T(8,128)S(1)}, f32[208,512]{1,0:T(8,128)S(1)}, u32[]{:S(2)}, u32[]{:S(2)}) %collective-permute-start.16) | collective-permute-done | bytes 426016 | tf_op jit(solution)/shard_map/ppermute | solution.py:55
  130.3 2.0 collective-permute-done.17
  132.2 1.8 dynamic-slice_add_fusion.11
  134.6 0.8 dynamic-slice_add_fusion.10
  135.4 2.0 collective-permute-start.21
  137.4 5.6 %collective-permute-done.19 = f32[104,512]{1,0:T(8,128)} collective-permute-done((f32[104,512]{1,0:T(8,128)}, f32[104,512]{1,0:T(8,128)}, u32[]{:S(2)}, u32[]{:S(2)}) %collective-permute-start.19) | collective-permute-done | bytes 213024 | tf_op jit(solution)/shard_map/ppermute | solution.py:55
  143.0 1.0 add.302
  144.2 1.3 collective-permute-done.20
  145.5 1.0 dynamic-slice_add_fusion.21
  146.5 2.1 collective-permute-start.23
  148.6 1.0 dynamic-slice_add_fusion.20
  150.1 4.2 %collective-permute-done.22 = f32[104,512]{1,0:T(8,128)S(1)} collective-permute-done((f32[104,512]{1,0:T(8,128)S(1)}, f32[104,512]{1,0:T(8,128)S(1)}, u32[]{:S(2)}, u32[]{:S(2)}) %collective-permute-start.22) | collective-permute-done | bytes 213024 | tf_op jit(solution)/shard_map/ppermute | solution.py:55
  154.5 1.0 dynamic-slice_add_fusion.19
  155.5 1.0 dynamic-slice_add_fusion.18
  156.6 9.7 %collective-permute-done.25 = f32[208,512]{1,0:T(8,128)S(1)} collective-permute-done((f32[208,512]{1,0:T(8,128)S(1)}, f32[208,512]{1,0:T(8,128)S(1)}, u32[]{:S(2)}, u32[]{:S(2)}) %collective-permute-start.25) | collective-permute-done | bytes 426016 | tf_op jit(solution)/shard_map/ppermute | solution.py:55
  166.4 2.1 collective-permute-start.28
  168.8 5.4 %collective-permute-done.26 = f32[96,512]{1,0:T(8,128)S(1)} collective-permute-done((f32[96,512]{1,0:T(8,128)S(1)}, f32[96,512]{1,0:T(8,128)S(1)}, u32[]{:S(2)}, u32[]{:S(2)}) %collective-permute-start.26) | collective-permute-done | bytes 196640 | tf_op jit(solution)/shard_map/ppermute | solution.py:55
  175.4 5.4 %collective-permute-done.27 = f32[48,512]{1,0:T(8,128)S(1)} collective-permute-done((f32[48,512]{1,0:T(8,128)S(1)}, f32[48,512]{1,0:T(8,128)S(1)}, u32[]{:S(2)}, u32[]{:S(2)}) %collective-permute-start.27) | collective-permute-done | bytes 98336 | tf_op jit(solution)/shard_map/ppermute | solution.py:55
  181.6 4.6 %collective-permute-done.30 = f32[192,512]{1,0:T(8,128)S(1)} collective-permute-done((f32[192,512]{1,0:T(8,128)S(1)}, f32[192,512]{1,0:T(8,128)S(1)}, u32[]{:S(2)}, u32[]{:S(2)}) %collective-permute-start.30) | collective-permute-done | bytes 393248 | tf_op jit(solution)/shard_map/ppermute | solution.py:55
  187.0 2.9 %collective-permute-start.32 = (f32[48,512]{1,0:T(8,128)S(1)}, f32[48,512]{1,0:T(8,128)S(1)}, u32[]{:S(2)}, u32[]{:S(2)}) collective-permute-start(f32[48,512]{1,0:T(8,128)S(1)} %add.322), channel_id=1, source_target_pairs={{0,16},{8,24},{16,0},{24,8},{1,17},{9,25},{17,1},{25,9},{2,18},{10... | collective-permute-start | bytes 294920 | tf_op jit(solution)/shard_map/ppermute | solution.py:55
  189.9 3.7 %collective-permute-done.32 = f32[48,512]{1,0:T(8,128)S(1)} collective-permute-done((f32[48,512]{1,0:T(8,128)S(1)}, f32[48,512]{1,0:T(8,128)S(1)}, u32[]{:S(2)}, u32[]{:S(2)}) %collective-permute-start.32) | collective-permute-done | bytes 98336 | tf_op jit(solution)/shard_map/ppermute | solution.py:55
  193.6 9.5 %collective-permute-done.29 = f32[448,512]{1,0:T(8,128)S(1)} collective-permute-done((f32[448,512]{1,0:T(8,128)S(1)}, f32[448,512]{1,0:T(8,128)S(1)}, u32[]{:S(2)}, u32[]{:S(2)}) %collective-permute-start.29) | collective-permute-done | bytes 917536 | tf_op jit(solution)/shard_map/ppermute | solution.py:55
  203.8 0.8 copy-done
  204.7 1.0 collective-permute-start.33
  205.7 6.4 %collective-permute-done.33 = f32[96,512]{1,0:T(8,128)S(1)} collective-permute-done((f32[96,512]{1,0:T(8,128)S(1)}, f32[96,512]{1,0:T(8,128)S(1)}, u32[]{:S(2)}, u32[]{:S(2)}) %collective-permute-start.33) | collective-permute-done | bytes 196640 | tf_op jit(solution)/shard_map/ppermute | solution.py:55
  213.3 5.4 %collective-permute-done.34 = f32[96,512]{1,0:T(8,128)S(1)} collective-permute-done((f32[96,512]{1,0:T(8,128)S(1)}, f32[96,512]{1,0:T(8,128)S(1)}, u32[]{:S(2)}, u32[]{:S(2)}) %collective-permute-start.34) | collective-permute-done | bytes 196640 | tf_op jit(solution)/shard_map/ppermute | solution.py:55
  219.5 1.1 collective-permute-start.39
  220.6 1.2 copy-done.16
  221.8 1.2 copy-done.15
  223.0 5.9 %shard_map.399 = (f32[2,512,512]{2,1,0:T(8,128)}, f32[2,256,512]{2,1,0:T(8,128)}, f32[64,1024]{1,0:T(8,128)}, f32[64,512]{1,0:T(8,128)}, f32[32,1024]{1,0:T(8,12...) custom-call(f32[896,512]{1,0:T(8,128)} %copy-done, ...), custom_call_target="tpu_custom_call" | custom-call | flops 5750000128 | bytes 1024 | tf_op jit(solution)/shard_map/pallas_call | solution.py:717
  229.8 1.8 collective-permute-done.41.d_other
  231.6 1.1 collective-permute-done.40.c_other
  232.8 0.9 copy-done.18
  233.6 4.0 %shard_map.400 = (f32[2,512,512]{2,1,0:T(8,128)}, f32[5,128,512]{2,1,0:T(8,128)}, f32[64,512]{1,0:T(8,128)}, f32[32,512]{1,0:T(8,128)}, f32[3,256]{1,0:T(4,128)}) custom-call(f32[384,512]{1,0:T(8,128)} %copy-done.4, f32[384,512]{1,0:T(8,128)} %copy-done.18, f32[384,512]{1,0:T(8,128)} %copy-done.5, f32[384,512]{1,0:T(8,128)} %copy-done.17, ...), custom_call_target="tpu_custom_call" | custom-call | flops 3449999872 | bytes 1024 | tf_op jit(solution)/shard_map/pallas_call | solution.py:717
  (150 shorter events, 19.7 us)
Async XLA Ops:
  0.7 7.7 %copy-start.14 = (s32[240]{0:T(256)S(1)}, s32[240]{0:T(256)}, u32[]{:S(2)}) copy-start(s32[240]{0:T(256)} %param.32) | copy-start | bytes 2884
  0.7 7.7 %copy-start.10 = (s32[240,8]{0,1:T(8,128)S(1)}, s32[240,8]{0,1:T(8,128)}, u32[]{:S(2)}) copy-start(s32[240,8]{0,1:T(8,128)} %param.33) | copy-start | bytes 23044
  0.7 7.7 %copy-start.12 = (s32[240,8]{0,1:T(8,128)S(1)}, s32[240,8]{0,1:T(8,128)}, u32[]{:S(2)}) copy-start(s32[240,8]{0,1:T(8,128)} %param.35) | copy-start | bytes 23044
  0.7 22.7 %copy-start.11 = (s32[240,8]{0,1:T(8,128)S(1)}, s32[240,8]{0,1:T(8,128)}, u32[]{:S(2)}) copy-start(s32[240,8]{0,1:T(8,128)} %param.34) | copy-start | bytes 23044
  0.7 22.7 %copy-start.13 = (s32[240,8]{0,1:T(8,128)S(1)}, s32[240,8]{0,1:T(8,128)}, u32[]{:S(2)}) copy-start(s32[240,8]{0,1:T(8,128)} %param.36) | copy-start | bytes 23044
  5.4 5.5 %collective-permute-start = (f32[17,8,128]{2,1,0:T(8,128)}, f32[17,8,128]{2,1,0:T(8,128)S(1)}, u32[]{:S(2)}, u32[]{:S(2)}) collective-permute-start(f32[17,8,128]{2,1,0:T(8,128)} %get-tuple-element.165), channel_id=1, source_target_pairs={{0,1},{1,0},{2,3},{3,2},{4,5},{5,4},{6,7},{7,6},{8,9},{9,8},{10,11... | collective-permute-start | bytes 208904 | tf_op jit(solution)/shard_map/ppermute | solution.py:36
  11.8 7.5 %collective-permute-start.2 = (f32[2,17,8,128]{3,2,1,0:T(8,128)S(1)}, f32[2,17,8,128]{3,2,1,0:T(8,128)S(1)}, u32[]{:S(2)}, u32[]{:S(2)}) collective-permute-start(f32[2,17,8,128]{3,2,1,0:T(8,128)S(1)} %pad_maximum_fusion.16), channel_id=1, source_target_pairs={{0,24},{8,0},{16,8},{24,16},{1,25},{9,1},{17,9},{25,17},{2,26},{10... | collective-permute-start | bytes 417800 | tf_op jit(solution)/shard_map/ppermute | solution.py:31
  16.0 6.9 %collective-permute-start.1 = (f32[2,17,8,128]{3,2,1,0:T(8,128)S(1)}, f32[2,17,8,128]{3,2,1,0:T(8,128)S(1)}, u32[]{:S(2)}, u32[]{:S(2)}) collective-permute-start(f32[2,17,8,128]{3,2,1,0:T(8,128)S(1)} %pad_maximum_fusion.16), channel_id=1, source_target_pairs={{0,8},{8,16},{16,24},{24,0},{1,9},{9,17},{17,25},{25,1},{2,10},{10... | collective-permute-start | bytes 417800 | tf_op jit(solution)/shard_map/ppermute | solution.py:31
  22.9 12.1 %copy-start.8 = (f32[6,17,8,128]{3,2,1,0:T(8,128)}, f32[6,17,8,128]{3,2,1,0:T(8,128)S(1)}, u32[]{:S(2)}) copy-start(f32[6,17,8,128]{3,2,1,0:T(8,128)S(1)} %pad_maximum_fusion.10.halo_here) | copy-start | bytes 1253380
  22.9 8.9 %collective-permute-start.4 = (f32[6,17,8,128]{3,2,1,0:T(8,128)S(1)}, f32[6,17,8,128]{3,2,1,0:T(8,128)S(1)}, u32[]{:S(2)}, u32[]{:S(2)}) collective-permute-start(f32[6,17,8,128]{3,2,1,0:T(8,128)S(1)} %pad_maximum_fusion.10.halo_here), channel_id=1, source_target_pairs={{0,6},{2,0},{4,2},{6,4},{1,7},{3,1},{5,3},{7,5},{8,14},{10,8},{12,... | collective-permute-start | bytes 1253384 | tf_op jit(solution)/shard_map/ppermute | solution.py:31
  22.9 12.0 %collective-permute-start.3 = (f32[6,17,8,128]{3,2,1,0:T(8,128)S(1)}, f32[6,17,8,128]{3,2,1,0:T(8,128)S(1)}, u32[]{:S(2)}, u32[]{:S(2)}) collective-permute-start(f32[6,17,8,128]{3,2,1,0:T(8,128)S(1)} %pad_maximum_fusion.10.halo_here), channel_id=1, source_target_pairs={{0,2},{2,4},{4,6},{6,0},{1,3},{3,5},{5,7},{7,1},{8,10},{10,12},{12... | collective-permute-start | bytes 1253384 | tf_op jit(solution)/shard_map/ppermute | solution.py:31
  31.7 3.2 %copy-start.19 = (f32[6,17,8,128]{3,2,1,0:T(8,128)}, f32[6,17,8,128]{3,2,1,0:T(8,128)S(1)}, u32[]{:S(2)}) copy-start(f32[6,17,8,128]{3,2,1,0:T(8,128)S(1)} %collective-permute-done.4.halo_after) | copy-start | bytes 1253380
  34.9 0.8 copy-start.20
  61.6 8.0 %collective-permute-start.5 = (f32[896,512]{1,0:T(8,128)}, f32[896,512]{1,0:T(8,128)}, u32[]{:S(2)}, u32[]{:S(2)}) collective-permute-start(f32[896,512]{1,0:T(8,128)} %get-tuple-element.176), channel_id=1, source_target_pairs={{0,2},{2,0},{1,3},{3,1},{4,6},{6,4},{5,7},{7,5},{8,10},{10,8},{9,1... | collective-permute-start | bytes 5505032 | tf_op jit(solution)/shard_map/ppermute | solution.py:55
  61.7 7.9 %copy-start.1 = (f32[896,512]{1,0:T(8,128)S(1)}, f32[896,512]{1,0:T(8,128)}, u32[]{:S(2)}) copy-start(f32[896,512]{1,0:T(8,128)} %get-tuple-element.188) | copy-start | bytes 5505028
  65.9 6.6 %collective-permute-start.6 = (f32[768,512]{1,0:T(8,128)}, f32[768,512]{1,0:T(8,128)}, u32[]{:S(2)}, u32[]{:S(2)}) collective-permute-start(f32[768,512]{1,0:T(8,128)} %get-tuple-element.181), channel_id=1, source_target_pairs={{0,2},{2,0},{1,3},{3,1},{4,6},{6,4},{5,7},{7,5},{8,10},{10,8},{9,1... | collective-permute-start | bytes 4718600 | tf_op jit(solution)/shard_map/ppermute | solution.py:55
  67.2 5.3 %copy-start.2 = (f32[768,512]{1,0:T(8,128)S(1)}, f32[768,512]{1,0:T(8,128)}, u32[]{:S(2)}) copy-start(f32[768,512]{1,0:T(8,128)} %get-tuple-element.194) | copy-start | bytes 4718596
  71.0 22.4 %collective-permute-start.7 = (f32[448,512]{1,0:T(8,128)S(1)}, f32[448,512]{1,0:T(8,128)S(1)}, u32[]{:S(2)}, u32[]{:S(2)}) collective-permute-start(f32[448,512]{1,0:T(8,128)S(1)} %dynamic-slice_add_fusion.1), channel_id=1, source_target_pairs={{0,1},{1,0},{2,3},{3,2},{4,5},{5,4},{6,7},{7,6},{8,9},{9,8},{10,11... | collective-permute-start | bytes 2752520 | tf_op jit(solution)/shard_map/ppermute | solution.py:55
  73.8 20.5 %collective-permute-start.8 = (f32[384,512]{1,0:T(8,128)S(1)}, f32[384,512]{1,0:T(8,128)S(1)}, u32[]{:S(2)}, u32[]{:S(2)}) collective-permute-start(f32[384,512]{1,0:T(8,128)S(1)} %dynamic-slice_add_fusion.3), channel_id=1, source_target_pairs={{0,4},{4,0},{1,5},{5,1},{2,6},{6,2},{3,7},{7,3},{8,12},{12,8},{9,1... | collective-permute-start | bytes 2359304 | tf_op jit(solution)/shard_map/ppermute | solution.py:55
  83.0 16.6 %collective-permute-start.9 = (f32[6,16,8,128]{3,2,1,0:T(8,128)}, f32[6,16,8,128]{3,2,1,0:T(8,128)S(1)}, u32[]{:S(2)}, u32[]{:S(2)}) collective-permute-start(f32[6,16,8,128]{3,2,1,0:T(8,128)} %get-tuple-element.200), channel_id=1, source_target_pairs={{0,6},{2,0},{4,2},{6,4},{1,7},{3,1},{5,3},{7,5},{8,14},{10,8},{12,... | collective-permute-start | bytes 1179656 | tf_op jit(solution)/shard_map/ppermute | solution.py:31
  83.7 16.6 %collective-permute-start.10 = (f32[6,16,8,128]{3,2,1,0:T(8,128)}, f32[6,16,8,128]{3,2,1,0:T(8,128)S(1)}, u32[]{:S(2)}, u32[]{:S(2)}) collective-permute-start(f32[6,16,8,128]{3,2,1,0:T(8,128)} %get-tuple-element.201), channel_id=1, source_target_pairs={{0,2},{2,4},{4,6},{6,0},{1,3},{3,5},{5,7},{7,1},{8,10},{10,12},{12... | collective-permute-start | bytes 1179656 | tf_op jit(solution)/shard_map/ppermute | solution.py:31
  93.4 6.9 %copy-start.9 = (f32[6,16,8,128]{3,2,1,0:T(8,128)S(1)}, f32[6,16,8,128]{3,2,1,0:T(8,128)}, u32[]{:S(2)}) copy-start(f32[6,16,8,128]{3,2,1,0:T(8,128)} %get-tuple-element.203) | copy-start | bytes 1179652
  100.4 8.3 %collective-permute-start.12 = (f32[2,16,8,128]{3,2,1,0:T(8,128)S(1)}, f32[2,16,8,128]{3,2,1,0:T(8,128)S(1)}, u32[]{:S(2)}, u32[]{:S(2)}) collective-permute-start(f32[2,16,8,128]{3,2,1,0:T(8,128)S(1)} %get-tuple-element.337), channel_id=1, source_target_pairs={{0,8},{8,16},{16,24},{24,0},{1,9},{9,17},{17,25},{25,1},{2,10},{10... | collective-permute-start | bytes 393224 | tf_op jit(solution)/shard_map/ppermute | solution.py:31
  100.9 9.0 %collective-permute-start.11 = (f32[2,16,8,128]{3,2,1,0:T(8,128)S(1)}, f32[2,16,8,128]{3,2,1,0:T(8,128)S(1)}, u32[]{:S(2)}, u32[]{:S(2)}) collective-permute-start(f32[2,16,8,128]{3,2,1,0:T(8,128)S(1)} %get-tuple-element.338), channel_id=1, source_target_pairs={{0,24},{8,0},{16,8},{24,16},{1,25},{9,1},{17,9},{25,17},{2,26},{10... | collective-permute-start | bytes 393224 | tf_op jit(solution)/shard_map/ppermute | solution.py:31
  104.3 13.7 %collective-permute-start.13 = (f32[224,512]{1,0:T(8,128)S(1)}, f32[224,512]{1,0:T(8,128)S(1)}, u32[]{:S(2)}, u32[]{:S(2)}) collective-permute-start(f32[224,512]{1,0:T(8,128)S(1)} %dynamic-slice_add_fusion.5), channel_id=1, source_target_pairs={{0,4},{4,0},{1,5},{5,1},{2,6},{6,2},{3,7},{7,3},{8,12},{12,8},{9,1... | collective-permute-start | bytes 1376264 | tf_op jit(solution)/shard_map/ppermute | solution.py:55
  105.2 12.9 %collective-permute-start.14 = (f32[192,512]{1,0:T(8,128)S(1)}, f32[192,512]{1,0:T(8,128)S(1)}, u32[]{:S(2)}, u32[]{:S(2)}) collective-permute-start(f32[192,512]{1,0:T(8,128)S(1)} %dynamic-slice_add_fusion.13), channel_id=1, source_target_pairs={{0,1},{1,0},{2,3},{3,2},{4,5},{5,4},{6,7},{7,6},{8,9},{9,8},{10,11... | collective-permute-start | bytes 1179656 | tf_op jit(solution)/shard_map/ppermute | solution.py:55
  109.9 7.5 %collective-permute-start.15 = (f32[16,8,128]{2,1,0:T(8,128)S(1)}, f32[16,8,128]{2,1,0:T(8,128)S(1)}, u32[]{:S(2)}, u32[]{:S(2)}) collective-permute-start(f32[16,8,128]{2,1,0:T(8,128)S(1)} %select_bitcast_fusion.2), channel_id=1, source_target_pairs={{0,1},{1,0},{2,3},{3,2},{4,5},{5,4},{6,7},{7,6},{8,9},{9,8},{10,11... | collective-permute-start | bytes 196616 | tf_op jit(solution)/shard_map/ppermute | solution.py:842
  118.2 10.7 %collective-permute-start.16 = (f32[208,512]{1,0:T(8,128)S(1)}, f32[208,512]{1,0:T(8,128)S(1)}, u32[]{:S(2)}, u32[]{:S(2)}) collective-permute-start(f32[208,512]{1,0:T(8,128)S(1)} %dynamic-slice_add_fusion.7), channel_id=1, source_target_pairs={{0,8},{8,0},{16,24},{24,16},{1,9},{9,1},{17,25},{25,17},{2,10},{10... | collective-permute-start | bytes 1277960 | tf_op jit(solution)/shard_map/ppermute | solution.py:55
  125.2 9.4 %copy-start.6 = (f32[384,512]{1,0:T(8,128)S(1)}, f32[384,512]{1,0:T(8,128)}, u32[]{:S(2)}) copy-start(f32[384,512]{1,0:T(8,128)} %get-tuple-element.244) | copy-start | bytes 2359300
  129.6 14.4 %copy-start.7 = (f32[384,512]{1,0:T(8,128)S(1)}, f32[384,512]{1,0:T(8,128)}, u32[]{:S(2)}) copy-start(f32[384,512]{1,0:T(8,128)} %get-tuple-element.240) | copy-start | bytes 2359300
  129.7 2.6 %collective-permute-start.17 = (f32[384,512]{1,0:T(8,128)}, f32[384,512]{1,0:T(8,128)S(1)}, u32[]{:S(2)}, u32[]{:S(2)}) collective-permute-start(f32[384,512]{1,0:T(8,128)} %get-tuple-element.231), channel_id=1, source_target_pairs={{0,2},{2,0},{1,3},{3,1},{4,6},{6,4},{5,7},{7,5},{8,10},{10,8},{9,1... | collective-permute-start | bytes 2359304 | tf_op jit(solution)/shard_map/ppermute | solution.py:55
  129.8 4.8 %collective-permute-start.18 = (f32[384,512]{1,0:T(8,128)}, f32[384,512]{1,0:T(8,128)S(1)}, u32[]{:S(2)}, u32[]{:S(2)}) collective-permute-start(f32[384,512]{1,0:T(8,128)} %get-tuple-element.235), channel_id=1, source_target_pairs={{0,2},{2,0},{1,3},{3,1},{4,6},{6,4},{5,7},{7,5},{8,10},{10,8},{9,1... | collective-permute-start | bytes 2359304 | tf_op jit(solution)/shard_map/ppermute | solution.py:55
  130.3 12.7 %collective-permute-start.19 = (f32[104,512]{1,0:T(8,128)}, f32[104,512]{1,0:T(8,128)}, u32[]{:S(2)}, u32[]{:S(2)}) collective-permute-start(f32[104,512]{1,0:T(8,128)} %dynamic-slice_add_fusion.15), channel_id=1, source_target_pairs={{0,16},{8,24},{16,0},{24,8},{1,17},{9,25},{17,1},{25,9},{2,18},{10... | collective-permute-start | bytes 638984 | tf_op jit(solution)/shard_map/ppermute | solution.py:55
  134.0 11.5 %collective-permute-start.20 = (f32[192,512]{1,0:T(8,128)}, f32[192,512]{1,0:T(8,128)}, u32[]{:S(2)}, u32[]{:S(2)}) collective-permute-start(f32[192,512]{1,0:T(8,128)} %dynamic-slice_add_fusion.11), channel_id=1, source_target_pairs={{0,1},{1,0},{2,3},{3,2},{4,5},{5,4},{6,7},{7,6},{8,9},{9,8},{10,11... | collective-permute-start | bytes 1179656 | tf_op jit(solution)/shard_map/ppermute | solution.py:55
  135.4 13.2 %collective-permute-start.21 = (f32[192,512]{1,0:T(8,128)}, f32[192,512]{1,0:T(8,128)}, u32[]{:S(2)}, u32[]{:S(2)}) collective-permute-start(f32[192,512]{1,0:T(8,128)} %dynamic-slice_add_fusion.10), channel_id=1, source_target_pairs={{0,4},{4,0},{1,5},{5,1},{2,6},{6,2},{3,7},{7,3},{8,12},{12,8},{9,1... | collective-permute-start | bytes 1179656 | tf_op jit(solution)/shard_map/ppermute | solution.py:55
  144.0 10.4 %collective-permute-start.22 = (f32[104,512]{1,0:T(8,128)S(1)}, f32[104,512]{1,0:T(8,128)S(1)}, u32[]{:S(2)}, u32[]{:S(2)}) collective-permute-start(f32[104,512]{1,0:T(8,128)S(1)} %add.302), channel_id=1, source_target_pairs={{0,16},{8,24},{16,0},{24,8},{1,17},{9,25},{17,1},{25,9},{2,18},{10... | collective-permute-start | bytes 638984 | tf_op jit(solution)/shard_map/ppermute | solution.py:55
  146.5 10.0 %collective-permute-start.23 = (f32[96,512]{1,0:T(8,128)S(1)}, f32[96,512]{1,0:T(8,128)S(1)}, u32[]{:S(2)}, u32[]{:S(2)}) collective-permute-start(f32[96,512]{1,0:T(8,128)S(1)} %dynamic-slice_add_fusion.21), channel_id=1, source_target_pairs={{0,4},{4,0},{1,5},{5,1},{2,6},{6,2},{3,7},{7,3},{8,12},{12,8},{9,1... | collective-permute-start | bytes 589832 | tf_op jit(solution)/shard_map/ppermute | solution.py:55
  149.5 6.9 %collective-permute-start.24 = (f32[96,512]{1,0:T(8,128)S(1)}, f32[96,512]{1,0:T(8,128)S(1)}, u32[]{:S(2)}, u32[]{:S(2)}) collective-permute-start(f32[96,512]{1,0:T(8,128)S(1)} %dynamic-slice_add_fusion.20), channel_id=1, source_target_pairs={{0,1},{1,0},{2,3},{3,2},{4,5},{5,4},{6,7},{7,6},{8,9},{9,8},{10,11... | collective-permute-start | bytes 589832 | tf_op jit(solution)/shard_map/ppermute | solution.py:55
  154.4 11.8 %collective-permute-start.25 = (f32[208,512]{1,0:T(8,128)S(1)}, f32[208,512]{1,0:T(8,128)S(1)}, u32[]{:S(2)}, u32[]{:S(2)}) collective-permute-start(f32[208,512]{1,0:T(8,128)S(1)} %pad_maximum_fusion.9), channel_id=1, source_target_pairs={{0,8},{8,0},{16,24},{24,16},{1,9},{9,1},{17,25},{25,17},{2,10},{10... | collective-permute-start | bytes 1277960 | tf_op jit(solution)/shard_map/ppermute | solution.py:55
  166.4 14.5 %collective-permute-start.28 = (f32[224,512]{1,0:T(8,128)S(1)}, f32[224,512]{1,0:T(8,128)S(1)}, u32[]{:S(2)}, u32[]{:S(2)}) collective-permute-start(f32[224,512]{1,0:T(8,128)S(1)} %fusion), channel_id=1, source_target_pairs={{0,4},{4,0},{1,5},{5,1},{2,6},{6,2},{3,7},{7,3},{8,12},{12,8},{9,1... | collective-permute-start | bytes 1376264 | tf_op jit(solution)/shard_map/ppermute | solution.py:55
  168.4 5.7 %collective-permute-start.26 = (f32[96,512]{1,0:T(8,128)S(1)}, f32[96,512]{1,0:T(8,128)S(1)}, u32[]{:S(2)}, u32[]{:S(2)}) collective-permute-start(f32[96,512]{1,0:T(8,128)S(1)} %dynamic-slice_add_fusion.17), channel_id=1, source_target_pairs={{0,8},{8,0},{16,24},{24,16},{1,9},{9,1},{17,25},{25,17},{2,10},{10... | collective-permute-start | bytes 589832 | tf_op jit(solution)/shard_map/ppermute | solution.py:55
  174.2 6.6 %collective-permute-start.27 = (f32[48,512]{1,0:T(8,128)S(1)}, f32[48,512]{1,0:T(8,128)S(1)}, u32[]{:S(2)}, u32[]{:S(2)}) collective-permute-start(f32[48,512]{1,0:T(8,128)S(1)} %dynamic-slice_add_fusion.23), channel_id=1, source_target_pairs={{0,16},{8,24},{16,0},{24,8},{1,17},{9,25},{17,1},{25,9},{2,18},{10... | collective-permute-start | bytes 294920 | tf_op jit(solution)/shard_map/ppermute | solution.py:55
  174.8 11.5 %collective-permute-start.30 = (f32[192,512]{1,0:T(8,128)S(1)}, f32[192,512]{1,0:T(8,128)S(1)}, u32[]{:S(2)}, u32[]{:S(2)}) collective-permute-start(f32[192,512]{1,0:T(8,128)S(1)} %slice.37), channel_id=1, source_target_pairs={{0,1},{1,0},{2,3},{3,2},{4,5},{5,4},{6,7},{7,6},{8,9},{9,8},{10,11... | collective-permute-start | bytes 1179656 | tf_op jit(solution)/shard_map/ppermute | solution.py:55
  181.0 22.1 %collective-permute-start.29 = (f32[448,512]{1,0:T(8,128)S(1)}, f32[448,512]{1,0:T(8,128)S(1)}, u32[]{:S(2)}, u32[]{:S(2)}) collective-permute-start(f32[448,512]{1,0:T(8,128)S(1)} %pad_maximum_fusion.3), channel_id=1, source_target_pairs={{0,1},{1,0},{2,3},{3,2},{4,5},{5,4},{6,7},{7,6},{8,9},{9,8},{10,11... | collective-permute-start | bytes 2752520 | tf_op jit(solution)/shard_map/ppermute | solution.py:55
  186.4 17.1 %collective-permute-start.31 = (f32[384,512]{1,0:T(8,128)S(1)}, f32[384,512]{1,0:T(8,128)S(1)}, u32[]{:S(2)}, u32[]{:S(2)}) collective-permute-start(f32[384,512]{1,0:T(8,128)S(1)} %pad_maximum_fusion.6), channel_id=1, source_target_pairs={{0,4},{4,0},{1,5},{5,1},{2,6},{6,2},{3,7},{7,3},{8,12},{12,8},{9,1... | collective-permute-start | bytes 2359304 | tf_op jit(solution)/shard_map/ppermute | solution.py:55
  187.0 6.6 %collective-permute-start.32 = (f32[48,512]{1,0:T(8,128)S(1)}, f32[48,512]{1,0:T(8,128)S(1)}, u32[]{:S(2)}, u32[]{:S(2)}) collective-permute-start(f32[48,512]{1,0:T(8,128)S(1)} %add.322), channel_id=1, source_target_pairs={{0,16},{8,24},{16,0},{24,8},{1,17},{9,25},{17,1},{25,9},{2,18},{10... | collective-permute-start | bytes 294920 | tf_op jit(solution)/shard_map/ppermute | solution.py:55
  203.4 1.2 copy-start
  203.4 17.2 %collective-permute-start.36 = (f32[896,512]{1,0:T(8,128)S(1)}, f32[896,512]{1,0:T(8,128)S(1)}, u32[]{:S(2)}, u32[]{:S(2)}) collective-permute-start(f32[896,512]{1,0:T(8,128)S(1)} %pad_maximum_fusion.a_mine), channel_id=1, source_target_pairs={{0,2},{2,0},{1,3},{3,1},{4,6},{6,4},{5,7},{7,5},{8,10},{10,8},{9,1... | collective-permute-start | bytes 5505032 | tf_op jit(solution)/shard_map/ppermute | solution.py:55
  204.7 14.8 %copy-start.3 = (f32[768,512]{1,0:T(8,128)}, f32[768,512]{1,0:T(8,128)S(1)}, u32[]{:S(2)}) copy-start(f32[768,512]{1,0:T(8,128)S(1)} %pad_maximum_fusion.1.b_mine) | copy-start | bytes 4718596
  204.7 15.9 %collective-permute-start.37 = (f32[768,512]{1,0:T(8,128)S(1)}, f32[768,512]{1,0:T(8,128)S(1)}, u32[]{:S(2)}, u32[]{:S(2)}) collective-permute-start(f32[768,512]{1,0:T(8,128)S(1)} %pad_maximum_fusion.1.b_mine), channel_id=1, source_target_pairs={{0,2},{2,0},{1,3},{3,1},{4,6},{6,4},{5,7},{7,5},{8,10},{10,8},{9,1... | collective-permute-start | bytes 4718600 | tf_op jit(solution)/shard_map/ppermute | solution.py:55
  204.7 7.4 %collective-permute-start.33 = (f32[96,512]{1,0:T(8,128)S(1)}, f32[96,512]{1,0:T(8,128)S(1)}, u32[]{:S(2)}, u32[]{:S(2)}) collective-permute-start(f32[96,512]{1,0:T(8,128)S(1)} %pad_maximum_fusion.15), channel_id=1, source_target_pairs={{0,8},{8,0},{16,24},{24,16},{1,9},{9,1},{17,25},{25,17},{2,10},{10... | collective-permute-start | bytes 589832 | tf_op jit(solution)/shard_map/ppermute | solution.py:55
  212.1 6.6 %collective-permute-start.34 = (f32[96,512]{1,0:T(8,128)S(1)}, f32[96,512]{1,0:T(8,128)S(1)}, u32[]{:S(2)}, u32[]{:S(2)}) collective-permute-start(f32[96,512]{1,0:T(8,128)S(1)} %get-tuple-element.283), channel_id=1, source_target_pairs={{0,4},{4,0},{1,5},{5,1},{2,6},{6,2},{3,7},{7,3},{8,12},{12,8},{9,1... | collective-permute-start | bytes 589832 | tf_op jit(solution)/shard_map/ppermute | solution.py:55
  212.8 6.6 %collective-permute-start.35 = (f32[96,512]{1,0:T(8,128)S(1)}, f32[96,512]{1,0:T(8,128)S(1)}, u32[]{:S(2)}, u32[]{:S(2)}) collective-permute-start(f32[96,512]{1,0:T(8,128)S(1)} %get-tuple-element.285), channel_id=1, source_target_pairs={{0,1},{1,0},{2,3},{3,2},{4,5},{5,4},{6,7},{7,6},{8,9},{9,8},{10,11... | collective-permute-start | bytes 589832 | tf_op jit(solution)/shard_map/ppermute | solution.py:55
  218.8 10.1 %collective-permute-start.38 = (f32[192,512]{1,0:T(8,128)S(1)}, f32[192,512]{1,0:T(8,128)S(1)}, u32[]{:S(2)}, u32[]{:S(2)}) collective-permute-start(f32[192,512]{1,0:T(8,128)S(1)} %pad_maximum_fusion.13), channel_id=1, source_target_pairs={{0,1},{1,0},{2,3},{3,2},{4,5},{5,4},{6,7},{7,6},{8,9},{9,8},{10,11... | collective-permute-start | bytes 1179656 | tf_op jit(solution)/shard_map/ppermute | solution.py:55
  219.5 9.6 %collective-permute-start.39 = (f32[192,512]{1,0:T(8,128)S(1)}, f32[192,512]{1,0:T(8,128)S(1)}, u32[]{:S(2)}, u32[]{:S(2)}) collective-permute-start(f32[192,512]{1,0:T(8,128)S(1)} %pad_maximum_fusion.14), channel_id=1, source_target_pairs={{0,4},{4,0},{1,5},{5,1},{2,6},{6,2},{3,7},{7,3},{8,12},{12,8},{9,1... | collective-permute-start | bytes 1179656 | tf_op jit(solution)/shard_map/ppermute | solution.py:55
  220.6 1.2 copy-start.16
  221.8 1.2 copy-start.15
  229.0 3.7 %copy-start.4 = (f32[384,512]{1,0:T(8,128)}, f32[384,512]{1,0:T(8,128)S(1)}, u32[]{:S(2)}) copy-start(f32[384,512]{1,0:T(8,128)S(1)} %pad_maximum_fusion.7.c_mine) | copy-start | bytes 2359300
  229.3 3.5 %copy-start.5 = (f32[384,512]{1,0:T(8,128)}, f32[384,512]{1,0:T(8,128)S(1)}, u32[]{:S(2)}) copy-start(f32[384,512]{1,0:T(8,128)S(1)} %pad_maximum_fusion.8.d_mine) | copy-start | bytes 2359300
  229.3 2.4 collective-permute-start.41
  229.4 3.4 %collective-permute-start.40 = (f32[384,512]{1,0:T(8,128)S(1)}, f32[384,512]{1,0:T(8,128)S(1)}, u32[]{:S(2)}, u32[]{:S(2)}) collective-permute-start(f32[384,512]{1,0:T(8,128)S(1)} %pad_maximum_fusion.7.c_mine), channel_id=1, source_target_pairs={{0,2},{2,0},{1,3},{3,1},{4,6},{6,4},{5,7},{7,5},{8,10},{10,8},{9,1... | collective-permute-start | bytes 2359304 | tf_op jit(solution)/shard_map/ppermute | solution.py:55
  231.6 1.1 copy-start.17
  232.8 0.9 copy-start.18

commit v4 on v3

--- a/solution.py
+++ b/solution.py
@@ -1,4 +1,4 @@
-import functools
+import itertools
 import math
 
 import jax
@@ -59,13 +59,6 @@
     return (lax.axis_index(axis) >> bit) & 1
 
 
-def part(arrays, at, size):
-    total = lax.dynamic_slice_in_dim(arrays[0], at, size)
-    for x in arrays[1:]:
-        total = total + lax.dynamic_slice_in_dim(x, at, size)
-    return total
-
-
 class Chain:
     def __init__(self):
         self.last = None
@@ -80,60 +73,140 @@
         return value
 
 
-def halved(chain, arrays, axis, bit, tight=False):
-    arrays = chain.after(arrays)
-    half = arrays[0].shape[0] // 2
-    one = bit_value(axis, bit)
-    send = chain.step(part(arrays, (1 - one) * half, half))
-    got = swap(send, axis, bit)
-    send, arrays = lax.optimization_barrier((send, arrays))
-    keep = part(arrays, one * half, half)
-    if tight:
-        chain.step((send, keep))
-    return [keep, got]
-
-
-def joined_halves(value, other, axis, bit):
-    one = bit_value(axis, bit) == 1
-    return jnp.concatenate([jnp.where(one, other, value), jnp.where(one, value, other)])
-
-
-def reduction(chain, first, second, tight=False):
+def upper_half(me, axis, bit):
+    return ((me[ROWS.index(axis)] >> bit) & 1) == 1
+
+
+def halved(chain, me, lanes, bits, weight):
+    def kernel(me_ref, *refs):
+        for i, (axis, bit) in enumerate(bits):
+            x, y, send, keep = refs[2 * i], refs[2 * i + 1], refs[count + 2 * i], refs[count + 2 * i + 1]
+            half = x.shape[0] // 2
+            upper = upper_half(me_ref, axis, bit)
+            low, high = x[:half] + y[:half], x[half:] + y[half:]
+            send[...] = jnp.where(upper, low, high)
+            keep[...] = jnp.where(upper, high, low)
+
+    count = 2 * len(lanes)
+    shapes = [(x.shape[0] // 2, x.shape[1]) for lane in lanes for x in lane]
+    args = [me] + chain.after([x for lane in lanes for x in lane])
+    outs = chain.step(call(kernel, shapes, args, weight=weight))
+    return [(outs[2 * i + 1], swap(outs[2 * i], *bits[i])) for i in range(len(lanes))]
+
+
+def halved_joint(chain, me, lanes, axis, bit, weight):
+    def kernel(me_ref, *refs):
+        send, keep, total = refs[-3:]
+        at = 0
+        for x, y in zip(refs[:-3:2], refs[1:-3:2]):
+            total[at : at + x.shape[0]] = x[...] + y[...]
+            at += x.shape[0]
+        upper = upper_half(me_ref, axis, bit)
+        low, high = total[:half], total[half:]
+        send[...] = jnp.where(upper, low, high)
+        keep[...] = jnp.where(upper, high, low)
+
+    rows, width = sum(x.shape[0] for x, _ in lanes), lanes[0][0].shape[1]
+    half = rows // 2
+    args = [me] + chain.after([x for lane in lanes for x in lane])
+    outs = call(kernel, [(half, width)] * 2, args, [pltpu.VMEM((rows, width), F32)], weight)
+    send, keep = chain.step(outs)
+    return keep, swap(send, axis, bit)
+
+
+def joined(chain, me, lanes, bits, weight, cuts=None):
+    def kernel(me_ref, *refs):
+        for i, (axis, bit) in enumerate(bits):
+            mine, other = refs[2 * i], refs[2 * i + 1]
+            upper = upper_half(me_ref, axis, bit)
+            low, high = jnp.where(upper, other[...], mine[...]), jnp.where(upper, mine[...], other[...])
+            whole = refs[count + i] if cuts is None else refs[-1]
+            half = mine.shape[0]
+            whole[:half] = low
+            whole[half:] = high
+        at = 0
+        for out, size in zip(refs[count:], cuts or ()):
+            out[...] = refs[-1][at : at + size]
+            at += size
+
+    count = 2 * len(lanes)
+    width = lanes[0][0].shape[1]
+    shapes = [(2 * x.shape[0], width) for x, _ in lanes]
+    scratch = [] if cuts is None else [pltpu.VMEM(shapes[0], F32)]
+    shapes = shapes if cuts is None else [(size, width) for size in cuts]
+    args = [me] + chain.after([x for lane in lanes for x in lane])
+    return list(chain.step(call(kernel, shapes, args, scratch, weight)))
+
+
+def added(chain, pair, weight):
+    def kernel(x, y, out):
+        out[...] = x[...] + y[...]
+
+    return chain.step(call(kernel, [pair[0].shape], chain.after(list(pair)), weight=weight))[0]
+
+
+def reduction(chain, me, first, second, weights):
     across, along = bits_of("gz"), bits_of("gyh")
     lanes = [first, second]
-    for turn, plan in enumerate(((across, along), (along, across))):
-        for i in range(2):
-            for axis, bit in plan[i]:
-                lanes[i] = halved(chain, lanes[i], axis, bit, tight and turn == 1)
+    step = itertools.count(1).__next__
+    turns = range(max(len(across), len(along)))
+    for plan in ((across, along), (along, across)):
+        for turn in turns:
+            on = [i for i in range(2) if turn < len(plan[i])]
+            for i, got in zip(on, halved(chain, me, [lanes[i] for i in on], [plan[i][turn] for i in on], weights(step()))):
+                lanes[i] = got
+            yield
+    sizes = [x.shape[0] for x, _ in lanes]
+    for axis, bit in bits_of("gx"):
+        if bit == 0:
+            joint = halved_joint(chain, me, lanes, axis, bit, weights(step()))
+        else:
+            (joint,) = halved(chain, me, [joint], [(axis, bit)], weights(step()))
         yield
-    sizes = [x[0].shape[0] for x in lanes]
-    joint = [jnp.concatenate(pair) for pair in zip(*chain.after(lanes))]
-    for axis, bit in bits_of("gx"):
-        joint = halved(chain, joint, axis, bit, tight)
-        yield
-    joint = chain.after(joint)
-    value = chain.step(sum(joint[1:], joint[0]))
+    value = added(chain, joint, weights(step()))
     for axis, bit in bits_of("gx")[::-1]:
         other = swap(value, axis, bit)
         yield
-        value, other = chain.after((value, other))
-        value = chain.step(joined_halves(value, other, axis, bit))
-    values = [value[: sizes[0]], value[sizes[0] :]]
-    for plan in ((along, across), (across, along)):
-        for turn in range(max(len(across), len(along))):
-            others = [None, None]
-            for i in range(2):
-                if turn < len(plan[i]):
-                    others[i] = swap(values[i], *plan[i][::-1][turn])
+        if bit == 0:
+            values = joined(chain, me, [(value, other)], [(axis, bit)], weights(step()), sizes)
+        else:
+            (value,) = joined(chain, me, [(value, other)], [(axis, bit)], weights(step()))
+    for plan in ((along[::-1], across[::-1]), (across[::-1], along[::-1])):
+        for turn in turns:
+            on = [i for i in range(2) if turn < len(plan[i])]
+            others = [swap(values[i], *plan[i][turn]) for i in on]
             yield
-            for i in range(2):
-                if turn < len(plan[i]):
-                    values[i], others[i] = chain.after((values[i], others[i]))
-                    values[i] = chain.step(joined_halves(values[i], others[i], *plan[i][::-1][turn]))
+            pairs = [(values[i], x) for i, x in zip(on, others)]
+            for i, got in zip(on, joined(chain, me, pairs, [plan[i][turn] for i in on], weights(step()))):
+                values[i] = got
     others = [swap(x, "gyl", 0) for x in values]
     yield
-    values, others = chain.after((values, others))
-    return [(value, chain.step(other)) for value, other in zip(values, others)]
+    return [(value, other) for value, other in zip(values, others)]
+
+
+def return_along(chain, here, got, planes):
+    def kernel(x, y, z, *outs):
+        for i, out in enumerate(outs):
+            cut = slice(i * planes, (i + 1) * planes)
+            out[...] = x[cut] + y[cut] + z[cut]
+
+    shapes = [(planes,) + here.shape[1:]] * 3
+    return chain.step(call(kernel, shapes, chain.after([here, *got]), weight=0))
+
+
+def return_up(chain, me, middle, got, planes):
+    def kernel(me_ref, x, y, z, *outs):
+        if planes == 2:
+            top = upper_half(me_ref, "gz", 0)
+            low, high = x[0] + y[0] + z[0], x[1] + y[1] + z[1]
+            outs[0][...] = jnp.where(top, high, low)
+            outs[1][...] = jnp.where(top, low, high)
+        else:
+            for i, out in enumerate(outs):
+                out[...] = x[i] + y[i] + z[i]
+
+    shapes = [middle.shape[1:]] * planes
+    return chain.step(call(kernel, shapes, [me] + chain.after([middle, *got]), weight=0))
 
 
 def iota(shape, dim):
@@ -712,8 +785,7 @@
     rad[2:5] = late_rad[...]
 
 
-def call(kernel, outs, args, scratch=(), micros=1):
-    flops = int(micros * 1.15e9)
+def call(kernel, outs, args, scratch=(), weight=30):
     return pl.pallas_call(
         kernel,
         out_shape=[jax.ShapeDtypeStruct(shape, F32) for shape in outs],
@@ -721,7 +793,7 @@
         out_specs=[pl.BlockSpec(memory_space=pltpu.VMEM)] * len(outs),
         scratch_shapes=list(scratch),
         compiler_params=pltpu.CompilerParams(vmem_limit_bytes=56 * 1024 * 1024),
-        cost_estimate=pl.CostEstimate(flops=flops, bytes_accessed=1 << 10, transcendentals=0),
+        cost_estimate=pl.CostEstimate(flops=weight * 10**9, bytes_accessed=0, transcendentals=0),
     )(*args)
 
 
@@ -780,9 +852,9 @@
         + [(EDGES, 128)] * 2,
         [edge_states, edge_vectors, edge_mask[None, :], hidden_atoms, tag_row, send_row, tag_table,
          w_inputs, w_radial, trip_down_t, quad_down_t],
-        micros=5,
     )
     core = bit_value("gyl", 0)[None]
+    me = jnp.stack([lax.axis_index(axis) for axis in ROWS]).astype(jnp.int32)
     before, here, after = with_halo(payload)
     (
         atoms_out, edges_out, energy_out, grad_edges, grad_tag,
@@ -804,7 +876,6 @@
             pltpu.VMEM((EDGES, 128), F32),
             pltpu.VMEM((1792, 512), F32),
         ],
-        micros=26,
     )
     chain = Chain()
     got_a = swap(send_a, "gyl", 0)
@@ -813,35 +884,29 @@
         [(768, 512)] * 2,
         [grad_rads, radial, atom_rows, quad_up_grad, core],
         scratch=[pltpu.VMEM((1536, 512), F32)],
-        micros=4,
-    )
-    late = reduction(chain, [keep_a, got_a], [keep_b, swap(send_b, "gyl", 0)], True)
+    )
+    late = reduction(chain, me, (keep_a, got_a), (keep_b, swap(send_b, "gyl", 0)), lambda step: 30)
     next(late)
     grad_sums = chain.after(grad_sums)
-    back_before, back_here, back_after, back_local = call(
-        scatter_kernel,
-        [(group, 16, 8, 128)] * 3 + [(16, 16, 128)],
-        [cosines, grad_sums, grad_src, src, mark_rows],
-        scratch=[pltpu.VMEM((32, EDGES, 256), BF)],
-        micros=13,
+    back_before, back_here, back_after, back_local = chain.step(
+        call(
+            scatter_kernel,
+            [(group, 16, 8, 128)] * 3 + [(16, 16, 128)],
+            [cosines, grad_sums, grad_src, src, mark_rows],
+            scratch=[pltpu.VMEM((32, EDGES, 256), BF)],
+        )
     )
     got = shifted(back_before, GY, -1, True), shifted(back_after, GY, 1, True)
-    chain.step(back_local)
     next(late)
-    got, value = chain.after((got, back_here))
-    value = chain.step(value + got[0] + got[1])
-    first_plane, middle, last_plane = value[:planes], value[planes : 2 * planes], value[2 * planes :]
-    got = shifted(first_plane, "gx", -1, True), shifted(last_plane, "gx", 1, True)
-    got, middle = chain.after((got, middle))
-    value = chain.step(middle + got[0] + got[1])
+    back_first, back_middle, back_last = return_along(chain, back_here, got, planes)
+    got = shifted(back_first, "gx", -1, True), shifted(back_last, "gx", 1, True)
+    back = return_up(chain, me, back_middle, got, planes)
+    if planes == 2:
+        returned = back[0], lax.ppermute(back[1], "gz", [(0, 1), (1, 0)])
+    else:
+        returned = back[1], shifted(back[0], "gz", -1, False), shifted(back[2], "gz", 1, False)
     next(late)
-    if planes == 2:
-        top = lax.axis_index("gz") == 1
-        mine = jnp.where(top, value[1], value[0])
-        theirs = jnp.where(top, value[0], value[1])
-        returned = mine + lax.ppermute(theirs, "gz", [(0, 1), (1, 0)])
-    else:
-        returned = value[1] + shifted(value[0], "gz", -1, False) + shifted(value[2], "gz", 1, False)
+    returned = sum(returned[1:], returned[0])
     returned = chain.after(returned)
     grad_atoms, grad_edges, keep_c, send_c, keep_d, send_d = call(
         finish_kernel,
@@ -849,12 +914,9 @@
         [back_local, returned, grad_edges, grad_tag, edge_states, radial, columns, pre, downs, rads,
          tag_row, send_row, w_inputs, trip_down_t, quad_down_t, core],
         scratch=[pltpu.VMEM((768, 512), F32)] * 2,
-        micros=7,
-    )
-    next(late)
-    send_c, send_d = chain.after((send_c, send_d))
+    )
     got_c, got_d = swap(send_c, "gyl", 0), swap(send_d, "gyl", 0)
-    early = reduction(chain, [keep_c, got_c], [keep_d, got_d])
+    early = reduction(chain, me, (keep_c, got_c), (keep_d, got_d), lambda step: {3: 30, 5: 2, 7: 7}.get(step, 0))
     running = {"L": late, "E": early}
     done = {}
 
@@ -866,7 +928,7 @@
         except StopIteration as end:
             done[name] = end.value
 
-    for name in "ELELELEELEELE":
+    for name in "LELELELEELEELE":
         resume(name)
     while "L" not in done:
         resume("L")
@@ -876,7 +938,6 @@
         [(2, 512, 512), (2, 256, 512), (64, 1024), (64, 512), (32, 1024), (32, 512), (3, 128, 512)]
         + [(2, 512, 256), (4, 256, 256)],
         [a_mine, a_other, b_mine, b_other, core],
-        micros=5,
     )
     chain.step(g_rad)
     while "E" not in done:
@@ -886,7 +947,6 @@
         early_outputs,
         [(2, 512, 512), (5, 128, 512), (64, 512), (32, 512), (3, 256)],
         [c_mine, c_other, d_mine, d_other, g_rad, core],
-        micros=3,
     )
     return (
         atoms_out,

time: 238 us -> 265 us (1.11)
  Pallas kernels: 60.1 us -> 107 us
  waiting for transfers between devices: 112 us -> 81.9 us
  local copies, waits for them, and re-layouts: 9.08 us -> 25.7 us
  other arithmetic: 19.6 us -> 4.43 us
  starting transfers between devices: 35.2 us -> 43.8 us
    pallas_call x7 -> x27, Pallas kernels: 60.1 us -> 107 us  [call(): pl.pallas_call(kernel, out_shape=[jax.ShapeDtypeStruct(shape, F32) for sh...]
    ppermute x32, waiting for transfers between devices: 77.7 us -> 57.5 us  [swap(): return lax.ppermute(value, axis, [(i, i ^ 1 << bit) for i in range(count)])]
    unnamed x43 -> x91, local copies, waits for them, and re-layouts: 4.91 us -> 22.8 us
    add x29 -> x1, other arithmetic: 14.8 us -> 1.48 us  [per_device(): returned = sum(returned[1:], returned[0])]
    ppermute x8, waiting for transfers between devices: 26.1 us -> 18.8 us  [shifted(): return lax.ppermute(value, axis, pairs)]
    ppermute x32, starting transfers between devices: 22.4 us -> 29.7 us  [swap(): return lax.ppermute(value, axis, [(i, i ^ 1 << bit) for i in range(count)])]
    ppermute x1, waiting for transfers between devices: 6.9 us -> 3.95 us  [per_device(): returned = (back[0], lax.ppermute(back[1], 'gz', [(0, 1), (1, 0)]))]
  transfers between devices with their start and end apart: 42 -> 42, of which waited for: 28 -> 25; matrix products, arithmetic and copies ran while one was open for 9% -> 2% of each run, Pallas kernels for 11% -> 22%
where the time goes in v4:
time: 265 us; the launch traced here: 264 us
  Pallas kernels  107 us (40%)
  waiting for transfers between devices  81.9 us (31%)
  starting transfers between devices  43.8 us (17%)
  local copies, waits for them, and re-layouts  25.7 us (10%)
  other arithmetic  4.43 us (2%)
    pallas_call x27, Pallas kernels, call(): pl.pallas_call(kernel, out_shape=[jax.ShapeDtypeStruct(shape, F32) for sh...  107 us
    ppermute x32, waiting for transfers between devices, swap(): return lax.ppermute(value, axis, [(i, i ^ 1 << bit) for i in range(count)])  57.5 us
    ppermute x32, starting transfers between devices, swap(): return lax.ppermute(value, axis, [(i, i ^ 1 << bit) for i in range(count)])  29.7 us
    unnamed x91, local copies, waits for them, and re-layouts  22.8 us
    ppermute x8, waiting for transfers between devices, shifted(): return lax.ppermute(value, axis, pairs)  18.8 us
    ppermute x8, starting transfers between devices, shifted(): return lax.ppermute(value, axis, pairs)  10.6 us
  transfers between devices with their start and end apart: 42, of which 25 were waited for; matrix products, arithmetic and copies ran while one was open for 2% of the time, Pallas kernels for 22%

profile of v4, /device:TPU:0, one launch (start us, length us, event | category | flops | bytes accessed | tf_op | source)
XLA Modules:
  0.0 263.9 jit_solution(3019398810568495509)
XLA Ops:
  0.7 4.7 %shard_map.394 = (f32[17,8,128]{2,1,0:T(8,128)}, f32[17,16,128]{2,1,0:T(8,128)}, f32[8,256]{1,0:T(8,128)}, f32[2,240,512]{2,1,0:T(8,128)}, f32[240,128]{1,0:T(8,...) custom-call(f32[240,512]{1,0:T(8,128)} %edge.5, f32[3,240]{1,0:T(4,128)} %vec.1, ...), custom_call_target="tpu_custom_call" | custom-call | flops 30000001024 | tf_op jit(solution)/shard_map/pallas_call | solution.py:789
  5.4 3.0 %collective-permute-start = (f32[17,8,128]{2,1,0:T(8,128)}, f32[17,8,128]{2,1,0:T(8,128)S(1)}, u32[]{:S(2)}, u32[]{:S(2)}) collective-permute-start(f32[17,8,128]{2,1,0:T(8,128)} %get-tuple-element.166), channel_id=1, source_target_pairs={{0,1},{1,0},{2,3},{3,2},{4,5},{5,4},{6,7},{7,6},{8,9},{9,8},{10,11... | collective-permute-start | bytes 208904 | tf_op jit(solution)/shard_map/ppermute | solution.py:36
  9.2 1.7 collective-permute-done
  11.8 2.2 collective-permute-start.1
  13.9 2.1 collective-permute-start.2
  16.1 4.1 %collective-permute-done.1 = f32[2,17,8,128]{3,2,1,0:T(8,128)S(1)} collective-permute-done((f32[2,17,8,128]{3,2,1,0:T(8,128)S(1)}, f32[2,17,8,128]{3,2,1,0:T(8,128)S(1)}, u32[]{:S(2)}, u32[]{:S(2)}) %collective-permute-start.1) | collective-permute-done | bytes 139296 | tf_op jit(solution)/shard_map/ppermute | solution.py:31
  21.0 1.7 collective-permute-start.4
  25.1 6.0 %collective-permute-done.3.halo_before = f32[6,17,8,128]{3,2,1,0:T(8,128)S(1)} collective-permute-done((f32[6,17,8,128]{3,2,1,0:T(8,128)S(1)}, f32[6,17,8,128]{3,2,1,0:T(8,128)S(1)}, u32[]{:S(2)}, u32[]{:S(2)}) %collective-permute-start.3) | collective-permute-done | bytes 417824 | tf_op jit(solution)/shard_map/ppermute | solution.py:31
  32.7 25.9 %shard_map.395 = (f32[8,256]{1,0:T(8,128)}, f32[240,512]{1,0:T(8,128)}, f32[8,256]{1,0:T(8,128)}, f32[240,512]{1,0:T(8,128)}, f32[8,256]{1,0:T(8,128)}, /*index=...) custom-call(f32[6,17,8,128]{3,2,1,0:T(8,128)} %copy-done.35, ...), custom_call_target="tpu_custom_call" | custom-call | flops 30000001024 | tf_op jit(solution)/shard_map/pallas_call | solution.py:789
  59.5 4.0 %shard_map.396 = (f32[768,512]{1,0:T(8,128)}, f32[768,512]{1,0:T(8,128)}) custom-call(f32[3,240,512]{2,1,0:T(8,128)} %get-tuple-element.178.grad_rads, f32[240,128]{1,0:T(8,128)} %get-tuple-element.171.radial, f32[8,3328]{1,0:T(8,128)} %get-tuple-element.179.atom_rows, f32[32,512]{1,0:T(8,128)} %get-tuple-element.180.quad_up_grad, s32[1]{0:T(128)} %bitcast.12.core), custom_call_target="tpu_custom_call" | custom-call | flops 30000001024 | tf_op jit(solution)/shard_map/pallas_call | solution.py:789
  65.3 1.9 collective-permute-done.6.refs_3_
  67.2 1.3 copy-done.22
  68.5 5.0 %shard_map.397 = (f32[448,512]{1,0:T(8,128)}, f32[448,512]{1,0:T(8,128)}, f32[384,512]{1,0:T(8,128)}, f32[384,512]{1,0:T(8,128)}) custom-call(s32[4]{0:T(128)} %pad_add_fusion.1.me_ref, f32[896,512]{1,0:T(8,128)} %get-tuple-element.176.refs_0_, f32[896,512]{1,0:T(8,128)} %copy-done.22, f32[768,512]{1,0:T(8,128)} %get-tuple-element.181.refs_2_, ...), custom_call_target="tpu_custom_call" | custom-call | flops 30000001024 | tf_op jit(solution)/shard_map/pallas_call | solution.py:789
  73.5 1.5 collective-permute-start.7
  75.0 1.5 collective-permute-start.8
  76.5 8.7 %shard_map.398 = (f32[6,16,8,128]{3,2,1,0:T(8,128)}, f32[6,16,8,128]{3,2,1,0:T(8,128)}, f32[6,16,8,128]{3,2,1,0:T(8,128)}, f32[16,16,128]{2,1,0:T(8,128)}) custom-call(f32[30,8,8,128]{3,2,1,0:T(8,128)} %get-tuple-element.175.cosines, f32[240,2048]{1,0:T(8,128)} %get-tuple-element.188.sums, f32[240,256]{1,0:T(8,128)} %get-tuple-element.189.grad_src, ...), custom_call_target="tpu_custom_call" | custom-call | flops 30000001024 | tf_op jit(solution)/shard_map/pallas_call | solution.py:789
  85.2 1.7 collective-permute-start.9
  86.9 8.7 %collective-permute-done.8.refs_3_ = f32[384,512]{1,0:T(8,128)S(1)} collective-permute-done((f32[384,512]{1,0:T(8,128)}, f32[384,512]{1,0:T(8,128)S(1)}, u32[]{:S(2)}, u32[]{:S(2)}) %collective-permute-start.8) | collective-permute-done | bytes 786464 | tf_op jit(solution)/shard_map/ppermute | solution.py:55
  97.0 3.2 %shard_map.399 = (f32[224,512]{1,0:T(8,128)}, f32[224,512]{1,0:T(8,128)}, f32[192,512]{1,0:T(8,128)}, f32[192,512]{1,0:T(8,128)}) custom-call(s32[4]{0:T(128)} %pad_add_fusion.1.me_ref, f32[448,512]{1,0:T(8,128)} %get-tuple-element.194.refs_0_, f32[448,512]{1,0:T(8,128)} %copy-done.25, f32[384,512]{1,0:T(8,128)} %get-tuple-element.196.refs_2_, ...), custom_call_target="tpu_custom_call" | custom-call | flops 30000001024 | tf_op jit(solution)/shard_map/pallas_call | solution.py:789
  100.2 1.5 collective-permute-start.13
  101.8 1.5 collective-permute-start.14
  104.1 2.0 shard_map.400
  106.1 2.8 %collective-permute-start.11 = (f32[2,16,8,128]{3,2,1,0:T(8,128)}, f32[2,16,8,128]{3,2,1,0:T(8,128)S(1)}, u32[]{:S(2)}, u32[]{:S(2)}) collective-permute-start(f32[2,16,8,128]{3,2,1,0:T(8,128)} %get-tuple-element.205), channel_id=1, source_target_pairs={{0,24},{8,0},{16,8},{24,16},{1,25},{9,1},{17,9},{25,17},{2,26},{10... | collective-permute-start | bytes 393224 | tf_op jit(solution)/shard_map/ppermute | solution.py:31
  108.9 4.3 %collective-permute-done.11.y = f32[2,16,8,128]{3,2,1,0:T(8,128)S(1)} collective-permute-done((f32[2,16,8,128]{3,2,1,0:T(8,128)}, f32[2,16,8,128]{3,2,1,0:T(8,128)S(1)}, u32[]{:S(2)}, u32[]{:S(2)}) %collective-permute-start.11) | collective-permute-done | bytes 131104 | tf_op jit(solution)/shard_map/ppermute | solution.py:31
  113.2 2.7 %collective-permute-done.12.z = f32[2,16,8,128]{3,2,1,0:T(8,128)S(1)} collective-permute-done((f32[2,16,8,128]{3,2,1,0:T(8,128)}, f32[2,16,8,128]{3,2,1,0:T(8,128)S(1)}, u32[]{:S(2)}, u32[]{:S(2)}) %collective-permute-start.12) | collective-permute-done | bytes 131104 | tf_op jit(solution)/shard_map/ppermute | solution.py:31
  116.5 1.7 shard_map.401
  118.8 4.0 %collective-permute-done.15 = f32[16,8,128]{2,1,0:T(8,128)S(1)} collective-permute-done((f32[16,8,128]{2,1,0:T(8,128)}, f32[16,8,128]{2,1,0:T(8,128)S(1)}, u32[]{:S(2)}, u32[]{:S(2)}) %collective-permute-start.15) | collective-permute-done | bytes 65568 | tf_op jit(solution)/shard_map/ppermute | solution.py:905
  122.7 1.5 add.88.returned
  125.7 2.4 shard_map.402
  128.1 1.3 collective-permute-start.16
  129.5 6.8 %shard_map.403 = (f32[8,256]{1,0:T(8,128)}, f32[240,512]{1,0:T(8,128)}, f32[384,512]{1,0:T(8,128)}, f32[384,512]{1,0:T(8,128)}, f32[384,512]{1,0:T(8,128)}, /*index=5*/f32[384,512]{1,0:T(8,128)}) custom-call(f32[16,16,128]{2,1,0:T(8,128)} %get-tuple-element.190.back_local, f32[16,8,128]{2,1,0:T(8,128)} %add.88.returned, ...), custom_call_target="tpu_custom_call" | custom-call | flops 30000001024 | tf_op jit(solution)/shard_map/pallas_call | solution.py:789
  138.3 1.9 shard_map.404
  141.3 3.1 %shard_map.405 = (f32[192,512]{1,0:T(8,128)}, f32[192,512]{1,0:T(8,128)}, f32[192,512]{1,0:T(8,128)}, f32[192,512]{1,0:T(8,128)}) custom-call(s32[4]{0:T(128)} %pad_add_fusion.1.me_ref, f32[384,512]{1,0:T(8,128)} %get-tuple-element.234.refs_0_, f32[384,512]{1,0:T(8,128)} %copy-done, f32[384,512]{1,0:T(8,128)} %get-tuple-element.236.refs_2_, f32[384,512]{1,0:T(8,128)} %copy-done.1), custom_call_target="tpu_custom_call" | custom-call | tf_op jit(solution)/shard_map/pallas_call | solution.py:789
  144.7 3.5 %collective-permute-start.21 = (f32[192,512]{1,0:T(8,128)}, f32[192,512]{1,0:T(8,128)S(1)}, u32[]{:S(2)}, u32[]{:S(2)}) collective-permute-start(f32[192,512]{1,0:T(8,128)} %get-tuple-element.240), channel_id=1, source_target_pairs={{0,4},{4,0},{1,5},{5,1},{2,6},{6,2},{3,7},{7,3},{8,12},{12,8},{9,1... | collective-permute-start | bytes 1179656 | tf_op jit(solution)/shard_map/ppermute | solution.py:55
  148.3 4.1 %collective-permute-done.19.y = f32[104,512]{1,0:T(8,128)S(1)} collective-permute-done((f32[104,512]{1,0:T(8,128)}, f32[104,512]{1,0:T(8,128)S(1)}, u32[]{:S(2)}, u32[]{:S(2)}) %collective-permute-start.19) | collective-permute-done | bytes 213024 | tf_op jit(solution)/shard_map/ppermute | solution.py:55
  153.1 1.7 shard_map.406.refs_0_
  156.9 2.3 shard_map.407
  159.2 1.3 collective-permute-start.23
  161.6 3.7 %collective-permute-done.22.refs_1_ = f32[104,512]{1,0:T(8,128)S(1)} collective-permute-done((f32[104,512]{1,0:T(8,128)}, f32[104,512]{1,0:T(8,128)S(1)}, u32[]{:S(2)}, u32[]{:S(2)}) %collective-permute-start.22) | collective-permute-done | bytes 213024 | tf_op jit(solution)/shard_map/ppermute | solution.py:55
  165.9 1.8 shard_map.408.refs_0_
  169.1 2.0 shard_map.409
  171.1 2.0 collective-permute-start.26
  173.2 7.5 %collective-permute-done.25.refs_1_ = f32[208,512]{1,0:T(8,128)S(1)} collective-permute-done((f32[208,512]{1,0:T(8,128)}, f32[208,512]{1,0:T(8,128)S(1)}, u32[]{:S(2)}, u32[]{:S(2)}) %collective-permute-start.25) | collective-permute-done | bytes 426016 | tf_op jit(solution)/shard_map/ppermute | solution.py:55
  181.4 2.1 shard_map.410
  183.5 1.9 collective-permute-start.28
  186.6 1.7 shard_map.411
  188.7 5.8 %collective-permute-done.27.y = f32[48,512]{1,0:T(8,128)S(1)} collective-permute-done((f32[48,512]{1,0:T(8,128)}, f32[48,512]{1,0:T(8,128)S(1)}, u32[]{:S(2)}, u32[]{:S(2)}) %collective-permute-start.27) | collective-permute-done | bytes 98336 | tf_op jit(solution)/shard_map/ppermute | solution.py:55
  195.1 1.6 shard_map.412.refs_0_
  198.2 2.6 %shard_map.413 = (f32[448,512]{1,0:T(8,128)}, f32[384,512]{1,0:T(8,128)}) custom-call(s32[4]{0:T(128)} %pad_add_fusion.1.me_ref, f32[224,512]{1,0:T(8,128)} %get-tuple-element.270.refs_0_, f32[224,512]{1,0:T(8,128)} %copy-done.32, f32[192,512]{1,0:T(8,128)} %get-tuple-element.272.refs_2_, f32[192,512]{1,0:T(8,128)} %copy-done.38), custom_call_target="tpu_custom_call" | custom-call | flops 30000001024 | tf_op jit(solution)/shard_map/pallas_call | solution.py:789
  200.9 2.0 collective-permute-start.32
  203.5 1.6 shard_map.414.refs_0_
  205.1 2.5 collective-permute-start.31
  208.2 3.3 %collective-permute-done.31.refs_1_ = f32[96,512]{1,0:T(8,128)S(1)} collective-permute-done((f32[96,512]{1,0:T(8,128)}, f32[96,512]{1,0:T(8,128)S(1)}, u32[]{:S(2)}, u32[]{:S(2)}) %collective-permute-start.31) | collective-permute-done | bytes 196640 | tf_op jit(solution)/shard_map/ppermute | solution.py:55
  212.2 1.8 shard_map.415
  214.0 11.0 %collective-permute-done.33.refs_3_ = f32[384,512]{1,0:T(8,128)S(1)} collective-permute-done((f32[384,512]{1,0:T(8,128)}, f32[384,512]{1,0:T(8,128)S(1)}, u32[]{:S(2)}, u32[]{:S(2)}) %collective-permute-start.33) | collective-permute-done | bytes 786464 | tf_op jit(solution)/shard_map/ppermute | solution.py:55
  226.2 3.9 %shard_map.416 = (f32[896,512]{1,0:T(8,128)}, f32[768,512]{1,0:T(8,128)}) custom-call(s32[4]{0:T(128)} %pad_add_fusion.1.me_ref, f32[448,512]{1,0:T(8,128)} %get-tuple-element.282.refs_0_, f32[448,512]{1,0:T(8,128)} %copy-done.26, f32[384,512]{1,0:T(8,128)} %get-tuple-element.284.refs_2_, f32[384,512]{1,0:T(8,128)} %copy-done.28), custom_call_target="tpu_custom_call" | custom-call | flops 30000001024 | tf_op jit(solution)/shard_map/pallas_call | solution.py:789
  230.6 1.7 collective-permute-start.36
  232.9 4.4 %collective-permute-done.36.refs_1_ = f32[96,512]{1,0:T(8,128)S(1)} collective-permute-done((f32[96,512]{1,0:T(8,128)S(1)}, f32[96,512]{1,0:T(8,128)S(1)}, u32[]{:S(2)}, u32[]{:S(2)}) %collective-permute-start.36) | collective-permute-done | bytes 196640 | tf_op jit(solution)/shard_map/ppermute | solution.py:55
  237.4 1.5 collective-permute-done.37.refs_3_
  239.5 2.1 shard_map.418
  245.7 5.9 %shard_map.417 = (f32[2,512,512]{2,1,0:T(8,128)}, f32[2,256,512]{2,1,0:T(8,128)}, f32[64,1024]{1,0:T(8,128)}, f32[64,512]{1,0:T(8,128)}, f32[32,1024]{1,0:T(8,12...) custom-call(f32[896,512]{1,0:T(8,128)} %get-tuple-element.286.a_mine, ...), custom_call_target="tpu_custom_call" | custom-call | flops 30000001024 | tf_op jit(solution)/shard_map/pallas_call | solution.py:789
  252.8 2.6 shard_map.419
  255.9 2.0 collective-permute-done.40.c_other
  259.9 4.0 %shard_map.420 = (f32[2,512,512]{2,1,0:T(8,128)}, f32[5,128,512]{2,1,0:T(8,128)}, f32[64,512]{1,0:T(8,128)}, f32[32,512]{1,0:T(8,128)}, f32[3,256]{1,0:T(4,128)}) custom-call(f32[384,512]{1,0:T(8,128)} %get-tuple-element.299.c_mine, f32[384,512]{1,0:T(8,128)} %copy-done.29, f32[384,512]{1,0:T(8,128)} %get-tuple-element.300.d_mine, f32[384,512]{1,0:T(8,128)} %copy-done.30, ...), custom_call_target="tpu_custom_call" | custom-call | flops 30000001024 | tf_op jit(solution)/shard_map/pallas_call | solution.py:789
  (162 shorter events, 40.5 us)
Async XLA Ops:
  0.7 7.7 %copy-start.19 = (s32[240,8]{0,1:T(8,128)S(1)}, s32[240,8]{0,1:T(8,128)}, u32[]{:S(2)}) copy-start(s32[240,8]{0,1:T(8,128)} %param.33) | copy-start | bytes 23044
  0.7 7.7 %copy-start.20 = (s32[240,8]{0,1:T(8,128)S(1)}, s32[240,8]{0,1:T(8,128)}, u32[]{:S(2)}) copy-start(s32[240,8]{0,1:T(8,128)} %param.35) | copy-start | bytes 23044
  0.7 15.4 %copy-start.21 = (s32[240]{0:T(256)S(1)}, s32[240]{0:T(256)}, u32[]{:S(2)}) copy-start(s32[240]{0:T(256)} %param.32) | copy-start | bytes 2884
  5.3 18.9 %copy-start.17 = (s32[240,8]{0,1:T(8,128)S(1)}, s32[240,8]{0,1:T(8,128)}, u32[]{:S(2)}) copy-start(s32[240,8]{0,1:T(8,128)} %param.34) | copy-start | bytes 23044
  5.4 18.9 %copy-start.18 = (s32[240,8]{0,1:T(8,128)S(1)}, s32[240,8]{0,1:T(8,128)}, u32[]{:S(2)}) copy-start(s32[240,8]{0,1:T(8,128)} %param.36) | copy-start | bytes 23044
  5.4 5.5 %collective-permute-start = (f32[17,8,128]{2,1,0:T(8,128)}, f32[17,8,128]{2,1,0:T(8,128)S(1)}, u32[]{:S(2)}, u32[]{:S(2)}) collective-permute-start(f32[17,8,128]{2,1,0:T(8,128)} %get-tuple-element.166), channel_id=1, source_target_pairs={{0,1},{1,0},{2,3},{3,2},{4,5},{5,4},{6,7},{7,6},{8,9},{9,8},{10,11... | collective-permute-start | bytes 208904 | tf_op jit(solution)/shard_map/ppermute | solution.py:36
  11.8 8.4 %collective-permute-start.1 = (f32[2,17,8,128]{3,2,1,0:T(8,128)S(1)}, f32[2,17,8,128]{3,2,1,0:T(8,128)S(1)}, u32[]{:S(2)}, u32[]{:S(2)}) collective-permute-start(f32[2,17,8,128]{3,2,1,0:T(8,128)S(1)} %pad_maximum_fusion.1), channel_id=1, source_target_pairs={{0,8},{8,16},{16,24},{24,0},{1,9},{9,17},{17,25},{25,1},{2,10},{10... | collective-permute-start | bytes 417800 | tf_op jit(solution)/shard_map/ppermute | solution.py:31
  13.9 7.0 %collective-permute-start.2 = (f32[2,17,8,128]{3,2,1,0:T(8,128)S(1)}, f32[2,17,8,128]{3,2,1,0:T(8,128)S(1)}, u32[]{:S(2)}, u32[]{:S(2)}) collective-permute-start(f32[2,17,8,128]{3,2,1,0:T(8,128)S(1)} %pad_maximum_fusion.1), channel_id=1, source_target_pairs={{0,24},{8,0},{16,8},{24,16},{1,25},{9,1},{17,9},{25,17},{2,26},{10... | collective-permute-start | bytes 417800 | tf_op jit(solution)/shard_map/ppermute | solution.py:31
  21.0 11.0 %copy-start.2 = (f32[6,17,8,128]{3,2,1,0:T(8,128)}, f32[6,17,8,128]{3,2,1,0:T(8,128)S(1)}, u32[]{:S(2)}) copy-start(f32[6,17,8,128]{3,2,1,0:T(8,128)S(1)} %pad_maximum_fusion.halo_here) | copy-start | bytes 1253380
  21.0 10.1 %collective-permute-start.3 = (f32[6,17,8,128]{3,2,1,0:T(8,128)S(1)}, f32[6,17,8,128]{3,2,1,0:T(8,128)S(1)}, u32[]{:S(2)}, u32[]{:S(2)}) collective-permute-start(f32[6,17,8,128]{3,2,1,0:T(8,128)S(1)} %pad_maximum_fusion.halo_here), channel_id=1, source_target_pairs={{0,2},{2,4},{4,6},{6,0},{1,3},{3,5},{5,7},{7,1},{8,10},{10,12},{12... | collective-permute-start | bytes 1253384 | tf_op jit(solution)/shard_map/ppermute | solution.py:31
  21.0 11.0 %collective-permute-start.4 = (f32[6,17,8,128]{3,2,1,0:T(8,128)S(1)}, f32[6,17,8,128]{3,2,1,0:T(8,128)S(1)}, u32[]{:S(2)}, u32[]{:S(2)}) collective-permute-start(f32[6,17,8,128]{3,2,1,0:T(8,128)S(1)} %pad_maximum_fusion.halo_here), channel_id=1, source_target_pairs={{0,6},{2,0},{4,2},{6,4},{1,7},{3,1},{5,3},{7,5},{8,14},{10,8},{12,... | collective-permute-start | bytes 1253384 | tf_op jit(solution)/shard_map/ppermute | solution.py:31
  31.1 0.9 copy-start.35
  58.6 8.6 %collective-permute-start.5 = (f32[896,512]{1,0:T(8,128)}, f32[896,512]{1,0:T(8,128)S(1)}, u32[]{:S(2)}, u32[]{:S(2)}) collective-permute-start(f32[896,512]{1,0:T(8,128)} %get-tuple-element.177), channel_id=1, source_target_pairs={{0,2},{2,0},{1,3},{3,1},{4,6},{6,4},{5,7},{7,5},{8,10},{10,8},{9,1... | collective-permute-start | bytes 5505032 | tf_op jit(solution)/shard_map/ppermute | solution.py:55
  63.5 3.8 %collective-permute-start.6 = (f32[768,512]{1,0:T(8,128)}, f32[768,512]{1,0:T(8,128)}, u32[]{:S(2)}, u32[]{:S(2)}) collective-permute-start(f32[768,512]{1,0:T(8,128)} %get-tuple-element.182), channel_id=1, source_target_pairs={{0,2},{2,0},{1,3},{3,1},{4,6},{6,4},{5,7},{7,5},{8,10},{10,8},{9,1... | collective-permute-start | bytes 4718600 | tf_op jit(solution)/shard_map/ppermute | solution.py:55
  67.2 1.3 copy-start.22
  73.5 22.6 %collective-permute-start.7 = (f32[448,512]{1,0:T(8,128)}, f32[448,512]{1,0:T(8,128)S(1)}, u32[]{:S(2)}, u32[]{:S(2)}) collective-permute-start(f32[448,512]{1,0:T(8,128)} %get-tuple-element.183), channel_id=1, source_target_pairs={{0,1},{1,0},{2,3},{3,2},{4,5},{5,4},{6,7},{7,6},{8,9},{9,8},{10,11... | collective-permute-start | bytes 2752520 | tf_op jit(solution)/shard_map/ppermute | solution.py:55
  75.0 20.6 %collective-permute-start.8 = (f32[384,512]{1,0:T(8,128)}, f32[384,512]{1,0:T(8,128)S(1)}, u32[]{:S(2)}, u32[]{:S(2)}) collective-permute-start(f32[384,512]{1,0:T(8,128)} %get-tuple-element.185), channel_id=1, source_target_pairs={{0,4},{4,0},{1,5},{5,1},{2,6},{6,2},{3,7},{7,3},{8,12},{12,8},{9,1... | collective-permute-start | bytes 2359304 | tf_op jit(solution)/shard_map/ppermute | solution.py:55
  85.2 18.1 %collective-permute-start.10 = (f32[6,16,8,128]{3,2,1,0:T(8,128)}, f32[6,16,8,128]{3,2,1,0:T(8,128)S(1)}, u32[]{:S(2)}, u32[]{:S(2)}) collective-permute-start(f32[6,16,8,128]{3,2,1,0:T(8,128)} %get-tuple-element.193), channel_id=1, source_target_pairs={{0,2},{2,4},{4,6},{6,0},{1,3},{3,5},{5,7},{7,1},{8,10},{10,12},{12... | collective-permute-start | bytes 1179656 | tf_op jit(solution)/shard_map/ppermute | solution.py:31
  85.2 18.1 %collective-permute-start.9 = (f32[6,16,8,128]{3,2,1,0:T(8,128)}, f32[6,16,8,128]{3,2,1,0:T(8,128)S(1)}, u32[]{:S(2)}, u32[]{:S(2)}) collective-permute-start(f32[6,16,8,128]{3,2,1,0:T(8,128)} %get-tuple-element.191), channel_id=1, source_target_pairs={{0,6},{2,0},{4,2},{6,4},{1,7},{3,1},{5,3},{7,5},{8,14},{10,8},{12,... | collective-permute-start | bytes 1179656 | tf_op jit(solution)/shard_map/ppermute | solution.py:31
  95.6 0.9 copy-start.27
  96.1 0.9 copy-start.25
  100.2 24.0 %collective-permute-start.13 = (f32[224,512]{1,0:T(8,128)}, f32[224,512]{1,0:T(8,128)S(1)}, u32[]{:S(2)}, u32[]{:S(2)}) collective-permute-start(f32[224,512]{1,0:T(8,128)} %get-tuple-element.198), channel_id=1, source_target_pairs={{0,4},{4,0},{1,5},{5,1},{2,6},{6,2},{3,7},{7,3},{8,12},{12,8},{9,1... | collective-permute-start | bytes 1376264 | tf_op jit(solution)/shard_map/ppermute | solution.py:55
  101.8 22.5 %collective-permute-start.14 = (f32[192,512]{1,0:T(8,128)}, f32[192,512]{1,0:T(8,128)S(1)}, u32[]{:S(2)}, u32[]{:S(2)}) collective-permute-start(f32[192,512]{1,0:T(8,128)} %get-tuple-element.200), channel_id=1, source_target_pairs={{0,1},{1,0},{2,3},{3,2},{4,5},{5,4},{6,7},{7,6},{8,9},{9,8},{10,11... | collective-permute-start | bytes 1179656 | tf_op jit(solution)/shard_map/ppermute | solution.py:55
  106.1 7.0 %collective-permute-start.11 = (f32[2,16,8,128]{3,2,1,0:T(8,128)}, f32[2,16,8,128]{3,2,1,0:T(8,128)S(1)}, u32[]{:S(2)}, u32[]{:S(2)}) collective-permute-start(f32[2,16,8,128]{3,2,1,0:T(8,128)} %get-tuple-element.205), channel_id=1, source_target_pairs={{0,24},{8,0},{16,8},{24,16},{1,25},{9,1},{17,9},{25,17},{2,26},{10... | collective-permute-start | bytes 393224 | tf_op jit(solution)/shard_map/ppermute | solution.py:31
  108.9 7.0 %collective-permute-start.12 = (f32[2,16,8,128]{3,2,1,0:T(8,128)}, f32[2,16,8,128]{3,2,1,0:T(8,128)S(1)}, u32[]{:S(2)}, u32[]{:S(2)}) collective-permute-start(f32[2,16,8,128]{3,2,1,0:T(8,128)} %get-tuple-element.206), channel_id=1, source_target_pairs={{0,8},{8,16},{16,24},{24,0},{1,9},{9,17},{17,25},{25,1},{2,10},{10... | collective-permute-start | bytes 393224 | tf_op jit(solution)/shard_map/ppermute | solution.py:31
  113.2 2.7 %copy-start.14 = (f32[2,16,8,128]{3,2,1,0:T(8,128)}, f32[2,16,8,128]{3,2,1,0:T(8,128)S(1)}, u32[]{:S(2)}) copy-start(f32[2,16,8,128]{3,2,1,0:T(8,128)S(1)} %collective-permute-done.11.y) | copy-start | bytes 393220
  118.3 4.5 %collective-permute-start.15 = (f32[16,8,128]{2,1,0:T(8,128)}, f32[16,8,128]{2,1,0:T(8,128)S(1)}, u32[]{:S(2)}, u32[]{:S(2)}) collective-permute-start(f32[16,8,128]{2,1,0:T(8,128)} %get-tuple-element.212), channel_id=1, source_target_pairs={{0,1},{1,0},{2,3},{3,2},{4,5},{5,4},{6,7},{7,6},{8,9},{9,8},{10,11... | collective-permute-start | bytes 196616 | tf_op jit(solution)/shard_map/ppermute | solution.py:905
  128.1 9.4 %collective-permute-start.16 = (f32[208,512]{1,0:T(8,128)}, f32[208,512]{1,0:T(8,128)S(1)}, u32[]{:S(2)}, u32[]{:S(2)}) collective-permute-start(f32[208,512]{1,0:T(8,128)} %get-tuple-element.217), channel_id=1, source_target_pairs={{0,8},{8,0},{16,24},{24,16},{1,9},{9,1},{17,25},{25,17},{2,10},{10... | collective-permute-start | bytes 1277960 | tf_op jit(solution)/shard_map/ppermute | solution.py:55
  136.3 3.9 %collective-permute-start.17 = (f32[384,512]{1,0:T(8,128)}, f32[384,512]{1,0:T(8,128)S(1)}, u32[]{:S(2)}, u32[]{:S(2)}) collective-permute-start(f32[384,512]{1,0:T(8,128)} %get-tuple-element.231), channel_id=1, source_target_pairs={{0,2},{2,0},{1,3},{3,1},{4,6},{6,4},{5,7},{7,5},{8,10},{10,8},{9,1... | collective-permute-start | bytes 2359304 | tf_op jit(solution)/shard_map/ppermute | solution.py:55
  136.3 3.9 %collective-permute-start.18 = (f32[384,512]{1,0:T(8,128)}, f32[384,512]{1,0:T(8,128)S(1)}, u32[]{:S(2)}, u32[]{:S(2)}) collective-permute-start(f32[384,512]{1,0:T(8,128)} %get-tuple-element.233), channel_id=1, source_target_pairs={{0,2},{2,0},{1,3},{3,1},{4,6},{6,4},{5,7},{7,5},{8,10},{10,8},{9,1... | collective-permute-start | bytes 2359304 | tf_op jit(solution)/shard_map/ppermute | solution.py:55
  140.2 12.2 %collective-permute-start.19 = (f32[104,512]{1,0:T(8,128)}, f32[104,512]{1,0:T(8,128)S(1)}, u32[]{:S(2)}, u32[]{:S(2)}) collective-permute-start(f32[104,512]{1,0:T(8,128)} %get-tuple-element.228), channel_id=1, source_target_pairs={{0,16},{8,24},{16,0},{24,8},{1,17},{9,25},{17,1},{25,9},{2,18},{10... | collective-permute-start | bytes 638984 | tf_op jit(solution)/shard_map/ppermute | solution.py:55
  140.2 0.9 copy-start
  140.2 1.1 copy-start.1
  144.4 11.0 %collective-permute-start.20 = (f32[192,512]{1,0:T(8,128)}, f32[192,512]{1,0:T(8,128)S(1)}, u32[]{:S(2)}, u32[]{:S(2)}) collective-permute-start(f32[192,512]{1,0:T(8,128)} %get-tuple-element.238), channel_id=1, source_target_pairs={{0,1},{1,0},{2,3},{3,2},{4,5},{5,4},{6,7},{7,6},{8,9},{9,8},{10,11... | collective-permute-start | bytes 1179656 | tf_op jit(solution)/shard_map/ppermute | solution.py:55
  144.7 10.7 %collective-permute-start.21 = (f32[192,512]{1,0:T(8,128)}, f32[192,512]{1,0:T(8,128)S(1)}, u32[]{:S(2)}, u32[]{:S(2)}) collective-permute-start(f32[192,512]{1,0:T(8,128)} %get-tuple-element.240), channel_id=1, source_target_pairs={{0,4},{4,0},{1,5},{5,1},{2,6},{6,2},{3,7},{7,3},{8,12},{12,8},{9,1... | collective-permute-start | bytes 1179656 | tf_op jit(solution)/shard_map/ppermute | solution.py:55
  154.8 10.4 %collective-permute-start.22 = (f32[104,512]{1,0:T(8,128)}, f32[104,512]{1,0:T(8,128)S(1)}, u32[]{:S(2)}, u32[]{:S(2)}) collective-permute-start(f32[104,512]{1,0:T(8,128)} %shard_map.406.refs_0_), channel_id=1, source_target_pairs={{0,16},{8,24},{16,0},{24,8},{1,17},{9,25},{17,1},{25,9},{2,18},{10... | collective-permute-start | bytes 638984 | tf_op jit(solution)/shard_map/ppermute | solution.py:55
  159.2 8.6 %collective-permute-start.23 = (f32[96,512]{1,0:T(8,128)}, f32[96,512]{1,0:T(8,128)S(1)}, u32[]{:S(2)}, u32[]{:S(2)}) collective-permute-start(f32[96,512]{1,0:T(8,128)} %get-tuple-element.248), channel_id=1, source_target_pairs={{0,4},{4,0},{1,5},{5,1},{2,6},{6,2},{3,7},{7,3},{8,12},{12,8},{9,1... | collective-permute-start | bytes 589832 | tf_op jit(solution)/shard_map/ppermute | solution.py:55
  160.6 7.2 %collective-permute-start.24 = (f32[96,512]{1,0:T(8,128)}, f32[96,512]{1,0:T(8,128)S(1)}, u32[]{:S(2)}, u32[]{:S(2)}) collective-permute-start(f32[96,512]{1,0:T(8,128)} %get-tuple-element.250), channel_id=1, source_target_pairs={{0,1},{1,0},{2,3},{3,2},{4,5},{5,4},{6,7},{7,6},{8,9},{9,8},{10,11... | collective-permute-start | bytes 589832 | tf_op jit(solution)/shard_map/ppermute | solution.py:55
  167.8 12.9 %collective-permute-start.25 = (f32[208,512]{1,0:T(8,128)}, f32[208,512]{1,0:T(8,128)S(1)}, u32[]{:S(2)}, u32[]{:S(2)}) collective-permute-start(f32[208,512]{1,0:T(8,128)} %shard_map.408.refs_0_), channel_id=1, source_target_pairs={{0,8},{8,0},{16,24},{24,16},{1,9},{9,1},{17,25},{25,17},{2,10},{10... | collective-permute-start | bytes 1277960 | tf_op jit(solution)/shard_map/ppermute | solution.py:55
  171.1 14.7 %collective-permute-start.26 = (f32[96,512]{1,0:T(8,128)}, f32[96,512]{1,0:T(8,128)S(1)}, u32[]{:S(2)}, u32[]{:S(2)}) collective-permute-start(f32[96,512]{1,0:T(8,128)} %get-tuple-element.258), channel_id=1, source_target_pairs={{0,8},{8,0},{16,24},{24,16},{1,9},{9,1},{17,25},{25,17},{2,10},{10... | collective-permute-start | bytes 589832 | tf_op jit(solution)/shard_map/ppermute | solution.py:55
  183.5 13.2 %collective-permute-start.28 = (f32[224,512]{1,0:T(8,128)}, f32[224,512]{1,0:T(8,128)S(1)}, u32[]{:S(2)}, u32[]{:S(2)}) collective-permute-start(f32[224,512]{1,0:T(8,128)} %get-tuple-element.270.refs_0_), channel_id=1, source_target_pairs={{0,4},{4,0},{1,5},{5,1},{2,6},{6,2},{3,7},{7,3},{8,12},{12,8},{9,1... | collective-permute-start | bytes 1376264 | tf_op jit(solution)/shard_map/ppermute | solution.py:55
  185.4 11.3 %collective-permute-start.29 = (f32[192,512]{1,0:T(8,128)}, f32[192,512]{1,0:T(8,128)S(1)}, u32[]{:S(2)}, u32[]{:S(2)}) collective-permute-start(f32[192,512]{1,0:T(8,128)} %get-tuple-element.272.refs_2_), channel_id=1, source_target_pairs={{0,1},{1,0},{2,3},{3,2},{4,5},{5,4},{6,7},{7,6},{8,9},{9,8},{10,11... | collective-permute-start | bytes 1179656 | tf_op jit(solution)/shard_map/ppermute | solution.py:55
  188.3 6.2 %collective-permute-start.27 = (f32[48,512]{1,0:T(8,128)}, f32[48,512]{1,0:T(8,128)S(1)}, u32[]{:S(2)}, u32[]{:S(2)}) collective-permute-start(f32[48,512]{1,0:T(8,128)} %get-tuple-element.266), channel_id=1, source_target_pairs={{0,16},{8,24},{16,0},{24,8},{1,17},{9,25},{17,1},{25,9},{2,18},{10... | collective-permute-start | bytes 294920 | tf_op jit(solution)/shard_map/ppermute | solution.py:55
  196.7 6.2 %collective-permute-start.30 = (f32[48,512]{1,0:T(8,128)}, f32[48,512]{1,0:T(8,128)S(1)}, u32[]{:S(2)}, u32[]{:S(2)}) collective-permute-start(f32[48,512]{1,0:T(8,128)} %shard_map.412.refs_0_), channel_id=1, source_target_pairs={{0,16},{8,24},{16,0},{24,8},{1,17},{9,25},{17,1},{25,9},{2,18},{10... | collective-permute-start | bytes 294920 | tf_op jit(solution)/shard_map/ppermute | solution.py:55
  200.9 24.1 %collective-permute-start.32 = (f32[448,512]{1,0:T(8,128)}, f32[448,512]{1,0:T(8,128)S(1)}, u32[]{:S(2)}, u32[]{:S(2)}) collective-permute-start(f32[448,512]{1,0:T(8,128)} %get-tuple-element.282.refs_0_), channel_id=1, source_target_pairs={{0,1},{1,0},{2,3},{3,2},{4,5},{5,4},{6,7},{7,6},{8,9},{9,8},{10,11... | collective-permute-start | bytes 2752520 | tf_op jit(solution)/shard_map/ppermute | solution.py:55
  205.1 6.3 %collective-permute-start.31 = (f32[96,512]{1,0:T(8,128)}, f32[96,512]{1,0:T(8,128)S(1)}, u32[]{:S(2)}, u32[]{:S(2)}) collective-permute-start(f32[96,512]{1,0:T(8,128)} %shard_map.414.refs_0_), channel_id=1, source_target_pairs={{0,8},{8,0},{16,24},{24,16},{1,9},{9,1},{17,25},{25,17},{2,10},{10... | collective-permute-start | bytes 589832 | tf_op jit(solution)/shard_map/ppermute | solution.py:55
  207.6 17.4 %collective-permute-start.33 = (f32[384,512]{1,0:T(8,128)}, f32[384,512]{1,0:T(8,128)S(1)}, u32[]{:S(2)}, u32[]{:S(2)}) collective-permute-start(f32[384,512]{1,0:T(8,128)} %get-tuple-element.284.refs_2_), channel_id=1, source_target_pairs={{0,4},{4,0},{1,5},{5,1},{2,6},{6,2},{3,7},{7,3},{8,12},{12,8},{9,1... | collective-permute-start | bytes 2359304 | tf_op jit(solution)/shard_map/ppermute | solution.py:55
  225.0 0.9 copy-start.28
  225.0 1.2 copy-start.26
  226.2 4.4 %copy-start.10 = (f32[96,512]{1,0:T(8,128)S(1)}, f32[96,512]{1,0:T(8,128)}, u32[]{:S(2)}) copy-start(f32[96,512]{1,0:T(8,128)} %get-tuple-element.289.refs_0_) | copy-start | bytes 589828
  226.2 6.1 %copy-start.11 = (f32[96,512]{1,0:T(8,128)S(1)}, f32[96,512]{1,0:T(8,128)}, u32[]{:S(2)}) copy-start(f32[96,512]{1,0:T(8,128)} %get-tuple-element.291.refs_2_) | copy-start | bytes 589828
  230.0 13.2 %collective-permute-start.34 = (f32[896,512]{1,0:T(8,128)}, f32[896,512]{1,0:T(8,128)S(1)}, u32[]{:S(2)}, u32[]{:S(2)}) collective-permute-start(f32[896,512]{1,0:T(8,128)} %get-tuple-element.286.a_mine), channel_id=1, source_target_pairs={{0,2},{2,0},{1,3},{3,1},{4,6},{6,4},{5,7},{7,5},{8,10},{10,8},{9,1... | collective-permute-start | bytes 5505032 | tf_op jit(solution)/shard_map/ppermute | solution.py:55
  230.0 13.2 %collective-permute-start.35 = (f32[768,512]{1,0:T(8,128)}, f32[768,512]{1,0:T(8,128)S(1)}, u32[]{:S(2)}, u32[]{:S(2)}) collective-permute-start(f32[768,512]{1,0:T(8,128)} %get-tuple-element.287.b_mine), channel_id=1, source_target_pairs={{0,2},{2,0},{1,3},{3,1},{4,6},{6,4},{5,7},{7,5},{8,10},{10,8},{9,1... | collective-permute-start | bytes 4718600 | tf_op jit(solution)/shard_map/ppermute | solution.py:55
  230.6 6.8 %collective-permute-start.36 = (f32[96,512]{1,0:T(8,128)S(1)}, f32[96,512]{1,0:T(8,128)S(1)}, u32[]{:S(2)}, u32[]{:S(2)}) collective-permute-start(f32[96,512]{1,0:T(8,128)S(1)} %copy-done.10), channel_id=1, source_target_pairs={{0,4},{4,0},{1,5},{5,1},{2,6},{6,2},{3,7},{7,3},{8,12},{12,8},{9,1... | collective-permute-start | bytes 589832 | tf_op jit(solution)/shard_map/ppermute | solution.py:55
  232.3 6.5 %collective-permute-start.37 = (f32[96,512]{1,0:T(8,128)S(1)}, f32[96,512]{1,0:T(8,128)S(1)}, u32[]{:S(2)}, u32[]{:S(2)}) collective-permute-start(f32[96,512]{1,0:T(8,128)S(1)} %copy-done.11), channel_id=1, source_target_pairs={{0,1},{1,0},{2,3},{3,2},{4,5},{5,4},{6,7},{7,6},{8,9},{9,8},{10,11... | collective-permute-start | bytes 589832 | tf_op jit(solution)/shard_map/ppermute | solution.py:55
  237.4 1.5 copy-start.12
  241.6 10.1 %collective-permute-start.38 = (f32[192,512]{1,0:T(8,128)}, f32[192,512]{1,0:T(8,128)S(1)}, u32[]{:S(2)}, u32[]{:S(2)}) collective-permute-start(f32[192,512]{1,0:T(8,128)} %get-tuple-element.295.refs_0_), channel_id=1, source_target_pairs={{0,1},{1,0},{2,3},{3,2},{4,5},{5,4},{6,7},{7,6},{8,9},{9,8},{10,11... | collective-permute-start | bytes 1179656 | tf_op jit(solution)/shard_map/ppermute | solution.py:55
  242.3 9.8 %collective-permute-start.39 = (f32[192,512]{1,0:T(8,128)}, f32[192,512]{1,0:T(8,128)S(1)}, u32[]{:S(2)}, u32[]{:S(2)}) collective-permute-start(f32[192,512]{1,0:T(8,128)} %get-tuple-element.297.refs_2_), channel_id=1, source_target_pairs={{0,4},{4,0},{1,5},{5,1},{2,6},{6,2},{3,7},{7,3},{8,12},{12,8},{9,1... | collective-permute-start | bytes 1179656 | tf_op jit(solution)/shard_map/ppermute | solution.py:55
  243.2 1.2 copy-start.24
  244.4 1.2 copy-start.23
  255.4 2.5 collective-permute-start.40
  255.4 3.6 %collective-permute-start.41 = (f32[384,512]{1,0:T(8,128)}, f32[384,512]{1,0:T(8,128)S(1)}, u32[]{:S(2)}, u32[]{:S(2)}) collective-permute-start(f32[384,512]{1,0:T(8,128)} %get-tuple-element.300.d_mine), channel_id=1, source_target_pairs={{0,2},{2,0},{1,3},{3,1},{4,6},{6,4},{5,7},{7,5},{8,10},{10,8},{9,1... | collective-permute-start | bytes 2359304 | tf_op jit(solution)/shard_map/ppermute | solution.py:55
  257.9 1.1 copy-start.29
  259.0 0.9 copy-start.30
  (23 other events, 16.6 us)

commit v5 on v3

--- a/solution.py
+++ b/solution.py
@@ -79,6 +79,11 @@
         self.last = value
         return value
 
+    def zero(self):
+        first = jax.tree.leaves(self.last)[0]
+        corner = first[(slice(0, 1),) * first.ndim].reshape(())
+        return jnp.minimum(jnp.abs(corner), 0.0)
+
 
 def halved(chain, arrays, axis, bit, tight=False):
     arrays = chain.after(arrays)
@@ -98,7 +103,7 @@
     return jnp.concatenate([jnp.where(one, other, value), jnp.where(one, value, other)])
 
 
-def reduction(chain, first, second, tight=False):
+def reduction(chain, first, second, tight=False, firm=False):
     across, along = bits_of("gz"), bits_of("gyh")
     lanes = [first, second]
     for turn, plan in enumerate(((across, along), (along, across))):
@@ -129,7 +134,10 @@
             for i in range(2):
                 if turn < len(plan[i]):
                     values[i], others[i] = chain.after((values[i], others[i]))
-                    values[i] = chain.step(joined_halves(values[i], others[i], *plan[i][::-1][turn]))
+                    whole = joined_halves(values[i], others[i], *plan[i][::-1][turn])
+                    if firm and plan[0] is across:
+                        whole = whole + chain.zero()
+                    values[i] = chain.step(whole)
     others = [swap(x, "gyl", 0) for x in values]
     yield
     values, others = chain.after((values, others))
@@ -815,7 +823,7 @@
         scratch=[pltpu.VMEM((1536, 512), F32)],
         micros=4,
     )
-    late = reduction(chain, [keep_a, got_a], [keep_b, swap(send_b, "gyl", 0)], True)
+    late = reduction(chain, [keep_a, got_a], [keep_b, swap(send_b, "gyl", 0)], True, True)
     next(late)
     grad_sums = chain.after(grad_sums)
     back_before, back_here, back_after, back_local = call(

time: 238 us -> 234 us (0.983)
  starting transfers between devices: 35.2 us -> 31.4 us
    ppermute x32, starting transfers between devices: 22.4 us -> 18.5 us  [swap(): return lax.ppermute(value, axis, [(i, i ^ 1 << bit) for i in range(count)])]
  transfers between devices with their start and end apart: 42 -> 42, of which waited for: 28 -> 29; matrix products, arithmetic and copies ran while one was open for 9% -> 10% of each run, Pallas kernels for 11% -> 11%
where the time goes in v5:
time: 234 us; the launch traced here: 233 us
  waiting for transfers between devices  110 us (47%)
  Pallas kernels  60.1 us (26%)
  starting transfers between devices  31.4 us (13%)
  other arithmetic  19.8 us (8%)
  local copies, waits for them, and re-layouts  9.49 us (4%)
  between operations  2.66 us (1%)
    ppermute x32, waiting for transfers between devices, swap(): return lax.ppermute(value, axis, [(i, i ^ 1 << bit) for i in range(count)])  75.4 us
    pallas_call x7, Pallas kernels, call(): pl.pallas_call(kernel, out_shape=[jax.ShapeDtypeStruct(shape, F32) for sh...  60.1 us
    ppermute x8, waiting for transfers between devices, shifted(): return lax.ppermute(value, axis, pairs)  26.1 us
    ppermute x32, starting transfers between devices, swap(): return lax.ppermute(value, axis, [(i, i ^ 1 << bit) for i in range(count)])  18.5 us
    add x24, other arithmetic, part(): total = total + lax.dynamic_slice_in_dim(x, at, size)  13.1 us
    ppermute x8, starting transfers between devices, shifted(): return lax.ppermute(value, axis, pairs)  9.26 us
    ppermute x1, waiting for transfers between devices, per_device(): returned = mine + lax.ppermute(theirs, 'gz', [(0, 1), (1, 0)])  6.9 us
  transfers between devices with their start and end apart: 42, of which 29 were waited for; matrix products, arithmetic and copies ran while one was open for 10% of the time, Pallas kernels for 11%

profile of v5, /device:TPU:0, one launch (start us, length us, event | category | flops | bytes accessed | tf_op | source)
XLA Modules:
  0.0 233.4 jit_solution(1214399405472888177)
XLA Ops:
  0.7 4.6 %shard_map.394 = (f32[17,8,128]{2,1,0:T(8,128)}, f32[17,16,128]{2,1,0:T(8,128)}, f32[8,256]{1,0:T(8,128)}, f32[2,240,512]{2,1,0:T(8,128)}, f32[240,128]{1,0:T(8,...) custom-call(f32[240,512]{1,0:T(8,128)} %edge.5, f32[3,240]{1,0:T(4,128)} %vec.1, ...), custom_call_target="tpu_custom_call" | custom-call | flops 5750000128 | bytes 1024 | tf_op jit(solution)/shard_map/pallas_call | solution.py:725
  5.4 3.0 %collective-permute-start = (f32[17,8,128]{2,1,0:T(8,128)}, f32[17,8,128]{2,1,0:T(8,128)S(1)}, u32[]{:S(2)}, u32[]{:S(2)}) collective-permute-start(f32[17,8,128]{2,1,0:T(8,128)} %get-tuple-element.167), channel_id=1, source_target_pairs={{0,1},{1,0},{2,3},{3,2},{4,5},{5,4},{6,7},{7,6},{8,9},{9,8},{10,11... | collective-permute-start | bytes 208904 | tf_op jit(solution)/shard_map/ppermute | solution.py:36
  8.4 0.8 copy.71.slots
  9.2 1.6 collective-permute-done
  10.9 0.9 select_bitcast_fusion.1
  11.8 4.2 %collective-permute-start.2 = (f32[2,17,8,128]{3,2,1,0:T(8,128)S(1)}, f32[2,17,8,128]{3,2,1,0:T(8,128)S(1)}, u32[]{:S(2)}, u32[]{:S(2)}) collective-permute-start(f32[2,17,8,128]{3,2,1,0:T(8,128)S(1)} %pad_maximum_fusion.15), channel_id=1, source_target_pairs={{0,24},{8,0},{16,8},{24,16},{1,25},{9,1},{17,9},{25,17},{2,26},{10... | collective-permute-start | bytes 417800 | tf_op jit(solution)/shard_map/ppermute | solution.py:31
  16.0 3.3 %collective-permute-done.2 = f32[2,17,8,128]{3,2,1,0:T(8,128)S(1)} collective-permute-done((f32[2,17,8,128]{3,2,1,0:T(8,128)S(1)}, f32[2,17,8,128]{3,2,1,0:T(8,128)S(1)}, u32[]{:S(2)}, u32[]{:S(2)}) %collective-permute-start.2) | collective-permute-done | bytes 139296 | tf_op jit(solution)/shard_map/ppermute | solution.py:31
  19.2 3.6 %collective-permute-done.1 = f32[2,17,8,128]{3,2,1,0:T(8,128)S(1)} collective-permute-done((f32[2,17,8,128]{3,2,1,0:T(8,128)S(1)}, f32[2,17,8,128]{3,2,1,0:T(8,128)S(1)}, u32[]{:S(2)}, u32[]{:S(2)}) %collective-permute-start.1) | collective-permute-done | bytes 139296 | tf_op jit(solution)/shard_map/ppermute | solution.py:31
  24.3 0.8 copy.70.src_cols
  25.7 6.0 %collective-permute-done.4.halo_after = f32[6,17,8,128]{3,2,1,0:T(8,128)S(1)} collective-permute-done((f32[6,17,8,128]{3,2,1,0:T(8,128)S(1)}, f32[6,17,8,128]{3,2,1,0:T(8,128)S(1)}, u32[]{:S(2)}, u32[]{:S(2)}) %collective-permute-start.4) | collective-permute-done | bytes 417824 | tf_op jit(solution)/shard_map/ppermute | solution.py:31
  31.8 3.2 %collective-permute-done.3.halo_before = f32[6,17,8,128]{3,2,1,0:T(8,128)S(1)} collective-permute-done((f32[6,17,8,128]{3,2,1,0:T(8,128)S(1)}, f32[6,17,8,128]{3,2,1,0:T(8,128)S(1)}, u32[]{:S(2)}, u32[]{:S(2)}) %collective-permute-start.3) | collective-permute-done | bytes 417824 | tf_op jit(solution)/shard_map/ppermute | solution.py:31
  34.9 0.7 copy-done.20
  35.7 25.9 %shard_map.395 = (f32[8,256]{1,0:T(8,128)}, f32[240,512]{1,0:T(8,128)}, f32[8,256]{1,0:T(8,128)}, f32[240,512]{1,0:T(8,128)}, f32[8,256]{1,0:T(8,128)}, /*index=...) custom-call(f32[6,17,8,128]{3,2,1,0:T(8,128)} %copy-done.20, ...), custom_call_target="tpu_custom_call" | custom-call | flops 29899999232 | bytes 1024 | tf_op jit(solution)/shard_map/pallas_call | solution.py:725
  61.7 4.2 %shard_map.396 = (f32[768,512]{1,0:T(8,128)}, f32[768,512]{1,0:T(8,128)}) custom-call(f32[3,240,512]{2,1,0:T(8,128)} %get-tuple-element.179.grad_rads, f32[240,128]{1,0:T(8,128)} %get-tuple-element.172.radial, f32[8,3328]{1,0:T(8,128)} %get-tuple-element.180.atom_rows, f32[32,512]{1,0:T(8,128)} %get-tuple-element.181.quad_up_grad, s32[1]{0:T(128)} %bitcast.12.core), custom_call_target="tpu_custom_call" | custom-call | flops 4600000000 | bytes 1024 | tf_op jit(solution)/shard_map/pallas_call | solution.py:725
  66.5 0.7 concatenate.79
  67.9 0.9 fusion.3
  68.9 0.7 reshape.71.mark_rows
  69.6 1.4 dynamic-slice_add_fusion.1
  71.0 1.6 collective-permute-start.7
  72.5 1.3 dynamic-slice_add_fusion.3
  74.4 8.7 %shard_map.397 = (f32[6,16,8,128]{3,2,1,0:T(8,128)}, f32[6,16,8,128]{3,2,1,0:T(8,128)}, f32[6,16,8,128]{3,2,1,0:T(8,128)}, f32[16,16,128]{2,1,0:T(8,128)}) custom-call(f32[30,8,8,128]{3,2,1,0:T(8,128)} %get-tuple-element.176.cosines, f32[240,2048]{1,0:T(8,128)} %get-tuple-element.187.sums, f32[240,256]{1,0:T(8,128)} %get-tuple-element.188.grad_src, ...), custom_call_target="tpu_custom_call" | custom-call | flops 14949999616 | bytes 1024 | tf_op jit(solution)/shard_map/pallas_call | solution.py:725
  83.7 1.3 dynamic-slice_add_fusion.2
  85.0 1.4 dynamic-slice_add_fusion
  86.3 7.0 %collective-permute-done.7 = f32[448,512]{1,0:T(8,128)S(1)} collective-permute-done((f32[448,512]{1,0:T(8,128)S(1)}, f32[448,512]{1,0:T(8,128)S(1)}, u32[]{:S(2)}, u32[]{:S(2)}) %collective-permute-start.7) | collective-permute-done | bytes 917536 | tf_op jit(solution)/shard_map/ppermute | solution.py:55
  93.5 0.8 collective-permute-done.8
  94.4 5.2 %collective-permute-done.9 = f32[6,16,8,128]{3,2,1,0:T(8,128)S(1)} collective-permute-done((f32[6,16,8,128]{3,2,1,0:T(8,128)}, f32[6,16,8,128]{3,2,1,0:T(8,128)S(1)}, u32[]{:S(2)}, u32[]{:S(2)}) %collective-permute-start.9) | collective-permute-done | bytes 393248 | tf_op jit(solution)/shard_map/ppermute | solution.py:31
  100.9 3.4 %collective-permute-start.11 = (f32[2,16,8,128]{3,2,1,0:T(8,128)S(1)}, f32[2,16,8,128]{3,2,1,0:T(8,128)S(1)}, u32[]{:S(2)}, u32[]{:S(2)}) collective-permute-start(f32[2,16,8,128]{3,2,1,0:T(8,128)S(1)} %get-tuple-element.342), channel_id=1, source_target_pairs={{0,24},{8,0},{16,8},{24,16},{1,25},{9,1},{17,9},{25,17},{2,26},{10... | collective-permute-start | bytes 393224 | tf_op jit(solution)/shard_map/ppermute | solution.py:31
  104.3 0.9 collective-permute-start.13
  105.7 3.0 %collective-permute-done.12 = f32[2,16,8,128]{3,2,1,0:T(8,128)S(1)} collective-permute-done((f32[2,16,8,128]{3,2,1,0:T(8,128)S(1)}, f32[2,16,8,128]{3,2,1,0:T(8,128)S(1)}, u32[]{:S(2)}, u32[]{:S(2)}) %collective-permute-start.12) | collective-permute-done | bytes 131104 | tf_op jit(solution)/shard_map/ppermute | solution.py:31
  108.7 1.1 collective-permute-done.11
  110.5 6.9 %collective-permute-done.15 = f32[16,8,128]{2,1,0:T(8,128)S(1)} collective-permute-done((f32[16,8,128]{2,1,0:T(8,128)S(1)}, f32[16,8,128]{2,1,0:T(8,128)S(1)}, u32[]{:S(2)}, u32[]{:S(2)}) %collective-permute-start.15) | collective-permute-done | bytes 65568 | tf_op jit(solution)/shard_map/ppermute | solution.py:850
  118.4 6.8 %shard_map.398 = (f32[8,256]{1,0:T(8,128)}, f32[240,512]{1,0:T(8,128)}, f32[384,512]{1,0:T(8,128)}, f32[384,512]{1,0:T(8,128)}, f32[384,512]{1,0:T(8,128)}, /*index=5*/f32[384,512]{1,0:T(8,128)}) custom-call(f32[16,16,128]{2,1,0:T(8,128)} %get-tuple-element.189.back_local, f32[16,8,128]{2,1,0:T(8,128)} %bitcast_add_fusion.returned, ...), custom_call_target="tpu_custom_call" | custom-call | flops 8049999872 | bytes 1024 | tf_op jit(solution)/shard_map/pallas_call | solution.py:725
  125.2 3.7 %collective-permute-done.16 = f32[208,512]{1,0:T(8,128)S(1)} collective-permute-done((f32[208,512]{1,0:T(8,128)S(1)}, f32[208,512]{1,0:T(8,128)S(1)}, u32[]{:S(2)}, u32[]{:S(2)}) %collective-permute-start.16) | collective-permute-done | bytes 426016 | tf_op jit(solution)/shard_map/ppermute | solution.py:55
  130.3 2.0 collective-permute-done.17
  132.2 1.8 dynamic-slice_add_fusion.11
  134.6 0.8 dynamic-slice_add_fusion.10
  135.4 2.0 collective-permute-start.21
  137.4 5.6 %collective-permute-done.19 = f32[104,512]{1,0:T(8,128)} collective-permute-done((f32[104,512]{1,0:T(8,128)}, f32[104,512]{1,0:T(8,128)}, u32[]{:S(2)}, u32[]{:S(2)}) %collective-permute-start.19) | collective-permute-done | bytes 213024 | tf_op jit(solution)/shard_map/ppermute | solution.py:55
  143.0 1.0 add.314
  144.2 1.3 collective-permute-done.20
  145.5 1.0 dynamic-slice_add_fusion.21
  146.5 2.1 collective-permute-start.23
  148.6 1.0 dynamic-slice_add_fusion.20
  150.1 4.2 %collective-permute-done.22 = f32[104,512]{1,0:T(8,128)S(1)} collective-permute-done((f32[104,512]{1,0:T(8,128)S(1)}, f32[104,512]{1,0:T(8,128)S(1)}, u32[]{:S(2)}, u32[]{:S(2)}) %collective-permute-start.22) | collective-permute-done | bytes 213024 | tf_op jit(solution)/shard_map/ppermute | solution.py:55
  154.5 1.0 dynamic-slice_add_fusion.19
  155.5 1.0 dynamic-slice_add_fusion.18
  156.6 9.7 %collective-permute-done.25 = f32[208,512]{1,0:T(8,128)S(1)} collective-permute-done((f32[208,512]{1,0:T(8,128)S(1)}, f32[208,512]{1,0:T(8,128)S(1)}, u32[]{:S(2)}, u32[]{:S(2)}) %collective-permute-start.25) | collective-permute-done | bytes 426016 | tf_op jit(solution)/shard_map/ppermute | solution.py:55
  166.4 2.1 collective-permute-start.28
  168.8 5.4 %collective-permute-done.26 = f32[96,512]{1,0:T(8,128)S(1)} collective-permute-done((f32[96,512]{1,0:T(8,128)S(1)}, f32[96,512]{1,0:T(8,128)S(1)}, u32[]{:S(2)}, u32[]{:S(2)}) %collective-permute-start.26) | collective-permute-done | bytes 196640 | tf_op jit(solution)/shard_map/ppermute | solution.py:55
  175.4 6.5 %collective-permute-done.27 = f32[48,512]{1,0:T(8,128)S(1)} collective-permute-done((f32[48,512]{1,0:T(8,128)S(1)}, f32[48,512]{1,0:T(8,128)S(1)}, u32[]{:S(2)}, u32[]{:S(2)}) %collective-permute-start.27) | collective-permute-done | bytes 98336 | tf_op jit(solution)/shard_map/ppermute | solution.py:55
  182.8 3.4 %collective-permute-done.29 = f32[192,512]{1,0:T(8,128)S(1)} collective-permute-done((f32[192,512]{1,0:T(8,128)S(1)}, f32[192,512]{1,0:T(8,128)S(1)}, u32[]{:S(2)}, u32[]{:S(2)}) %collective-permute-start.29) | collective-permute-done | bytes 393248 | tf_op jit(solution)/shard_map/ppermute | solution.py:55
  186.3 1.3 collective-permute-done.30
  188.0 5.4 %collective-permute-done.31 = f32[96,512]{1,0:T(8,128)S(1)} collective-permute-done((f32[96,512]{1,0:T(8,128)S(1)}, f32[96,512]{1,0:T(8,128)S(1)}, u32[]{:S(2)}, u32[]{:S(2)}) %collective-permute-start.31) | collective-permute-done | bytes 196640 | tf_op jit(solution)/shard_map/ppermute | solution.py:55
  193.4 9.6 %collective-permute-done.32 = f32[448,512]{1,0:T(8,128)S(1)} collective-permute-done((f32[448,512]{1,0:T(8,128)S(1)}, f32[448,512]{1,0:T(8,128)S(1)}, u32[]{:S(2)}, u32[]{:S(2)}) %collective-permute-start.32) | collective-permute-done | bytes 917536 | tf_op jit(solution)/shard_map/ppermute | solution.py:55
  204.9 0.7 slice.37
  208.0 5.9 %collective-permute-done.34 = f32[96,512]{1,0:T(8,128)S(1)} collective-permute-done((f32[96,512]{1,0:T(8,128)S(1)}, f32[96,512]{1,0:T(8,128)S(1)}, u32[]{:S(2)}, u32[]{:S(2)}) %collective-permute-start.34) | collective-permute-done | bytes 196640 | tf_op jit(solution)/shard_map/ppermute | solution.py:55
  214.6 1.1 collective-permute-start.39
  215.8 1.1 copy-done.16
  216.9 1.2 copy-done.15
  218.2 5.9 %shard_map.399 = (f32[2,512,512]{2,1,0:T(8,128)}, f32[2,256,512]{2,1,0:T(8,128)}, f32[64,1024]{1,0:T(8,128)}, f32[64,512]{1,0:T(8,128)}, f32[32,1024]{1,0:T(8,12...) custom-call(f32[896,512]{1,0:T(8,128)} %copy-done.1, ...), custom_call_target="tpu_custom_call" | custom-call | flops 5750000128 | bytes 1024 | tf_op jit(solution)/shard_map/pallas_call | solution.py:725
  225.6 1.8 collective-permute-done.41.d_other
  227.4 1.1 collective-permute-done.40.c_other
  228.5 0.9 copy-done.18
  229.4 4.0 %shard_map.400 = (f32[2,512,512]{2,1,0:T(8,128)}, f32[5,128,512]{2,1,0:T(8,128)}, f32[64,512]{1,0:T(8,128)}, f32[32,512]{1,0:T(8,128)}, f32[3,256]{1,0:T(4,128)}) custom-call(f32[384,512]{1,0:T(8,128)} %copy-done.4, f32[384,512]{1,0:T(8,128)} %copy-done.18, f32[384,512]{1,0:T(8,128)} %copy-done.5, f32[384,512]{1,0:T(8,128)} %copy-done.17, ...), custom_call_target="tpu_custom_call" | custom-call | flops 3449999872 | bytes 1024 | tf_op jit(solution)/shard_map/pallas_call | solution.py:725
  (153 shorter events, 19.5 us)
Async XLA Ops:
  0.7 7.7 %copy-start.14 = (s32[240]{0:T(256)S(1)}, s32[240]{0:T(256)}, u32[]{:S(2)}) copy-start(s32[240]{0:T(256)} %param.32) | copy-start | bytes 2884
  0.7 7.7 %copy-start.10 = (s32[240,8]{0,1:T(8,128)S(1)}, s32[240,8]{0,1:T(8,128)}, u32[]{:S(2)}) copy-start(s32[240,8]{0,1:T(8,128)} %param.33) | copy-start | bytes 23044
  0.7 7.7 %copy-start.12 = (s32[240,8]{0,1:T(8,128)S(1)}, s32[240,8]{0,1:T(8,128)}, u32[]{:S(2)}) copy-start(s32[240,8]{0,1:T(8,128)} %param.35) | copy-start | bytes 23044
  0.7 22.7 %copy-start.11 = (s32[240,8]{0,1:T(8,128)S(1)}, s32[240,8]{0,1:T(8,128)}, u32[]{:S(2)}) copy-start(s32[240,8]{0,1:T(8,128)} %param.34) | copy-start | bytes 23044
  0.7 22.7 %copy-start.13 = (s32[240,8]{0,1:T(8,128)S(1)}, s32[240,8]{0,1:T(8,128)}, u32[]{:S(2)}) copy-start(s32[240,8]{0,1:T(8,128)} %param.36) | copy-start | bytes 23044
  5.4 5.5 %collective-permute-start = (f32[17,8,128]{2,1,0:T(8,128)}, f32[17,8,128]{2,1,0:T(8,128)S(1)}, u32[]{:S(2)}, u32[]{:S(2)}) collective-permute-start(f32[17,8,128]{2,1,0:T(8,128)} %get-tuple-element.167), channel_id=1, source_target_pairs={{0,1},{1,0},{2,3},{3,2},{4,5},{5,4},{6,7},{7,6},{8,9},{9,8},{10,11... | collective-permute-start | bytes 208904 | tf_op jit(solution)/shard_map/ppermute | solution.py:36
  11.8 7.5 %collective-permute-start.2 = (f32[2,17,8,128]{3,2,1,0:T(8,128)S(1)}, f32[2,17,8,128]{3,2,1,0:T(8,128)S(1)}, u32[]{:S(2)}, u32[]{:S(2)}) collective-permute-start(f32[2,17,8,128]{3,2,1,0:T(8,128)S(1)} %pad_maximum_fusion.15), channel_id=1, source_target_pairs={{0,24},{8,0},{16,8},{24,16},{1,25},{9,1},{17,9},{25,17},{2,26},{10... | collective-permute-start | bytes 417800 | tf_op jit(solution)/shard_map/ppermute | solution.py:31
  16.0 6.9 %collective-permute-start.1 = (f32[2,17,8,128]{3,2,1,0:T(8,128)S(1)}, f32[2,17,8,128]{3,2,1,0:T(8,128)S(1)}, u32[]{:S(2)}, u32[]{:S(2)}) collective-permute-start(f32[2,17,8,128]{3,2,1,0:T(8,128)S(1)} %pad_maximum_fusion.15), channel_id=1, source_target_pairs={{0,8},{8,16},{16,24},{24,0},{1,9},{9,17},{17,25},{25,1},{2,10},{10... | collective-permute-start | bytes 417800 | tf_op jit(solution)/shard_map/ppermute | solution.py:31
  22.9 12.1 %copy-start.8 = (f32[6,17,8,128]{3,2,1,0:T(8,128)}, f32[6,17,8,128]{3,2,1,0:T(8,128)S(1)}, u32[]{:S(2)}) copy-start(f32[6,17,8,128]{3,2,1,0:T(8,128)S(1)} %pad_maximum_fusion.8.halo_here) | copy-start | bytes 1253380
  22.9 8.9 %collective-permute-start.4 = (f32[6,17,8,128]{3,2,1,0:T(8,128)S(1)}, f32[6,17,8,128]{3,2,1,0:T(8,128)S(1)}, u32[]{:S(2)}, u32[]{:S(2)}) collective-permute-start(f32[6,17,8,128]{3,2,1,0:T(8,128)S(1)} %pad_maximum_fusion.8.halo_here), channel_id=1, source_target_pairs={{0,6},{2,0},{4,2},{6,4},{1,7},{3,1},{5,3},{7,5},{8,14},{10,8},{12,... | collective-permute-start | bytes 1253384 | tf_op jit(solution)/shard_map/ppermute | solution.py:31
  22.9 12.0 %collective-permute-start.3 = (f32[6,17,8,128]{3,2,1,0:T(8,128)S(1)}, f32[6,17,8,128]{3,2,1,0:T(8,128)S(1)}, u32[]{:S(2)}, u32[]{:S(2)}) collective-permute-start(f32[6,17,8,128]{3,2,1,0:T(8,128)S(1)} %pad_maximum_fusion.8.halo_here), channel_id=1, source_target_pairs={{0,2},{2,4},{4,6},{6,0},{1,3},{3,5},{5,7},{7,1},{8,10},{10,12},{12... | collective-permute-start | bytes 1253384 | tf_op jit(solution)/shard_map/ppermute | solution.py:31
  31.7 3.2 %copy-start.19 = (f32[6,17,8,128]{3,2,1,0:T(8,128)}, f32[6,17,8,128]{3,2,1,0:T(8,128)S(1)}, u32[]{:S(2)}) copy-start(f32[6,17,8,128]{3,2,1,0:T(8,128)S(1)} %collective-permute-done.4.halo_after) | copy-start | bytes 1253380
  34.9 0.8 copy-start.20
  61.6 8.0 %collective-permute-start.5 = (f32[896,512]{1,0:T(8,128)}, f32[896,512]{1,0:T(8,128)}, u32[]{:S(2)}, u32[]{:S(2)}) collective-permute-start(f32[896,512]{1,0:T(8,128)} %get-tuple-element.178), channel_id=1, source_target_pairs={{0,2},{2,0},{1,3},{3,1},{4,6},{6,4},{5,7},{7,5},{8,10},{10,8},{9,1... | collective-permute-start | bytes 5505032 | tf_op jit(solution)/shard_map/ppermute | solution.py:55
  61.7 7.9 %copy-start = (f32[896,512]{1,0:T(8,128)S(1)}, f32[896,512]{1,0:T(8,128)}, u32[]{:S(2)}) copy-start(f32[896,512]{1,0:T(8,128)} %get-tuple-element.190) | copy-start | bytes 5505028
  65.9 6.6 %collective-permute-start.6 = (f32[768,512]{1,0:T(8,128)}, f32[768,512]{1,0:T(8,128)}, u32[]{:S(2)}, u32[]{:S(2)}) collective-permute-start(f32[768,512]{1,0:T(8,128)} %get-tuple-element.183), channel_id=1, source_target_pairs={{0,2},{2,0},{1,3},{3,1},{4,6},{6,4},{5,7},{7,5},{8,10},{10,8},{9,1... | collective-permute-start | bytes 4718600 | tf_op jit(solution)/shard_map/ppermute | solution.py:55
  67.2 5.3 %copy-start.2 = (f32[768,512]{1,0:T(8,128)S(1)}, f32[768,512]{1,0:T(8,128)}, u32[]{:S(2)}) copy-start(f32[768,512]{1,0:T(8,128)} %get-tuple-element.196) | copy-start | bytes 4718596
  71.0 22.4 %collective-permute-start.7 = (f32[448,512]{1,0:T(8,128)S(1)}, f32[448,512]{1,0:T(8,128)S(1)}, u32[]{:S(2)}, u32[]{:S(2)}) collective-permute-start(f32[448,512]{1,0:T(8,128)S(1)} %dynamic-slice_add_fusion.1), channel_id=1, source_target_pairs={{0,1},{1,0},{2,3},{3,2},{4,5},{5,4},{6,7},{7,6},{8,9},{9,8},{10,11... | collective-permute-start | bytes 2752520 | tf_op jit(solution)/shard_map/ppermute | solution.py:55
  73.8 20.5 %collective-permute-start.8 = (f32[384,512]{1,0:T(8,128)S(1)}, f32[384,512]{1,0:T(8,128)S(1)}, u32[]{:S(2)}, u32[]{:S(2)}) collective-permute-start(f32[384,512]{1,0:T(8,128)S(1)} %dynamic-slice_add_fusion.3), channel_id=1, source_target_pairs={{0,4},{4,0},{1,5},{5,1},{2,6},{6,2},{3,7},{7,3},{8,12},{12,8},{9,1... | collective-permute-start | bytes 2359304 | tf_op jit(solution)/shard_map/ppermute | solution.py:55
  83.0 16.6 %collective-permute-start.9 = (f32[6,16,8,128]{3,2,1,0:T(8,128)}, f32[6,16,8,128]{3,2,1,0:T(8,128)S(1)}, u32[]{:S(2)}, u32[]{:S(2)}) collective-permute-start(f32[6,16,8,128]{3,2,1,0:T(8,128)} %get-tuple-element.202), channel_id=1, source_target_pairs={{0,6},{2,0},{4,2},{6,4},{1,7},{3,1},{5,3},{7,5},{8,14},{10,8},{12,... | collective-permute-start | bytes 1179656 | tf_op jit(solution)/shard_map/ppermute | solution.py:31
  83.7 16.6 %collective-permute-start.10 = (f32[6,16,8,128]{3,2,1,0:T(8,128)}, f32[6,16,8,128]{3,2,1,0:T(8,128)S(1)}, u32[]{:S(2)}, u32[]{:S(2)}) collective-permute-start(f32[6,16,8,128]{3,2,1,0:T(8,128)} %get-tuple-element.203), channel_id=1, source_target_pairs={{0,2},{2,4},{4,6},{6,0},{1,3},{3,5},{5,7},{7,1},{8,10},{10,12},{12... | collective-permute-start | bytes 1179656 | tf_op jit(solution)/shard_map/ppermute | solution.py:31
  93.4 6.9 %copy-start.9 = (f32[6,16,8,128]{3,2,1,0:T(8,128)S(1)}, f32[6,16,8,128]{3,2,1,0:T(8,128)}, u32[]{:S(2)}) copy-start(f32[6,16,8,128]{3,2,1,0:T(8,128)} %get-tuple-element.205) | copy-start | bytes 1179652
  100.4 8.3 %collective-permute-start.12 = (f32[2,16,8,128]{3,2,1,0:T(8,128)S(1)}, f32[2,16,8,128]{3,2,1,0:T(8,128)S(1)}, u32[]{:S(2)}, u32[]{:S(2)}) collective-permute-start(f32[2,16,8,128]{3,2,1,0:T(8,128)S(1)} %get-tuple-element.341), channel_id=1, source_target_pairs={{0,8},{8,16},{16,24},{24,0},{1,9},{9,17},{17,25},{25,1},{2,10},{10... | collective-permute-start | bytes 393224 | tf_op jit(solution)/shard_map/ppermute | solution.py:31
  100.9 9.0 %collective-permute-start.11 = (f32[2,16,8,128]{3,2,1,0:T(8,128)S(1)}, f32[2,16,8,128]{3,2,1,0:T(8,128)S(1)}, u32[]{:S(2)}, u32[]{:S(2)}) collective-permute-start(f32[2,16,8,128]{3,2,1,0:T(8,128)S(1)} %get-tuple-element.342), channel_id=1, source_target_pairs={{0,24},{8,0},{16,8},{24,16},{1,25},{9,1},{17,9},{25,17},{2,26},{10... | collective-permute-start | bytes 393224 | tf_op jit(solution)/shard_map/ppermute | solution.py:31
  104.3 13.7 %collective-permute-start.13 = (f32[224,512]{1,0:T(8,128)S(1)}, f32[224,512]{1,0:T(8,128)S(1)}, u32[]{:S(2)}, u32[]{:S(2)}) collective-permute-start(f32[224,512]{1,0:T(8,128)S(1)} %dynamic-slice_add_fusion.5), channel_id=1, source_target_pairs={{0,4},{4,0},{1,5},{5,1},{2,6},{6,2},{3,7},{7,3},{8,12},{12,8},{9,1... | collective-permute-start | bytes 1376264 | tf_op jit(solution)/shard_map/ppermute | solution.py:55
  105.2 12.9 %collective-permute-start.14 = (f32[192,512]{1,0:T(8,128)S(1)}, f32[192,512]{1,0:T(8,128)S(1)}, u32[]{:S(2)}, u32[]{:S(2)}) collective-permute-start(f32[192,512]{1,0:T(8,128)S(1)} %dynamic-slice_add_fusion.13), channel_id=1, source_target_pairs={{0,1},{1,0},{2,3},{3,2},{4,5},{5,4},{6,7},{7,6},{8,9},{9,8},{10,11... | collective-permute-start | bytes 1179656 | tf_op jit(solution)/shard_map/ppermute | solution.py:55
  109.9 7.5 %collective-permute-start.15 = (f32[16,8,128]{2,1,0:T(8,128)S(1)}, f32[16,8,128]{2,1,0:T(8,128)S(1)}, u32[]{:S(2)}, u32[]{:S(2)}) collective-permute-start(f32[16,8,128]{2,1,0:T(8,128)S(1)} %select_bitcast_fusion.2), channel_id=1, source_target_pairs={{0,1},{1,0},{2,3},{3,2},{4,5},{5,4},{6,7},{7,6},{8,9},{9,8},{10,11... | collective-permute-start | bytes 196616 | tf_op jit(solution)/shard_map/ppermute | solution.py:850
  118.2 10.7 %collective-permute-start.16 = (f32[208,512]{1,0:T(8,128)S(1)}, f32[208,512]{1,0:T(8,128)S(1)}, u32[]{:S(2)}, u32[]{:S(2)}) collective-permute-start(f32[208,512]{1,0:T(8,128)S(1)} %dynamic-slice_add_fusion.7), channel_id=1, source_target_pairs={{0,8},{8,0},{16,24},{24,16},{1,9},{9,1},{17,25},{25,17},{2,10},{10... | collective-permute-start | bytes 1277960 | tf_op jit(solution)/shard_map/ppermute | solution.py:55
  125.2 9.4 %copy-start.6 = (f32[384,512]{1,0:T(8,128)S(1)}, f32[384,512]{1,0:T(8,128)}, u32[]{:S(2)}) copy-start(f32[384,512]{1,0:T(8,128)} %get-tuple-element.246) | copy-start | bytes 2359300
  129.6 14.4 %copy-start.7 = (f32[384,512]{1,0:T(8,128)S(1)}, f32[384,512]{1,0:T(8,128)}, u32[]{:S(2)}) copy-start(f32[384,512]{1,0:T(8,128)} %get-tuple-element.242) | copy-start | bytes 2359300
  129.7 2.6 %collective-permute-start.17 = (f32[384,512]{1,0:T(8,128)}, f32[384,512]{1,0:T(8,128)S(1)}, u32[]{:S(2)}, u32[]{:S(2)}) collective-permute-start(f32[384,512]{1,0:T(8,128)} %get-tuple-element.233), channel_id=1, source_target_pairs={{0,2},{2,0},{1,3},{3,1},{4,6},{6,4},{5,7},{7,5},{8,10},{10,8},{9,1... | collective-permute-start | bytes 2359304 | tf_op jit(solution)/shard_map/ppermute | solution.py:55
  129.8 4.8 %collective-permute-start.18 = (f32[384,512]{1,0:T(8,128)}, f32[384,512]{1,0:T(8,128)S(1)}, u32[]{:S(2)}, u32[]{:S(2)}) collective-permute-start(f32[384,512]{1,0:T(8,128)} %get-tuple-element.237), channel_id=1, source_target_pairs={{0,2},{2,0},{1,3},{3,1},{4,6},{6,4},{5,7},{7,5},{8,10},{10,8},{9,1... | collective-permute-start | bytes 2359304 | tf_op jit(solution)/shard_map/ppermute | solution.py:55
  130.3 12.7 %collective-permute-start.19 = (f32[104,512]{1,0:T(8,128)}, f32[104,512]{1,0:T(8,128)}, u32[]{:S(2)}, u32[]{:S(2)}) collective-permute-start(f32[104,512]{1,0:T(8,128)} %dynamic-slice_add_fusion.15), channel_id=1, source_target_pairs={{0,16},{8,24},{16,0},{24,8},{1,17},{9,25},{17,1},{25,9},{2,18},{10... | collective-permute-start | bytes 638984 | tf_op jit(solution)/shard_map/ppermute | solution.py:55
  134.0 11.5 %collective-permute-start.20 = (f32[192,512]{1,0:T(8,128)}, f32[192,512]{1,0:T(8,128)}, u32[]{:S(2)}, u32[]{:S(2)}) collective-permute-start(f32[192,512]{1,0:T(8,128)} %dynamic-slice_add_fusion.11), channel_id=1, source_target_pairs={{0,1},{1,0},{2,3},{3,2},{4,5},{5,4},{6,7},{7,6},{8,9},{9,8},{10,11... | collective-permute-start | bytes 1179656 | tf_op jit(solution)/shard_map/ppermute | solution.py:55
  135.4 13.2 %collective-permute-start.21 = (f32[192,512]{1,0:T(8,128)}, f32[192,512]{1,0:T(8,128)}, u32[]{:S(2)}, u32[]{:S(2)}) collective-permute-start(f32[192,512]{1,0:T(8,128)} %dynamic-slice_add_fusion.10), channel_id=1, source_target_pairs={{0,4},{4,0},{1,5},{5,1},{2,6},{6,2},{3,7},{7,3},{8,12},{12,8},{9,1... | collective-permute-start | bytes 1179656 | tf_op jit(solution)/shard_map/ppermute | solution.py:55
  144.0 10.4 %collective-permute-start.22 = (f32[104,512]{1,0:T(8,128)S(1)}, f32[104,512]{1,0:T(8,128)S(1)}, u32[]{:S(2)}, u32[]{:S(2)}) collective-permute-start(f32[104,512]{1,0:T(8,128)S(1)} %add.314), channel_id=1, source_target_pairs={{0,16},{8,24},{16,0},{24,8},{1,17},{9,25},{17,1},{25,9},{2,18},{10... | collective-permute-start | bytes 638984 | tf_op jit(solution)/shard_map/ppermute | solution.py:55
  146.5 10.0 %collective-permute-start.23 = (f32[96,512]{1,0:T(8,128)S(1)}, f32[96,512]{1,0:T(8,128)S(1)}, u32[]{:S(2)}, u32[]{:S(2)}) collective-permute-start(f32[96,512]{1,0:T(8,128)S(1)} %dynamic-slice_add_fusion.21), channel_id=1, source_target_pairs={{0,4},{4,0},{1,5},{5,1},{2,6},{6,2},{3,7},{7,3},{8,12},{12,8},{9,1... | collective-permute-start | bytes 589832 | tf_op jit(solution)/shard_map/ppermute | solution.py:55
  149.5 6.9 %collective-permute-start.24 = (f32[96,512]{1,0:T(8,128)S(1)}, f32[96,512]{1,0:T(8,128)S(1)}, u32[]{:S(2)}, u32[]{:S(2)}) collective-permute-start(f32[96,512]{1,0:T(8,128)S(1)} %dynamic-slice_add_fusion.20), channel_id=1, source_target_pairs={{0,1},{1,0},{2,3},{3,2},{4,5},{5,4},{6,7},{7,6},{8,9},{9,8},{10,11... | collective-permute-start | bytes 589832 | tf_op jit(solution)/shard_map/ppermute | solution.py:55
  154.4 11.8 %collective-permute-start.25 = (f32[208,512]{1,0:T(8,128)S(1)}, f32[208,512]{1,0:T(8,128)S(1)}, u32[]{:S(2)}, u32[]{:S(2)}) collective-permute-start(f32[208,512]{1,0:T(8,128)S(1)} %pad_maximum_fusion.7), channel_id=1, source_target_pairs={{0,8},{8,0},{16,24},{24,16},{1,9},{9,1},{17,25},{25,17},{2,10},{10... | collective-permute-start | bytes 1277960 | tf_op jit(solution)/shard_map/ppermute | solution.py:55
  166.4 15.6 %collective-permute-start.28 = (f32[224,512]{1,0:T(8,128)S(1)}, f32[224,512]{1,0:T(8,128)S(1)}, u32[]{:S(2)}, u32[]{:S(2)}) collective-permute-start(f32[224,512]{1,0:T(8,128)S(1)} %fusion), channel_id=1, source_target_pairs={{0,4},{4,0},{1,5},{5,1},{2,6},{6,2},{3,7},{7,3},{8,12},{12,8},{9,1... | collective-permute-start | bytes 1376264 | tf_op jit(solution)/shard_map/ppermute | solution.py:55
  168.4 5.7 %collective-permute-start.26 = (f32[96,512]{1,0:T(8,128)S(1)}, f32[96,512]{1,0:T(8,128)S(1)}, u32[]{:S(2)}, u32[]{:S(2)}) collective-permute-start(f32[96,512]{1,0:T(8,128)S(1)} %dynamic-slice_add_fusion.17), channel_id=1, source_target_pairs={{0,8},{8,0},{16,24},{24,16},{1,9},{9,1},{17,25},{25,17},{2,10},{10... | collective-permute-start | bytes 589832 | tf_op jit(solution)/shard_map/ppermute | solution.py:55
  174.2 7.7 %collective-permute-start.27 = (f32[48,512]{1,0:T(8,128)S(1)}, f32[48,512]{1,0:T(8,128)S(1)}, u32[]{:S(2)}, u32[]{:S(2)}) collective-permute-start(f32[48,512]{1,0:T(8,128)S(1)} %dynamic-slice_add_fusion.23), channel_id=1, source_target_pairs={{0,16},{8,24},{16,0},{24,8},{1,17},{9,25},{17,1},{25,9},{2,18},{10... | collective-permute-start | bytes 294920 | tf_op jit(solution)/shard_map/ppermute | solution.py:55
  174.8 11.4 %collective-permute-start.29 = (f32[192,512]{1,0:T(8,128)S(1)}, f32[192,512]{1,0:T(8,128)S(1)}, u32[]{:S(2)}, u32[]{:S(2)}) collective-permute-start(f32[192,512]{1,0:T(8,128)S(1)} %slice.45), channel_id=1, source_target_pairs={{0,1},{1,0},{2,3},{3,2},{4,5},{5,4},{6,7},{7,6},{8,9},{9,8},{10,11... | collective-permute-start | bytes 1179656 | tf_op jit(solution)/shard_map/ppermute | solution.py:55
  181.9 5.7 %collective-permute-start.30 = (f32[48,512]{1,0:T(8,128)S(1)}, f32[48,512]{1,0:T(8,128)S(1)}, u32[]{:S(2)}, u32[]{:S(2)}) collective-permute-start(f32[48,512]{1,0:T(8,128)S(1)} %add.334), channel_id=1, source_target_pairs={{0,16},{8,24},{16,0},{24,8},{1,17},{9,25},{17,1},{25,9},{2,18},{10... | collective-permute-start | bytes 294920 | tf_op jit(solution)/shard_map/ppermute | solution.py:55
  182.2 20.9 %collective-permute-start.32 = (f32[448,512]{1,0:T(8,128)S(1)}, f32[448,512]{1,0:T(8,128)S(1)}, u32[]{:S(2)}, u32[]{:S(2)}) collective-permute-start(f32[448,512]{1,0:T(8,128)S(1)} %pad_maximum_fusion.1), channel_id=1, source_target_pairs={{0,1},{1,0},{2,3},{3,2},{4,5},{5,4},{6,7},{7,6},{8,9},{9,8},{10,11... | collective-permute-start | bytes 2752520 | tf_op jit(solution)/shard_map/ppermute | solution.py:55
  187.6 5.7 %collective-permute-start.31 = (f32[96,512]{1,0:T(8,128)S(1)}, f32[96,512]{1,0:T(8,128)S(1)}, u32[]{:S(2)}, u32[]{:S(2)}) collective-permute-start(f32[96,512]{1,0:T(8,128)S(1)} %pad_maximum_fusion.14), channel_id=1, source_target_pairs={{0,8},{8,0},{16,24},{24,16},{1,9},{9,1},{17,25},{25,17},{2,10},{10... | collective-permute-start | bytes 589832 | tf_op jit(solution)/shard_map/ppermute | solution.py:55
  187.7 17.0 %collective-permute-start.33 = (f32[384,512]{1,0:T(8,128)S(1)}, f32[384,512]{1,0:T(8,128)S(1)}, u32[]{:S(2)}, u32[]{:S(2)}) collective-permute-start(f32[384,512]{1,0:T(8,128)S(1)} %pad_maximum_fusion.4), channel_id=1, source_target_pairs={{0,4},{4,0},{1,5},{5,1},{2,6},{6,2},{3,7},{7,3},{8,12},{12,8},{9,1... | collective-permute-start | bytes 2359304 | tf_op jit(solution)/shard_map/ppermute | solution.py:55
  204.6 1.8 copy-start.1
  204.6 11.1 %collective-permute-start.36 = (f32[896,512]{1,0:T(8,128)S(1)}, f32[896,512]{1,0:T(8,128)S(1)}, u32[]{:S(2)}, u32[]{:S(2)}) collective-permute-start(f32[896,512]{1,0:T(8,128)S(1)} %maximum_add_fusion.a_mine), channel_id=1, source_target_pairs={{0,2},{2,0},{1,3},{3,1},{4,6},{6,4},{5,7},{7,5},{8,10},{10,8},{9,1... | collective-permute-start | bytes 5505032 | tf_op jit(solution)/shard_map/ppermute | solution.py:55
  206.5 9.3 %copy-start.3 = (f32[768,512]{1,0:T(8,128)}, f32[768,512]{1,0:T(8,128)S(1)}, u32[]{:S(2)}) copy-start(f32[768,512]{1,0:T(8,128)S(1)} %maximum_add_fusion.1.b_mine) | copy-start | bytes 4718596
  206.5 9.3 %collective-permute-start.37 = (f32[768,512]{1,0:T(8,128)S(1)}, f32[768,512]{1,0:T(8,128)S(1)}, u32[]{:S(2)}, u32[]{:S(2)}) collective-permute-start(f32[768,512]{1,0:T(8,128)S(1)} %maximum_add_fusion.1.b_mine), channel_id=1, source_target_pairs={{0,2},{2,0},{1,3},{3,1},{4,6},{6,4},{5,7},{7,5},{8,10},{10,8},{9,1... | collective-permute-start | bytes 4718600 | tf_op jit(solution)/shard_map/ppermute | solution.py:55
  206.8 7.0 %collective-permute-start.34 = (f32[96,512]{1,0:T(8,128)S(1)}, f32[96,512]{1,0:T(8,128)S(1)}, u32[]{:S(2)}, u32[]{:S(2)}) collective-permute-start(f32[96,512]{1,0:T(8,128)S(1)} %get-tuple-element.287), channel_id=1, source_target_pairs={{0,4},{4,0},{1,5},{5,1},{2,6},{6,2},{3,7},{7,3},{8,12},{12,8},{9,1... | collective-permute-start | bytes 589832 | tf_op jit(solution)/shard_map/ppermute | solution.py:55
  207.4 7.1 %collective-permute-start.35 = (f32[96,512]{1,0:T(8,128)S(1)}, f32[96,512]{1,0:T(8,128)S(1)}, u32[]{:S(2)}, u32[]{:S(2)}) collective-permute-start(f32[96,512]{1,0:T(8,128)S(1)} %get-tuple-element.289), channel_id=1, source_target_pairs={{0,1},{1,0},{2,3},{3,2},{4,5},{5,4},{6,7},{7,6},{8,9},{9,8},{10,11... | collective-permute-start | bytes 589832 | tf_op jit(solution)/shard_map/ppermute | solution.py:55
  214.0 10.5 %collective-permute-start.38 = (f32[192,512]{1,0:T(8,128)S(1)}, f32[192,512]{1,0:T(8,128)S(1)}, u32[]{:S(2)}, u32[]{:S(2)}) collective-permute-start(f32[192,512]{1,0:T(8,128)S(1)} %pad_maximum_fusion.12), channel_id=1, source_target_pairs={{0,1},{1,0},{2,3},{3,2},{4,5},{5,4},{6,7},{7,6},{8,9},{9,8},{10,11... | collective-permute-start | bytes 1179656 | tf_op jit(solution)/shard_map/ppermute | solution.py:55
  214.6 10.2 %collective-permute-start.39 = (f32[192,512]{1,0:T(8,128)S(1)}, f32[192,512]{1,0:T(8,128)S(1)}, u32[]{:S(2)}, u32[]{:S(2)}) collective-permute-start(f32[192,512]{1,0:T(8,128)S(1)} %pad_maximum_fusion.13), channel_id=1, source_target_pairs={{0,4},{4,0},{1,5},{5,1},{2,6},{6,2},{3,7},{7,3},{8,12},{12,8},{9,1... | collective-permute-start | bytes 1179656 | tf_op jit(solution)/shard_map/ppermute | solution.py:55
  215.8 1.2 copy-start.16
  216.9 1.2 copy-start.15
  224.6 3.9 %copy-start.4 = (f32[384,512]{1,0:T(8,128)}, f32[384,512]{1,0:T(8,128)S(1)}, u32[]{:S(2)}) copy-start(f32[384,512]{1,0:T(8,128)S(1)} %pad_maximum_fusion.5.c_mine) | copy-start | bytes 2359300
  225.0 3.5 %copy-start.5 = (f32[384,512]{1,0:T(8,128)}, f32[384,512]{1,0:T(8,128)S(1)}, u32[]{:S(2)}) copy-start(f32[384,512]{1,0:T(8,128)S(1)} %pad_maximum_fusion.6.d_mine) | copy-start | bytes 2359300
  225.0 2.4 %collective-permute-start.41 = (f32[384,512]{1,0:T(8,128)S(1)}, f32[384,512]{1,0:T(8,128)S(1)}, u32[]{:S(2)}, u32[]{:S(2)}) collective-permute-start(f32[384,512]{1,0:T(8,128)S(1)} %pad_maximum_fusion.6.d_mine), channel_id=1, source_target_pairs={{0,2},{2,0},{1,3},{3,1},{4,6},{6,4},{5,7},{7,5},{8,10},{10,8},{9,1... | collective-permute-start | bytes 2359304 | tf_op jit(solution)/shard_map/ppermute | solution.py:55
  225.1 3.4 %collective-permute-start.40 = (f32[384,512]{1,0:T(8,128)S(1)}, f32[384,512]{1,0:T(8,128)S(1)}, u32[]{:S(2)}, u32[]{:S(2)}) collective-permute-start(f32[384,512]{1,0:T(8,128)S(1)} %pad_maximum_fusion.5.c_mine), channel_id=1, source_target_pairs={{0,2},{2,0},{1,3},{3,1},{4,6},{6,4},{5,7},{7,5},{8,10},{10,8},{9,1... | collective-permute-start | bytes 2359304 | tf_op jit(solution)/shard_map/ppermute | solution.py:55
  227.4 1.1 copy-start.17
  228.5 0.9 copy-start.18

commit v6 on v5

--- a/solution.py
+++ b/solution.py
@@ -103,7 +103,7 @@
     return jnp.concatenate([jnp.where(one, other, value), jnp.where(one, value, other)])
 
 
-def reduction(chain, first, second, tight=False, firm=False):
+def reduction(chain, first, second, tight=False, firm=False, firm_total=False):
     across, along = bits_of("gz"), bits_of("gyh")
     lanes = [first, second]
     for turn, plan in enumerate(((across, along), (along, across))):
@@ -117,7 +117,8 @@
         joint = halved(chain, joint, axis, bit, tight)
         yield
     joint = chain.after(joint)
-    value = chain.step(sum(joint[1:], joint[0]))
+    value = sum(joint[1:], joint[0])
+    value = chain.step(value + chain.zero() if firm_total else value)
     for axis, bit in bits_of("gx")[::-1]:
         other = swap(value, axis, bit)
         yield
@@ -673,60 +674,94 @@
     split_cores(core, second, keep_second, send_second)
 
 
+def moved(core, pairs, held, copies, sems):
+    arriving = [pltpu.make_async_copy(pair[i % 2], held[i], sems.at[i]) for i, pair in zip(range(len(held)), [p for p in pairs for _ in range(2)])]
+    for upper in (0, 1):
+
+        @pl.when(core[0] == upper)
+        def _():
+            for i in range(len(held)):
+                pltpu.make_async_copy(pairs[i // 2][i % 2 ^ upper], held[i], sems.at[i]).start()
+
+    leaving, at = [], len(held)
+    for i, copy in enumerate(arriving):
+        copy.wait()
+        for source, target in copies[i]:
+            leaving.append(pltpu.make_async_copy(source, target, sems.at[at]))
+            leaving[-1].start()
+            at += 1
+    for x in leaving:
+        x.wait()
+
+
 def late_outputs(
     a_mine, a_other, b_mine, b_other, core,
     res, ae, trip_bil, trip_up, quad_bil, quad_up, rad, ea, ad,
+    a_low, a_high, b_low, b_high, sems,
 ):
-    upper = core[0] == 1
-
-    def rows(mine, other, at, size):
-        half = mine.shape[0]
-        where = slice(at % half, at % half + size)
-        if at < half:
-            return jnp.where(upper, other[where], mine[where])
-        return jnp.where(upper, mine[where], other[where])
-
-    a = lambda at, size: rows(a_mine, a_other, at, size)
-    b = lambda at, size: rows(b_mine, b_other, at, size)
-    for k in range(2):
-        res[k] = a(896 * k, 512)
-        ae[k] = a(896 * k + 512, 256)
-        trip_bil[:, 512 * k : 512 * k + 512] = a(768 + 64 * k, 64)
-        quad_bil[:, 512 * k : 512 * k + 512] = a(1728 + 32 * k, 32)
-    trip_up[...] = a(1664, 64)
-    quad_up[...] = b(1408, 32)
-    for k in range(3):
-        rad[k] = b(1024 + 128 * k, 128)
-    both = b(0, 512)
-    ea[0], ea[1] = both[:, :256], both[:, 256:]
-    both = b(512, 256)
-    ad[0], ad[1] = both[:, :256], both[:, 256:]
-    both = b(768, 256)
-    ad[2], ad[3] = both[:, :256], both[:, 256:]
-
-
-def early_outputs(c_mine, c_other, d_mine, d_other, late_rad, core, inputs, rad, trip_down, quad_down, tags):
-    upper = core[0] == 1
-    for k, (mine, other) in enumerate(((c_mine, c_other), (d_mine, d_other))):
-        inputs[k, 0:384] = jnp.where(upper, other[...], mine[...])
-        high = jnp.where(upper, mine[...], other[...])
-        inputs[k, 384:512] = high[:128]
-        rad[k] = high[128:256]
-        if k == 0:
-            trip_down[...] = high[256:320]
-        else:
-            quad_down[...] = high[256:288]
-            tags[...] = high[288:291, :256]
-    rad[2:5] = late_rad[...]
-
-
-def call(kernel, outs, args, scratch=(), micros=1):
+    left, right = slice(0, 256), slice(256, 512)
+    copies = [
+        [
+            (a_low.at[0:512], res.at[0]),
+            (a_low.at[512:768], ae.at[0]),
+            (a_low.at[768:832], trip_bil.at[:, 0:512]),
+            (a_low.at[832:896], trip_bil.at[:, 512:1024]),
+        ],
+        [
+            (a_high.at[0:512], res.at[1]),
+            (a_high.at[512:768], ae.at[1]),
+            (a_high.at[768:832], trip_up),
+            (a_high.at[832:864], quad_bil.at[:, 0:512]),
+            (a_high.at[864:896], quad_bil.at[:, 512:1024]),
+        ],
+        [
+            (b_low.at[0:512, left], ea.at[0]),
+            (b_low.at[0:512, right], ea.at[1]),
+            (b_low.at[512:768, left], ad.at[0]),
+            (b_low.at[512:768, right], ad.at[1]),
+        ],
+        [
+            (b_high.at[0:256, left], ad.at[2]),
+            (b_high.at[0:256, right], ad.at[3]),
+            (b_high.at[640:672], quad_up),
+        ]
+        + [(b_high.at[256 + 128 * k : 384 + 128 * k], rad.at[k]) for k in range(3)],
+    ]
+    pairs = [(a_mine, a_other), (b_mine, b_other)]
+    moved(core, pairs, (a_low, a_high, b_low, b_high), copies, sems)
+
+
+def early_outputs(
+    c_mine, c_other, d_mine, d_other, late_rad, core,
+    inputs, rad, trip_down, quad_down, tags,
+    c_low, c_high, d_low, d_high, held_rad, sems,
+):
+    other_rad = pltpu.make_async_copy(late_rad, held_rad, sems.at[16])
+    other_rad.start()
+    copies = []
+    for k, (low, high) in enumerate(((c_low, c_high), (d_low, d_high))):
+        copies.append([(low, inputs.at[k, 0:384])])
+        copies.append([(high.at[0:128], inputs.at[k, 384:512]), (high.at[128:256], rad.at[k])])
+    copies[1].append((c_high.at[256:320], trip_down))
+    copies[3].append((d_high.at[256:288], quad_down))
+    pairs = [(c_mine, c_other), (d_mine, d_other)]
+    moved(core, pairs, (c_low, c_high, d_low, d_high), copies, sems)
+    other_rad.wait()
+    last = pltpu.make_async_copy(held_rad, rad.at[2:5], sems.at[17])
+    last.start()
+    tags[...] = d_high[288:291, 0:256]
+    last.wait()
+
+
+def call(kernel, outs, args, scratch=(), micros=1, inside=None):
+    spaces = [pl.ANY if inside is not None and i not in inside else pltpu.VMEM for i in range(len(outs))]
+    space = pltpu.VMEM if inside is None else pl.ANY
     flops = int(micros * 1.15e9)
     return pl.pallas_call(
         kernel,
         out_shape=[jax.ShapeDtypeStruct(shape, F32) for shape in outs],
-        in_specs=[pl.BlockSpec(memory_space=pltpu.SMEM if x.ndim == 1 else pltpu.VMEM) for x in args],
-        out_specs=[pl.BlockSpec(memory_space=pltpu.VMEM)] * len(outs),
+        in_specs=[pl.BlockSpec(memory_space=pltpu.SMEM if x.ndim == 1 else space) for x in args],
+        out_specs=[pl.BlockSpec(memory_space=x) for x in spaces],
         scratch_shapes=list(scratch),
         compiler_params=pltpu.CompilerParams(vmem_limit_bytes=56 * 1024 * 1024),
         cost_estimate=pl.CostEstimate(flops=flops, bytes_accessed=1 << 10, transcendentals=0),
@@ -840,9 +875,9 @@
     value = chain.step(value + got[0] + got[1])
     first_plane, middle, last_plane = value[:planes], value[planes : 2 * planes], value[2 * planes :]
     got = shifted(first_plane, "gx", -1, True), shifted(last_plane, "gx", 1, True)
+    next(late)
     got, middle = chain.after((got, middle))
     value = chain.step(middle + got[0] + got[1])
-    next(late)
     if planes == 2:
         top = lax.axis_index("gz") == 1
         mine = jnp.where(top, value[1], value[0])
@@ -862,7 +897,7 @@
     next(late)
     send_c, send_d = chain.after((send_c, send_d))
     got_c, got_d = swap(send_c, "gyl", 0), swap(send_d, "gyl", 0)
-    early = reduction(chain, [keep_c, got_c], [keep_d, got_d])
+    early = reduction(chain, [keep_c, got_c], [keep_d, got_d], firm_total=True)
     running = {"L": late, "E": early}
     done = {}
 
@@ -874,7 +909,7 @@
         except StopIteration as end:
             done[name] = end.value
 
-    for name in "ELELELEELEELE":
+    for name in "ELEELELEEELEL":
         resume(name)
     while "L" not in done:
         resume("L")
@@ -884,9 +919,13 @@
         [(2, 512, 512), (2, 256, 512), (64, 1024), (64, 512), (32, 1024), (32, 512), (3, 128, 512)]
         + [(2, 512, 256), (4, 256, 256)],
         [a_mine, a_other, b_mine, b_other, core],
-        micros=5,
-    )
-    chain.step(g_rad)
+        scratch=[pltpu.VMEM((896, 512), F32)] * 2
+        + [pltpu.VMEM((768, 512), F32)] * 2
+        + [pltpu.SemaphoreType.DMA((23,))],
+        micros=0,
+        inside=(),
+    )
+    chain.step(g_quad_up)
     while "E" not in done:
         resume("E")
     (c_mine, c_other), (d_mine, d_other) = done["E"]
@@ -894,7 +933,10 @@
         early_outputs,
         [(2, 512, 512), (5, 128, 512), (64, 512), (32, 512), (3, 256)],
         [c_mine, c_other, d_mine, d_other, g_rad, core],
+        scratch=[pltpu.VMEM((384, 512), F32)] * 4
+        + [pltpu.VMEM((3, 128, 512), F32), pltpu.SemaphoreType.DMA((18,))],
         micros=3,
+        inside=(4,),
     )
     return (
         atoms_out,

time: 234 us -> 230 us (0.983)
  waiting for transfers between devices: 110 us -> 97.1 us
  starting transfers between devices: 31.4 us -> 39.6 us
    ppermute x32, starting transfers between devices: 18.5 us -> 26.7 us  [swap(): return lax.ppermute(value, axis, [(i, i ^ 1 << bit) for i in range(count)])]
    ppermute x8, waiting for transfers between devices: 26.1 us -> 21.2 us  [shifted(): return lax.ppermute(value, axis, pairs)]
    ppermute x32, waiting for transfers between devices: 75.4 us -> 71 us  [swap(): return lax.ppermute(value, axis, [(i, i ^ 1 << bit) for i in range(count)])]
    ppermute x1, waiting for transfers between devices: 6.9 us -> 3.34 us  [per_device(): returned = mine + lax.ppermute(theirs, 'gz', [(0, 1), (1, 0)])]
  transfers between devices with their start and end apart: 42 -> 42, of which waited for: 29 -> 26; matrix products, arithmetic and copies ran while one was open for 10% -> 10% of each run, Pallas kernels for 11% -> 11%
where the time goes in v6:
time: 230 us
  waiting for transfers between devices  97.1 us (42%)
  Pallas kernels  60.2 us (26%)
  starting transfers between devices  39.6 us (17%)
  other arithmetic  19.3 us (8%)
  local copies, waits for them, and re-layouts  10 us (4%)
  between operations  3.46 us (2%)
    ppermute x32, waiting for transfers between devices, swap(): return lax.ppermute(value, axis, [(i, i ^ 1 << bit) for i in range(count)])  71 us
    pallas_call x7, Pallas kernels, call(): pl.pallas_call(kernel, out_shape=[jax.ShapeDtypeStruct(shape, F32) for sh...  60.2 us
    ppermute x32, starting transfers between devices, swap(): return lax.ppermute(value, axis, [(i, i ^ 1 << bit) for i in range(count)])  26.7 us
    ppermute x8, waiting for transfers between devices, shifted(): return lax.ppermute(value, axis, pairs)  21.2 us
    add x24, other arithmetic, part(): total = total + lax.dynamic_slice_in_dim(x, at, size)  12.5 us
    ppermute x8, starting transfers between devices, shifted(): return lax.ppermute(value, axis, pairs)  9.26 us
  transfers between devices with their start and end apart: 42, of which 26 were waited for; matrix products, arithmetic and copies ran while one was open for 10% of the time, Pallas kernels for 11%

profile of v6, /device:TPU:0, one launch (start us, length us, event | category | flops | bytes accessed | tf_op | source)
XLA Modules:
  0.0 229.8 jit_solution(714510202269401072)
XLA Ops:
  0.7 4.6 %shard_map.394 = (f32[17,8,128]{2,1,0:T(8,128)}, f32[17,16,128]{2,1,0:T(8,128)}, f32[8,256]{1,0:T(8,128)}, f32[2,240,512]{2,1,0:T(8,128)}, f32[240,128]{1,0:T(8,...) custom-call(f32[240,512]{1,0:T(8,128)} %edge.5, f32[3,240]{1,0:T(4,128)} %vec.1, ...), custom_call_target="tpu_custom_call" | custom-call | flops 5750000128 | bytes 1024 | tf_op jit(solution)/shard_map/pallas_call | solution.py:760
  5.4 3.0 %collective-permute-start = (f32[17,8,128]{2,1,0:T(8,128)}, f32[17,8,128]{2,1,0:T(8,128)S(1)}, u32[]{:S(2)}, u32[]{:S(2)}) collective-permute-start(f32[17,8,128]{2,1,0:T(8,128)} %get-tuple-element.168), channel_id=1, source_target_pairs={{0,1},{1,0},{2,3},{3,2},{4,5},{5,4},{6,7},{7,6},{8,9},{9,8},{10,11... | collective-permute-start | bytes 208904 | tf_op jit(solution)/shard_map/ppermute | solution.py:36
  9.2 1.6 collective-permute-done
  10.9 0.9 select_bitcast_fusion.1
  11.8 4.2 %collective-permute-start.2 = (f32[2,17,8,128]{3,2,1,0:T(8,128)S(1)}, f32[2,17,8,128]{3,2,1,0:T(8,128)S(1)}, u32[]{:S(2)}, u32[]{:S(2)}) collective-permute-start(f32[2,17,8,128]{3,2,1,0:T(8,128)S(1)} %pad_maximum_fusion.14), channel_id=1, source_target_pairs={{0,24},{8,0},{16,8},{24,16},{1,25},{9,1},{17,9},{25,17},{2,26},{10... | collective-permute-start | bytes 417800 | tf_op jit(solution)/shard_map/ppermute | solution.py:31
  16.0 3.3 %collective-permute-done.2 = f32[2,17,8,128]{3,2,1,0:T(8,128)S(1)} collective-permute-done((f32[2,17,8,128]{3,2,1,0:T(8,128)S(1)}, f32[2,17,8,128]{3,2,1,0:T(8,128)S(1)}, u32[]{:S(2)}, u32[]{:S(2)}) %collective-permute-start.2) | collective-permute-done | bytes 139296 | tf_op jit(solution)/shard_map/ppermute | solution.py:31
  19.2 3.6 %collective-permute-done.1 = f32[2,17,8,128]{3,2,1,0:T(8,128)S(1)} collective-permute-done((f32[2,17,8,128]{3,2,1,0:T(8,128)S(1)}, f32[2,17,8,128]{3,2,1,0:T(8,128)S(1)}, u32[]{:S(2)}, u32[]{:S(2)}) %collective-permute-start.1) | collective-permute-done | bytes 139296 | tf_op jit(solution)/shard_map/ppermute | solution.py:31
  25.7 6.0 %collective-permute-done.4.halo_after = f32[6,17,8,128]{3,2,1,0:T(8,128)S(1)} collective-permute-done((f32[6,17,8,128]{3,2,1,0:T(8,128)S(1)}, f32[6,17,8,128]{3,2,1,0:T(8,128)S(1)}, u32[]{:S(2)}, u32[]{:S(2)}) %collective-permute-start.4) | collective-permute-done | bytes 417824 | tf_op jit(solution)/shard_map/ppermute | solution.py:31
  31.8 3.2 %collective-permute-done.3.halo_before = f32[6,17,8,128]{3,2,1,0:T(8,128)S(1)} collective-permute-done((f32[6,17,8,128]{3,2,1,0:T(8,128)S(1)}, f32[6,17,8,128]{3,2,1,0:T(8,128)S(1)}, u32[]{:S(2)}, u32[]{:S(2)}) %collective-permute-start.3) | collective-permute-done | bytes 417824 | tf_op jit(solution)/shard_map/ppermute | solution.py:31
  35.7 25.9 %shard_map.395 = (f32[8,256]{1,0:T(8,128)}, f32[240,512]{1,0:T(8,128)}, f32[8,256]{1,0:T(8,128)}, f32[240,512]{1,0:T(8,128)}, f32[8,256]{1,0:T(8,128)}, /*index=...) custom-call(f32[6,17,8,128]{3,2,1,0:T(8,128)} %copy-done.20, ...), custom_call_target="tpu_custom_call" | custom-call | flops 29899999232 | bytes 1024 | tf_op jit(solution)/shard_map/pallas_call | solution.py:760
  61.7 4.2 %shard_map.396 = (f32[768,512]{1,0:T(8,128)}, f32[768,512]{1,0:T(8,128)}) custom-call(f32[3,240,512]{2,1,0:T(8,128)} %get-tuple-element.180.grad_rads, f32[240,128]{1,0:T(8,128)} %get-tuple-element.173.radial, f32[8,3328]{1,0:T(8,128)} %get-tuple-element.181.atom_rows, f32[32,512]{1,0:T(8,128)} %get-tuple-element.182.quad_up_grad, s32[1]{0:T(128)} %bitcast.12.core), custom_call_target="tpu_custom_call" | custom-call | flops 4600000000 | bytes 1024 | tf_op jit(solution)/shard_map/pallas_call | solution.py:760
  67.9 0.9 fusion.3
  69.6 1.4 dynamic-slice_add_fusion.1
  71.0 1.6 collective-permute-start.7
  72.5 1.3 dynamic-slice_add_fusion.3
  74.4 8.7 %shard_map.397 = (f32[6,16,8,128]{3,2,1,0:T(8,128)}, f32[6,16,8,128]{3,2,1,0:T(8,128)}, f32[6,16,8,128]{3,2,1,0:T(8,128)}, f32[16,16,128]{2,1,0:T(8,128)}) custom-call(f32[30,8,8,128]{3,2,1,0:T(8,128)} %get-tuple-element.177.cosines, f32[240,2048]{1,0:T(8,128)} %get-tuple-element.188.sums, f32[240,256]{1,0:T(8,128)} %get-tuple-element.189.grad_src, ...), custom_call_target="tpu_custom_call" | custom-call | flops 14949999616 | bytes 1024 | tf_op jit(solution)/shard_map/pallas_call | solution.py:760
  83.7 1.3 dynamic-slice_add_fusion.2
  85.0 1.4 dynamic-slice_add_fusion
  86.3 7.0 %collective-permute-done.7 = f32[448,512]{1,0:T(8,128)S(1)} collective-permute-done((f32[448,512]{1,0:T(8,128)S(1)}, f32[448,512]{1,0:T(8,128)S(1)}, u32[]{:S(2)}, u32[]{:S(2)}) %collective-permute-start.7) | collective-permute-done | bytes 917536 | tf_op jit(solution)/shard_map/ppermute | solution.py:55
  94.4 1.3 collective-permute-start.12
  95.7 5.1 %collective-permute-done.9 = f32[6,16,8,128]{3,2,1,0:T(8,128)S(1)} collective-permute-done((f32[6,16,8,128]{3,2,1,0:T(8,128)}, f32[6,16,8,128]{3,2,1,0:T(8,128)S(1)}, u32[]{:S(2)}, u32[]{:S(2)}) %collective-permute-start.9) | collective-permute-done | bytes 393248 | tf_op jit(solution)/shard_map/ppermute | solution.py:31
  101.4 3.4 %collective-permute-start.13 = (f32[2,16,8,128]{3,2,1,0:T(8,128)S(1)}, f32[2,16,8,128]{3,2,1,0:T(8,128)S(1)}, u32[]{:S(2)}, u32[]{:S(2)}) collective-permute-start(f32[2,16,8,128]{3,2,1,0:T(8,128)S(1)} %get-tuple-element.344), channel_id=1, source_target_pairs={{0,24},{8,0},{16,8},{24,16},{1,25},{9,1},{17,9},{25,17},{2,26},{10... | collective-permute-start | bytes 393224 | tf_op jit(solution)/shard_map/ppermute | solution.py:31
  104.9 6.5 %collective-permute-done.11 = f32[224,512]{1,0:T(8,128)S(1)} collective-permute-done((f32[224,512]{1,0:T(8,128)S(1)}, f32[224,512]{1,0:T(8,128)S(1)}, u32[]{:S(2)}, u32[]{:S(2)}) %collective-permute-start.11) | collective-permute-done | bytes 458784 | tf_op jit(solution)/shard_map/ppermute | solution.py:55
  112.7 3.3 %collective-permute-done.15 = f32[16,8,128]{2,1,0:T(8,128)S(1)} collective-permute-done((f32[16,8,128]{2,1,0:T(8,128)S(1)}, f32[16,8,128]{2,1,0:T(8,128)S(1)}, u32[]{:S(2)}, u32[]{:S(2)}) %collective-permute-start.15) | collective-permute-done | bytes 65568 | tf_op jit(solution)/shard_map/ppermute | solution.py:885
  116.7 6.8 %shard_map.398 = (f32[8,256]{1,0:T(8,128)}, f32[240,512]{1,0:T(8,128)}, f32[384,512]{1,0:T(8,128)}, f32[384,512]{1,0:T(8,128)}, f32[384,512]{1,0:T(8,128)}, /*index=5*/f32[384,512]{1,0:T(8,128)}) custom-call(f32[16,16,128]{2,1,0:T(8,128)} %get-tuple-element.190.back_local, f32[16,8,128]{2,1,0:T(8,128)} %bitcast_add_fusion.returned, ...), custom_call_target="tpu_custom_call" | custom-call | flops 8049999872 | bytes 1024 | tf_op jit(solution)/shard_map/pallas_call | solution.py:760
  124.2 1.0 collective-permute-start.19
  125.2 1.3 collective-permute-done.17
  126.5 1.8 dynamic-slice_add_fusion.11
  129.1 1.8 dynamic-slice_add_fusion.10
  130.9 1.2 collective-permute-start.21
  132.1 4.6 %collective-permute-done.19 = f32[104,512]{1,0:T(8,128)S(1)} collective-permute-done((f32[104,512]{1,0:T(8,128)S(1)}, f32[104,512]{1,0:T(8,128)S(1)}, u32[]{:S(2)}, u32[]{:S(2)}) %collective-permute-start.19) | collective-permute-done | bytes 213024 | tf_op jit(solution)/shard_map/ppermute | solution.py:55
  136.9 1.1 dynamic-slice_add_fusion.8
  138.0 1.7 collective-permute-done.20
  140.2 2.0 collective-permute-done.21
  142.2 1.0 dynamic-slice_add_fusion.20
  143.2 1.8 collective-permute-start.23
  145.0 1.0 dynamic-slice_add_fusion.18
  146.2 2.7 %collective-permute-done.23 = f32[96,512]{1,0:T(8,128)S(1)} collective-permute-done((f32[96,512]{1,0:T(8,128)S(1)}, f32[96,512]{1,0:T(8,128)S(1)}, u32[]{:S(2)}, u32[]{:S(2)}) %collective-permute-start.23) | collective-permute-done | bytes 196640 | tf_op jit(solution)/shard_map/ppermute | solution.py:55
  149.3 1.9 collective-permute-start.26
  151.3 6.7 %collective-permute-done.25 = f32[96,512]{1,0:T(8,128)S(1)} collective-permute-done((f32[96,512]{1,0:T(8,128)S(1)}, f32[96,512]{1,0:T(8,128)S(1)}, u32[]{:S(2)}, u32[]{:S(2)}) %collective-permute-start.25) | collective-permute-done | bytes 196640 | tf_op jit(solution)/shard_map/ppermute | solution.py:55
  158.0 1.0 collective-permute-start.29
  159.1 6.1 %collective-permute-done.26 = f32[208,512]{1,0:T(8,128)S(1)} collective-permute-done((f32[208,512]{1,0:T(8,128)S(1)}, f32[208,512]{1,0:T(8,128)S(1)}, u32[]{:S(2)}, u32[]{:S(2)}) %collective-permute-start.26) | collective-permute-done | bytes 426016 | tf_op jit(solution)/shard_map/ppermute | solution.py:55
  166.5 1.2 collective-permute-start.30
  167.7 1.1 collective-permute-start.27
  168.8 3.5 %collective-permute-done.30 = f32[48,512]{1,0:T(8,128)S(1)} collective-permute-done((f32[48,512]{1,0:T(8,128)S(1)}, f32[48,512]{1,0:T(8,128)S(1)}, u32[]{:S(2)}, u32[]{:S(2)}) %collective-permute-start.30) | collective-permute-done | bytes 98336 | tf_op jit(solution)/shard_map/ppermute | solution.py:55
  172.4 2.3 collective-permute-start.31
  174.6 1.0 collective-permute-start.28
  175.6 2.7 %collective-permute-done.31 = f32[96,512]{1,0:T(8,128)S(1)} collective-permute-done((f32[96,512]{1,0:T(8,128)S(1)}, f32[96,512]{1,0:T(8,128)S(1)}, u32[]{:S(2)}, u32[]{:S(2)}) %collective-permute-start.31) | collective-permute-done | bytes 196640 | tf_op jit(solution)/shard_map/ppermute | solution.py:55
  178.3 1.5 collective-permute-start.33
  180.5 1.0 collective-permute-start.34
  181.5 5.3 %collective-permute-done.28 = f32[192,512]{1,0:T(8,128)S(1)} collective-permute-done((f32[192,512]{1,0:T(8,128)S(1)}, f32[192,512]{1,0:T(8,128)S(1)}, u32[]{:S(2)}, u32[]{:S(2)}) %collective-permute-start.28) | collective-permute-done | bytes 393248 | tf_op jit(solution)/shard_map/ppermute | solution.py:55
  186.9 0.9 collective-permute-start.35
  187.9 3.1 %collective-permute-done.33 = f32[96,512]{1,0:T(8,128)S(1)} collective-permute-done((f32[96,512]{1,0:T(8,128)S(1)}, f32[96,512]{1,0:T(8,128)S(1)}, u32[]{:S(2)}, u32[]{:S(2)}) %collective-permute-start.33) | collective-permute-done | bytes 196640 | tf_op jit(solution)/shard_map/ppermute | solution.py:55
  191.0 12.7 %collective-permute-done.34 = f32[448,512]{1,0:T(8,128)S(1)} collective-permute-done((f32[448,512]{1,0:T(8,128)S(1)}, f32[448,512]{1,0:T(8,128)S(1)}, u32[]{:S(2)}, u32[]{:S(2)}) %collective-permute-start.34) | collective-permute-done | bytes 917536 | tf_op jit(solution)/shard_map/ppermute | solution.py:55
  207.5 1.4 collective-permute-start.38
  209.7 1.7 collective-permute-done.37.b_other
  211.5 1.2 copy-done.5
  212.6 1.2 copy-done.3
  213.8 5.5 %shard_map.399 = (f32[2,512,512]{2,1,0:T(8,128)}, f32[2,256,512]{2,1,0:T(8,128)}, f32[64,1024]{1,0:T(8,128)}, f32[64,512]{1,0:T(8,128)}, f32[32,1024]{1,0:T(8,12...) custom-call(f32[896,512]{1,0:T(8,128)} %copy-done, ...), custom_call_target="tpu_custom_call" | custom-call | bytes 1024 | tf_op jit(solution)/shard_map/pallas_call | solution.py:760
  219.4 1.1 broadcast_select_fusion.9
  221.3 1.8 collective-permute-done.41.d_other
  223.0 1.1 collective-permute-done.40.c_other
  224.2 0.9 copy-done.18
  225.0 4.5 %shard_map.400 = (f32[2,512,512]{2,1,0:T(8,128)}, f32[5,128,512]{2,1,0:T(8,128)}, f32[64,512]{1,0:T(8,128)}, f32[32,512]{1,0:T(8,128)}, f32[3,256]{1,0:T(4,128)}) custom-call(f32[384,512]{1,0:T(8,128)} %copy-done.6, f32[384,512]{1,0:T(8,128)} %copy-done.18, f32[384,512]{1,0:T(8,128)} %copy-done.7, f32[384,512]{1,0:T(8,128)} %copy-done.17, ...), custom_call_target="tpu_custom_call" | custom-call | flops 3449999872 | bytes 1024 | tf_op jit(solution)/shard_map/pallas_call | solution.py:760
  (154 shorter events, 20.7 us)
Async XLA Ops:
  0.7 7.7 %copy-start.16 = (s32[240]{0:T(256)S(1)}, s32[240]{0:T(256)}, u32[]{:S(2)}) copy-start(s32[240]{0:T(256)} %param.32) | copy-start | bytes 2884
  0.7 7.7 %copy-start.12 = (s32[240,8]{0,1:T(8,128)S(1)}, s32[240,8]{0,1:T(8,128)}, u32[]{:S(2)}) copy-start(s32[240,8]{0,1:T(8,128)} %param.33) | copy-start | bytes 23044
  0.7 7.7 %copy-start.14 = (s32[240,8]{0,1:T(8,128)S(1)}, s32[240,8]{0,1:T(8,128)}, u32[]{:S(2)}) copy-start(s32[240,8]{0,1:T(8,128)} %param.35) | copy-start | bytes 23044
  0.7 22.7 %copy-start.13 = (s32[240,8]{0,1:T(8,128)S(1)}, s32[240,8]{0,1:T(8,128)}, u32[]{:S(2)}) copy-start(s32[240,8]{0,1:T(8,128)} %param.34) | copy-start | bytes 23044
  0.7 22.7 %copy-start.15 = (s32[240,8]{0,1:T(8,128)S(1)}, s32[240,8]{0,1:T(8,128)}, u32[]{:S(2)}) copy-start(s32[240,8]{0,1:T(8,128)} %param.36) | copy-start | bytes 23044
  5.4 5.5 %collective-permute-start = (f32[17,8,128]{2,1,0:T(8,128)}, f32[17,8,128]{2,1,0:T(8,128)S(1)}, u32[]{:S(2)}, u32[]{:S(2)}) collective-permute-start(f32[17,8,128]{2,1,0:T(8,128)} %get-tuple-element.168), channel_id=1, source_target_pairs={{0,1},{1,0},{2,3},{3,2},{4,5},{5,4},{6,7},{7,6},{8,9},{9,8},{10,11... | collective-permute-start | bytes 208904 | tf_op jit(solution)/shard_map/ppermute | solution.py:36
  11.8 7.5 %collective-permute-start.2 = (f32[2,17,8,128]{3,2,1,0:T(8,128)S(1)}, f32[2,17,8,128]{3,2,1,0:T(8,128)S(1)}, u32[]{:S(2)}, u32[]{:S(2)}) collective-permute-start(f32[2,17,8,128]{3,2,1,0:T(8,128)S(1)} %pad_maximum_fusion.14), channel_id=1, source_target_pairs={{0,24},{8,0},{16,8},{24,16},{1,25},{9,1},{17,9},{25,17},{2,26},{10... | collective-permute-start | bytes 417800 | tf_op jit(solution)/shard_map/ppermute | solution.py:31
  16.0 6.9 %collective-permute-start.1 = (f32[2,17,8,128]{3,2,1,0:T(8,128)S(1)}, f32[2,17,8,128]{3,2,1,0:T(8,128)S(1)}, u32[]{:S(2)}, u32[]{:S(2)}) collective-permute-start(f32[2,17,8,128]{3,2,1,0:T(8,128)S(1)} %pad_maximum_fusion.14), channel_id=1, source_target_pairs={{0,8},{8,16},{16,24},{24,0},{1,9},{9,17},{17,25},{25,1},{2,10},{10... | collective-permute-start | bytes 417800 | tf_op jit(solution)/shard_map/ppermute | solution.py:31
  22.9 12.1 %copy-start.10 = (f32[6,17,8,128]{3,2,1,0:T(8,128)}, f32[6,17,8,128]{3,2,1,0:T(8,128)S(1)}, u32[]{:S(2)}) copy-start(f32[6,17,8,128]{3,2,1,0:T(8,128)S(1)} %pad_maximum_fusion.8.halo_here) | copy-start | bytes 1253380
  22.9 8.9 %collective-permute-start.4 = (f32[6,17,8,128]{3,2,1,0:T(8,128)S(1)}, f32[6,17,8,128]{3,2,1,0:T(8,128)S(1)}, u32[]{:S(2)}, u32[]{:S(2)}) collective-permute-start(f32[6,17,8,128]{3,2,1,0:T(8,128)S(1)} %pad_maximum_fusion.8.halo_here), channel_id=1, source_target_pairs={{0,6},{2,0},{4,2},{6,4},{1,7},{3,1},{5,3},{7,5},{8,14},{10,8},{12,... | collective-permute-start | bytes 1253384 | tf_op jit(solution)/shard_map/ppermute | solution.py:31
  22.9 12.0 %collective-permute-start.3 = (f32[6,17,8,128]{3,2,1,0:T(8,128)S(1)}, f32[6,17,8,128]{3,2,1,0:T(8,128)S(1)}, u32[]{:S(2)}, u32[]{:S(2)}) collective-permute-start(f32[6,17,8,128]{3,2,1,0:T(8,128)S(1)} %pad_maximum_fusion.8.halo_here), channel_id=1, source_target_pairs={{0,2},{2,4},{4,6},{6,0},{1,3},{3,5},{5,7},{7,1},{8,10},{10,12},{12... | collective-permute-start | bytes 1253384 | tf_op jit(solution)/shard_map/ppermute | solution.py:31
  31.7 3.2 %copy-start.19 = (f32[6,17,8,128]{3,2,1,0:T(8,128)}, f32[6,17,8,128]{3,2,1,0:T(8,128)S(1)}, u32[]{:S(2)}) copy-start(f32[6,17,8,128]{3,2,1,0:T(8,128)S(1)} %collective-permute-done.4.halo_after) | copy-start | bytes 1253380
  34.9 0.8 copy-start.20
  61.6 8.0 %collective-permute-start.5 = (f32[896,512]{1,0:T(8,128)}, f32[896,512]{1,0:T(8,128)}, u32[]{:S(2)}, u32[]{:S(2)}) collective-permute-start(f32[896,512]{1,0:T(8,128)} %get-tuple-element.179), channel_id=1, source_target_pairs={{0,2},{2,0},{1,3},{3,1},{4,6},{6,4},{5,7},{7,5},{8,10},{10,8},{9,1... | collective-permute-start | bytes 5505032 | tf_op jit(solution)/shard_map/ppermute | solution.py:55
  61.7 7.9 %copy-start.2 = (f32[896,512]{1,0:T(8,128)S(1)}, f32[896,512]{1,0:T(8,128)}, u32[]{:S(2)}) copy-start(f32[896,512]{1,0:T(8,128)} %get-tuple-element.191) | copy-start | bytes 5505028
  65.9 6.6 %collective-permute-start.6 = (f32[768,512]{1,0:T(8,128)}, f32[768,512]{1,0:T(8,128)}, u32[]{:S(2)}, u32[]{:S(2)}) collective-permute-start(f32[768,512]{1,0:T(8,128)} %get-tuple-element.184), channel_id=1, source_target_pairs={{0,2},{2,0},{1,3},{3,1},{4,6},{6,4},{5,7},{7,5},{8,10},{10,8},{9,1... | collective-permute-start | bytes 4718600 | tf_op jit(solution)/shard_map/ppermute | solution.py:55
  67.2 5.3 %copy-start.4 = (f32[768,512]{1,0:T(8,128)S(1)}, f32[768,512]{1,0:T(8,128)}, u32[]{:S(2)}) copy-start(f32[768,512]{1,0:T(8,128)} %get-tuple-element.197) | copy-start | bytes 4718596
  71.0 22.4 %collective-permute-start.7 = (f32[448,512]{1,0:T(8,128)S(1)}, f32[448,512]{1,0:T(8,128)S(1)}, u32[]{:S(2)}, u32[]{:S(2)}) collective-permute-start(f32[448,512]{1,0:T(8,128)S(1)} %dynamic-slice_add_fusion.1), channel_id=1, source_target_pairs={{0,1},{1,0},{2,3},{3,2},{4,5},{5,4},{6,7},{7,6},{8,9},{9,8},{10,11... | collective-permute-start | bytes 2752520 | tf_op jit(solution)/shard_map/ppermute | solution.py:55
  73.8 20.5 %collective-permute-start.8 = (f32[384,512]{1,0:T(8,128)S(1)}, f32[384,512]{1,0:T(8,128)S(1)}, u32[]{:S(2)}, u32[]{:S(2)}) collective-permute-start(f32[384,512]{1,0:T(8,128)S(1)} %dynamic-slice_add_fusion.3), channel_id=1, source_target_pairs={{0,4},{4,0},{1,5},{5,1},{2,6},{6,2},{3,7},{7,3},{8,12},{12,8},{9,1... | collective-permute-start | bytes 2359304 | tf_op jit(solution)/shard_map/ppermute | solution.py:55
  83.0 17.8 %collective-permute-start.9 = (f32[6,16,8,128]{3,2,1,0:T(8,128)}, f32[6,16,8,128]{3,2,1,0:T(8,128)S(1)}, u32[]{:S(2)}, u32[]{:S(2)}) collective-permute-start(f32[6,16,8,128]{3,2,1,0:T(8,128)} %get-tuple-element.203), channel_id=1, source_target_pairs={{0,6},{2,0},{4,2},{6,4},{1,7},{3,1},{5,3},{7,5},{8,14},{10,8},{12,... | collective-permute-start | bytes 1179656 | tf_op jit(solution)/shard_map/ppermute | solution.py:31
  83.7 17.2 %collective-permute-start.10 = (f32[6,16,8,128]{3,2,1,0:T(8,128)}, f32[6,16,8,128]{3,2,1,0:T(8,128)S(1)}, u32[]{:S(2)}, u32[]{:S(2)}) collective-permute-start(f32[6,16,8,128]{3,2,1,0:T(8,128)} %get-tuple-element.204), channel_id=1, source_target_pairs={{0,2},{2,4},{4,6},{6,0},{1,3},{3,5},{5,7},{7,1},{8,10},{10,12},{12... | collective-permute-start | bytes 1179656 | tf_op jit(solution)/shard_map/ppermute | solution.py:31
  93.4 7.4 %copy-start.11 = (f32[6,16,8,128]{3,2,1,0:T(8,128)S(1)}, f32[6,16,8,128]{3,2,1,0:T(8,128)}, u32[]{:S(2)}) copy-start(f32[6,16,8,128]{3,2,1,0:T(8,128)} %get-tuple-element.206) | copy-start | bytes 1179652
  93.4 17.9 %collective-permute-start.11 = (f32[224,512]{1,0:T(8,128)S(1)}, f32[224,512]{1,0:T(8,128)S(1)}, u32[]{:S(2)}, u32[]{:S(2)}) collective-permute-start(f32[224,512]{1,0:T(8,128)S(1)} %dynamic-slice_add_fusion.5), channel_id=1, source_target_pairs={{0,4},{4,0},{1,5},{5,1},{2,6},{6,2},{3,7},{7,3},{8,12},{12,8},{9,1... | collective-permute-start | bytes 1376264 | tf_op jit(solution)/shard_map/ppermute | solution.py:55
  94.4 10.5 %collective-permute-start.12 = (f32[192,512]{1,0:T(8,128)S(1)}, f32[192,512]{1,0:T(8,128)S(1)}, u32[]{:S(2)}, u32[]{:S(2)}) collective-permute-start(f32[192,512]{1,0:T(8,128)S(1)} %dynamic-slice_add_fusion.13), channel_id=1, source_target_pairs={{0,1},{1,0},{2,3},{3,2},{4,5},{5,4},{6,7},{7,6},{8,9},{9,8},{10,11... | collective-permute-start | bytes 1179656 | tf_op jit(solution)/shard_map/ppermute | solution.py:55
  101.0 10.7 %collective-permute-start.14 = (f32[2,16,8,128]{3,2,1,0:T(8,128)S(1)}, f32[2,16,8,128]{3,2,1,0:T(8,128)S(1)}, u32[]{:S(2)}, u32[]{:S(2)}) collective-permute-start(f32[2,16,8,128]{3,2,1,0:T(8,128)S(1)} %get-tuple-element.343), channel_id=1, source_target_pairs={{0,8},{8,16},{16,24},{24,0},{1,9},{9,17},{17,25},{25,1},{2,10},{10... | collective-permute-start | bytes 393224 | tf_op jit(solution)/shard_map/ppermute | solution.py:31
  101.4 10.2 %collective-permute-start.13 = (f32[2,16,8,128]{3,2,1,0:T(8,128)S(1)}, f32[2,16,8,128]{3,2,1,0:T(8,128)S(1)}, u32[]{:S(2)}, u32[]{:S(2)}) collective-permute-start(f32[2,16,8,128]{3,2,1,0:T(8,128)S(1)} %get-tuple-element.344), channel_id=1, source_target_pairs={{0,24},{8,0},{16,8},{24,16},{1,25},{9,1},{17,9},{25,17},{2,26},{10... | collective-permute-start | bytes 393224 | tf_op jit(solution)/shard_map/ppermute | solution.py:31
  111.7 4.3 %collective-permute-start.15 = (f32[16,8,128]{2,1,0:T(8,128)S(1)}, f32[16,8,128]{2,1,0:T(8,128)S(1)}, u32[]{:S(2)}, u32[]{:S(2)}) collective-permute-start(f32[16,8,128]{2,1,0:T(8,128)S(1)} %select_bitcast_fusion.2), channel_id=1, source_target_pairs={{0,1},{1,0},{2,3},{3,2},{4,5},{5,4},{6,7},{7,6},{8,9},{9,8},{10,11... | collective-permute-start | bytes 196616 | tf_op jit(solution)/shard_map/ppermute | solution.py:885
  112.3 11.2 %collective-permute-start.16 = (f32[208,512]{1,0:T(8,128)S(1)}, f32[208,512]{1,0:T(8,128)S(1)}, u32[]{:S(2)}, u32[]{:S(2)}) collective-permute-start(f32[208,512]{1,0:T(8,128)S(1)} %dynamic-slice_add_fusion.7), channel_id=1, source_target_pairs={{0,8},{8,0},{16,24},{24,16},{1,9},{9,1},{17,25},{25,17},{2,10},{10... | collective-permute-start | bytes 1277960 | tf_op jit(solution)/shard_map/ppermute | solution.py:55
  123.5 5.6 %copy-start.8 = (f32[384,512]{1,0:T(8,128)S(1)}, f32[384,512]{1,0:T(8,128)}, u32[]{:S(2)}) copy-start(f32[384,512]{1,0:T(8,128)} %get-tuple-element.247) | copy-start | bytes 2359300
  123.6 13.3 %copy-start.9 = (f32[384,512]{1,0:T(8,128)S(1)}, f32[384,512]{1,0:T(8,128)}, u32[]{:S(2)}) copy-start(f32[384,512]{1,0:T(8,128)} %get-tuple-element.243) | copy-start | bytes 2359300
  123.6 2.9 %collective-permute-start.17 = (f32[384,512]{1,0:T(8,128)}, f32[384,512]{1,0:T(8,128)S(1)}, u32[]{:S(2)}, u32[]{:S(2)}) collective-permute-start(f32[384,512]{1,0:T(8,128)} %get-tuple-element.234), channel_id=1, source_target_pairs={{0,2},{2,0},{1,3},{3,1},{4,6},{6,4},{5,7},{7,5},{8,10},{10,8},{9,1... | collective-permute-start | bytes 2359304 | tf_op jit(solution)/shard_map/ppermute | solution.py:55
  123.7 5.4 %collective-permute-start.18 = (f32[384,512]{1,0:T(8,128)}, f32[384,512]{1,0:T(8,128)}, u32[]{:S(2)}, u32[]{:S(2)}) collective-permute-start(f32[384,512]{1,0:T(8,128)} %get-tuple-element.238), channel_id=1, source_target_pairs={{0,2},{2,0},{1,3},{3,1},{4,6},{6,4},{5,7},{7,5},{8,10},{10,8},{9,1... | collective-permute-start | bytes 2359304 | tf_op jit(solution)/shard_map/ppermute | solution.py:55
  124.2 12.5 %collective-permute-start.19 = (f32[104,512]{1,0:T(8,128)S(1)}, f32[104,512]{1,0:T(8,128)S(1)}, u32[]{:S(2)}, u32[]{:S(2)}) collective-permute-start(f32[104,512]{1,0:T(8,128)S(1)} %dynamic-slice_add_fusion.15), channel_id=1, source_target_pairs={{0,16},{8,24},{16,0},{24,8},{1,17},{9,25},{17,1},{25,9},{2,18},{10... | collective-permute-start | bytes 638984 | tf_op jit(solution)/shard_map/ppermute | solution.py:55
  128.3 11.4 %collective-permute-start.20 = (f32[192,512]{1,0:T(8,128)}, f32[192,512]{1,0:T(8,128)S(1)}, u32[]{:S(2)}, u32[]{:S(2)}) collective-permute-start(f32[192,512]{1,0:T(8,128)} %dynamic-slice_add_fusion.11), channel_id=1, source_target_pairs={{0,1},{1,0},{2,3},{3,2},{4,5},{5,4},{6,7},{7,6},{8,9},{9,8},{10,11... | collective-permute-start | bytes 1179656 | tf_op jit(solution)/shard_map/ppermute | solution.py:55
  130.9 11.3 %collective-permute-start.21 = (f32[192,512]{1,0:T(8,128)}, f32[192,512]{1,0:T(8,128)}, u32[]{:S(2)}, u32[]{:S(2)}) collective-permute-start(f32[192,512]{1,0:T(8,128)} %dynamic-slice_add_fusion.10), channel_id=1, source_target_pairs={{0,4},{4,0},{1,5},{5,1},{2,6},{6,2},{3,7},{7,3},{8,12},{12,8},{9,1... | collective-permute-start | bytes 1179656 | tf_op jit(solution)/shard_map/ppermute | solution.py:55
  136.8 12.5 %collective-permute-start.24 = (f32[104,512]{1,0:T(8,128)S(1)}, f32[104,512]{1,0:T(8,128)S(1)}, u32[]{:S(2)}, u32[]{:S(2)}) collective-permute-start(f32[104,512]{1,0:T(8,128)S(1)} %add.320), channel_id=1, source_target_pairs={{0,16},{8,24},{16,0},{24,8},{1,17},{9,25},{17,1},{25,9},{2,18},{10... | collective-permute-start | bytes 638984 | tf_op jit(solution)/shard_map/ppermute | solution.py:55
  139.7 6.5 %collective-permute-start.22 = (f32[96,512]{1,0:T(8,128)S(1)}, f32[96,512]{1,0:T(8,128)S(1)}, u32[]{:S(2)}, u32[]{:S(2)}) collective-permute-start(f32[96,512]{1,0:T(8,128)S(1)} %dynamic-slice_add_fusion.21), channel_id=1, source_target_pairs={{0,4},{4,0},{1,5},{5,1},{2,6},{6,2},{3,7},{7,3},{8,12},{12,8},{9,1... | collective-permute-start | bytes 589832 | tf_op jit(solution)/shard_map/ppermute | solution.py:55
  143.2 5.7 %collective-permute-start.23 = (f32[96,512]{1,0:T(8,128)S(1)}, f32[96,512]{1,0:T(8,128)S(1)}, u32[]{:S(2)}, u32[]{:S(2)}) collective-permute-start(f32[96,512]{1,0:T(8,128)S(1)} %dynamic-slice_add_fusion.20), channel_id=1, source_target_pairs={{0,1},{1,0},{2,3},{3,2},{4,5},{5,4},{6,7},{7,6},{8,9},{9,8},{10,11... | collective-permute-start | bytes 589832 | tf_op jit(solution)/shard_map/ppermute | solution.py:55
  149.0 9.0 %collective-permute-start.25 = (f32[96,512]{1,0:T(8,128)S(1)}, f32[96,512]{1,0:T(8,128)S(1)}, u32[]{:S(2)}, u32[]{:S(2)}) collective-permute-start(f32[96,512]{1,0:T(8,128)S(1)} %dynamic-slice_add_fusion.17), channel_id=1, source_target_pairs={{0,8},{8,0},{16,24},{24,16},{1,9},{9,1},{17,25},{25,17},{2,10},{10... | collective-permute-start | bytes 589832 | tf_op jit(solution)/shard_map/ppermute | solution.py:55
  149.3 15.8 %collective-permute-start.26 = (f32[208,512]{1,0:T(8,128)S(1)}, f32[208,512]{1,0:T(8,128)S(1)}, u32[]{:S(2)}, u32[]{:S(2)}) collective-permute-start(f32[208,512]{1,0:T(8,128)S(1)} %pad_maximum_fusion.7), channel_id=1, source_target_pairs={{0,8},{8,0},{16,24},{24,16},{1,9},{9,1},{17,25},{25,17},{2,10},{10... | collective-permute-start | bytes 1277960 | tf_op jit(solution)/shard_map/ppermute | solution.py:55
  158.0 7.3 %collective-permute-start.29 = (f32[48,512]{1,0:T(8,128)S(1)}, f32[48,512]{1,0:T(8,128)S(1)}, u32[]{:S(2)}, u32[]{:S(2)}) collective-permute-start(f32[48,512]{1,0:T(8,128)S(1)} %dynamic-slice_add_fusion.23), channel_id=1, source_target_pairs={{0,16},{8,24},{16,0},{24,8},{1,17},{9,25},{17,1},{25,9},{2,18},{10... | collective-permute-start | bytes 294920 | tf_op jit(solution)/shard_map/ppermute | solution.py:55
  166.5 5.8 %collective-permute-start.30 = (f32[48,512]{1,0:T(8,128)S(1)}, f32[48,512]{1,0:T(8,128)S(1)}, u32[]{:S(2)}, u32[]{:S(2)}) collective-permute-start(f32[48,512]{1,0:T(8,128)S(1)} %add_add_fusion.2), channel_id=1, source_target_pairs={{0,16},{8,24},{16,0},{24,8},{1,17},{9,25},{17,1},{25,9},{2,18},{10... | collective-permute-start | bytes 294920 | tf_op jit(solution)/shard_map/ppermute | solution.py:55
  167.7 12.6 %collective-permute-start.27 = (f32[224,512]{1,0:T(8,128)S(1)}, f32[224,512]{1,0:T(8,128)S(1)}, u32[]{:S(2)}, u32[]{:S(2)}) collective-permute-start(f32[224,512]{1,0:T(8,128)S(1)} %fusion), channel_id=1, source_target_pairs={{0,4},{4,0},{1,5},{5,1},{2,6},{6,2},{3,7},{7,3},{8,12},{12,8},{9,1... | collective-permute-start | bytes 1376264 | tf_op jit(solution)/shard_map/ppermute | solution.py:55
  172.4 5.9 %collective-permute-start.31 = (f32[96,512]{1,0:T(8,128)S(1)}, f32[96,512]{1,0:T(8,128)S(1)}, u32[]{:S(2)}, u32[]{:S(2)}) collective-permute-start(f32[96,512]{1,0:T(8,128)S(1)} %pad_maximum_fusion.13), channel_id=1, source_target_pairs={{0,8},{8,0},{16,24},{24,16},{1,9},{9,1},{17,25},{25,17},{2,10},{10... | collective-permute-start | bytes 589832 | tf_op jit(solution)/shard_map/ppermute | solution.py:55
  174.6 12.1 %collective-permute-start.28 = (f32[192,512]{1,0:T(8,128)S(1)}, f32[192,512]{1,0:T(8,128)S(1)}, u32[]{:S(2)}, u32[]{:S(2)}) collective-permute-start(f32[192,512]{1,0:T(8,128)S(1)} %slice.49), channel_id=1, source_target_pairs={{0,1},{1,0},{2,3},{3,2},{4,5},{5,4},{6,7},{7,6},{8,9},{9,8},{10,11... | collective-permute-start | bytes 1179656 | tf_op jit(solution)/shard_map/ppermute | solution.py:55
  178.3 12.7 %collective-permute-start.33 = (f32[96,512]{1,0:T(8,128)S(1)}, f32[96,512]{1,0:T(8,128)S(1)}, u32[]{:S(2)}, u32[]{:S(2)}) collective-permute-start(f32[96,512]{1,0:T(8,128)S(1)} %get-tuple-element.285), channel_id=1, source_target_pairs={{0,1},{1,0},{2,3},{3,2},{4,5},{5,4},{6,7},{7,6},{8,9},{9,8},{10,11... | collective-permute-start | bytes 589832 | tf_op jit(solution)/shard_map/ppermute | solution.py:55
  179.8 8.1 %collective-permute-start.32 = (f32[96,512]{1,0:T(8,128)S(1)}, f32[96,512]{1,0:T(8,128)S(1)}, u32[]{:S(2)}, u32[]{:S(2)}) collective-permute-start(f32[96,512]{1,0:T(8,128)S(1)} %get-tuple-element.283), channel_id=1, source_target_pairs={{0,4},{4,0},{1,5},{5,1},{2,6},{6,2},{3,7},{7,3},{8,12},{12,8},{9,1... | collective-permute-start | bytes 589832 | tf_op jit(solution)/shard_map/ppermute | solution.py:55
  180.5 23.3 %collective-permute-start.34 = (f32[448,512]{1,0:T(8,128)S(1)}, f32[448,512]{1,0:T(8,128)S(1)}, u32[]{:S(2)}, u32[]{:S(2)}) collective-permute-start(f32[448,512]{1,0:T(8,128)S(1)} %pad_maximum_fusion.1), channel_id=1, source_target_pairs={{0,1},{1,0},{2,3},{3,2},{4,5},{5,4},{6,7},{7,6},{8,9},{9,8},{10,11... | collective-permute-start | bytes 2752520 | tf_op jit(solution)/shard_map/ppermute | solution.py:55
  186.9 18.5 %collective-permute-start.35 = (f32[384,512]{1,0:T(8,128)S(1)}, f32[384,512]{1,0:T(8,128)S(1)}, u32[]{:S(2)}, u32[]{:S(2)}) collective-permute-start(f32[384,512]{1,0:T(8,128)S(1)} %pad_maximum_fusion.4), channel_id=1, source_target_pairs={{0,4},{4,0},{1,5},{5,1},{2,6},{6,2},{3,7},{7,3},{8,12},{12,8},{9,1... | collective-permute-start | bytes 2359304 | tf_op jit(solution)/shard_map/ppermute | solution.py:55
  205.3 1.8 copy-start
  205.3 6.1 %collective-permute-start.36 = (f32[896,512]{1,0:T(8,128)S(1)}, f32[896,512]{1,0:T(8,128)S(1)}, u32[]{:S(2)}, u32[]{:S(2)}) collective-permute-start(f32[896,512]{1,0:T(8,128)S(1)} %maximum_add_fusion.a_mine), channel_id=1, source_target_pairs={{0,2},{2,0},{1,3},{3,1},{4,6},{6,4},{5,7},{7,5},{8,10},{10,8},{9,1... | collective-permute-start | bytes 5505032 | tf_op jit(solution)/shard_map/ppermute | solution.py:55
  207.2 4.3 %copy-start.1 = (f32[768,512]{1,0:T(8,128)}, f32[768,512]{1,0:T(8,128)S(1)}, u32[]{:S(2)}) copy-start(f32[768,512]{1,0:T(8,128)S(1)} %maximum_add_fusion.1.b_mine) | copy-start | bytes 4718596
  207.2 4.2 %collective-permute-start.37 = (f32[768,512]{1,0:T(8,128)S(1)}, f32[768,512]{1,0:T(8,128)S(1)}, u32[]{:S(2)}, u32[]{:S(2)}) collective-permute-start(f32[768,512]{1,0:T(8,128)S(1)} %maximum_add_fusion.1.b_mine), channel_id=1, source_target_pairs={{0,2},{2,0},{1,3},{3,1},{4,6},{6,4},{5,7},{7,5},{8,10},{10,8},{9,1... | collective-permute-start | bytes 4718600 | tf_op jit(solution)/shard_map/ppermute | solution.py:55
  207.5 11.8 %collective-permute-start.38 = (f32[192,512]{1,0:T(8,128)S(1)}, f32[192,512]{1,0:T(8,128)}, u32[]{:S(2)}, u32[]{:S(2)}) collective-permute-start(f32[192,512]{1,0:T(8,128)S(1)} %pad_maximum_fusion.11), channel_id=1, source_target_pairs={{0,1},{1,0},{2,3},{3,2},{4,5},{5,4},{6,7},{7,6},{8,9},{9,8},{10,11... | collective-permute-start | bytes 1179656 | tf_op jit(solution)/shard_map/ppermute | solution.py:55
  208.9 11.6 %collective-permute-start.39 = (f32[192,512]{1,0:T(8,128)S(1)}, f32[192,512]{1,0:T(8,128)S(1)}, u32[]{:S(2)}, u32[]{:S(2)}) collective-permute-start(f32[192,512]{1,0:T(8,128)S(1)} %pad_maximum_fusion.12), channel_id=1, source_target_pairs={{0,4},{4,0},{1,5},{5,1},{2,6},{6,2},{3,7},{7,3},{8,12},{12,8},{9,1... | collective-permute-start | bytes 1179656 | tf_op jit(solution)/shard_map/ppermute | solution.py:55
  211.4 1.2 copy-start.5
  212.6 1.2 copy-start.3
  220.5 3.7 %copy-start.6 = (f32[384,512]{1,0:T(8,128)}, f32[384,512]{1,0:T(8,128)S(1)}, u32[]{:S(2)}) copy-start(f32[384,512]{1,0:T(8,128)S(1)} %pad_maximum_fusion.5.c_mine) | copy-start | bytes 2359300
  220.7 3.5 %copy-start.7 = (f32[384,512]{1,0:T(8,128)}, f32[384,512]{1,0:T(8,128)S(1)}, u32[]{:S(2)}) copy-start(f32[384,512]{1,0:T(8,128)S(1)} %pad_maximum_fusion.6.d_mine) | copy-start | bytes 2359300
  220.7 2.4 %collective-permute-start.41 = (f32[384,512]{1,0:T(8,128)S(1)}, f32[384,512]{1,0:T(8,128)S(1)}, u32[]{:S(2)}, u32[]{:S(2)}) collective-permute-start(f32[384,512]{1,0:T(8,128)S(1)} %pad_maximum_fusion.6.d_mine), channel_id=1, source_target_pairs={{0,2},{2,0},{1,3},{3,1},{4,6},{6,4},{5,7},{7,5},{8,10},{10,8},{9,1... | collective-permute-start | bytes 2359304 | tf_op jit(solution)/shard_map/ppermute | solution.py:55
  220.9 3.3 %collective-permute-start.40 = (f32[384,512]{1,0:T(8,128)S(1)}, f32[384,512]{1,0:T(8,128)S(1)}, u32[]{:S(2)}, u32[]{:S(2)}) collective-permute-start(f32[384,512]{1,0:T(8,128)S(1)} %pad_maximum_fusion.5.c_mine), channel_id=1, source_target_pairs={{0,2},{2,0},{1,3},{3,1},{4,6},{6,4},{5,7},{7,5},{8,10},{10,8},{9,1... | collective-permute-start | bytes 2359304 | tf_op jit(solution)/shard_map/ppermute | solution.py:55
  223.0 1.1 copy-start.17
  224.2 0.9 copy-start.18

commit v7 on v6

--- a/solution.py
+++ b/solution.py
@@ -753,7 +753,7 @@
     last.wait()
 
 
-def call(kernel, outs, args, scratch=(), micros=1, inside=None):
+def call(kernel, outs, args, scratch=(), micros=1, inside=None, room=63):
     spaces = [pl.ANY if inside is not None and i not in inside else pltpu.VMEM for i in range(len(outs))]
     space = pltpu.VMEM if inside is None else pl.ANY
     flops = int(micros * 1.15e9)
@@ -763,7 +763,7 @@
         in_specs=[pl.BlockSpec(memory_space=pltpu.SMEM if x.ndim == 1 else space) for x in args],
         out_specs=[pl.BlockSpec(memory_space=x) for x in spaces],
         scratch_shapes=list(scratch),
-        compiler_params=pltpu.CompilerParams(vmem_limit_bytes=56 * 1024 * 1024),
+        compiler_params=pltpu.CompilerParams(vmem_limit_bytes=room * 1024 * 1024),
         cost_estimate=pl.CostEstimate(flops=flops, bytes_accessed=1 << 10, transcendentals=0),
     )(*args)
 
@@ -823,7 +823,7 @@
         + [(EDGES, 128)] * 2,
         [edge_states, edge_vectors, edge_mask[None, :], hidden_atoms, tag_row, send_row, tag_table,
          w_inputs, w_radial, trip_down_t, quad_down_t],
-        micros=5,
+        micros=5, room=22,
     )
     core = bit_value("gyl", 0)[None]
     before, here, after = with_halo(payload)
@@ -847,7 +847,7 @@
             pltpu.VMEM((EDGES, 128), F32),
             pltpu.VMEM((1792, 512), F32),
         ],
-        micros=26,
+        micros=26, room=44,
     )
     chain = Chain()
     got_a = swap(send_a, "gyl", 0)
@@ -856,7 +856,7 @@
         [(768, 512)] * 2,
         [grad_rads, radial, atom_rows, quad_up_grad, core],
         scratch=[pltpu.VMEM((1536, 512), F32)],
-        micros=4,
+        micros=4, room=18,
     )
     late = reduction(chain, [keep_a, got_a], [keep_b, swap(send_b, "gyl", 0)], True, True)
     next(late)
@@ -866,7 +866,7 @@
         [(group, 16, 8, 128)] * 3 + [(16, 16, 128)],
         [cosines, grad_sums, grad_src, src, mark_rows],
         scratch=[pltpu.VMEM((32, EDGES, 256), BF)],
-        micros=13,
+        micros=13, room=18,
     )
     got = shifted(back_before, GY, -1, True), shifted(back_after, GY, 1, True)
     chain.step(back_local)
@@ -892,7 +892,7 @@
         [back_local, returned, grad_edges, grad_tag, edge_states, radial, columns, pre, downs, rads,
          tag_row, send_row, w_inputs, trip_down_t, quad_down_t, core],
         scratch=[pltpu.VMEM((768, 512), F32)] * 2,
-        micros=7,
+        micros=7, room=28,
     )
     next(late)
     send_c, send_d = chain.after((send_c, send_d))
@@ -923,6 +923,7 @@
         + [pltpu.VMEM((768, 512), F32)] * 2
         + [pltpu.SemaphoreType.DMA((23,))],
         micros=0,
+        room=12,
         inside=(),
     )
     chain.step(g_quad_up)
@@ -936,6 +937,7 @@
         scratch=[pltpu.VMEM((384, 512), F32)] * 4
         + [pltpu.VMEM((3, 128, 512), F32), pltpu.SemaphoreType.DMA((18,))],
         micros=3,
+        room=8,
         inside=(4,),
     )
     return (

time: 230 us -> 241 us (1.048)
  Pallas kernels: 60.2 us -> 42.9 us
  local copies, waits for them, and re-layouts: 10 us -> 27 us
  waiting for transfers between devices: 97.1 us -> 109 us
    unnamed x43 -> x123, local copies, waits for them, and re-layouts: 4.08 us -> 23.8 us
    pallas_call x7, Pallas kernels: 60.2 us -> 42.9 us  [call(): pl.pallas_call(kernel, out_shape=[jax.ShapeDtypeStruct(shape, F32) for sh...]
    ppermute x32, waiting for transfers between devices: 71 us -> 82.3 us  [swap(): return lax.ppermute(value, axis, [(i, i ^ 1 << bit) for i in range(count)])]
  transfers between devices with their start and end apart: 42 -> 42, of which waited for: 26 -> 28; matrix products, arithmetic and copies ran while one was open for 10% -> 8% of each run, Pallas kernels for 11% -> 5%
where the time goes in v7:
time: 241 us; the launch traced here: 240 us
  waiting for transfers between devices  109 us (45%)
  Pallas kernels  42.9 us (18%)
  starting transfers between devices  40.2 us (17%)
  local copies, waits for them, and re-layouts  27 us (11%)
  other arithmetic  17.3 us (7%)
  between operations  3.8 us (2%)
    ppermute x32, waiting for transfers between devices, swap(): return lax.ppermute(value, axis, [(i, i ^ 1 << bit) for i in range(count)])  82.3 us
    pallas_call x7, Pallas kernels, call(): pl.pallas_call(kernel, out_shape=[jax.ShapeDtypeStruct(shape, F32) for sh...  42.9 us
    ppermute x32, starting transfers between devices, swap(): return lax.ppermute(value, axis, [(i, i ^ 1 << bit) for i in range(count)])  27.1 us
    unnamed x123, local copies, waits for them, and re-layouts  23.8 us
    ppermute x8, waiting for transfers between devices, shifted(): return lax.ppermute(value, axis, pairs)  21.4 us
    add x24, other arithmetic, part(): total = total + lax.dynamic_slice_in_dim(x, at, size)  13.3 us
    ppermute x8, starting transfers between devices, shifted(): return lax.ppermute(value, axis, pairs)  9.37 us
  transfers between devices with their start and end apart: 42, of which 28 were waited for; matrix products, arithmetic and copies ran while one was open for 8% of the time, Pallas kernels for 5%

profile of v7, /device:TPU:0, one launch (start us, length us, event | category | flops | bytes accessed | tf_op | source)
XLA Modules:
  0.0 240.2 jit_solution(12166111656067397743)
XLA Ops:
  0.7 1.2 copy-done.1
  1.9 1.1 copy-done.3
  3.0 1.0 copy-done.8
  9.7 2.3 shard_map.394
  12.0 1.4 copy-done.29
  15.1 3.0 %collective-permute-start = (f32[17,8,128]{2,1,0:T(8,128)S(1)}, f32[17,8,128]{2,1,0:T(8,128)S(1)}, u32[]{:S(2)}, u32[]{:S(2)}) collective-permute-start(f32[17,8,128]{2,1,0:T(8,128)S(1)} %get-tuple-element.168), channel_id=1, source_target_pairs={{0,1},{1,0},{2,3},{3,2},{4,5},{5,4},{6,7},{7,6},{8,9},{9,8},{10,11... | collective-permute-start | bytes 208904 | tf_op jit(solution)/shard_map/ppermute | solution.py:36
  18.2 2.1 collective-permute-done
  20.4 4.2 %collective-permute-start.2 = (f32[2,17,8,128]{3,2,1,0:T(8,128)S(1)}, f32[2,17,8,128]{3,2,1,0:T(8,128)S(1)}, u32[]{:S(2)}, u32[]{:S(2)}) collective-permute-start(f32[2,17,8,128]{3,2,1,0:T(8,128)S(1)} %pad_maximum_fusion.14), channel_id=1, source_target_pairs={{0,24},{8,0},{16,8},{24,16},{1,25},{9,1},{17,9},{25,17},{2,26},{10... | collective-permute-start | bytes 417800 | tf_op jit(solution)/shard_map/ppermute | solution.py:31
  24.6 3.3 %collective-permute-done.2 = f32[2,17,8,128]{3,2,1,0:T(8,128)S(1)} collective-permute-done((f32[2,17,8,128]{3,2,1,0:T(8,128)S(1)}, f32[2,17,8,128]{3,2,1,0:T(8,128)S(1)}, u32[]{:S(2)}, u32[]{:S(2)}) %collective-permute-start.2) | collective-permute-done | bytes 139296 | tf_op jit(solution)/shard_map/ppermute | solution.py:31
  27.8 3.6 %collective-permute-done.1 = f32[2,17,8,128]{3,2,1,0:T(8,128)S(1)} collective-permute-done((f32[2,17,8,128]{3,2,1,0:T(8,128)S(1)}, f32[2,17,8,128]{3,2,1,0:T(8,128)S(1)}, u32[]{:S(2)}, u32[]{:S(2)}) %collective-permute-start.1) | collective-permute-done | bytes 139296 | tf_op jit(solution)/shard_map/ppermute | solution.py:31
  34.0 6.4 %collective-permute-done.4.halo_after = f32[6,17,8,128]{3,2,1,0:T(8,128)} collective-permute-done((f32[6,17,8,128]{3,2,1,0:T(8,128)S(1)}, f32[6,17,8,128]{3,2,1,0:T(8,128)}, u32[]{:S(2)}, u32[]{:S(2)}) %collective-permute-start.4) | collective-permute-done | bytes 417824 | tf_op jit(solution)/shard_map/ppermute | solution.py:31
  40.4 3.3 %collective-permute-done.3.halo_before = f32[6,17,8,128]{3,2,1,0:T(8,128)} collective-permute-done((f32[6,17,8,128]{3,2,1,0:T(8,128)S(1)}, f32[6,17,8,128]{3,2,1,0:T(8,128)}, u32[]{:S(2)}, u32[]{:S(2)}) %collective-permute-start.3) | collective-permute-done | bytes 417824 | tf_op jit(solution)/shard_map/ppermute | solution.py:31
  43.7 1.0 copy-done.6
  44.8 1.0 copy-done.7
  45.8 1.0 copy-done.9
  46.8 24.1 %shard_map.395 = (f32[8,256]{1,0:T(8,128)}, f32[240,512]{1,0:T(8,128)}, f32[8,256]{1,0:T(8,128)}, f32[240,512]{1,0:T(8,128)S(1)}, f32[8,256]{1,0:T(8,128)S(1)}, ...) custom-call(f32[6,17,8,128]{3,2,1,0:T(8,128)} %collective-permute-do, ...), custom_call_target="tpu_custom_call" | custom-call | flops 29899999232 | bytes 1024 | tf_op jit(solution)/shard_map/pallas_call | solution.py:760
  71.1 1.0 shard_map.396
  73.2 1.9 collective-permute-done.5
  75.1 1.7 dynamic-slice_add_fusion.1
  76.9 1.6 collective-permute-start.7
  78.4 1.3 dynamic-slice_add_fusion.3
  80.3 5.8 %shard_map.397 = (f32[6,16,8,128]{3,2,1,0:T(8,128)S(1)}, f32[6,16,8,128]{3,2,1,0:T(8,128)S(1)}, f32[6,16,8,128]{3,2,1,0:T(8,128)S(1)}, f32[16,16,128]{2,1,0:T(8,128)S(1)}) custom-call(f32[30,8,8,128]{3,2,1,0:T(8,128)S(1)} %copy-done.39, f32[240,2048]{1,0:T(8,128)S(1)} %copy-done.35, f32[240,256]{1,0:T(8,128)S(1)} %copy-done.47, ...), custom_call_target="tpu_custom_call" | custom-call | flops 14949999616 | bytes 1024 | tf_op jit(solution)/shard_map/pallas_call | solution.py:760
  86.9 1.3 dynamic-slice_add_fusion.2
  88.2 1.4 dynamic-slice_add_fusion
  89.5 9.8 %collective-permute-done.7 = f32[448,512]{1,0:T(8,128)S(1)} collective-permute-done((f32[448,512]{1,0:T(8,128)S(1)}, f32[448,512]{1,0:T(8,128)S(1)}, u32[]{:S(2)}, u32[]{:S(2)}) %collective-permute-start.7) | collective-permute-done | bytes 917536 | tf_op jit(solution)/shard_map/ppermute | solution.py:55
  100.3 1.4 collective-permute-start.12
  101.8 4.9 %collective-permute-done.9 = f32[6,16,8,128]{3,2,1,0:T(8,128)S(1)} collective-permute-done((f32[6,16,8,128]{3,2,1,0:T(8,128)S(1)}, f32[6,16,8,128]{3,2,1,0:T(8,128)S(1)}, u32[]{:S(2)}, u32[]{:S(2)}) %collective-permute-start.9) | collective-permute-done | bytes 393248 | tf_op jit(solution)/shard_map/ppermute | solution.py:31
  107.2 3.4 %collective-permute-start.13 = (f32[2,16,8,128]{3,2,1,0:T(8,128)S(1)}, f32[2,16,8,128]{3,2,1,0:T(8,128)S(1)}, u32[]{:S(2)}, u32[]{:S(2)}) collective-permute-start(f32[2,16,8,128]{3,2,1,0:T(8,128)S(1)} %get-tuple-element.344), channel_id=1, source_target_pairs={{0,24},{8,0},{16,8},{24,16},{1,25},{9,1},{17,9},{25,17},{2,26},{10... | collective-permute-start | bytes 393224 | tf_op jit(solution)/shard_map/ppermute | solution.py:31
  110.7 6.7 %collective-permute-done.11 = f32[224,512]{1,0:T(8,128)S(1)} collective-permute-done((f32[224,512]{1,0:T(8,128)S(1)}, f32[224,512]{1,0:T(8,128)S(1)}, u32[]{:S(2)}, u32[]{:S(2)}) %collective-permute-start.11) | collective-permute-done | bytes 458784 | tf_op jit(solution)/shard_map/ppermute | solution.py:55
  120.4 3.2 %collective-permute-done.15 = f32[16,8,128]{2,1,0:T(8,128)S(1)} collective-permute-done((f32[16,8,128]{2,1,0:T(8,128)S(1)}, f32[16,8,128]{2,1,0:T(8,128)S(1)}, u32[]{:S(2)}, u32[]{:S(2)}) %collective-permute-start.15) | collective-permute-done | bytes 65568 | tf_op jit(solution)/shard_map/ppermute | solution.py:885
  123.6 1.0 copy-done.10
  124.7 1.7 copy-done.30
  126.4 1.2 copy-done.32
  127.6 1.0 copy-done.34
  132.2 3.3 %shard_map.398 = (f32[8,256]{1,0:T(8,128)}, f32[240,512]{1,0:T(8,128)}, f32[384,512]{1,0:T(8,128)S(1)}, f32[384,512]{1,0:T(8,128)}, f32[384,512]{1,0:T(8,128)S(1)}, /*index=5*/f32[384,512]{1,0:T(8,128)S(1)}) custom-call(f32[16,16,128]{2,1,0:T(8,128)S(1)} %copy-done.45, f32[16,8,128]{2,1,0:T(8,128)S(1)} %bitcast_add_fusion.returned, ...), custom_call_target="tpu_custom_call" | custom-call | flops 8049999872 | bytes 1024 | tf_op jit(solution)/shard_map/pallas_call | solution.py:760
  136.8 2.3 collective-permute-done.17
  140.6 1.1 dynamic-slice_add_fusion.10
  142.2 7.4 %collective-permute-done.19 = f32[104,512]{1,0:T(8,128)} collective-permute-done((f32[104,512]{1,0:T(8,128)}, f32[104,512]{1,0:T(8,128)}, u32[]{:S(2)}, u32[]{:S(2)}) %collective-permute-start.19) | collective-permute-done | bytes 213024 | tf_op jit(solution)/shard_map/ppermute | solution.py:55
  149.6 1.0 add.320
  150.8 1.1 dynamic-slice_add_fusion.8
  151.8 1.0 dynamic-slice_add_fusion.21
  154.2 1.0 dynamic-slice_add_fusion.19
  155.2 4.5 %collective-permute-done.22 = f32[96,512]{1,0:T(8,128)S(1)} collective-permute-done((f32[96,512]{1,0:T(8,128)S(1)}, f32[96,512]{1,0:T(8,128)S(1)}, u32[]{:S(2)}, u32[]{:S(2)}) %collective-permute-start.22) | collective-permute-done | bytes 196640 | tf_op jit(solution)/shard_map/ppermute | solution.py:55
  161.2 1.2 collective-permute-start.26
  162.4 6.5 %collective-permute-done.25 = f32[96,512]{1,0:T(8,128)S(1)} collective-permute-done((f32[96,512]{1,0:T(8,128)S(1)}, f32[96,512]{1,0:T(8,128)S(1)}, u32[]{:S(2)}, u32[]{:S(2)}) %collective-permute-start.25) | collective-permute-done | bytes 196640 | tf_op jit(solution)/shard_map/ppermute | solution.py:55
  169.0 1.8 collective-permute-start.29
  170.8 6.3 %collective-permute-done.26 = f32[208,512]{1,0:T(8,128)S(1)} collective-permute-done((f32[208,512]{1,0:T(8,128)S(1)}, f32[208,512]{1,0:T(8,128)S(1)}, u32[]{:S(2)}, u32[]{:S(2)}) %collective-permute-start.26) | collective-permute-done | bytes 426016 | tf_op jit(solution)/shard_map/ppermute | solution.py:55
  178.5 1.3 collective-permute-start.30
  179.8 1.6 collective-permute-start.27
  181.4 2.6 %collective-permute-done.30 = f32[48,512]{1,0:T(8,128)S(1)} collective-permute-done((f32[48,512]{1,0:T(8,128)S(1)}, f32[48,512]{1,0:T(8,128)S(1)}, u32[]{:S(2)}, u32[]{:S(2)}) %collective-permute-start.30) | collective-permute-done | bytes 98336 | tf_op jit(solution)/shard_map/ppermute | solution.py:55
  184.1 3.1 %collective-permute-start.31 = (f32[96,512]{1,0:T(8,128)S(1)}, f32[96,512]{1,0:T(8,128)S(1)}, u32[]{:S(2)}, u32[]{:S(2)}) collective-permute-start(f32[96,512]{1,0:T(8,128)S(1)} %pad_maximum_fusion.13), channel_id=1, source_target_pairs={{0,8},{8,0},{16,24},{24,16},{1,9},{9,1},{17,25},{25,17},{2,10},{10... | collective-permute-start | bytes 589832 | tf_op jit(solution)/shard_map/ppermute | solution.py:55
  188.1 2.8 %collective-permute-done.31 = f32[96,512]{1,0:T(8,128)S(1)} collective-permute-done((f32[96,512]{1,0:T(8,128)S(1)}, f32[96,512]{1,0:T(8,128)S(1)}, u32[]{:S(2)}, u32[]{:S(2)}) %collective-permute-start.31) | collective-permute-done | bytes 196640 | tf_op jit(solution)/shard_map/ppermute | solution.py:55
  191.7 1.5 collective-permute-start.32
  193.4 1.4 collective-permute-start.34
  194.8 4.6 %collective-permute-done.28 = f32[192,512]{1,0:T(8,128)S(1)} collective-permute-done((f32[192,512]{1,0:T(8,128)S(1)}, f32[192,512]{1,0:T(8,128)S(1)}, u32[]{:S(2)}, u32[]{:S(2)}) %collective-permute-start.28) | collective-permute-done | bytes 393248 | tf_op jit(solution)/shard_map/ppermute | solution.py:55
  199.5 1.6 collective-permute-start.35
  201.2 2.3 collective-permute-done.33
  203.6 14.1 %collective-permute-done.34 = f32[448,512]{1,0:T(8,128)S(1)} collective-permute-done((f32[448,512]{1,0:T(8,128)S(1)}, f32[448,512]{1,0:T(8,128)S(1)}, u32[]{:S(2)}, u32[]{:S(2)}) %collective-permute-start.34) | collective-permute-done | bytes 917536 | tf_op jit(solution)/shard_map/ppermute | solution.py:55
  223.1 2.3 collective-permute-done.37.b_other
  225.4 3.1 %shard_map.399 = (f32[2,512,512]{2,1,0:T(8,128)}, f32[2,256,512]{2,1,0:T(8,128)}, f32[64,1024]{1,0:T(8,128)}, f32[64,512]{1,0:T(8,128)}, f32[32,1024]{1,0:T(8,12...) custom-call(f32[896,512]{1,0:T(8,128)S(1)} %maximum_add_fusion.a_mine, ...), custom_call_target="tpu_custom_call" | custom-call | bytes 1024 | tf_op jit(solution)/shard_map/pallas_call | solution.py:760
  228.6 4.0 %collective-permute-done.38 = f32[192,512]{1,0:T(8,128)S(1)} collective-permute-done((f32[192,512]{1,0:T(8,128)S(1)}, f32[192,512]{1,0:T(8,128)S(1)}, u32[]{:S(2)}, u32[]{:S(2)}) %collective-permute-start.38) | collective-permute-done | bytes 393248 | tf_op jit(solution)/shard_map/ppermute | solution.py:55
  233.7 1.8 collective-permute-done.41.d_other
  235.5 1.1 collective-permute-done.40.c_other
  236.6 3.4 %shard_map.400 = (f32[2,512,512]{2,1,0:T(8,128)}, f32[5,128,512]{2,1,0:T(8,128)}, f32[64,512]{1,0:T(8,128)}, f32[32,512]{1,0:T(8,128)}, f32[3,256]{1,0:T(4,128)}) custom-call(f32[384,512]{1,0:T(8,128)S(1)} %pad_maximum_fusion.5.c_mine, f32[384,512]{1,0:T(8,128)S(1)} %collective-permute-done.40.c_other, f32[384,512]{1,0:T(8,128)S(1)} %pad_maximum_fusion.6.d_mine, ...), custom_call_target="tpu_custom_call" | custom-call | flops 3449999872 | bytes 1024 | tf_op jit(solution)/shard_map/pallas_call | solution.py:760
  (234 shorter events, 35.0 us)
Async XLA Ops:
  9.7 8.4 %copy-start.60 = (s32[240]{0:T(256)S(1)}, s32[240]{0:T(256)}, u32[]{:S(2)}) copy-start(s32[240]{0:T(256)} %param.32) | copy-start | bytes 2884
  9.7 8.4 %copy-start.52 = (s32[240,8]{0,1:T(8,128)S(1)}, s32[240,8]{0,1:T(8,128)}, u32[]{:S(2)}) copy-start(s32[240,8]{0,1:T(8,128)} %param.33) | copy-start | bytes 23044
  9.7 8.5 %copy-start.56 = (s32[240,8]{0,1:T(8,128)S(1)}, s32[240,8]{0,1:T(8,128)}, u32[]{:S(2)}) copy-start(s32[240,8]{0,1:T(8,128)} %param.35) | copy-start | bytes 23044
  9.7 22.4 %copy-start.54 = (s32[240,8]{0,1:T(8,128)S(1)}, s32[240,8]{0,1:T(8,128)}, u32[]{:S(2)}) copy-start(s32[240,8]{0,1:T(8,128)} %param.34) | copy-start | bytes 23044
  9.7 22.4 %copy-start.58 = (s32[240,8]{0,1:T(8,128)S(1)}, s32[240,8]{0,1:T(8,128)}, u32[]{:S(2)}) copy-start(s32[240,8]{0,1:T(8,128)} %param.36) | copy-start | bytes 23044
  9.7 34.0 %copy-start.12 = (bf16[64,512]{1,0:T(8,128)(2,1)S(1)}, bf16[64,512]{1,0:T(8,128)(2,1)}, u32[]{:S(2)}) copy-start(bf16[64,512]{1,0:T(8,128)(2,1)} %trip_up.1) | copy-start | bytes 196612
  9.7 33.9 %copy-start.13 = (bf16[1024,32]{0,1:T(8,128)(2,1)S(1)}, bf16[1024,32]{0,1:T(8,128)(2,1)}, u32[]{:S(2)}) copy-start(bf16[1024,32]{0,1:T(8,128)(2,1)} %param.44) | copy-start | bytes 196612
  9.7 33.9 %copy-start.16 = (bf16[32,512]{1,0:T(8,128)(2,1)S(1)}, bf16[32,512]{1,0:T(8,128)(2,1)}, u32[]{:S(2)}) copy-start(bf16[32,512]{1,0:T(8,128)(2,1)} %quad_up.1) | copy-start | bytes 98308
  15.0 55.9 %copy-start.42 = (f32[240,128]{1,0:T(8,128)}, f32[240,128]{1,0:T(8,128)S(1)}, u32[]{:S(2)}) copy-start(f32[240,128]{1,0:T(8,128)S(1)} %get-tuple-element.171.columns) | copy-start | bytes 368644
  15.0 56.0 %copy-start.36 = (f32[240,128]{1,0:T(8,128)}, f32[240,128]{1,0:T(8,128)S(1)}, u32[]{:S(2)}) copy-start(f32[240,128]{1,0:T(8,128)S(1)} %get-tuple-element.173.radial) | copy-start | bytes 368644
  15.0 28.6 %copy-start = (bf16[2,512,512]{2,1,0:T(8,128)(2,1)S(1)}, bf16[2,512,512]{2,1,0:T(8,128)(2,1)}, u32[]{:S(2)}) copy-start(bf16[2,512,512]{2,1,0:T(8,128)(2,1)} %w_res.1) | copy-start | bytes 3145732
  15.0 28.7 %copy-start.4 = (bf16[2,256,512]{2,1,0:T(8,128)(2,1)S(1)}, bf16[2,256,512]{2,1,0:T(8,128)(2,1)}, u32[]{:S(2)}) copy-start(bf16[2,256,512]{2,1,0:T(8,128)(2,1)} %w_ae.1) | copy-start | bytes 1572868
  15.0 28.7 %copy-start.5 = (bf16[2,512,256]{2,1,0:T(8,128)(2,1)S(1)}, bf16[2,512,256]{2,1,0:T(8,128)(2,1)}, u32[]{:S(2)}) copy-start(bf16[2,512,256]{2,1,0:T(8,128)(2,1)} %w_ea.1) | copy-start | bytes 1572868
  15.0 28.7 %copy-start.11 = (bf16[1024,64]{0,1:T(8,128)(2,1)S(1)}, bf16[1024,64]{0,1:T(8,128)(2,1)}, u32[]{:S(2)}) copy-start(bf16[1024,64]{0,1:T(8,128)(2,1)} %param.41) | copy-start | bytes 393220
  15.0 28.7 %copy-start.20 = (f32[8,256]{1,0:T(8,128)S(1)}, f32[8,256]{1,0:T(8,128)}, u32[]{:S(2)}) copy-start(f32[8,256]{1,0:T(8,128)} %cot_atoms.1) | copy-start | bytes 24580
  15.0 28.7 %copy-start.21 = (f32[8,256]{1,0:T(8,128)S(1)}, f32[8,256]{1,0:T(8,128)}, u32[]{:S(2)}) copy-start(f32[8,256]{1,0:T(8,128)} %cot_energy.1) | copy-start | bytes 24580
  15.1 5.3 %collective-permute-start = (f32[17,8,128]{2,1,0:T(8,128)S(1)}, f32[17,8,128]{2,1,0:T(8,128)S(1)}, u32[]{:S(2)}, u32[]{:S(2)}) collective-permute-start(f32[17,8,128]{2,1,0:T(8,128)S(1)} %get-tuple-element.168), channel_id=1, source_target_pairs={{0,1},{1,0},{2,3},{3,2},{4,5},{5,4},{6,7},{7,6},{8,9},{9,8},{10,11... | collective-permute-start | bytes 208904 | tf_op jit(solution)/shard_map/ppermute | solution.py:36
  20.4 7.5 %collective-permute-start.2 = (f32[2,17,8,128]{3,2,1,0:T(8,128)S(1)}, f32[2,17,8,128]{3,2,1,0:T(8,128)S(1)}, u32[]{:S(2)}, u32[]{:S(2)}) collective-permute-start(f32[2,17,8,128]{3,2,1,0:T(8,128)S(1)} %pad_maximum_fusion.14), channel_id=1, source_target_pairs={{0,24},{8,0},{16,8},{24,16},{1,25},{9,1},{17,9},{25,17},{2,26},{10... | collective-permute-start | bytes 417800 | tf_op jit(solution)/shard_map/ppermute | solution.py:31
  24.6 6.9 %collective-permute-start.1 = (f32[2,17,8,128]{3,2,1,0:T(8,128)S(1)}, f32[2,17,8,128]{3,2,1,0:T(8,128)S(1)}, u32[]{:S(2)}, u32[]{:S(2)}) collective-permute-start(f32[2,17,8,128]{3,2,1,0:T(8,128)S(1)} %pad_maximum_fusion.14), channel_id=1, source_target_pairs={{0,8},{8,16},{16,24},{24,0},{1,9},{9,17},{17,25},{25,1},{2,10},{10... | collective-permute-start | bytes 417800 | tf_op jit(solution)/shard_map/ppermute | solution.py:31
  31.5 8.9 %collective-permute-start.4 = (f32[6,17,8,128]{3,2,1,0:T(8,128)S(1)}, f32[6,17,8,128]{3,2,1,0:T(8,128)}, u32[]{:S(2)}, u32[]{:S(2)}) collective-permute-start(f32[6,17,8,128]{3,2,1,0:T(8,128)S(1)} %pad_maximum_fusion.8.halo_here), channel_id=1, source_target_pairs={{0,6},{2,0},{4,2},{6,4},{1,7},{3,1},{5,3},{7,5},{8,14},{10,8},{12,... | collective-permute-start | bytes 1253384 | tf_op jit(solution)/shard_map/ppermute | solution.py:31
  31.5 12.1 %collective-permute-start.3 = (f32[6,17,8,128]{3,2,1,0:T(8,128)S(1)}, f32[6,17,8,128]{3,2,1,0:T(8,128)}, u32[]{:S(2)}, u32[]{:S(2)}) collective-permute-start(f32[6,17,8,128]{3,2,1,0:T(8,128)S(1)} %pad_maximum_fusion.8.halo_here), channel_id=1, source_target_pairs={{0,2},{2,4},{4,6},{6,0},{1,3},{3,5},{5,7},{7,1},{8,10},{10,12},{12... | collective-permute-start | bytes 1253384 | tf_op jit(solution)/shard_map/ppermute | solution.py:31
  70.9 4.2 %collective-permute-start.5 = (f32[896,512]{1,0:T(8,128)}, f32[896,512]{1,0:T(8,128)}, u32[]{:S(2)}, u32[]{:S(2)}) collective-permute-start(f32[896,512]{1,0:T(8,128)} %get-tuple-element.179), channel_id=1, source_target_pairs={{0,2},{2,0},{1,3},{3,1},{4,6},{6,4},{5,7},{7,5},{8,10},{10,8},{9,1... | collective-permute-start | bytes 5505032 | tf_op jit(solution)/shard_map/ppermute | solution.py:55
  72.1 6.4 %collective-permute-start.6 = (f32[768,512]{1,0:T(8,128)S(1)}, f32[768,512]{1,0:T(8,128)}, u32[]{:S(2)}, u32[]{:S(2)}) collective-permute-start(f32[768,512]{1,0:T(8,128)S(1)} %get-tuple-element.184), channel_id=1, source_target_pairs={{0,2},{2,0},{1,3},{3,1},{4,6},{6,4},{5,7},{7,5},{8,10},{10,8},{9,1... | collective-permute-start | bytes 4718600 | tf_op jit(solution)/shard_map/ppermute | solution.py:55
  76.9 22.5 %collective-permute-start.7 = (f32[448,512]{1,0:T(8,128)S(1)}, f32[448,512]{1,0:T(8,128)S(1)}, u32[]{:S(2)}, u32[]{:S(2)}) collective-permute-start(f32[448,512]{1,0:T(8,128)S(1)} %dynamic-slice_add_fusion.1), channel_id=1, source_target_pairs={{0,1},{1,0},{2,3},{3,2},{4,5},{5,4},{6,7},{7,6},{8,9},{9,8},{10,11... | collective-permute-start | bytes 2752520 | tf_op jit(solution)/shard_map/ppermute | solution.py:55
  79.7 20.5 %collective-permute-start.8 = (f32[384,512]{1,0:T(8,128)S(1)}, f32[384,512]{1,0:T(8,128)S(1)}, u32[]{:S(2)}, u32[]{:S(2)}) collective-permute-start(f32[384,512]{1,0:T(8,128)S(1)} %dynamic-slice_add_fusion.3), channel_id=1, source_target_pairs={{0,4},{4,0},{1,5},{5,1},{2,6},{6,2},{3,7},{7,3},{8,12},{12,8},{9,1... | collective-permute-start | bytes 2359304 | tf_op jit(solution)/shard_map/ppermute | solution.py:55
  86.1 20.5 %collective-permute-start.9 = (f32[6,16,8,128]{3,2,1,0:T(8,128)S(1)}, f32[6,16,8,128]{3,2,1,0:T(8,128)S(1)}, u32[]{:S(2)}, u32[]{:S(2)}) collective-permute-start(f32[6,16,8,128]{3,2,1,0:T(8,128)S(1)} %get-tuple-element.203), channel_id=1, source_target_pairs={{0,6},{2,0},{4,2},{6,4},{1,7},{3,1},{5,3},{7,5},{8,14},{10,8},{12,... | collective-permute-start | bytes 1179656 | tf_op jit(solution)/shard_map/ppermute | solution.py:31
  86.9 19.8 %collective-permute-start.10 = (f32[6,16,8,128]{3,2,1,0:T(8,128)S(1)}, f32[6,16,8,128]{3,2,1,0:T(8,128)S(1)}, u32[]{:S(2)}, u32[]{:S(2)}) collective-permute-start(f32[6,16,8,128]{3,2,1,0:T(8,128)S(1)} %get-tuple-element.204), channel_id=1, source_target_pairs={{0,2},{2,4},{4,6},{6,0},{1,3},{3,5},{5,7},{7,1},{8,10},{10,12},{12... | collective-permute-start | bytes 1179656 | tf_op jit(solution)/shard_map/ppermute | solution.py:31
  99.4 17.9 %collective-permute-start.11 = (f32[224,512]{1,0:T(8,128)S(1)}, f32[224,512]{1,0:T(8,128)S(1)}, u32[]{:S(2)}, u32[]{:S(2)}) collective-permute-start(f32[224,512]{1,0:T(8,128)S(1)} %dynamic-slice_add_fusion.5), channel_id=1, source_target_pairs={{0,4},{4,0},{1,5},{5,1},{2,6},{6,2},{3,7},{7,3},{8,12},{12,8},{9,1... | collective-permute-start | bytes 1376264 | tf_op jit(solution)/shard_map/ppermute | solution.py:55
  100.3 10.4 %collective-permute-start.12 = (f32[192,512]{1,0:T(8,128)S(1)}, f32[192,512]{1,0:T(8,128)S(1)}, u32[]{:S(2)}, u32[]{:S(2)}) collective-permute-start(f32[192,512]{1,0:T(8,128)S(1)} %dynamic-slice_add_fusion.13), channel_id=1, source_target_pairs={{0,1},{1,0},{2,3},{3,2},{4,5},{5,4},{6,7},{7,6},{8,9},{9,8},{10,11... | collective-permute-start | bytes 1179656 | tf_op jit(solution)/shard_map/ppermute | solution.py:55
  106.8 12.4 %collective-permute-start.14 = (f32[2,16,8,128]{3,2,1,0:T(8,128)S(1)}, f32[2,16,8,128]{3,2,1,0:T(8,128)S(1)}, u32[]{:S(2)}, u32[]{:S(2)}) collective-permute-start(f32[2,16,8,128]{3,2,1,0:T(8,128)S(1)} %get-tuple-element.343), channel_id=1, source_target_pairs={{0,8},{8,16},{16,24},{24,0},{1,9},{9,17},{17,25},{25,1},{2,10},{10... | collective-permute-start | bytes 393224 | tf_op jit(solution)/shard_map/ppermute | solution.py:31
  107.2 12.0 %collective-permute-start.13 = (f32[2,16,8,128]{3,2,1,0:T(8,128)S(1)}, f32[2,16,8,128]{3,2,1,0:T(8,128)S(1)}, u32[]{:S(2)}, u32[]{:S(2)}) collective-permute-start(f32[2,16,8,128]{3,2,1,0:T(8,128)S(1)} %get-tuple-element.344), channel_id=1, source_target_pairs={{0,24},{8,0},{16,8},{24,16},{1,25},{9,1},{17,9},{25,17},{2,26},{10... | collective-permute-start | bytes 393224 | tf_op jit(solution)/shard_map/ppermute | solution.py:31
  117.5 6.1 %copy-start.2 = (bf16[2,512,512]{2,1,0:T(8,128)(2,1)S(1)}, bf16[2,512,512]{2,1,0:T(8,128)(2,1)}, u32[]{:S(2)}) copy-start(bf16[2,512,512]{2,1,0:T(8,128)(2,1)} %w_in.3) | copy-start | bytes 3145732
  117.5 6.1 %copy-start.15 = (bf16[512,64]{0,1:T(8,128)(2,1)S(1)}, bf16[512,64]{0,1:T(8,128)(2,1)}, u32[]{:S(2)}) copy-start(bf16[512,64]{0,1:T(8,128)(2,1)} %param.40) | copy-start | bytes 196612
  117.5 6.1 %copy-start.18 = (bf16[512,32]{0,1:T(8,128)(2,1)S(1)}, bf16[512,32]{0,1:T(8,128)(2,1)}, u32[]{:S(2)}) copy-start(bf16[512,32]{0,1:T(8,128)(2,1)} %param.43) | copy-start | bytes 98308
  117.5 6.1 %copy-start.26 = (s32[8]{0:T(128)S(1)}, s32[8]{0:T(128)}, u32[]{:S(2)}) copy-start(s32[8]{0:T(128)} %param.30) | copy-start | bytes 100
  117.5 6.1 %copy-start.28 = (s32[4]{0:T(128)S(1)}, s32[4]{0:T(128)}, u32[]{:S(2)}) copy-start(s32[4]{0:T(128)} %param.31) | copy-start | bytes 52
  117.5 6.1 %copy-start.49 = (f32[8,256]{1,0:T(8,128)S(1)}, f32[8,256]{1,0:T(8,128)}, u32[]{:S(2)}) copy-start(f32[8,256]{1,0:T(8,128)} %copy-done.48) | copy-start | bytes 24580
  119.2 4.3 %collective-permute-start.15 = (f32[16,8,128]{2,1,0:T(8,128)S(1)}, f32[16,8,128]{2,1,0:T(8,128)S(1)}, u32[]{:S(2)}, u32[]{:S(2)}) collective-permute-start(f32[16,8,128]{2,1,0:T(8,128)S(1)} %select_bitcast_fusion.2), channel_id=1, source_target_pairs={{0,1},{1,0},{2,3},{3,2},{4,5},{5,4},{6,7},{7,6},{8,9},{9,8},{10,11... | collective-permute-start | bytes 196616 | tf_op jit(solution)/shard_map/ppermute | solution.py:885
  120.0 15.5 %collective-permute-start.16 = (f32[208,512]{1,0:T(8,128)}, f32[208,512]{1,0:T(8,128)S(1)}, u32[]{:S(2)}, u32[]{:S(2)}) collective-permute-start(f32[208,512]{1,0:T(8,128)} %dynamic-slice_add_fusion.7), channel_id=1, source_target_pairs={{0,8},{8,0},{16,24},{24,16},{1,9},{9,1},{17,25},{25,17},{2,10},{10... | collective-permute-start | bytes 1277960 | tf_op jit(solution)/shard_map/ppermute | solution.py:55
  136.2 2.9 %collective-permute-start.17 = (f32[384,512]{1,0:T(8,128)}, f32[384,512]{1,0:T(8,128)S(1)}, u32[]{:S(2)}, u32[]{:S(2)}) collective-permute-start(f32[384,512]{1,0:T(8,128)} %get-tuple-element.234), channel_id=1, source_target_pairs={{0,2},{2,0},{1,3},{3,1},{4,6},{6,4},{5,7},{7,5},{8,10},{10,8},{9,1... | collective-permute-start | bytes 2359304 | tf_op jit(solution)/shard_map/ppermute | solution.py:55
  136.3 4.3 %collective-permute-start.18 = (f32[384,512]{1,0:T(8,128)S(1)}, f32[384,512]{1,0:T(8,128)}, u32[]{:S(2)}, u32[]{:S(2)}) collective-permute-start(f32[384,512]{1,0:T(8,128)S(1)} %get-tuple-element.238), channel_id=1, source_target_pairs={{0,2},{2,0},{1,3},{3,1},{4,6},{6,4},{5,7},{7,5},{8,10},{10,8},{9,1... | collective-permute-start | bytes 2359304 | tf_op jit(solution)/shard_map/ppermute | solution.py:55
  136.8 12.8 %collective-permute-start.19 = (f32[104,512]{1,0:T(8,128)}, f32[104,512]{1,0:T(8,128)}, u32[]{:S(2)}, u32[]{:S(2)}) collective-permute-start(f32[104,512]{1,0:T(8,128)} %dynamic-slice_add_fusion.15), channel_id=1, source_target_pairs={{0,16},{8,24},{16,0},{24,8},{1,17},{9,25},{17,1},{25,9},{2,18},{10... | collective-permute-start | bytes 638984 | tf_op jit(solution)/shard_map/ppermute | solution.py:55
  139.9 11.9 %collective-permute-start.20 = (f32[192,512]{1,0:T(8,128)}, f32[192,512]{1,0:T(8,128)}, u32[]{:S(2)}, u32[]{:S(2)}) collective-permute-start(f32[192,512]{1,0:T(8,128)} %dynamic-slice_add_fusion.11), channel_id=1, source_target_pairs={{0,1},{1,0},{2,3},{3,2},{4,5},{5,4},{6,7},{7,6},{8,9},{9,8},{10,11... | collective-permute-start | bytes 1179656 | tf_op jit(solution)/shard_map/ppermute | solution.py:55
  141.7 11.7 %collective-permute-start.21 = (f32[192,512]{1,0:T(8,128)S(1)}, f32[192,512]{1,0:T(8,128)S(1)}, u32[]{:S(2)}, u32[]{:S(2)}) collective-permute-start(f32[192,512]{1,0:T(8,128)S(1)} %dynamic-slice_add_fusion.10), channel_id=1, source_target_pairs={{0,4},{4,0},{1,5},{5,1},{2,6},{6,2},{3,7},{7,3},{8,12},{12,8},{9,1... | collective-permute-start | bytes 1179656 | tf_op jit(solution)/shard_map/ppermute | solution.py:55
  150.6 10.5 %collective-permute-start.24 = (f32[104,512]{1,0:T(8,128)S(1)}, f32[104,512]{1,0:T(8,128)S(1)}, u32[]{:S(2)}, u32[]{:S(2)}) collective-permute-start(f32[104,512]{1,0:T(8,128)S(1)} %add.320), channel_id=1, source_target_pairs={{0,16},{8,24},{16,0},{24,8},{1,17},{9,25},{17,1},{25,9},{2,18},{10... | collective-permute-start | bytes 638984 | tf_op jit(solution)/shard_map/ppermute | solution.py:55
  152.8 6.9 %collective-permute-start.22 = (f32[96,512]{1,0:T(8,128)S(1)}, f32[96,512]{1,0:T(8,128)S(1)}, u32[]{:S(2)}, u32[]{:S(2)}) collective-permute-start(f32[96,512]{1,0:T(8,128)S(1)} %dynamic-slice_add_fusion.21), channel_id=1, source_target_pairs={{0,4},{4,0},{1,5},{5,1},{2,6},{6,2},{3,7},{7,3},{8,12},{12,8},{9,1... | collective-permute-start | bytes 589832 | tf_op jit(solution)/shard_map/ppermute | solution.py:55
  153.4 6.6 %collective-permute-start.23 = (f32[96,512]{1,0:T(8,128)S(1)}, f32[96,512]{1,0:T(8,128)S(1)}, u32[]{:S(2)}, u32[]{:S(2)}) collective-permute-start(f32[96,512]{1,0:T(8,128)S(1)} %dynamic-slice_add_fusion.20), channel_id=1, source_target_pairs={{0,1},{1,0},{2,3},{3,2},{4,5},{5,4},{6,7},{7,6},{8,9},{9,8},{10,11... | collective-permute-start | bytes 589832 | tf_op jit(solution)/shard_map/ppermute | solution.py:55
  160.1 8.8 %collective-permute-start.25 = (f32[96,512]{1,0:T(8,128)S(1)}, f32[96,512]{1,0:T(8,128)S(1)}, u32[]{:S(2)}, u32[]{:S(2)}) collective-permute-start(f32[96,512]{1,0:T(8,128)S(1)} %dynamic-slice_add_fusion.17), channel_id=1, source_target_pairs={{0,8},{8,0},{16,24},{24,16},{1,9},{9,1},{17,25},{25,17},{2,10},{10... | collective-permute-start | bytes 589832 | tf_op jit(solution)/shard_map/ppermute | solution.py:55
  161.2 15.9 %collective-permute-start.26 = (f32[208,512]{1,0:T(8,128)S(1)}, f32[208,512]{1,0:T(8,128)S(1)}, u32[]{:S(2)}, u32[]{:S(2)}) collective-permute-start(f32[208,512]{1,0:T(8,128)S(1)} %pad_maximum_fusion.7), channel_id=1, source_target_pairs={{0,8},{8,0},{16,24},{24,16},{1,9},{9,1},{17,25},{25,17},{2,10},{10... | collective-permute-start | bytes 1277960 | tf_op jit(solution)/shard_map/ppermute | solution.py:55
  169.0 8.3 %collective-permute-start.29 = (f32[48,512]{1,0:T(8,128)S(1)}, f32[48,512]{1,0:T(8,128)S(1)}, u32[]{:S(2)}, u32[]{:S(2)}) collective-permute-start(f32[48,512]{1,0:T(8,128)S(1)} %dynamic-slice_add_fusion.23), channel_id=1, source_target_pairs={{0,16},{8,24},{16,0},{24,8},{1,17},{9,25},{17,1},{25,9},{2,18},{10... | collective-permute-start | bytes 294920 | tf_op jit(solution)/shard_map/ppermute | solution.py:55
  178.5 5.6 %collective-permute-start.30 = (f32[48,512]{1,0:T(8,128)S(1)}, f32[48,512]{1,0:T(8,128)S(1)}, u32[]{:S(2)}, u32[]{:S(2)}) collective-permute-start(f32[48,512]{1,0:T(8,128)S(1)} %add_add_fusion.2), channel_id=1, source_target_pairs={{0,16},{8,24},{16,0},{24,8},{1,17},{9,25},{17,1},{25,9},{2,18},{10... | collective-permute-start | bytes 294920 | tf_op jit(solution)/shard_map/ppermute | solution.py:55
  179.8 13.4 %collective-permute-start.27 = (f32[224,512]{1,0:T(8,128)S(1)}, f32[224,512]{1,0:T(8,128)S(1)}, u32[]{:S(2)}, u32[]{:S(2)}) collective-permute-start(f32[224,512]{1,0:T(8,128)S(1)} %fusion), channel_id=1, source_target_pairs={{0,4},{4,0},{1,5},{5,1},{2,6},{6,2},{3,7},{7,3},{8,12},{12,8},{9,1... | collective-permute-start | bytes 1376264 | tf_op jit(solution)/shard_map/ppermute | solution.py:55
  184.1 6.8 %collective-permute-start.31 = (f32[96,512]{1,0:T(8,128)S(1)}, f32[96,512]{1,0:T(8,128)S(1)}, u32[]{:S(2)}, u32[]{:S(2)}) collective-permute-start(f32[96,512]{1,0:T(8,128)S(1)} %pad_maximum_fusion.13), channel_id=1, source_target_pairs={{0,8},{8,0},{16,24},{24,16},{1,9},{9,1},{17,25},{25,17},{2,10},{10... | collective-permute-start | bytes 589832 | tf_op jit(solution)/shard_map/ppermute | solution.py:55
  187.3 12.1 %collective-permute-start.28 = (f32[192,512]{1,0:T(8,128)S(1)}, f32[192,512]{1,0:T(8,128)S(1)}, u32[]{:S(2)}, u32[]{:S(2)}) collective-permute-start(f32[192,512]{1,0:T(8,128)S(1)} %slice.49), channel_id=1, source_target_pairs={{0,1},{1,0},{2,3},{3,2},{4,5},{5,4},{6,7},{7,6},{8,9},{9,8},{10,11... | collective-permute-start | bytes 1179656 | tf_op jit(solution)/shard_map/ppermute | solution.py:55
  190.9 12.6 %collective-permute-start.33 = (f32[96,512]{1,0:T(8,128)S(1)}, f32[96,512]{1,0:T(8,128)S(1)}, u32[]{:S(2)}, u32[]{:S(2)}) collective-permute-start(f32[96,512]{1,0:T(8,128)S(1)} %get-tuple-element.285), channel_id=1, source_target_pairs={{0,1},{1,0},{2,3},{3,2},{4,5},{5,4},{6,7},{7,6},{8,9},{9,8},{10,11... | collective-permute-start | bytes 589832 | tf_op jit(solution)/shard_map/ppermute | solution.py:55
  191.7 9.4 %collective-permute-start.32 = (f32[96,512]{1,0:T(8,128)S(1)}, f32[96,512]{1,0:T(8,128)S(1)}, u32[]{:S(2)}, u32[]{:S(2)}) collective-permute-start(f32[96,512]{1,0:T(8,128)S(1)} %get-tuple-element.283), channel_id=1, source_target_pairs={{0,4},{4,0},{1,5},{5,1},{2,6},{6,2},{3,7},{7,3},{8,12},{12,8},{9,1... | collective-permute-start | bytes 589832 | tf_op jit(solution)/shard_map/ppermute | solution.py:55
  193.4 24.4 %collective-permute-start.34 = (f32[448,512]{1,0:T(8,128)S(1)}, f32[448,512]{1,0:T(8,128)S(1)}, u32[]{:S(2)}, u32[]{:S(2)}) collective-permute-start(f32[448,512]{1,0:T(8,128)S(1)} %pad_maximum_fusion.1), channel_id=1, source_target_pairs={{0,1},{1,0},{2,3},{3,2},{4,5},{5,4},{6,7},{7,6},{8,9},{9,8},{10,11... | collective-permute-start | bytes 2752520 | tf_op jit(solution)/shard_map/ppermute | solution.py:55
  199.5 19.9 %collective-permute-start.35 = (f32[384,512]{1,0:T(8,128)S(1)}, f32[384,512]{1,0:T(8,128)S(1)}, u32[]{:S(2)}, u32[]{:S(2)}) collective-permute-start(f32[384,512]{1,0:T(8,128)S(1)} %pad_maximum_fusion.4), channel_id=1, source_target_pairs={{0,4},{4,0},{1,5},{5,1},{2,6},{6,2},{3,7},{7,3},{8,12},{12,8},{9,1... | collective-permute-start | bytes 2359304 | tf_op jit(solution)/shard_map/ppermute | solution.py:55
  219.3 6.1 %collective-permute-start.36 = (f32[896,512]{1,0:T(8,128)S(1)}, f32[896,512]{1,0:T(8,128)S(1)}, u32[]{:S(2)}, u32[]{:S(2)}) collective-permute-start(f32[896,512]{1,0:T(8,128)S(1)} %maximum_add_fusion.a_mine), channel_id=1, source_target_pairs={{0,2},{2,0},{1,3},{3,1},{4,6},{6,4},{5,7},{7,5},{8,10},{10,8},{9,1... | collective-permute-start | bytes 5505032 | tf_op jit(solution)/shard_map/ppermute | solution.py:55
  220.9 4.5 %collective-permute-start.37 = (f32[768,512]{1,0:T(8,128)S(1)}, f32[768,512]{1,0:T(8,128)S(1)}, u32[]{:S(2)}, u32[]{:S(2)}) collective-permute-start(f32[768,512]{1,0:T(8,128)S(1)} %maximum_add_fusion.1.b_mine), channel_id=1, source_target_pairs={{0,2},{2,0},{1,3},{3,1},{4,6},{6,4},{5,7},{7,5},{8,10},{10,8},{9,1... | collective-permute-start | bytes 4718600 | tf_op jit(solution)/shard_map/ppermute | solution.py:55
  221.5 11.1 %collective-permute-start.38 = (f32[192,512]{1,0:T(8,128)S(1)}, f32[192,512]{1,0:T(8,128)S(1)}, u32[]{:S(2)}, u32[]{:S(2)}) collective-permute-start(f32[192,512]{1,0:T(8,128)S(1)} %pad_maximum_fusion.11), channel_id=1, source_target_pairs={{0,1},{1,0},{2,3},{3,2},{4,5},{5,4},{6,7},{7,6},{8,9},{9,8},{10,11... | collective-permute-start | bytes 1179656 | tf_op jit(solution)/shard_map/ppermute | solution.py:55
  222.2 10.8 %collective-permute-start.39 = (f32[192,512]{1,0:T(8,128)S(1)}, f32[192,512]{1,0:T(8,128)S(1)}, u32[]{:S(2)}, u32[]{:S(2)}) collective-permute-start(f32[192,512]{1,0:T(8,128)S(1)} %pad_maximum_fusion.12), channel_id=1, source_target_pairs={{0,4},{4,0},{1,5},{5,1},{2,6},{6,2},{3,7},{7,3},{8,12},{12,8},{9,1... | collective-permute-start | bytes 1179656 | tf_op jit(solution)/shard_map/ppermute | solution.py:55
  233.1 2.4 collective-permute-start.41
  233.2 3.4 %collective-permute-start.40 = (f32[384,512]{1,0:T(8,128)S(1)}, f32[384,512]{1,0:T(8,128)S(1)}, u32[]{:S(2)}, u32[]{:S(2)}) collective-permute-start(f32[384,512]{1,0:T(8,128)S(1)} %pad_maximum_fusion.5.c_mine), channel_id=1, source_target_pairs={{0,2},{2,0},{1,3},{3,1},{4,6},{6,4},{5,7},{7,5},{8,10},{10,8},{9,1... | collective-permute-start | bytes 2359304 | tf_op jit(solution)/shard_map/ppermute | solution.py:55
  (39 other events, 55.9 us)

commit v8 on v7

--- a/solution.py
+++ b/solution.py
@@ -823,7 +823,7 @@
         + [(EDGES, 128)] * 2,
         [edge_states, edge_vectors, edge_mask[None, :], hidden_atoms, tag_row, send_row, tag_table,
          w_inputs, w_radial, trip_down_t, quad_down_t],
-        micros=5, room=22,
+        micros=5, room=58,
     )
     core = bit_value("gyl", 0)[None]
     before, here, after = with_halo(payload)
@@ -892,7 +892,7 @@
         [back_local, returned, grad_edges, grad_tag, edge_states, radial, columns, pre, downs, rads,
          tag_row, send_row, w_inputs, trip_down_t, quad_down_t, core],
         scratch=[pltpu.VMEM((768, 512), F32)] * 2,
-        micros=7, room=28,
+        micros=7, room=58,
     )
     next(late)
     send_c, send_d = chain.after((send_c, send_d))

time: 241 us -> 228 us (0.946)
  local copies, waits for them, and re-layouts: 27 us -> 9.8 us
  Pallas kernels: 42.9 us -> 48.9 us
    unnamed x123 -> x61, local copies, waits for them, and re-layouts: 23.8 us -> 6.03 us
    pallas_call x7, Pallas kernels: 42.9 us -> 48.9 us  [call(): pl.pallas_call(kernel, out_shape=[jax.ShapeDtypeStruct(shape, F32) for sh...]
    ppermute x32, waiting for transfers between devices: 82.3 us -> 78 us  [swap(): return lax.ppermute(value, axis, [(i, i ^ 1 << bit) for i in range(count)])]
  transfers between devices with their start and end apart: 42 -> 42, of which waited for: 28 -> 28; matrix products, arithmetic and copies ran while one was open for 8% -> 9% of each run, Pallas kernels for 5% -> 7%
where the time goes in v8:
time: 228 us; the launch traced here: 227 us
  waiting for transfers between devices  107 us (47%)
  Pallas kernels  48.9 us (21%)
  starting transfers between devices  40.6 us (18%)
  other arithmetic  17.4 us (8%)
  local copies, waits for them, and re-layouts  9.8 us (4%)
  between operations  3.65 us (2%)
    ppermute x32, waiting for transfers between devices, swap(): return lax.ppermute(value, axis, [(i, i ^ 1 << bit) for i in range(count)])  78 us
    pallas_call x7, Pallas kernels, call(): pl.pallas_call(kernel, out_shape=[jax.ShapeDtypeStruct(shape, F32) for sh...  48.9 us
    ppermute x32, starting transfers between devices, swap(): return lax.ppermute(value, axis, [(i, i ^ 1 << bit) for i in range(count)])  27.5 us
    ppermute x8, waiting for transfers between devices, shifted(): return lax.ppermute(value, axis, pairs)  23 us
    add x24, other arithmetic, part(): total = total + lax.dynamic_slice_in_dim(x, at, size)  12.9 us
    ppermute x8, starting transfers between devices, shifted(): return lax.ppermute(value, axis, pairs)  9.3 us
    unnamed x61, local copies, waits for them, and re-layouts  6.03 us
  transfers between devices with their start and end apart: 42, of which 28 were waited for; matrix products, arithmetic and copies ran while one was open for 9% of the time, Pallas kernels for 7%

profile of v8, /device:TPU:0, one launch (start us, length us, event | category | flops | bytes accessed | tf_op | source)
XLA Modules:
  0.0 226.9 jit_solution(14167026714824113240)
XLA Ops:
  0.7 4.7 %shard_map.394 = (f32[17,8,128]{2,1,0:T(8,128)}, f32[17,16,128]{2,1,0:T(8,128)}, f32[8,256]{1,0:T(8,128)}, f32[2,240,512]{2,1,0:T(8,128)}, f32[240,128]{1,0:T(8,...) custom-call(f32[240,512]{1,0:T(8,128)} %edge.5, f32[3,240]{1,0:T(4,128)} %vec.1, ...), custom_call_target="tpu_custom_call" | custom-call | flops 5750000128 | bytes 1024 | tf_op jit(solution)/shard_map/pallas_call | solution.py:760
  5.5 3.0 %collective-permute-start = (f32[17,8,128]{2,1,0:T(8,128)}, f32[17,8,128]{2,1,0:T(8,128)S(1)}, u32[]{:S(2)}, u32[]{:S(2)}) collective-permute-start(f32[17,8,128]{2,1,0:T(8,128)} %get-tuple-element.168), channel_id=1, source_target_pairs={{0,1},{1,0},{2,3},{3,2},{4,5},{5,4},{6,7},{7,6},{8,9},{9,8},{10,11... | collective-permute-start | bytes 208904 | tf_op jit(solution)/shard_map/ppermute | solution.py:36
  8.7 2.3 %collective-permute-done = f32[17,8,128]{2,1,0:T(8,128)S(1)} collective-permute-done((f32[17,8,128]{2,1,0:T(8,128)}, f32[17,8,128]{2,1,0:T(8,128)S(1)}, u32[]{:S(2)}, u32[]{:S(2)}) %collective-permute-start) | collective-permute-done | bytes 69664 | tf_op jit(solution)/shard_map/ppermute | solution.py:36
  11.9 4.2 %collective-permute-start.2 = (f32[2,17,8,128]{3,2,1,0:T(8,128)S(1)}, f32[2,17,8,128]{3,2,1,0:T(8,128)S(1)}, u32[]{:S(2)}, u32[]{:S(2)}) collective-permute-start(f32[2,17,8,128]{3,2,1,0:T(8,128)S(1)} %pad_maximum_fusion.14), channel_id=1, source_target_pairs={{0,24},{8,0},{16,8},{24,16},{1,25},{9,1},{17,9},{25,17},{2,26},{10... | collective-permute-start | bytes 417800 | tf_op jit(solution)/shard_map/ppermute | solution.py:31
  16.1 3.3 %collective-permute-done.2 = f32[2,17,8,128]{3,2,1,0:T(8,128)S(1)} collective-permute-done((f32[2,17,8,128]{3,2,1,0:T(8,128)S(1)}, f32[2,17,8,128]{3,2,1,0:T(8,128)S(1)}, u32[]{:S(2)}, u32[]{:S(2)}) %collective-permute-start.2) | collective-permute-done | bytes 139296 | tf_op jit(solution)/shard_map/ppermute | solution.py:31
  19.4 3.6 %collective-permute-done.1 = f32[2,17,8,128]{3,2,1,0:T(8,128)S(1)} collective-permute-done((f32[2,17,8,128]{3,2,1,0:T(8,128)S(1)}, f32[2,17,8,128]{3,2,1,0:T(8,128)S(1)}, u32[]{:S(2)}, u32[]{:S(2)}) %collective-permute-start.1) | collective-permute-done | bytes 139296 | tf_op jit(solution)/shard_map/ppermute | solution.py:31
  24.0 7.9 %collective-permute-done.4.halo_after = f32[6,17,8,128]{3,2,1,0:T(8,128)} collective-permute-done((f32[6,17,8,128]{3,2,1,0:T(8,128)S(1)}, f32[6,17,8,128]{3,2,1,0:T(8,128)}, u32[]{:S(2)}, u32[]{:S(2)}) %collective-permute-start.4) | collective-permute-done | bytes 417824 | tf_op jit(solution)/shard_map/ppermute | solution.py:31
  31.9 3.3 %collective-permute-done.3.halo_before = f32[6,17,8,128]{3,2,1,0:T(8,128)} collective-permute-done((f32[6,17,8,128]{3,2,1,0:T(8,128)S(1)}, f32[6,17,8,128]{3,2,1,0:T(8,128)}, u32[]{:S(2)}, u32[]{:S(2)}) %collective-permute-start.3) | collective-permute-done | bytes 417824 | tf_op jit(solution)/shard_map/ppermute | solution.py:31
  35.3 1.0 copy-done.3
  36.3 1.0 copy-done.4
  37.3 1.0 copy-done.5
  38.4 0.9 copy-done.14
  39.3 0.9 copy-done.15
  40.2 0.9 copy-done.18
  41.1 24.1 %shard_map.395 = (f32[8,256]{1,0:T(8,128)}, f32[240,512]{1,0:T(8,128)}, f32[8,256]{1,0:T(8,128)}, f32[240,512]{1,0:T(8,128)S(1)}, f32[8,256]{1,0:T(8,128)S(1)}, ...) custom-call(f32[6,17,8,128]{3,2,1,0:T(8,128)} %collective-permute-do, ...), custom_call_target="tpu_custom_call" | custom-call | flops 29899999232 | bytes 1024 | tf_op jit(solution)/shard_map/pallas_call | solution.py:760
  68.4 0.9 fusion.3
  69.5 1.7 dynamic-slice_add_fusion.1
  71.2 1.6 collective-permute-start.7
  72.8 1.3 dynamic-slice_add_fusion.3
  74.6 5.8 %shard_map.397 = (f32[6,16,8,128]{3,2,1,0:T(8,128)S(1)}, f32[6,16,8,128]{3,2,1,0:T(8,128)S(1)}, f32[6,16,8,128]{3,2,1,0:T(8,128)S(1)}, f32[16,16,128]{2,1,0:T(8,128)S(1)}) custom-call(f32[30,8,8,128]{3,2,1,0:T(8,128)S(1)} %copy-done.17, f32[240,2048]{1,0:T(8,128)S(1)} %copy-done.13, f32[240,256]{1,0:T(8,128)S(1)} %get-tuple-element.189.grad_src, ...), custom_call_target="tpu_custom_call" | custom-call | flops 14949999616 | bytes 1024 | tf_op jit(solution)/shard_map/pallas_call | solution.py:760
  81.2 1.3 dynamic-slice_add_fusion.2
  82.4 1.4 dynamic-slice_add_fusion
  83.8 9.8 %collective-permute-done.7 = f32[448,512]{1,0:T(8,128)S(1)} collective-permute-done((f32[448,512]{1,0:T(8,128)S(1)}, f32[448,512]{1,0:T(8,128)S(1)}, u32[]{:S(2)}, u32[]{:S(2)}) %collective-permute-start.7) | collective-permute-done | bytes 917536 | tf_op jit(solution)/shard_map/ppermute | solution.py:55
  94.6 1.3 collective-permute-start.12
  96.0 5.0 %collective-permute-done.9 = f32[6,16,8,128]{3,2,1,0:T(8,128)S(1)} collective-permute-done((f32[6,16,8,128]{3,2,1,0:T(8,128)S(1)}, f32[6,16,8,128]{3,2,1,0:T(8,128)S(1)}, u32[]{:S(2)}, u32[]{:S(2)}) %collective-permute-start.9) | collective-permute-done | bytes 393248 | tf_op jit(solution)/shard_map/ppermute | solution.py:31
  101.6 3.5 %collective-permute-start.13 = (f32[2,16,8,128]{3,2,1,0:T(8,128)S(1)}, f32[2,16,8,128]{3,2,1,0:T(8,128)S(1)}, u32[]{:S(2)}, u32[]{:S(2)}) collective-permute-start(f32[2,16,8,128]{3,2,1,0:T(8,128)S(1)} %get-tuple-element.344), channel_id=1, source_target_pairs={{0,24},{8,0},{16,8},{24,16},{1,25},{9,1},{17,9},{25,17},{2,26},{10... | collective-permute-start | bytes 393224 | tf_op jit(solution)/shard_map/ppermute | solution.py:31
  105.0 6.6 %collective-permute-done.11 = f32[224,512]{1,0:T(8,128)S(1)} collective-permute-done((f32[224,512]{1,0:T(8,128)S(1)}, f32[224,512]{1,0:T(8,128)S(1)}, u32[]{:S(2)}, u32[]{:S(2)}) %collective-permute-start.11) | collective-permute-done | bytes 458784 | tf_op jit(solution)/shard_map/ppermute | solution.py:55
  113.1 3.2 %collective-permute-done.15 = f32[16,8,128]{2,1,0:T(8,128)S(1)} collective-permute-done((f32[16,8,128]{2,1,0:T(8,128)S(1)}, f32[16,8,128]{2,1,0:T(8,128)S(1)}, u32[]{:S(2)}, u32[]{:S(2)}) %collective-permute-start.15) | collective-permute-done | bytes 65568 | tf_op jit(solution)/shard_map/ppermute | solution.py:885
  116.9 6.8 %shard_map.398 = (f32[8,256]{1,0:T(8,128)}, f32[240,512]{1,0:T(8,128)}, f32[384,512]{1,0:T(8,128)}, f32[384,512]{1,0:T(8,128)}, f32[384,512]{1,0:T(8,128)}, /*index=5*/f32[384,512]{1,0:T(8,128)}) custom-call(f32[16,16,128]{2,1,0:T(8,128)} %copy-done.19, f32[16,8,128]{2,1,0:T(8,128)} %bitcast_add_fusion.returned, f32[240,512]{1,0:T(8,128)} %copy-done.12, ...), custom_call_target="tpu_custom_call" | custom-call | flops 8049999872 | bytes 1024 | tf_op jit(solution)/shard_map/pallas_call | solution.py:760
  125.3 1.4 collective-permute-done.17
  126.8 1.8 dynamic-slice_add_fusion.11
  129.3 1.8 dynamic-slice_add_fusion.10
  131.1 1.1 collective-permute-start.21
  132.2 4.8 %collective-permute-done.19 = f32[104,512]{1,0:T(8,128)S(1)} collective-permute-done((f32[104,512]{1,0:T(8,128)S(1)}, f32[104,512]{1,0:T(8,128)S(1)}, u32[]{:S(2)}, u32[]{:S(2)}) %collective-permute-start.19) | collective-permute-done | bytes 213024 | tf_op jit(solution)/shard_map/ppermute | solution.py:55
  137.2 1.1 dynamic-slice_add_fusion.8
  138.2 1.7 collective-permute-done.20
  140.5 1.8 collective-permute-done.21
  142.3 1.0 dynamic-slice_add_fusion.20
  143.3 2.0 collective-permute-start.23
  145.3 1.0 dynamic-slice_add_fusion.18
  146.4 2.7 %collective-permute-done.23 = f32[96,512]{1,0:T(8,128)S(1)} collective-permute-done((f32[96,512]{1,0:T(8,128)S(1)}, f32[96,512]{1,0:T(8,128)S(1)}, u32[]{:S(2)}, u32[]{:S(2)}) %collective-permute-start.23) | collective-permute-done | bytes 196640 | tf_op jit(solution)/shard_map/ppermute | solution.py:55
  149.7 1.7 collective-permute-start.26
  151.4 6.7 %collective-permute-done.25 = f32[96,512]{1,0:T(8,128)S(1)} collective-permute-done((f32[96,512]{1,0:T(8,128)S(1)}, f32[96,512]{1,0:T(8,128)S(1)}, u32[]{:S(2)}, u32[]{:S(2)}) %collective-permute-start.25) | collective-permute-done | bytes 196640 | tf_op jit(solution)/shard_map/ppermute | solution.py:55
  158.2 1.0 collective-permute-start.29
  159.2 6.1 %collective-permute-done.26 = f32[208,512]{1,0:T(8,128)S(1)} collective-permute-done((f32[208,512]{1,0:T(8,128)S(1)}, f32[208,512]{1,0:T(8,128)S(1)}, u32[]{:S(2)}, u32[]{:S(2)}) %collective-permute-start.26) | collective-permute-done | bytes 426016 | tf_op jit(solution)/shard_map/ppermute | solution.py:55
  166.7 1.3 collective-permute-start.30
  168.0 1.1 collective-permute-start.27
  169.1 3.6 %collective-permute-done.30 = f32[48,512]{1,0:T(8,128)S(1)} collective-permute-done((f32[48,512]{1,0:T(8,128)S(1)}, f32[48,512]{1,0:T(8,128)S(1)}, u32[]{:S(2)}, u32[]{:S(2)}) %collective-permute-start.30) | collective-permute-done | bytes 98336 | tf_op jit(solution)/shard_map/ppermute | solution.py:55
  172.7 1.9 collective-permute-start.31
  174.6 0.9 collective-permute-start.28
  175.5 2.9 %collective-permute-done.31 = f32[96,512]{1,0:T(8,128)S(1)} collective-permute-done((f32[96,512]{1,0:T(8,128)S(1)}, f32[96,512]{1,0:T(8,128)S(1)}, u32[]{:S(2)}, u32[]{:S(2)}) %collective-permute-start.31) | collective-permute-done | bytes 196640 | tf_op jit(solution)/shard_map/ppermute | solution.py:55
  178.5 1.9 collective-permute-start.33
  180.8 1.1 collective-permute-start.34
  181.9 4.8 %collective-permute-done.28 = f32[192,512]{1,0:T(8,128)S(1)} collective-permute-done((f32[192,512]{1,0:T(8,128)S(1)}, f32[192,512]{1,0:T(8,128)S(1)}, u32[]{:S(2)}, u32[]{:S(2)}) %collective-permute-start.28) | collective-permute-done | bytes 393248 | tf_op jit(solution)/shard_map/ppermute | solution.py:55
  186.8 1.4 collective-permute-start.35
  188.3 2.6 %collective-permute-done.33 = f32[96,512]{1,0:T(8,128)S(1)} collective-permute-done((f32[96,512]{1,0:T(8,128)S(1)}, f32[96,512]{1,0:T(8,128)S(1)}, u32[]{:S(2)}, u32[]{:S(2)}) %collective-permute-start.33) | collective-permute-done | bytes 196640 | tf_op jit(solution)/shard_map/ppermute | solution.py:55
  190.9 13.3 %collective-permute-done.34 = f32[448,512]{1,0:T(8,128)S(1)} collective-permute-done((f32[448,512]{1,0:T(8,128)S(1)}, f32[448,512]{1,0:T(8,128)S(1)}, u32[]{:S(2)}, u32[]{:S(2)}) %collective-permute-start.34) | collective-permute-done | bytes 917536 | tf_op jit(solution)/shard_map/ppermute | solution.py:55
  208.8 1.6 collective-permute-start.39
  210.4 1.5 collective-permute-done.37.b_other
  211.9 3.1 %shard_map.399 = (f32[2,512,512]{2,1,0:T(8,128)}, f32[2,256,512]{2,1,0:T(8,128)}, f32[64,1024]{1,0:T(8,128)}, f32[64,512]{1,0:T(8,128)}, f32[32,1024]{1,0:T(8,12...) custom-call(f32[896,512]{1,0:T(8,128)S(1)} %maximum_add_fusion.a_mine, ...), custom_call_target="tpu_custom_call" | custom-call | bytes 1024 | tf_op jit(solution)/shard_map/pallas_call | solution.py:760
  215.1 4.0 %collective-permute-done.38 = f32[192,512]{1,0:T(8,128)S(1)} collective-permute-done((f32[192,512]{1,0:T(8,128)S(1)}, f32[192,512]{1,0:T(8,128)S(1)}, u32[]{:S(2)}, u32[]{:S(2)}) %collective-permute-start.38) | collective-permute-done | bytes 393248 | tf_op jit(solution)/shard_map/ppermute | solution.py:55
  220.3 1.8 collective-permute-done.41.d_other
  222.1 1.1 collective-permute-done.40.c_other
  223.2 3.4 %shard_map.400 = (f32[2,512,512]{2,1,0:T(8,128)}, f32[5,128,512]{2,1,0:T(8,128)}, f32[64,512]{1,0:T(8,128)}, f32[32,512]{1,0:T(8,128)}, f32[3,256]{1,0:T(4,128)}) custom-call(f32[384,512]{1,0:T(8,128)S(1)} %pad_maximum_fusion.5.c_mine, f32[384,512]{1,0:T(8,128)S(1)} %collective-permute-done.40.c_other, f32[384,512]{1,0:T(8,128)S(1)} %pad_maximum_fusion.6.d_mine, ...), custom_call_target="tpu_custom_call" | custom-call | flops 3449999872 | bytes 1024 | tf_op jit(solution)/shard_map/pallas_call | solution.py:760
  (172 shorter events, 20.1 us)
Async XLA Ops:
  0.7 7.9 %copy-start.29 = (s32[240]{0:T(256)S(1)}, s32[240]{0:T(256)}, u32[]{:S(2)}) copy-start(s32[240]{0:T(256)} %param.32) | copy-start | bytes 2884
  0.7 7.9 %copy-start.25 = (s32[240,8]{0,1:T(8,128)S(1)}, s32[240,8]{0,1:T(8,128)}, u32[]{:S(2)}) copy-start(s32[240,8]{0,1:T(8,128)} %param.33) | copy-start | bytes 23044
  0.7 7.9 %copy-start.27 = (s32[240,8]{0,1:T(8,128)S(1)}, s32[240,8]{0,1:T(8,128)}, u32[]{:S(2)}) copy-start(s32[240,8]{0,1:T(8,128)} %param.35) | copy-start | bytes 23044
  0.7 22.9 %copy-start.26 = (s32[240,8]{0,1:T(8,128)S(1)}, s32[240,8]{0,1:T(8,128)}, u32[]{:S(2)}) copy-start(s32[240,8]{0,1:T(8,128)} %param.34) | copy-start | bytes 23044
  0.7 22.9 %copy-start.28 = (s32[240,8]{0,1:T(8,128)S(1)}, s32[240,8]{0,1:T(8,128)}, u32[]{:S(2)}) copy-start(s32[240,8]{0,1:T(8,128)} %param.36) | copy-start | bytes 23044
  0.7 34.5 %copy-start.7 = (bf16[64,512]{1,0:T(8,128)(2,1)S(1)}, bf16[64,512]{1,0:T(8,128)(2,1)}, u32[]{:S(2)}) copy-start(bf16[64,512]{1,0:T(8,128)(2,1)} %trip_up.1) | copy-start | bytes 196612
  0.7 34.5 %copy-start.8 = (bf16[1024,32]{0,1:T(8,128)(2,1)S(1)}, bf16[1024,32]{0,1:T(8,128)(2,1)}, u32[]{:S(2)}) copy-start(bf16[1024,32]{0,1:T(8,128)(2,1)} %param.44) | copy-start | bytes 196612
  0.7 34.5 %copy-start.9 = (bf16[32,512]{1,0:T(8,128)(2,1)S(1)}, bf16[32,512]{1,0:T(8,128)(2,1)}, u32[]{:S(2)}) copy-start(bf16[32,512]{1,0:T(8,128)(2,1)} %quad_up.1) | copy-start | bytes 98308
  5.4 29.8 %copy-start = (bf16[2,512,512]{2,1,0:T(8,128)(2,1)S(1)}, bf16[2,512,512]{2,1,0:T(8,128)(2,1)}, u32[]{:S(2)}) copy-start(bf16[2,512,512]{2,1,0:T(8,128)(2,1)} %w_res.1) | copy-start | bytes 3145732
  5.4 29.8 %copy-start.1 = (bf16[2,256,512]{2,1,0:T(8,128)(2,1)S(1)}, bf16[2,256,512]{2,1,0:T(8,128)(2,1)}, u32[]{:S(2)}) copy-start(bf16[2,256,512]{2,1,0:T(8,128)(2,1)} %w_ae.1) | copy-start | bytes 1572868
  5.5 29.8 %copy-start.2 = (bf16[2,512,256]{2,1,0:T(8,128)(2,1)S(1)}, bf16[2,512,256]{2,1,0:T(8,128)(2,1)}, u32[]{:S(2)}) copy-start(bf16[2,512,256]{2,1,0:T(8,128)(2,1)} %w_ea.1) | copy-start | bytes 1572868
  5.5 29.8 %copy-start.6 = (bf16[1024,64]{0,1:T(8,128)(2,1)S(1)}, bf16[1024,64]{0,1:T(8,128)(2,1)}, u32[]{:S(2)}) copy-start(bf16[1024,64]{0,1:T(8,128)(2,1)} %param.41) | copy-start | bytes 393220
  5.5 29.8 %copy-start.10 = (f32[8,256]{1,0:T(8,128)S(1)}, f32[8,256]{1,0:T(8,128)}, u32[]{:S(2)}) copy-start(f32[8,256]{1,0:T(8,128)} %cot_atoms.1) | copy-start | bytes 24580
  5.5 29.8 %copy-start.11 = (f32[8,256]{1,0:T(8,128)S(1)}, f32[8,256]{1,0:T(8,128)}, u32[]{:S(2)}) copy-start(f32[8,256]{1,0:T(8,128)} %cot_energy.1) | copy-start | bytes 24580
  5.5 29.8 %copy-start.20 = (f32[8,256]{1,0:T(8,128)S(1)}, f32[8,256]{1,0:T(8,128)}, u32[]{:S(2)}) copy-start(f32[8,256]{1,0:T(8,128)} %get-tuple-element.170.tagged) | copy-start | bytes 24580
  5.5 5.5 %collective-permute-start = (f32[17,8,128]{2,1,0:T(8,128)}, f32[17,8,128]{2,1,0:T(8,128)S(1)}, u32[]{:S(2)}, u32[]{:S(2)}) collective-permute-start(f32[17,8,128]{2,1,0:T(8,128)} %get-tuple-element.168), channel_id=1, source_target_pairs={{0,1},{1,0},{2,3},{3,2},{4,5},{5,4},{6,7},{7,6},{8,9},{9,8},{10,11... | collective-permute-start | bytes 208904 | tf_op jit(solution)/shard_map/ppermute | solution.py:36
  11.9 7.5 %collective-permute-start.2 = (f32[2,17,8,128]{3,2,1,0:T(8,128)S(1)}, f32[2,17,8,128]{3,2,1,0:T(8,128)S(1)}, u32[]{:S(2)}, u32[]{:S(2)}) collective-permute-start(f32[2,17,8,128]{3,2,1,0:T(8,128)S(1)} %pad_maximum_fusion.14), channel_id=1, source_target_pairs={{0,24},{8,0},{16,8},{24,16},{1,25},{9,1},{17,9},{25,17},{2,26},{10... | collective-permute-start | bytes 417800 | tf_op jit(solution)/shard_map/ppermute | solution.py:31
  16.1 6.9 %collective-permute-start.1 = (f32[2,17,8,128]{3,2,1,0:T(8,128)S(1)}, f32[2,17,8,128]{3,2,1,0:T(8,128)S(1)}, u32[]{:S(2)}, u32[]{:S(2)}) collective-permute-start(f32[2,17,8,128]{3,2,1,0:T(8,128)S(1)} %pad_maximum_fusion.14), channel_id=1, source_target_pairs={{0,8},{8,16},{16,24},{24,0},{1,9},{9,17},{17,25},{25,1},{2,10},{10... | collective-permute-start | bytes 417800 | tf_op jit(solution)/shard_map/ppermute | solution.py:31
  23.0 8.9 %collective-permute-start.4 = (f32[6,17,8,128]{3,2,1,0:T(8,128)S(1)}, f32[6,17,8,128]{3,2,1,0:T(8,128)}, u32[]{:S(2)}, u32[]{:S(2)}) collective-permute-start(f32[6,17,8,128]{3,2,1,0:T(8,128)S(1)} %pad_maximum_fusion.8.halo_here), channel_id=1, source_target_pairs={{0,6},{2,0},{4,2},{6,4},{1,7},{3,1},{5,3},{7,5},{8,14},{10,8},{12,... | collective-permute-start | bytes 1253384 | tf_op jit(solution)/shard_map/ppermute | solution.py:31
  23.1 12.1 %collective-permute-start.3 = (f32[6,17,8,128]{3,2,1,0:T(8,128)S(1)}, f32[6,17,8,128]{3,2,1,0:T(8,128)}, u32[]{:S(2)}, u32[]{:S(2)}) collective-permute-start(f32[6,17,8,128]{3,2,1,0:T(8,128)S(1)} %pad_maximum_fusion.8.halo_here), channel_id=1, source_target_pairs={{0,2},{2,4},{4,6},{6,0},{1,3},{3,5},{5,7},{7,1},{8,10},{10,12},{12... | collective-permute-start | bytes 1253384 | tf_op jit(solution)/shard_map/ppermute | solution.py:31
  65.2 1.1 copy-start.21
  65.2 4.2 %collective-permute-start.5 = (f32[896,512]{1,0:T(8,128)}, f32[896,512]{1,0:T(8,128)}, u32[]{:S(2)}, u32[]{:S(2)}) collective-permute-start(f32[896,512]{1,0:T(8,128)} %get-tuple-element.179), channel_id=1, source_target_pairs={{0,2},{2,0},{1,3},{3,1},{4,6},{6,4},{5,7},{7,5},{8,10},{10,8},{9,1... | collective-permute-start | bytes 5505032 | tf_op jit(solution)/shard_map/ppermute | solution.py:55
  66.3 6.5 %collective-permute-start.6 = (f32[768,512]{1,0:T(8,128)S(1)}, f32[768,512]{1,0:T(8,128)}, u32[]{:S(2)}, u32[]{:S(2)}) collective-permute-start(f32[768,512]{1,0:T(8,128)S(1)} %get-tuple-element.184), channel_id=1, source_target_pairs={{0,2},{2,0},{1,3},{3,1},{4,6},{6,4},{5,7},{7,5},{8,10},{10,8},{9,1... | collective-permute-start | bytes 4718600 | tf_op jit(solution)/shard_map/ppermute | solution.py:55
  69.5 5.2 %copy-start.17 = (f32[30,8,8,128]{3,2,1,0:T(8,128)S(1)}, f32[30,8,8,128]{3,2,1,0:T(8,128)}, u32[]{:S(2)}) copy-start(f32[30,8,8,128]{3,2,1,0:T(8,128)} %copy-done.16) | copy-start | bytes 2949124
  71.2 3.4 %copy-start.13 = (f32[240,2048]{1,0:T(8,128)S(1)}, f32[240,2048]{1,0:T(8,128)}, u32[]{:S(2)}) copy-start(f32[240,2048]{1,0:T(8,128)} %get-tuple-element.188.sums) | copy-start | bytes 5898244
  71.2 22.4 %collective-permute-start.7 = (f32[448,512]{1,0:T(8,128)S(1)}, f32[448,512]{1,0:T(8,128)S(1)}, u32[]{:S(2)}, u32[]{:S(2)}) collective-permute-start(f32[448,512]{1,0:T(8,128)S(1)} %dynamic-slice_add_fusion.1), channel_id=1, source_target_pairs={{0,1},{1,0},{2,3},{3,2},{4,5},{5,4},{6,7},{7,6},{8,9},{9,8},{10,11... | collective-permute-start | bytes 2752520 | tf_op jit(solution)/shard_map/ppermute | solution.py:55
  74.1 20.5 %collective-permute-start.8 = (f32[384,512]{1,0:T(8,128)S(1)}, f32[384,512]{1,0:T(8,128)S(1)}, u32[]{:S(2)}, u32[]{:S(2)}) collective-permute-start(f32[384,512]{1,0:T(8,128)S(1)} %dynamic-slice_add_fusion.3), channel_id=1, source_target_pairs={{0,4},{4,0},{1,5},{5,1},{2,6},{6,2},{3,7},{7,3},{8,12},{12,8},{9,1... | collective-permute-start | bytes 2359304 | tf_op jit(solution)/shard_map/ppermute | solution.py:55
  80.4 3.4 %copy-start.19 = (f32[16,16,128]{2,1,0:T(8,128)}, f32[16,16,128]{2,1,0:T(8,128)S(1)}, u32[]{:S(2)}) copy-start(f32[16,16,128]{2,1,0:T(8,128)S(1)} %get-tuple-element.190.back_local) | copy-start | bytes 393220
  80.5 2.0 copy-start.22
  80.5 20.6 %collective-permute-start.9 = (f32[6,16,8,128]{3,2,1,0:T(8,128)S(1)}, f32[6,16,8,128]{3,2,1,0:T(8,128)S(1)}, u32[]{:S(2)}, u32[]{:S(2)}) collective-permute-start(f32[6,16,8,128]{3,2,1,0:T(8,128)S(1)} %get-tuple-element.203), channel_id=1, source_target_pairs={{0,6},{2,0},{4,2},{6,4},{1,7},{3,1},{5,3},{7,5},{8,14},{10,8},{12,... | collective-permute-start | bytes 1179656 | tf_op jit(solution)/shard_map/ppermute | solution.py:31
  81.1 19.9 %collective-permute-start.10 = (f32[6,16,8,128]{3,2,1,0:T(8,128)S(1)}, f32[6,16,8,128]{3,2,1,0:T(8,128)S(1)}, u32[]{:S(2)}, u32[]{:S(2)}) collective-permute-start(f32[6,16,8,128]{3,2,1,0:T(8,128)S(1)} %get-tuple-element.204), channel_id=1, source_target_pairs={{0,2},{2,4},{4,6},{6,0},{1,3},{3,5},{5,7},{7,1},{8,10},{10,12},{12... | collective-permute-start | bytes 1179656 | tf_op jit(solution)/shard_map/ppermute | solution.py:31
  93.7 17.9 %collective-permute-start.11 = (f32[224,512]{1,0:T(8,128)S(1)}, f32[224,512]{1,0:T(8,128)S(1)}, u32[]{:S(2)}, u32[]{:S(2)}) collective-permute-start(f32[224,512]{1,0:T(8,128)S(1)} %dynamic-slice_add_fusion.5), channel_id=1, source_target_pairs={{0,4},{4,0},{1,5},{5,1},{2,6},{6,2},{3,7},{7,3},{8,12},{12,8},{9,1... | collective-permute-start | bytes 1376264 | tf_op jit(solution)/shard_map/ppermute | solution.py:55
  94.6 10.4 %collective-permute-start.12 = (f32[192,512]{1,0:T(8,128)S(1)}, f32[192,512]{1,0:T(8,128)S(1)}, u32[]{:S(2)}, u32[]{:S(2)}) collective-permute-start(f32[192,512]{1,0:T(8,128)S(1)} %dynamic-slice_add_fusion.13), channel_id=1, source_target_pairs={{0,1},{1,0},{2,3},{3,2},{4,5},{5,4},{6,7},{7,6},{8,9},{9,8},{10,11... | collective-permute-start | bytes 1179656 | tf_op jit(solution)/shard_map/ppermute | solution.py:55
  101.1 10.8 %collective-permute-start.14 = (f32[2,16,8,128]{3,2,1,0:T(8,128)S(1)}, f32[2,16,8,128]{3,2,1,0:T(8,128)S(1)}, u32[]{:S(2)}, u32[]{:S(2)}) collective-permute-start(f32[2,16,8,128]{3,2,1,0:T(8,128)S(1)} %get-tuple-element.343), channel_id=1, source_target_pairs={{0,8},{8,16},{16,24},{24,0},{1,9},{9,17},{17,25},{25,1},{2,10},{10... | collective-permute-start | bytes 393224 | tf_op jit(solution)/shard_map/ppermute | solution.py:31
  101.6 10.3 %collective-permute-start.13 = (f32[2,16,8,128]{3,2,1,0:T(8,128)S(1)}, f32[2,16,8,128]{3,2,1,0:T(8,128)S(1)}, u32[]{:S(2)}, u32[]{:S(2)}) collective-permute-start(f32[2,16,8,128]{3,2,1,0:T(8,128)S(1)} %get-tuple-element.344), channel_id=1, source_target_pairs={{0,24},{8,0},{16,8},{24,16},{1,25},{9,1},{17,9},{25,17},{2,26},{10... | collective-permute-start | bytes 393224 | tf_op jit(solution)/shard_map/ppermute | solution.py:31
  112.0 4.3 %collective-permute-start.15 = (f32[16,8,128]{2,1,0:T(8,128)S(1)}, f32[16,8,128]{2,1,0:T(8,128)S(1)}, u32[]{:S(2)}, u32[]{:S(2)}) collective-permute-start(f32[16,8,128]{2,1,0:T(8,128)S(1)} %select_bitcast_fusion.2), channel_id=1, source_target_pairs={{0,1},{1,0},{2,3},{3,2},{4,5},{5,4},{6,7},{7,6},{8,9},{9,8},{10,11... | collective-permute-start | bytes 196616 | tf_op jit(solution)/shard_map/ppermute | solution.py:885
  112.7 11.0 %collective-permute-start.16 = (f32[208,512]{1,0:T(8,128)S(1)}, f32[208,512]{1,0:T(8,128)S(1)}, u32[]{:S(2)}, u32[]{:S(2)}) collective-permute-start(f32[208,512]{1,0:T(8,128)S(1)} %dynamic-slice_add_fusion.7), channel_id=1, source_target_pairs={{0,8},{8,0},{16,24},{24,16},{1,9},{9,1},{17,25},{25,17},{2,10},{10... | collective-permute-start | bytes 1277960 | tf_op jit(solution)/shard_map/ppermute | solution.py:55
  123.7 5.5 %copy-start.23 = (f32[384,512]{1,0:T(8,128)S(1)}, f32[384,512]{1,0:T(8,128)}, u32[]{:S(2)}) copy-start(f32[384,512]{1,0:T(8,128)} %get-tuple-element.247) | copy-start | bytes 2359300
  123.8 13.3 %copy-start.24 = (f32[384,512]{1,0:T(8,128)S(1)}, f32[384,512]{1,0:T(8,128)}, u32[]{:S(2)}) copy-start(f32[384,512]{1,0:T(8,128)} %get-tuple-element.243) | copy-start | bytes 2359300
  123.9 2.9 %collective-permute-start.17 = (f32[384,512]{1,0:T(8,128)}, f32[384,512]{1,0:T(8,128)S(1)}, u32[]{:S(2)}, u32[]{:S(2)}) collective-permute-start(f32[384,512]{1,0:T(8,128)} %get-tuple-element.234), channel_id=1, source_target_pairs={{0,2},{2,0},{1,3},{3,1},{4,6},{6,4},{5,7},{7,5},{8,10},{10,8},{9,1... | collective-permute-start | bytes 2359304 | tf_op jit(solution)/shard_map/ppermute | solution.py:55
  123.9 5.3 %collective-permute-start.18 = (f32[384,512]{1,0:T(8,128)}, f32[384,512]{1,0:T(8,128)}, u32[]{:S(2)}, u32[]{:S(2)}) collective-permute-start(f32[384,512]{1,0:T(8,128)} %get-tuple-element.238), channel_id=1, source_target_pairs={{0,2},{2,0},{1,3},{3,1},{4,6},{6,4},{5,7},{7,5},{8,10},{10,8},{9,1... | collective-permute-start | bytes 2359304 | tf_op jit(solution)/shard_map/ppermute | solution.py:55
  124.4 12.5 %collective-permute-start.19 = (f32[104,512]{1,0:T(8,128)S(1)}, f32[104,512]{1,0:T(8,128)S(1)}, u32[]{:S(2)}, u32[]{:S(2)}) collective-permute-start(f32[104,512]{1,0:T(8,128)S(1)} %dynamic-slice_add_fusion.15), channel_id=1, source_target_pairs={{0,16},{8,24},{16,0},{24,8},{1,17},{9,25},{17,1},{25,9},{2,18},{10... | collective-permute-start | bytes 638984 | tf_op jit(solution)/shard_map/ppermute | solution.py:55
  128.6 11.4 %collective-permute-start.20 = (f32[192,512]{1,0:T(8,128)}, f32[192,512]{1,0:T(8,128)S(1)}, u32[]{:S(2)}, u32[]{:S(2)}) collective-permute-start(f32[192,512]{1,0:T(8,128)} %dynamic-slice_add_fusion.11), channel_id=1, source_target_pairs={{0,1},{1,0},{2,3},{3,2},{4,5},{5,4},{6,7},{7,6},{8,9},{9,8},{10,11... | collective-permute-start | bytes 1179656 | tf_op jit(solution)/shard_map/ppermute | solution.py:55
  131.1 11.2 %collective-permute-start.21 = (f32[192,512]{1,0:T(8,128)}, f32[192,512]{1,0:T(8,128)}, u32[]{:S(2)}, u32[]{:S(2)}) collective-permute-start(f32[192,512]{1,0:T(8,128)} %dynamic-slice_add_fusion.10), channel_id=1, source_target_pairs={{0,4},{4,0},{1,5},{5,1},{2,6},{6,2},{3,7},{7,3},{8,12},{12,8},{9,1... | collective-permute-start | bytes 1179656 | tf_op jit(solution)/shard_map/ppermute | solution.py:55
  137.0 12.6 %collective-permute-start.24 = (f32[104,512]{1,0:T(8,128)S(1)}, f32[104,512]{1,0:T(8,128)S(1)}, u32[]{:S(2)}, u32[]{:S(2)}) collective-permute-start(f32[104,512]{1,0:T(8,128)S(1)} %add.320), channel_id=1, source_target_pairs={{0,16},{8,24},{16,0},{24,8},{1,17},{9,25},{17,1},{25,9},{2,18},{10... | collective-permute-start | bytes 638984 | tf_op jit(solution)/shard_map/ppermute | solution.py:55
  140.0 6.4 %collective-permute-start.22 = (f32[96,512]{1,0:T(8,128)S(1)}, f32[96,512]{1,0:T(8,128)S(1)}, u32[]{:S(2)}, u32[]{:S(2)}) collective-permute-start(f32[96,512]{1,0:T(8,128)S(1)} %dynamic-slice_add_fusion.21), channel_id=1, source_target_pairs={{0,4},{4,0},{1,5},{5,1},{2,6},{6,2},{3,7},{7,3},{8,12},{12,8},{9,1... | collective-permute-start | bytes 589832 | tf_op jit(solution)/shard_map/ppermute | solution.py:55
  143.3 5.8 %collective-permute-start.23 = (f32[96,512]{1,0:T(8,128)S(1)}, f32[96,512]{1,0:T(8,128)S(1)}, u32[]{:S(2)}, u32[]{:S(2)}) collective-permute-start(f32[96,512]{1,0:T(8,128)S(1)} %dynamic-slice_add_fusion.20), channel_id=1, source_target_pairs={{0,1},{1,0},{2,3},{3,2},{4,5},{5,4},{6,7},{7,6},{8,9},{9,8},{10,11... | collective-permute-start | bytes 589832 | tf_op jit(solution)/shard_map/ppermute | solution.py:55
  149.2 9.0 %collective-permute-start.25 = (f32[96,512]{1,0:T(8,128)S(1)}, f32[96,512]{1,0:T(8,128)S(1)}, u32[]{:S(2)}, u32[]{:S(2)}) collective-permute-start(f32[96,512]{1,0:T(8,128)S(1)} %dynamic-slice_add_fusion.17), channel_id=1, source_target_pairs={{0,8},{8,0},{16,24},{24,16},{1,9},{9,1},{17,25},{25,17},{2,10},{10... | collective-permute-start | bytes 589832 | tf_op jit(solution)/shard_map/ppermute | solution.py:55
  149.7 15.6 %collective-permute-start.26 = (f32[208,512]{1,0:T(8,128)S(1)}, f32[208,512]{1,0:T(8,128)S(1)}, u32[]{:S(2)}, u32[]{:S(2)}) collective-permute-start(f32[208,512]{1,0:T(8,128)S(1)} %pad_maximum_fusion.7), channel_id=1, source_target_pairs={{0,8},{8,0},{16,24},{24,16},{1,9},{9,1},{17,25},{25,17},{2,10},{10... | collective-permute-start | bytes 1277960 | tf_op jit(solution)/shard_map/ppermute | solution.py:55
  158.2 7.3 %collective-permute-start.29 = (f32[48,512]{1,0:T(8,128)S(1)}, f32[48,512]{1,0:T(8,128)S(1)}, u32[]{:S(2)}, u32[]{:S(2)}) collective-permute-start(f32[48,512]{1,0:T(8,128)S(1)} %dynamic-slice_add_fusion.23), channel_id=1, source_target_pairs={{0,16},{8,24},{16,0},{24,8},{1,17},{9,25},{17,1},{25,9},{2,18},{10... | collective-permute-start | bytes 294920 | tf_op jit(solution)/shard_map/ppermute | solution.py:55
  166.7 6.0 %collective-permute-start.30 = (f32[48,512]{1,0:T(8,128)S(1)}, f32[48,512]{1,0:T(8,128)S(1)}, u32[]{:S(2)}, u32[]{:S(2)}) collective-permute-start(f32[48,512]{1,0:T(8,128)S(1)} %add_add_fusion.2), channel_id=1, source_target_pairs={{0,16},{8,24},{16,0},{24,8},{1,17},{9,25},{17,1},{25,9},{2,18},{10... | collective-permute-start | bytes 294920 | tf_op jit(solution)/shard_map/ppermute | solution.py:55
  168.0 12.6 %collective-permute-start.27 = (f32[224,512]{1,0:T(8,128)S(1)}, f32[224,512]{1,0:T(8,128)S(1)}, u32[]{:S(2)}, u32[]{:S(2)}) collective-permute-start(f32[224,512]{1,0:T(8,128)S(1)} %fusion), channel_id=1, source_target_pairs={{0,4},{4,0},{1,5},{5,1},{2,6},{6,2},{3,7},{7,3},{8,12},{12,8},{9,1... | collective-permute-start | bytes 1376264 | tf_op jit(solution)/shard_map/ppermute | solution.py:55
  172.7 5.7 %collective-permute-start.31 = (f32[96,512]{1,0:T(8,128)S(1)}, f32[96,512]{1,0:T(8,128)S(1)}, u32[]{:S(2)}, u32[]{:S(2)}) collective-permute-start(f32[96,512]{1,0:T(8,128)S(1)} %pad_maximum_fusion.13), channel_id=1, source_target_pairs={{0,8},{8,0},{16,24},{24,16},{1,9},{9,1},{17,25},{25,17},{2,10},{10... | collective-permute-start | bytes 589832 | tf_op jit(solution)/shard_map/ppermute | solution.py:55
  174.6 12.0 %collective-permute-start.28 = (f32[192,512]{1,0:T(8,128)S(1)}, f32[192,512]{1,0:T(8,128)S(1)}, u32[]{:S(2)}, u32[]{:S(2)}) collective-permute-start(f32[192,512]{1,0:T(8,128)S(1)} %slice.49), channel_id=1, source_target_pairs={{0,1},{1,0},{2,3},{3,2},{4,5},{5,4},{6,7},{7,6},{8,9},{9,8},{10,11... | collective-permute-start | bytes 1179656 | tf_op jit(solution)/shard_map/ppermute | solution.py:55
  178.5 12.4 %collective-permute-start.33 = (f32[96,512]{1,0:T(8,128)S(1)}, f32[96,512]{1,0:T(8,128)S(1)}, u32[]{:S(2)}, u32[]{:S(2)}) collective-permute-start(f32[96,512]{1,0:T(8,128)S(1)} %get-tuple-element.285), channel_id=1, source_target_pairs={{0,1},{1,0},{2,3},{3,2},{4,5},{5,4},{6,7},{7,6},{8,9},{9,8},{10,11... | collective-permute-start | bytes 589832 | tf_op jit(solution)/shard_map/ppermute | solution.py:55
  180.3 7.9 %collective-permute-start.32 = (f32[96,512]{1,0:T(8,128)S(1)}, f32[96,512]{1,0:T(8,128)S(1)}, u32[]{:S(2)}, u32[]{:S(2)}) collective-permute-start(f32[96,512]{1,0:T(8,128)S(1)} %get-tuple-element.283), channel_id=1, source_target_pairs={{0,4},{4,0},{1,5},{5,1},{2,6},{6,2},{3,7},{7,3},{8,12},{12,8},{9,1... | collective-permute-start | bytes 589832 | tf_op jit(solution)/shard_map/ppermute | solution.py:55
  180.8 23.5 %collective-permute-start.34 = (f32[448,512]{1,0:T(8,128)S(1)}, f32[448,512]{1,0:T(8,128)S(1)}, u32[]{:S(2)}, u32[]{:S(2)}) collective-permute-start(f32[448,512]{1,0:T(8,128)S(1)} %pad_maximum_fusion.1), channel_id=1, source_target_pairs={{0,1},{1,0},{2,3},{3,2},{4,5},{5,4},{6,7},{7,6},{8,9},{9,8},{10,11... | collective-permute-start | bytes 2752520 | tf_op jit(solution)/shard_map/ppermute | solution.py:55
  186.8 19.1 %collective-permute-start.35 = (f32[384,512]{1,0:T(8,128)S(1)}, f32[384,512]{1,0:T(8,128)S(1)}, u32[]{:S(2)}, u32[]{:S(2)}) collective-permute-start(f32[384,512]{1,0:T(8,128)S(1)} %pad_maximum_fusion.4), channel_id=1, source_target_pairs={{0,4},{4,0},{1,5},{5,1},{2,6},{6,2},{3,7},{7,3},{8,12},{12,8},{9,1... | collective-permute-start | bytes 2359304 | tf_op jit(solution)/shard_map/ppermute | solution.py:55
  205.8 6.1 %collective-permute-start.36 = (f32[896,512]{1,0:T(8,128)S(1)}, f32[896,512]{1,0:T(8,128)S(1)}, u32[]{:S(2)}, u32[]{:S(2)}) collective-permute-start(f32[896,512]{1,0:T(8,128)S(1)} %maximum_add_fusion.a_mine), channel_id=1, source_target_pairs={{0,2},{2,0},{1,3},{3,1},{4,6},{6,4},{5,7},{7,5},{8,10},{10,8},{9,1... | collective-permute-start | bytes 5505032 | tf_op jit(solution)/shard_map/ppermute | solution.py:55
  207.4 4.5 %collective-permute-start.37 = (f32[768,512]{1,0:T(8,128)S(1)}, f32[768,512]{1,0:T(8,128)S(1)}, u32[]{:S(2)}, u32[]{:S(2)}) collective-permute-start(f32[768,512]{1,0:T(8,128)S(1)} %maximum_add_fusion.1.b_mine), channel_id=1, source_target_pairs={{0,2},{2,0},{1,3},{3,1},{4,6},{6,4},{5,7},{7,5},{8,10},{10,8},{9,1... | collective-permute-start | bytes 4718600 | tf_op jit(solution)/shard_map/ppermute | solution.py:55
  208.0 11.1 %collective-permute-start.38 = (f32[192,512]{1,0:T(8,128)S(1)}, f32[192,512]{1,0:T(8,128)S(1)}, u32[]{:S(2)}, u32[]{:S(2)}) collective-permute-start(f32[192,512]{1,0:T(8,128)S(1)} %pad_maximum_fusion.11), channel_id=1, source_target_pairs={{0,1},{1,0},{2,3},{3,2},{4,5},{5,4},{6,7},{7,6},{8,9},{9,8},{10,11... | collective-permute-start | bytes 1179656 | tf_op jit(solution)/shard_map/ppermute | solution.py:55
  208.8 10.8 %collective-permute-start.39 = (f32[192,512]{1,0:T(8,128)S(1)}, f32[192,512]{1,0:T(8,128)S(1)}, u32[]{:S(2)}, u32[]{:S(2)}) collective-permute-start(f32[192,512]{1,0:T(8,128)S(1)} %pad_maximum_fusion.12), channel_id=1, source_target_pairs={{0,4},{4,0},{1,5},{5,1},{2,6},{6,2},{3,7},{7,3},{8,12},{12,8},{9,1... | collective-permute-start | bytes 1179656 | tf_op jit(solution)/shard_map/ppermute | solution.py:55
  219.8 2.4 %collective-permute-start.41 = (f32[384,512]{1,0:T(8,128)S(1)}, f32[384,512]{1,0:T(8,128)S(1)}, u32[]{:S(2)}, u32[]{:S(2)}) collective-permute-start(f32[384,512]{1,0:T(8,128)S(1)} %pad_maximum_fusion.6.d_mine), channel_id=1, source_target_pairs={{0,2},{2,0},{1,3},{3,1},{4,6},{6,4},{5,7},{7,5},{8,10},{10,8},{9,1... | collective-permute-start | bytes 2359304 | tf_op jit(solution)/shard_map/ppermute | solution.py:55
  219.8 3.4 %collective-permute-start.40 = (f32[384,512]{1,0:T(8,128)S(1)}, f32[384,512]{1,0:T(8,128)S(1)}, u32[]{:S(2)}, u32[]{:S(2)}) collective-permute-start(f32[384,512]{1,0:T(8,128)S(1)} %pad_maximum_fusion.5.c_mine), channel_id=1, source_target_pairs={{0,2},{2,0},{1,3},{3,1},{4,6},{6,4},{5,7},{7,5},{8,10},{10,8},{9,1... | collective-permute-start | bytes 2359304 | tf_op jit(solution)/shard_map/ppermute | solution.py:55
  (8 other events, 7.9 us)

commit v9 on v8

--- a/solution.py
+++ b/solution.py
@@ -847,7 +847,7 @@
             pltpu.VMEM((EDGES, 128), F32),
             pltpu.VMEM((1792, 512), F32),
         ],
-        micros=26, room=44,
+        micros=26, room=50,
     )
     chain = Chain()
     got_a = swap(send_a, "gyl", 0)
@@ -892,7 +892,7 @@
         [back_local, returned, grad_edges, grad_tag, edge_states, radial, columns, pre, downs, rads,
          tag_row, send_row, w_inputs, trip_down_t, quad_down_t, core],
         scratch=[pltpu.VMEM((768, 512), F32)] * 2,
-        micros=7, room=58,
+        micros=7, room=50,
     )
     next(late)
     send_c, send_d = chain.after((send_c, send_d))

time: 228 us -> 230 us (level)
    unnamed x61 -> x67, local copies, waits for them, and re-layouts: 6.03 us -> 5.24 us
  transfers between devices with their start and end apart: 42 -> 42, of which waited for: 28 -> 28; matrix products, arithmetic and copies ran while one was open for 9% -> 8% of each run, Pallas kernels for 7% -> 7%
where the time goes in v9:
time: 230 us; the launch traced here: 229 us
  waiting for transfers between devices  108 us (47%)
  Pallas kernels  49 us (21%)
  starting transfers between devices  41.3 us (18%)
  other arithmetic  17.1 us (7%)
  local copies, waits for them, and re-layouts  9.71 us (4%)
  between operations  3.72 us (2%)
    ppermute x32, waiting for transfers between devices, swap(): return lax.ppermute(value, axis, [(i, i ^ 1 << bit) for i in range(count)])  79.7 us
    pallas_call x7, Pallas kernels, call(): pl.pallas_call(kernel, out_shape=[jax.ShapeDtypeStruct(shape, F32) for sh...  49 us
    ppermute x32, starting transfers between devices, swap(): return lax.ppermute(value, axis, [(i, i ^ 1 << bit) for i in range(count)])  28.1 us
    ppermute x8, waiting for transfers between devices, shifted(): return lax.ppermute(value, axis, pairs)  22.9 us
    add x24, other arithmetic, part(): total = total + lax.dynamic_slice_in_dim(x, at, size)  12.2 us
    ppermute x8, starting transfers between devices, shifted(): return lax.ppermute(value, axis, pairs)  9.37 us
    unnamed x67, local copies, waits for them, and re-layouts  5.24 us
  transfers between devices with their start and end apart: 42, of which 28 were waited for; matrix products, arithmetic and copies ran while one was open for 8% of the time, Pallas kernels for 7%

profile of v9, /device:TPU:0, one launch (start us, length us, event | category | flops | bytes accessed | tf_op | source)
XLA Modules:
  0.0 228.8 jit_solution(4025394432568228144)
XLA Ops:
  0.7 4.6 %shard_map.394 = (f32[17,8,128]{2,1,0:T(8,128)}, f32[17,16,128]{2,1,0:T(8,128)}, f32[8,256]{1,0:T(8,128)}, f32[2,240,512]{2,1,0:T(8,128)}, f32[240,128]{1,0:T(8,...) custom-call(f32[240,512]{1,0:T(8,128)} %edge.5, f32[3,240]{1,0:T(4,128)} %vec.1, ...), custom_call_target="tpu_custom_call" | custom-call | flops 5750000128 | bytes 1024 | tf_op jit(solution)/shard_map/pallas_call | solution.py:760
  5.5 3.0 %collective-permute-start = (f32[17,8,128]{2,1,0:T(8,128)}, f32[17,8,128]{2,1,0:T(8,128)S(1)}, u32[]{:S(2)}, u32[]{:S(2)}) collective-permute-start(f32[17,8,128]{2,1,0:T(8,128)} %get-tuple-element.168), channel_id=1, source_target_pairs={{0,1},{1,0},{2,3},{3,2},{4,5},{5,4},{6,7},{7,6},{8,9},{9,8},{10,11... | collective-permute-start | bytes 208904 | tf_op jit(solution)/shard_map/ppermute | solution.py:36
  8.7 2.3 %collective-permute-done = f32[17,8,128]{2,1,0:T(8,128)S(1)} collective-permute-done((f32[17,8,128]{2,1,0:T(8,128)}, f32[17,8,128]{2,1,0:T(8,128)S(1)}, u32[]{:S(2)}, u32[]{:S(2)}) %collective-permute-start) | collective-permute-done | bytes 69664 | tf_op jit(solution)/shard_map/ppermute | solution.py:36
  11.0 0.9 select_bitcast_fusion.1
  11.9 4.2 %collective-permute-start.2 = (f32[2,17,8,128]{3,2,1,0:T(8,128)S(1)}, f32[2,17,8,128]{3,2,1,0:T(8,128)S(1)}, u32[]{:S(2)}, u32[]{:S(2)}) collective-permute-start(f32[2,17,8,128]{3,2,1,0:T(8,128)S(1)} %pad_maximum_fusion.14), channel_id=1, source_target_pairs={{0,24},{8,0},{16,8},{24,16},{1,25},{9,1},{17,9},{25,17},{2,26},{10... | collective-permute-start | bytes 417800 | tf_op jit(solution)/shard_map/ppermute | solution.py:31
  16.1 3.3 %collective-permute-done.2 = f32[2,17,8,128]{3,2,1,0:T(8,128)S(1)} collective-permute-done((f32[2,17,8,128]{3,2,1,0:T(8,128)S(1)}, f32[2,17,8,128]{3,2,1,0:T(8,128)S(1)}, u32[]{:S(2)}, u32[]{:S(2)}) %collective-permute-start.2) | collective-permute-done | bytes 139296 | tf_op jit(solution)/shard_map/ppermute | solution.py:31
  19.4 3.6 %collective-permute-done.1 = f32[2,17,8,128]{3,2,1,0:T(8,128)S(1)} collective-permute-done((f32[2,17,8,128]{3,2,1,0:T(8,128)S(1)}, f32[2,17,8,128]{3,2,1,0:T(8,128)S(1)}, u32[]{:S(2)}, u32[]{:S(2)}) %collective-permute-start.1) | collective-permute-done | bytes 139296 | tf_op jit(solution)/shard_map/ppermute | solution.py:31
  24.0 7.9 %collective-permute-done.4.halo_after = f32[6,17,8,128]{3,2,1,0:T(8,128)S(1)} collective-permute-done((f32[6,17,8,128]{3,2,1,0:T(8,128)S(1)}, f32[6,17,8,128]{3,2,1,0:T(8,128)S(1)}, u32[]{:S(2)}, u32[]{:S(2)}) %collective-permute-start.4) | collective-permute-done | bytes 417824 | tf_op jit(solution)/shard_map/ppermute | solution.py:31
  31.9 3.2 %collective-permute-done.3.halo_before = f32[6,17,8,128]{3,2,1,0:T(8,128)S(1)} collective-permute-done((f32[6,17,8,128]{3,2,1,0:T(8,128)S(1)}, f32[6,17,8,128]{3,2,1,0:T(8,128)S(1)}, u32[]{:S(2)}, u32[]{:S(2)}) %collective-permute-start.3) | collective-permute-done | bytes 417824 | tf_op jit(solution)/shard_map/ppermute | solution.py:31
  35.1 24.9 %shard_map.395 = (f32[8,256]{1,0:T(8,128)}, f32[240,512]{1,0:T(8,128)}, f32[8,256]{1,0:T(8,128)}, f32[240,512]{1,0:T(8,128)S(1)}, f32[8,256]{1,0:T(8,128)S(1)}, ...) custom-call(f32[6,17,8,128]{3,2,1,0:T(8,128)S(1)} %collective-permut, ...), custom_call_target="tpu_custom_call" | custom-call | flops 29899999232 | bytes 1024 | tf_op jit(solution)/shard_map/pallas_call | solution.py:760
  60.1 1.5 copy-done.12
  61.6 1.0 shard_map.396
  63.9 1.4 concatenate.74
  65.3 0.9 fusion.3
  66.4 1.7 dynamic-slice_add_fusion.1
  68.2 1.6 collective-permute-start.7
  69.7 1.3 dynamic-slice_add_fusion.3
  71.6 5.8 %shard_map.397 = (f32[6,16,8,128]{3,2,1,0:T(8,128)S(1)}, f32[6,16,8,128]{3,2,1,0:T(8,128)S(1)}, f32[6,16,8,128]{3,2,1,0:T(8,128)S(1)}, f32[16,16,128]{2,1,0:T(8,128)S(1)}) custom-call(f32[30,8,8,128]{3,2,1,0:T(8,128)S(1)} %copy-done.19, f32[240,2048]{1,0:T(8,128)S(1)} %copy-done.15, f32[240,256]{1,0:T(8,128)S(1)} %get-tuple-element.189.grad_src, ...), custom_call_target="tpu_custom_call" | custom-call | flops 14949999616 | bytes 1024 | tf_op jit(solution)/shard_map/pallas_call | solution.py:760
  78.2 1.3 dynamic-slice_add_fusion.2
  79.4 1.4 dynamic-slice_add_fusion
  80.8 9.8 %collective-permute-done.7 = f32[448,512]{1,0:T(8,128)S(1)} collective-permute-done((f32[448,512]{1,0:T(8,128)S(1)}, f32[448,512]{1,0:T(8,128)S(1)}, u32[]{:S(2)}, u32[]{:S(2)}) %collective-permute-start.7) | collective-permute-done | bytes 917536 | tf_op jit(solution)/shard_map/ppermute | solution.py:55
  91.5 1.4 collective-permute-start.12
  93.0 4.9 %collective-permute-done.9 = f32[6,16,8,128]{3,2,1,0:T(8,128)S(1)} collective-permute-done((f32[6,16,8,128]{3,2,1,0:T(8,128)S(1)}, f32[6,16,8,128]{3,2,1,0:T(8,128)S(1)}, u32[]{:S(2)}, u32[]{:S(2)}) %collective-permute-start.9) | collective-permute-done | bytes 393248 | tf_op jit(solution)/shard_map/ppermute | solution.py:31
  98.5 3.4 %collective-permute-start.13 = (f32[2,16,8,128]{3,2,1,0:T(8,128)S(1)}, f32[2,16,8,128]{3,2,1,0:T(8,128)S(1)}, u32[]{:S(2)}, u32[]{:S(2)}) collective-permute-start(f32[2,16,8,128]{3,2,1,0:T(8,128)S(1)} %get-tuple-element.344), channel_id=1, source_target_pairs={{0,24},{8,0},{16,8},{24,16},{1,25},{9,1},{17,9},{25,17},{2,26},{10... | collective-permute-start | bytes 393224 | tf_op jit(solution)/shard_map/ppermute | solution.py:31
  101.9 6.7 %collective-permute-done.11 = f32[224,512]{1,0:T(8,128)S(1)} collective-permute-done((f32[224,512]{1,0:T(8,128)S(1)}, f32[224,512]{1,0:T(8,128)S(1)}, u32[]{:S(2)}, u32[]{:S(2)}) %collective-permute-start.11) | collective-permute-done | bytes 458784 | tf_op jit(solution)/shard_map/ppermute | solution.py:55
  108.8 0.8 dynamic-slice_add_fusion.7
  109.6 0.8 dynamic-slice_add_fusion.6
  111.7 3.2 %collective-permute-done.15 = f32[16,8,128]{2,1,0:T(8,128)S(1)} collective-permute-done((f32[16,8,128]{2,1,0:T(8,128)S(1)}, f32[16,8,128]{2,1,0:T(8,128)S(1)}, u32[]{:S(2)}, u32[]{:S(2)}) %collective-permute-start.15) | collective-permute-done | bytes 65568 | tf_op jit(solution)/shard_map/ppermute | solution.py:885
  114.9 0.9 copy-done.17
  115.8 0.9 copy-done.20
  116.7 0.9 copy-done.22
  117.6 0.9 copy-done.24
  118.5 6.1 %shard_map.398 = (f32[8,256]{1,0:T(8,128)}, f32[240,512]{1,0:T(8,128)}, f32[384,512]{1,0:T(8,128)S(1)}, f32[384,512]{1,0:T(8,128)S(1)}, f32[384,512]{1,0:T(8,128)S(1)}, /*index=5*/f32[384,512]{1,0:T(8,128)}) custom-call(f32[16,16,128]{2,1,0:T(8,128)S(1)} %copy-done.24, f32[16,8,128]{2,1,0:T(8,128)S(1)} %bitcast_add_fusion.returned, ...), custom_call_target="tpu_custom_call" | custom-call | flops 8049999872 | bytes 1024 | tf_op jit(solution)/shard_map/pallas_call | solution.py:760
  125.9 2.1 collective-permute-done.17
  128.1 0.8 dynamic-slice_add_fusion.11
  129.6 1.8 dynamic-slice_add_fusion.10
  131.9 6.9 %collective-permute-done.19 = f32[104,512]{1,0:T(8,128)} collective-permute-done((f32[104,512]{1,0:T(8,128)}, f32[104,512]{1,0:T(8,128)}, u32[]{:S(2)}, u32[]{:S(2)}) %collective-permute-start.19) | collective-permute-done | bytes 213024 | tf_op jit(solution)/shard_map/ppermute | solution.py:55
  138.8 1.0 add.320
  139.9 1.1 dynamic-slice_add_fusion.8
  141.6 0.9 collective-permute-done.21
  142.5 1.4 collective-permute-start.23
  143.9 4.0 %collective-permute-done.22 = f32[96,512]{1,0:T(8,128)S(1)} collective-permute-done((f32[96,512]{1,0:T(8,128)S(1)}, f32[96,512]{1,0:T(8,128)S(1)}, u32[]{:S(2)}, u32[]{:S(2)}) %collective-permute-start.22) | collective-permute-done | bytes 196640 | tf_op jit(solution)/shard_map/ppermute | solution.py:55
  149.1 1.2 collective-permute-done.24
  150.7 5.2 %collective-permute-done.25 = f32[96,512]{1,0:T(8,128)S(1)} collective-permute-done((f32[96,512]{1,0:T(8,128)S(1)}, f32[96,512]{1,0:T(8,128)S(1)}, u32[]{:S(2)}, u32[]{:S(2)}) %collective-permute-start.25) | collective-permute-done | bytes 196640 | tf_op jit(solution)/shard_map/ppermute | solution.py:55
  155.9 3.0 %collective-permute-start.29 = (f32[48,512]{1,0:T(8,128)S(1)}, f32[48,512]{1,0:T(8,128)S(1)}, u32[]{:S(2)}, u32[]{:S(2)}) collective-permute-start(f32[48,512]{1,0:T(8,128)S(1)} %dynamic-slice_add_fusion.23), channel_id=1, source_target_pairs={{0,16},{8,24},{16,0},{24,8},{1,17},{9,25},{17,1},{25,9},{2,18},{10... | collective-permute-start | bytes 294920 | tf_op jit(solution)/shard_map/ppermute | solution.py:55
  159.0 6.7 %collective-permute-done.26 = f32[208,512]{1,0:T(8,128)S(1)} collective-permute-done((f32[208,512]{1,0:T(8,128)S(1)}, f32[208,512]{1,0:T(8,128)S(1)}, u32[]{:S(2)}, u32[]{:S(2)}) %collective-permute-start.26) | collective-permute-done | bytes 426016 | tf_op jit(solution)/shard_map/ppermute | solution.py:55
  167.0 1.1 collective-permute-start.30
  168.2 1.4 collective-permute-start.27
  169.6 3.0 %collective-permute-done.30 = f32[48,512]{1,0:T(8,128)S(1)} collective-permute-done((f32[48,512]{1,0:T(8,128)S(1)}, f32[48,512]{1,0:T(8,128)S(1)}, u32[]{:S(2)}, u32[]{:S(2)}) %collective-permute-start.30) | collective-permute-done | bytes 98336 | tf_op jit(solution)/shard_map/ppermute | solution.py:55
  172.7 1.8 collective-permute-start.31
  174.5 0.9 collective-permute-start.28
  175.4 3.0 %collective-permute-done.31 = f32[96,512]{1,0:T(8,128)S(1)} collective-permute-done((f32[96,512]{1,0:T(8,128)S(1)}, f32[96,512]{1,0:T(8,128)S(1)}, u32[]{:S(2)}, u32[]{:S(2)}) %collective-permute-start.31) | collective-permute-done | bytes 196640 | tf_op jit(solution)/shard_map/ppermute | solution.py:55
  178.4 2.3 collective-permute-start.33
  181.6 1.4 collective-permute-start.34
  183.0 3.1 %collective-permute-done.28 = f32[192,512]{1,0:T(8,128)S(1)} collective-permute-done((f32[192,512]{1,0:T(8,128)S(1)}, f32[192,512]{1,0:T(8,128)S(1)}, u32[]{:S(2)}, u32[]{:S(2)}) %collective-permute-start.28) | collective-permute-done | bytes 393248 | tf_op jit(solution)/shard_map/ppermute | solution.py:55
  186.2 3.0 %collective-permute-start.35 = (f32[384,512]{1,0:T(8,128)S(1)}, f32[384,512]{1,0:T(8,128)S(1)}, u32[]{:S(2)}, u32[]{:S(2)}) collective-permute-start(f32[384,512]{1,0:T(8,128)S(1)} %pad_maximum_fusion.4), channel_id=1, source_target_pairs={{0,4},{4,0},{1,5},{5,1},{2,6},{6,2},{3,7},{7,3},{8,12},{12,8},{9,1... | collective-permute-start | bytes 2359304 | tf_op jit(solution)/shard_map/ppermute | solution.py:55
  189.4 0.9 collective-permute-done.33
  190.4 15.9 %collective-permute-done.34 = f32[448,512]{1,0:T(8,128)S(1)} collective-permute-done((f32[448,512]{1,0:T(8,128)S(1)}, f32[448,512]{1,0:T(8,128)S(1)}, u32[]{:S(2)}, u32[]{:S(2)}) %collective-permute-start.34) | collective-permute-done | bytes 917536 | tf_op jit(solution)/shard_map/ppermute | solution.py:55
  211.4 2.5 %collective-permute-done.37.b_other = f32[768,512]{1,0:T(8,128)S(1)} collective-permute-done((f32[768,512]{1,0:T(8,128)S(1)}, f32[768,512]{1,0:T(8,128)S(1)}, u32[]{:S(2)}, u32[]{:S(2)}) %collective-permute-start.37) | collective-permute-done | bytes 1572896 | tf_op jit(solution)/shard_map/ppermute | solution.py:55
  214.0 3.1 %shard_map.399 = (f32[2,512,512]{2,1,0:T(8,128)}, f32[2,256,512]{2,1,0:T(8,128)}, f32[64,1024]{1,0:T(8,128)}, f32[64,512]{1,0:T(8,128)}, f32[32,1024]{1,0:T(8,12...) custom-call(f32[896,512]{1,0:T(8,128)S(1)} %maximum_add_fusion.a_mine, ...), custom_call_target="tpu_custom_call" | custom-call | bytes 1024 | tf_op jit(solution)/shard_map/pallas_call | solution.py:760
  217.1 4.0 %collective-permute-done.38 = f32[192,512]{1,0:T(8,128)S(1)} collective-permute-done((f32[192,512]{1,0:T(8,128)S(1)}, f32[192,512]{1,0:T(8,128)S(1)}, u32[]{:S(2)}, u32[]{:S(2)}) %collective-permute-start.38) | collective-permute-done | bytes 393248 | tf_op jit(solution)/shard_map/ppermute | solution.py:55
  222.3 1.8 collective-permute-done.41.d_other
  224.1 1.1 collective-permute-done.40.c_other
  225.2 3.4 %shard_map.400 = (f32[2,512,512]{2,1,0:T(8,128)}, f32[5,128,512]{2,1,0:T(8,128)}, f32[64,512]{1,0:T(8,128)}, f32[32,512]{1,0:T(8,128)}, f32[3,256]{1,0:T(4,128)}) custom-call(f32[384,512]{1,0:T(8,128)S(1)} %pad_maximum_fusion.5.c_mine, f32[384,512]{1,0:T(8,128)S(1)} %collective-permute-done.40.c_other, f32[384,512]{1,0:T(8,128)S(1)} %pad_maximum_fusion.6.d_mine, ...), custom_call_target="tpu_custom_call" | custom-call | flops 3449999872 | bytes 1024 | tf_op jit(solution)/shard_map/pallas_call | solution.py:760
  (178 shorter events, 18.9 us)
Async XLA Ops:
  0.7 7.8 %copy-start.32 = (s32[240]{0:T(256)S(1)}, s32[240]{0:T(256)}, u32[]{:S(2)}) copy-start(s32[240]{0:T(256)} %param.32) | copy-start | bytes 2884
  0.7 7.9 %copy-start.28 = (s32[240,8]{0,1:T(8,128)S(1)}, s32[240,8]{0,1:T(8,128)}, u32[]{:S(2)}) copy-start(s32[240,8]{0,1:T(8,128)} %param.33) | copy-start | bytes 23044
  0.7 7.9 %copy-start.30 = (s32[240,8]{0,1:T(8,128)S(1)}, s32[240,8]{0,1:T(8,128)}, u32[]{:S(2)}) copy-start(s32[240,8]{0,1:T(8,128)} %param.35) | copy-start | bytes 23044
  0.7 22.9 %copy-start.29 = (s32[240,8]{0,1:T(8,128)S(1)}, s32[240,8]{0,1:T(8,128)}, u32[]{:S(2)}) copy-start(s32[240,8]{0,1:T(8,128)} %param.34) | copy-start | bytes 23044
  0.7 22.9 %copy-start.31 = (s32[240,8]{0,1:T(8,128)S(1)}, s32[240,8]{0,1:T(8,128)}, u32[]{:S(2)}) copy-start(s32[240,8]{0,1:T(8,128)} %param.36) | copy-start | bytes 23044
  5.4 29.7 %copy-start = (f32[240,512]{1,0:T(8,128)S(1)}, f32[240,512]{1,0:T(8,128)}, u32[]{:S(2)}) copy-start(f32[240,512]{1,0:T(8,128)} %edge.5) | copy-start | bytes 1474564
  5.4 29.7 %copy-start.2 = (bf16[1024,64]{0,1:T(8,128)(2,1)S(1)}, bf16[1024,64]{0,1:T(8,128)(2,1)}, u32[]{:S(2)}) copy-start(bf16[1024,64]{0,1:T(8,128)(2,1)} %param.41) | copy-start | bytes 393220
  5.4 29.7 %copy-start.3 = (bf16[64,512]{1,0:T(8,128)(2,1)S(1)}, bf16[64,512]{1,0:T(8,128)(2,1)}, u32[]{:S(2)}) copy-start(bf16[64,512]{1,0:T(8,128)(2,1)} %trip_up.1) | copy-start | bytes 196612
  5.4 29.7 %copy-start.4 = (bf16[1024,32]{0,1:T(8,128)(2,1)S(1)}, bf16[1024,32]{0,1:T(8,128)(2,1)}, u32[]{:S(2)}) copy-start(bf16[1024,32]{0,1:T(8,128)(2,1)} %param.44) | copy-start | bytes 196612
  5.4 29.7 %copy-start.6 = (bf16[32,512]{1,0:T(8,128)(2,1)S(1)}, bf16[32,512]{1,0:T(8,128)(2,1)}, u32[]{:S(2)}) copy-start(bf16[32,512]{1,0:T(8,128)(2,1)} %quad_up.1) | copy-start | bytes 98308
  5.4 29.7 %copy-start.8 = (f32[8,256]{1,0:T(8,128)S(1)}, f32[8,256]{1,0:T(8,128)}, u32[]{:S(2)}) copy-start(f32[8,256]{1,0:T(8,128)} %cot_atoms.1) | copy-start | bytes 24580
  5.4 29.7 %copy-start.9 = (f32[8,256]{1,0:T(8,128)S(1)}, f32[8,256]{1,0:T(8,128)}, u32[]{:S(2)}) copy-start(f32[8,256]{1,0:T(8,128)} %cot_energy.1) | copy-start | bytes 24580
  5.4 29.7 %copy-start.16 = (f32[240,128]{1,0:T(8,128)S(1)}, f32[240,128]{1,0:T(8,128)}, u32[]{:S(2)}) copy-start(f32[240,128]{1,0:T(8,128)} %get-tuple-element.173.radial) | copy-start | bytes 368644
  5.5 29.7 %copy-start.18 = (f32[17,16,128]{2,1,0:T(8,128)S(1)}, f32[17,16,128]{2,1,0:T(8,128)}, u32[]{:S(2)}) copy-start(f32[17,16,128]{2,1,0:T(8,128)} %get-tuple-element.169.local) | copy-start | bytes 417796
  5.5 29.7 %copy-start.21 = (f32[240,128]{1,0:T(8,128)S(1)}, f32[240,128]{1,0:T(8,128)}, u32[]{:S(2)}) copy-start(f32[240,128]{1,0:T(8,128)} %get-tuple-element.171.columns) | copy-start | bytes 368644
  5.5 29.7 %copy-start.25 = (f32[8,256]{1,0:T(8,128)S(1)}, f32[8,256]{1,0:T(8,128)}, u32[]{:S(2)}) copy-start(f32[8,256]{1,0:T(8,128)} %get-tuple-element.170.tagged) | copy-start | bytes 24580
  5.5 5.5 %collective-permute-start = (f32[17,8,128]{2,1,0:T(8,128)}, f32[17,8,128]{2,1,0:T(8,128)S(1)}, u32[]{:S(2)}, u32[]{:S(2)}) collective-permute-start(f32[17,8,128]{2,1,0:T(8,128)} %get-tuple-element.168), channel_id=1, source_target_pairs={{0,1},{1,0},{2,3},{3,2},{4,5},{5,4},{6,7},{7,6},{8,9},{9,8},{10,11... | collective-permute-start | bytes 208904 | tf_op jit(solution)/shard_map/ppermute | solution.py:36
  11.9 7.5 %collective-permute-start.2 = (f32[2,17,8,128]{3,2,1,0:T(8,128)S(1)}, f32[2,17,8,128]{3,2,1,0:T(8,128)S(1)}, u32[]{:S(2)}, u32[]{:S(2)}) collective-permute-start(f32[2,17,8,128]{3,2,1,0:T(8,128)S(1)} %pad_maximum_fusion.14), channel_id=1, source_target_pairs={{0,24},{8,0},{16,8},{24,16},{1,25},{9,1},{17,9},{25,17},{2,26},{10... | collective-permute-start | bytes 417800 | tf_op jit(solution)/shard_map/ppermute | solution.py:31
  16.1 6.9 %collective-permute-start.1 = (f32[2,17,8,128]{3,2,1,0:T(8,128)S(1)}, f32[2,17,8,128]{3,2,1,0:T(8,128)S(1)}, u32[]{:S(2)}, u32[]{:S(2)}) collective-permute-start(f32[2,17,8,128]{3,2,1,0:T(8,128)S(1)} %pad_maximum_fusion.14), channel_id=1, source_target_pairs={{0,8},{8,16},{16,24},{24,0},{1,9},{9,17},{17,25},{25,1},{2,10},{10... | collective-permute-start | bytes 417800 | tf_op jit(solution)/shard_map/ppermute | solution.py:31
  23.0 8.9 %collective-permute-start.4 = (f32[6,17,8,128]{3,2,1,0:T(8,128)S(1)}, f32[6,17,8,128]{3,2,1,0:T(8,128)S(1)}, u32[]{:S(2)}, u32[]{:S(2)}) collective-permute-start(f32[6,17,8,128]{3,2,1,0:T(8,128)S(1)} %pad_maximum_fusion.8.halo_here), channel_id=1, source_target_pairs={{0,6},{2,0},{4,2},{6,4},{1,7},{3,1},{5,3},{7,5},{8,14},{10,8},{12,... | collective-permute-start | bytes 1253384 | tf_op jit(solution)/shard_map/ppermute | solution.py:31
  23.0 12.0 %collective-permute-start.3 = (f32[6,17,8,128]{3,2,1,0:T(8,128)S(1)}, f32[6,17,8,128]{3,2,1,0:T(8,128)S(1)}, u32[]{:S(2)}, u32[]{:S(2)}) collective-permute-start(f32[6,17,8,128]{3,2,1,0:T(8,128)S(1)} %pad_maximum_fusion.8.halo_here), channel_id=1, source_target_pairs={{0,2},{2,4},{4,6},{6,0},{1,3},{3,5},{5,7},{7,1},{8,10},{10,12},{12... | collective-permute-start | bytes 1253384 | tf_op jit(solution)/shard_map/ppermute | solution.py:31
  60.0 6.4 %collective-permute-start.5 = (f32[896,512]{1,0:T(8,128)}, f32[896,512]{1,0:T(8,128)}, u32[]{:S(2)}, u32[]{:S(2)}) collective-permute-start(f32[896,512]{1,0:T(8,128)} %get-tuple-element.179), channel_id=1, source_target_pairs={{0,2},{2,0},{1,3},{3,1},{4,6},{6,4},{5,7},{7,5},{8,10},{10,8},{9,1... | collective-permute-start | bytes 5505032 | tf_op jit(solution)/shard_map/ppermute | solution.py:55
  62.6 7.1 %collective-permute-start.6 = (f32[768,512]{1,0:T(8,128)S(1)}, f32[768,512]{1,0:T(8,128)}, u32[]{:S(2)}, u32[]{:S(2)}) collective-permute-start(f32[768,512]{1,0:T(8,128)S(1)} %get-tuple-element.184), channel_id=1, source_target_pairs={{0,2},{2,0},{1,3},{3,1},{4,6},{6,4},{5,7},{7,5},{8,10},{10,8},{9,1... | collective-permute-start | bytes 4718600 | tf_op jit(solution)/shard_map/ppermute | solution.py:55
  68.2 22.5 %collective-permute-start.7 = (f32[448,512]{1,0:T(8,128)S(1)}, f32[448,512]{1,0:T(8,128)S(1)}, u32[]{:S(2)}, u32[]{:S(2)}) collective-permute-start(f32[448,512]{1,0:T(8,128)S(1)} %dynamic-slice_add_fusion.1), channel_id=1, source_target_pairs={{0,1},{1,0},{2,3},{3,2},{4,5},{5,4},{6,7},{7,6},{8,9},{9,8},{10,11... | collective-permute-start | bytes 2752520 | tf_op jit(solution)/shard_map/ppermute | solution.py:55
  71.0 20.5 %collective-permute-start.8 = (f32[384,512]{1,0:T(8,128)S(1)}, f32[384,512]{1,0:T(8,128)S(1)}, u32[]{:S(2)}, u32[]{:S(2)}) collective-permute-start(f32[384,512]{1,0:T(8,128)S(1)} %dynamic-slice_add_fusion.3), channel_id=1, source_target_pairs={{0,4},{4,0},{1,5},{5,1},{2,6},{6,2},{3,7},{7,3},{8,12},{12,8},{9,1... | collective-permute-start | bytes 2359304 | tf_op jit(solution)/shard_map/ppermute | solution.py:55
  77.4 20.5 %collective-permute-start.9 = (f32[6,16,8,128]{3,2,1,0:T(8,128)S(1)}, f32[6,16,8,128]{3,2,1,0:T(8,128)S(1)}, u32[]{:S(2)}, u32[]{:S(2)}) collective-permute-start(f32[6,16,8,128]{3,2,1,0:T(8,128)S(1)} %get-tuple-element.203), channel_id=1, source_target_pairs={{0,6},{2,0},{4,2},{6,4},{1,7},{3,1},{5,3},{7,5},{8,14},{10,8},{12,... | collective-permute-start | bytes 1179656 | tf_op jit(solution)/shard_map/ppermute | solution.py:31
  78.2 19.8 %collective-permute-start.10 = (f32[6,16,8,128]{3,2,1,0:T(8,128)S(1)}, f32[6,16,8,128]{3,2,1,0:T(8,128)S(1)}, u32[]{:S(2)}, u32[]{:S(2)}) collective-permute-start(f32[6,16,8,128]{3,2,1,0:T(8,128)S(1)} %get-tuple-element.204), channel_id=1, source_target_pairs={{0,2},{2,4},{4,6},{6,0},{1,3},{3,5},{5,7},{7,1},{8,10},{10,12},{12... | collective-permute-start | bytes 1179656 | tf_op jit(solution)/shard_map/ppermute | solution.py:31
  90.7 17.9 %collective-permute-start.11 = (f32[224,512]{1,0:T(8,128)S(1)}, f32[224,512]{1,0:T(8,128)S(1)}, u32[]{:S(2)}, u32[]{:S(2)}) collective-permute-start(f32[224,512]{1,0:T(8,128)S(1)} %dynamic-slice_add_fusion.5), channel_id=1, source_target_pairs={{0,4},{4,0},{1,5},{5,1},{2,6},{6,2},{3,7},{7,3},{8,12},{12,8},{9,1... | collective-permute-start | bytes 1376264 | tf_op jit(solution)/shard_map/ppermute | solution.py:55
  91.5 10.4 %collective-permute-start.12 = (f32[192,512]{1,0:T(8,128)S(1)}, f32[192,512]{1,0:T(8,128)S(1)}, u32[]{:S(2)}, u32[]{:S(2)}) collective-permute-start(f32[192,512]{1,0:T(8,128)S(1)} %dynamic-slice_add_fusion.13), channel_id=1, source_target_pairs={{0,1},{1,0},{2,3},{3,2},{4,5},{5,4},{6,7},{7,6},{8,9},{9,8},{10,11... | collective-permute-start | bytes 1179656 | tf_op jit(solution)/shard_map/ppermute | solution.py:55
  98.1 12.4 %collective-permute-start.14 = (f32[2,16,8,128]{3,2,1,0:T(8,128)S(1)}, f32[2,16,8,128]{3,2,1,0:T(8,128)S(1)}, u32[]{:S(2)}, u32[]{:S(2)}) collective-permute-start(f32[2,16,8,128]{3,2,1,0:T(8,128)S(1)} %get-tuple-element.343), channel_id=1, source_target_pairs={{0,8},{8,16},{16,24},{24,0},{1,9},{9,17},{17,25},{25,1},{2,10},{10... | collective-permute-start | bytes 393224 | tf_op jit(solution)/shard_map/ppermute | solution.py:31
  98.5 12.0 %collective-permute-start.13 = (f32[2,16,8,128]{3,2,1,0:T(8,128)S(1)}, f32[2,16,8,128]{3,2,1,0:T(8,128)S(1)}, u32[]{:S(2)}, u32[]{:S(2)}) collective-permute-start(f32[2,16,8,128]{3,2,1,0:T(8,128)S(1)} %get-tuple-element.344), channel_id=1, source_target_pairs={{0,24},{8,0},{16,8},{24,16},{1,25},{9,1},{17,9},{25,17},{2,26},{10... | collective-permute-start | bytes 393224 | tf_op jit(solution)/shard_map/ppermute | solution.py:31
  108.7 6.1 %copy-start.1 = (f32[240,512]{1,0:T(8,128)S(1)}, f32[240,512]{1,0:T(8,128)}, u32[]{:S(2)}) copy-start(f32[240,512]{1,0:T(8,128)} %edge.5) | copy-start | bytes 1474564
  108.8 6.1 %copy-start.5 = (bf16[512,64]{0,1:T(8,128)(2,1)S(1)}, bf16[512,64]{0,1:T(8,128)(2,1)}, u32[]{:S(2)}) copy-start(bf16[512,64]{0,1:T(8,128)(2,1)} %param.40) | copy-start | bytes 196612
  108.8 6.1 %copy-start.7 = (bf16[512,32]{0,1:T(8,128)(2,1)S(1)}, bf16[512,32]{0,1:T(8,128)(2,1)}, u32[]{:S(2)}) copy-start(bf16[512,32]{0,1:T(8,128)(2,1)} %param.43) | copy-start | bytes 98308
  108.8 6.1 %copy-start.10 = (s32[8]{0:T(128)S(1)}, s32[8]{0:T(128)}, u32[]{:S(2)}) copy-start(s32[8]{0:T(128)} %param.30) | copy-start | bytes 100
  108.8 6.1 %copy-start.11 = (s32[4]{0:T(128)S(1)}, s32[4]{0:T(128)}, u32[]{:S(2)}) copy-start(s32[4]{0:T(128)} %param.31) | copy-start | bytes 52
  108.8 6.1 %copy-start.14 = (f32[240,512]{1,0:T(8,128)S(1)}, f32[240,512]{1,0:T(8,128)}, u32[]{:S(2)}) copy-start(f32[240,512]{1,0:T(8,128)} %copy-done.13) | copy-start | bytes 1474564
  110.5 4.3 %collective-permute-start.15 = (f32[16,8,128]{2,1,0:T(8,128)S(1)}, f32[16,8,128]{2,1,0:T(8,128)S(1)}, u32[]{:S(2)}, u32[]{:S(2)}) collective-permute-start(f32[16,8,128]{2,1,0:T(8,128)S(1)} %select_bitcast_fusion.2), channel_id=1, source_target_pairs={{0,1},{1,0},{2,3},{3,2},{4,5},{5,4},{6,7},{7,6},{8,9},{9,8},{10,11... | collective-permute-start | bytes 196616 | tf_op jit(solution)/shard_map/ppermute | solution.py:885
  111.3 13.3 %collective-permute-start.16 = (f32[208,512]{1,0:T(8,128)}, f32[208,512]{1,0:T(8,128)S(1)}, u32[]{:S(2)}, u32[]{:S(2)}) collective-permute-start(f32[208,512]{1,0:T(8,128)} %dynamic-slice_add_fusion.7), channel_id=1, source_target_pairs={{0,8},{8,0},{16,24},{24,16},{1,9},{9,1},{17,25},{25,17},{2,10},{10... | collective-permute-start | bytes 1277960 | tf_op jit(solution)/shard_map/ppermute | solution.py:55
  125.4 2.7 %collective-permute-start.17 = (f32[384,512]{1,0:T(8,128)S(1)}, f32[384,512]{1,0:T(8,128)S(1)}, u32[]{:S(2)}, u32[]{:S(2)}) collective-permute-start(f32[384,512]{1,0:T(8,128)S(1)} %get-tuple-element.234), channel_id=1, source_target_pairs={{0,2},{2,0},{1,3},{3,1},{4,6},{6,4},{5,7},{7,5},{8,10},{10,8},{9,1... | collective-permute-start | bytes 2359304 | tf_op jit(solution)/shard_map/ppermute | solution.py:55
  125.4 4.1 %collective-permute-start.18 = (f32[384,512]{1,0:T(8,128)}, f32[384,512]{1,0:T(8,128)}, u32[]{:S(2)}, u32[]{:S(2)}) collective-permute-start(f32[384,512]{1,0:T(8,128)} %get-tuple-element.238), channel_id=1, source_target_pairs={{0,2},{2,0},{1,3},{3,1},{4,6},{6,4},{5,7},{7,5},{8,10},{10,8},{9,1... | collective-permute-start | bytes 2359304 | tf_op jit(solution)/shard_map/ppermute | solution.py:55
  125.9 12.8 %collective-permute-start.19 = (f32[104,512]{1,0:T(8,128)}, f32[104,512]{1,0:T(8,128)}, u32[]{:S(2)}, u32[]{:S(2)}) collective-permute-start(f32[104,512]{1,0:T(8,128)} %dynamic-slice_add_fusion.15), channel_id=1, source_target_pairs={{0,16},{8,24},{16,0},{24,8},{1,17},{9,25},{17,1},{25,9},{2,18},{10... | collective-permute-start | bytes 638984 | tf_op jit(solution)/shard_map/ppermute | solution.py:55
  128.9 12.1 %collective-permute-start.20 = (f32[192,512]{1,0:T(8,128)}, f32[192,512]{1,0:T(8,128)S(1)}, u32[]{:S(2)}, u32[]{:S(2)}) collective-permute-start(f32[192,512]{1,0:T(8,128)} %dynamic-slice_add_fusion.11), channel_id=1, source_target_pairs={{0,1},{1,0},{2,3},{3,2},{4,5},{5,4},{6,7},{7,6},{8,9},{9,8},{10,11... | collective-permute-start | bytes 1179656 | tf_op jit(solution)/shard_map/ppermute | solution.py:55
  131.4 11.1 %collective-permute-start.21 = (f32[192,512]{1,0:T(8,128)}, f32[192,512]{1,0:T(8,128)S(1)}, u32[]{:S(2)}, u32[]{:S(2)}) collective-permute-start(f32[192,512]{1,0:T(8,128)} %dynamic-slice_add_fusion.10), channel_id=1, source_target_pairs={{0,4},{4,0},{1,5},{5,1},{2,6},{6,2},{3,7},{7,3},{8,12},{12,8},{9,1... | collective-permute-start | bytes 1179656 | tf_op jit(solution)/shard_map/ppermute | solution.py:55
  139.7 10.5 %collective-permute-start.24 = (f32[104,512]{1,0:T(8,128)S(1)}, f32[104,512]{1,0:T(8,128)S(1)}, u32[]{:S(2)}, u32[]{:S(2)}) collective-permute-start(f32[104,512]{1,0:T(8,128)S(1)} %add.320), channel_id=1, source_target_pairs={{0,16},{8,24},{16,0},{24,8},{1,17},{9,25},{17,1},{25,9},{2,18},{10... | collective-permute-start | bytes 638984 | tf_op jit(solution)/shard_map/ppermute | solution.py:55
  141.0 6.9 %collective-permute-start.22 = (f32[96,512]{1,0:T(8,128)S(1)}, f32[96,512]{1,0:T(8,128)S(1)}, u32[]{:S(2)}, u32[]{:S(2)}) collective-permute-start(f32[96,512]{1,0:T(8,128)S(1)} %dynamic-slice_add_fusion.21), channel_id=1, source_target_pairs={{0,4},{4,0},{1,5},{5,1},{2,6},{6,2},{3,7},{7,3},{8,12},{12,8},{9,1... | collective-permute-start | bytes 589832 | tf_op jit(solution)/shard_map/ppermute | solution.py:55
  142.5 5.9 %collective-permute-start.23 = (f32[96,512]{1,0:T(8,128)S(1)}, f32[96,512]{1,0:T(8,128)S(1)}, u32[]{:S(2)}, u32[]{:S(2)}) collective-permute-start(f32[96,512]{1,0:T(8,128)S(1)} %dynamic-slice_add_fusion.20), channel_id=1, source_target_pairs={{0,1},{1,0},{2,3},{3,2},{4,5},{5,4},{6,7},{7,6},{8,9},{9,8},{10,11... | collective-permute-start | bytes 589832 | tf_op jit(solution)/shard_map/ppermute | solution.py:55
  148.4 7.5 %collective-permute-start.25 = (f32[96,512]{1,0:T(8,128)S(1)}, f32[96,512]{1,0:T(8,128)S(1)}, u32[]{:S(2)}, u32[]{:S(2)}) collective-permute-start(f32[96,512]{1,0:T(8,128)S(1)} %dynamic-slice_add_fusion.17), channel_id=1, source_target_pairs={{0,8},{8,0},{16,24},{24,16},{1,9},{9,1},{17,25},{25,17},{2,10},{10... | collective-permute-start | bytes 589832 | tf_op jit(solution)/shard_map/ppermute | solution.py:55
  150.3 15.3 %collective-permute-start.26 = (f32[208,512]{1,0:T(8,128)S(1)}, f32[208,512]{1,0:T(8,128)S(1)}, u32[]{:S(2)}, u32[]{:S(2)}) collective-permute-start(f32[208,512]{1,0:T(8,128)S(1)} %pad_maximum_fusion.7), channel_id=1, source_target_pairs={{0,8},{8,0},{16,24},{24,16},{1,9},{9,1},{17,25},{25,17},{2,10},{10... | collective-permute-start | bytes 1277960 | tf_op jit(solution)/shard_map/ppermute | solution.py:55
  155.9 9.9 %collective-permute-start.29 = (f32[48,512]{1,0:T(8,128)S(1)}, f32[48,512]{1,0:T(8,128)S(1)}, u32[]{:S(2)}, u32[]{:S(2)}) collective-permute-start(f32[48,512]{1,0:T(8,128)S(1)} %dynamic-slice_add_fusion.23), channel_id=1, source_target_pairs={{0,16},{8,24},{16,0},{24,8},{1,17},{9,25},{17,1},{25,9},{2,18},{10... | collective-permute-start | bytes 294920 | tf_op jit(solution)/shard_map/ppermute | solution.py:55
  167.0 5.6 %collective-permute-start.30 = (f32[48,512]{1,0:T(8,128)S(1)}, f32[48,512]{1,0:T(8,128)S(1)}, u32[]{:S(2)}, u32[]{:S(2)}) collective-permute-start(f32[48,512]{1,0:T(8,128)S(1)} %add_add_fusion.2), channel_id=1, source_target_pairs={{0,16},{8,24},{16,0},{24,8},{1,17},{9,25},{17,1},{25,9},{2,18},{10... | collective-permute-start | bytes 294920 | tf_op jit(solution)/shard_map/ppermute | solution.py:55
  168.2 13.3 %collective-permute-start.27 = (f32[224,512]{1,0:T(8,128)S(1)}, f32[224,512]{1,0:T(8,128)S(1)}, u32[]{:S(2)}, u32[]{:S(2)}) collective-permute-start(f32[224,512]{1,0:T(8,128)S(1)} %fusion), channel_id=1, source_target_pairs={{0,4},{4,0},{1,5},{5,1},{2,6},{6,2},{3,7},{7,3},{8,12},{12,8},{9,1... | collective-permute-start | bytes 1376264 | tf_op jit(solution)/shard_map/ppermute | solution.py:55
  172.7 5.7 %collective-permute-start.31 = (f32[96,512]{1,0:T(8,128)S(1)}, f32[96,512]{1,0:T(8,128)S(1)}, u32[]{:S(2)}, u32[]{:S(2)}) collective-permute-start(f32[96,512]{1,0:T(8,128)S(1)} %pad_maximum_fusion.13), channel_id=1, source_target_pairs={{0,8},{8,0},{16,24},{24,16},{1,9},{9,1},{17,25},{25,17},{2,10},{10... | collective-permute-start | bytes 589832 | tf_op jit(solution)/shard_map/ppermute | solution.py:55
  174.5 11.6 %collective-permute-start.28 = (f32[192,512]{1,0:T(8,128)S(1)}, f32[192,512]{1,0:T(8,128)S(1)}, u32[]{:S(2)}, u32[]{:S(2)}) collective-permute-start(f32[192,512]{1,0:T(8,128)S(1)} %slice.49), channel_id=1, source_target_pairs={{0,1},{1,0},{2,3},{3,2},{4,5},{5,4},{6,7},{7,6},{8,9},{9,8},{10,11... | collective-permute-start | bytes 1179656 | tf_op jit(solution)/shard_map/ppermute | solution.py:55
  178.4 11.9 %collective-permute-start.33 = (f32[96,512]{1,0:T(8,128)S(1)}, f32[96,512]{1,0:T(8,128)S(1)}, u32[]{:S(2)}, u32[]{:S(2)}) collective-permute-start(f32[96,512]{1,0:T(8,128)S(1)} %get-tuple-element.285), channel_id=1, source_target_pairs={{0,1},{1,0},{2,3},{3,2},{4,5},{5,4},{6,7},{7,6},{8,9},{9,8},{10,11... | collective-permute-start | bytes 589832 | tf_op jit(solution)/shard_map/ppermute | solution.py:55
  180.7 8.6 %collective-permute-start.32 = (f32[96,512]{1,0:T(8,128)S(1)}, f32[96,512]{1,0:T(8,128)S(1)}, u32[]{:S(2)}, u32[]{:S(2)}) collective-permute-start(f32[96,512]{1,0:T(8,128)S(1)} %get-tuple-element.283), channel_id=1, source_target_pairs={{0,4},{4,0},{1,5},{5,1},{2,6},{6,2},{3,7},{7,3},{8,12},{12,8},{9,1... | collective-permute-start | bytes 589832 | tf_op jit(solution)/shard_map/ppermute | solution.py:55
  181.6 24.7 %collective-permute-start.34 = (f32[448,512]{1,0:T(8,128)S(1)}, f32[448,512]{1,0:T(8,128)S(1)}, u32[]{:S(2)}, u32[]{:S(2)}) collective-permute-start(f32[448,512]{1,0:T(8,128)S(1)} %pad_maximum_fusion.1), channel_id=1, source_target_pairs={{0,1},{1,0},{2,3},{3,2},{4,5},{5,4},{6,7},{7,6},{8,9},{9,8},{10,11... | collective-permute-start | bytes 2752520 | tf_op jit(solution)/shard_map/ppermute | solution.py:55
  186.2 21.7 %collective-permute-start.35 = (f32[384,512]{1,0:T(8,128)S(1)}, f32[384,512]{1,0:T(8,128)S(1)}, u32[]{:S(2)}, u32[]{:S(2)}) collective-permute-start(f32[384,512]{1,0:T(8,128)S(1)} %pad_maximum_fusion.4), channel_id=1, source_target_pairs={{0,4},{4,0},{1,5},{5,1},{2,6},{6,2},{3,7},{7,3},{8,12},{12,8},{9,1... | collective-permute-start | bytes 2359304 | tf_op jit(solution)/shard_map/ppermute | solution.py:55
  207.8 6.1 %collective-permute-start.36 = (f32[896,512]{1,0:T(8,128)S(1)}, f32[896,512]{1,0:T(8,128)S(1)}, u32[]{:S(2)}, u32[]{:S(2)}) collective-permute-start(f32[896,512]{1,0:T(8,128)S(1)} %maximum_add_fusion.a_mine), channel_id=1, source_target_pairs={{0,2},{2,0},{1,3},{3,1},{4,6},{6,4},{5,7},{7,5},{8,10},{10,8},{9,1... | collective-permute-start | bytes 5505032 | tf_op jit(solution)/shard_map/ppermute | solution.py:55
  209.5 4.5 %collective-permute-start.37 = (f32[768,512]{1,0:T(8,128)S(1)}, f32[768,512]{1,0:T(8,128)S(1)}, u32[]{:S(2)}, u32[]{:S(2)}) collective-permute-start(f32[768,512]{1,0:T(8,128)S(1)} %maximum_add_fusion.1.b_mine), channel_id=1, source_target_pairs={{0,2},{2,0},{1,3},{3,1},{4,6},{6,4},{5,7},{7,5},{8,10},{10,8},{9,1... | collective-permute-start | bytes 4718600 | tf_op jit(solution)/shard_map/ppermute | solution.py:55
  210.0 11.1 %collective-permute-start.38 = (f32[192,512]{1,0:T(8,128)S(1)}, f32[192,512]{1,0:T(8,128)S(1)}, u32[]{:S(2)}, u32[]{:S(2)}) collective-permute-start(f32[192,512]{1,0:T(8,128)S(1)} %pad_maximum_fusion.11), channel_id=1, source_target_pairs={{0,1},{1,0},{2,3},{3,2},{4,5},{5,4},{6,7},{7,6},{8,9},{9,8},{10,11... | collective-permute-start | bytes 1179656 | tf_op jit(solution)/shard_map/ppermute | solution.py:55
  210.8 10.8 %collective-permute-start.39 = (f32[192,512]{1,0:T(8,128)S(1)}, f32[192,512]{1,0:T(8,128)S(1)}, u32[]{:S(2)}, u32[]{:S(2)}) collective-permute-start(f32[192,512]{1,0:T(8,128)S(1)} %pad_maximum_fusion.12), channel_id=1, source_target_pairs={{0,4},{4,0},{1,5},{5,1},{2,6},{6,2},{3,7},{7,3},{8,12},{12,8},{9,1... | collective-permute-start | bytes 1179656 | tf_op jit(solution)/shard_map/ppermute | solution.py:55
  221.7 2.4 %collective-permute-start.41 = (f32[384,512]{1,0:T(8,128)S(1)}, f32[384,512]{1,0:T(8,128)S(1)}, u32[]{:S(2)}, u32[]{:S(2)}) collective-permute-start(f32[384,512]{1,0:T(8,128)S(1)} %pad_maximum_fusion.6.d_mine), channel_id=1, source_target_pairs={{0,2},{2,0},{1,3},{3,1},{4,6},{6,4},{5,7},{7,5},{8,10},{10,8},{9,1... | collective-permute-start | bytes 2359304 | tf_op jit(solution)/shard_map/ppermute | solution.py:55
  221.8 3.4 %collective-permute-start.40 = (f32[384,512]{1,0:T(8,128)S(1)}, f32[384,512]{1,0:T(8,128)S(1)}, u32[]{:S(2)}, u32[]{:S(2)}) collective-permute-start(f32[384,512]{1,0:T(8,128)S(1)} %pad_maximum_fusion.5.c_mine), channel_id=1, source_target_pairs={{0,2},{2,0},{1,3},{3,1},{4,6},{6,4},{5,7},{7,5},{8,10},{10,8},{9,1... | collective-permute-start | bytes 2359304 | tf_op jit(solution)/shard_map/ppermute | solution.py:55
  (11 other events, 27.8 us)

commit v10 on v9

--- a/solution.py
+++ b/solution.py
@@ -892,7 +892,7 @@
         [back_local, returned, grad_edges, grad_tag, edge_states, radial, columns, pre, downs, rads,
          tag_row, send_row, w_inputs, trip_down_t, quad_down_t, core],
         scratch=[pltpu.VMEM((768, 512), F32)] * 2,
-        micros=7, room=50,
+        micros=7, room=58,
     )
     next(late)
     send_c, send_d = chain.after((send_c, send_d))

time: 230 us -> 222 us (0.965)
  local copies, waits for them, and re-layouts: 9.71 us -> 4.19 us
    unnamed x67 -> x55, local copies, waits for them, and re-layouts: 5.24 us -> 1.69 us
    ppermute x32, starting transfers between devices: 28.1 us -> 25.8 us  [swap(): return lax.ppermute(value, axis, [(i, i ^ 1 << bit) for i in range(count)])]
  transfers between devices with their start and end apart: 42 -> 42, of which waited for: 28 -> 30; matrix products, arithmetic and copies ran while one was open for 8% -> 8% of each run, Pallas kernels for 7% -> 8%
where the time goes in v10:
time: 222 us
  waiting for transfers between devices  108 us (49%)
  Pallas kernels  49.6 us (22%)
  starting transfers between devices  39.1 us (18%)
  other arithmetic  16.6 us (7%)
  local copies, waits for them, and re-layouts  4.19 us (2%)
  between operations  3.7 us (2%)
    ppermute x32, waiting for transfers between devices, swap(): return lax.ppermute(value, axis, [(i, i ^ 1 << bit) for i in range(count)])  80.2 us
    pallas_call x7, Pallas kernels, call(): pl.pallas_call(kernel, out_shape=[jax.ShapeDtypeStruct(shape, F32) for sh...  49.6 us
    ppermute x32, starting transfers between devices, swap(): return lax.ppermute(value, axis, [(i, i ^ 1 << bit) for i in range(count)])  25.8 us
    ppermute x8, waiting for transfers between devices, shifted(): return lax.ppermute(value, axis, pairs)  22.9 us
    add x24, other arithmetic, part(): total = total + lax.dynamic_slice_in_dim(x, at, size)  12.9 us
    ppermute x8, starting transfers between devices, shifted(): return lax.ppermute(value, axis, pairs)  9.37 us
  transfers between devices with their start and end apart: 42, of which 30 were waited for; matrix products, arithmetic and copies ran while one was open for 8% of the time, Pallas kernels for 8%

profile of v10, /device:TPU:0, one launch (start us, length us, event | category | flops | bytes accessed | tf_op | source)
XLA Modules:
  0.0 221.6 jit_solution(11051374171638818233)
XLA Ops:
  0.7 4.6 %shard_map.394 = (f32[17,8,128]{2,1,0:T(8,128)}, f32[17,16,128]{2,1,0:T(8,128)}, f32[8,256]{1,0:T(8,128)}, f32[2,240,512]{2,1,0:T(8,128)}, f32[240,128]{1,0:T(8,...) custom-call(f32[240,512]{1,0:T(8,128)} %edge.5, f32[3,240]{1,0:T(4,128)} %vec.1, ...), custom_call_target="tpu_custom_call" | custom-call | flops 5750000128 | bytes 1024 | tf_op jit(solution)/shard_map/pallas_call | solution.py:760
  5.5 3.0 %collective-permute-start = (f32[17,8,128]{2,1,0:T(8,128)}, f32[17,8,128]{2,1,0:T(8,128)S(1)}, u32[]{:S(2)}, u32[]{:S(2)}) collective-permute-start(f32[17,8,128]{2,1,0:T(8,128)} %get-tuple-element.168), channel_id=1, source_target_pairs={{0,1},{1,0},{2,3},{3,2},{4,5},{5,4},{6,7},{7,6},{8,9},{9,8},{10,11... | collective-permute-start | bytes 208904 | tf_op jit(solution)/shard_map/ppermute | solution.py:36
  8.7 2.3 %collective-permute-done = f32[17,8,128]{2,1,0:T(8,128)S(1)} collective-permute-done((f32[17,8,128]{2,1,0:T(8,128)}, f32[17,8,128]{2,1,0:T(8,128)S(1)}, u32[]{:S(2)}, u32[]{:S(2)}) %collective-permute-start) | collective-permute-done | bytes 69664 | tf_op jit(solution)/shard_map/ppermute | solution.py:36
  11.0 0.9 select_bitcast_fusion.1
  11.9 4.2 %collective-permute-start.2 = (f32[2,17,8,128]{3,2,1,0:T(8,128)S(1)}, f32[2,17,8,128]{3,2,1,0:T(8,128)S(1)}, u32[]{:S(2)}, u32[]{:S(2)}) collective-permute-start(f32[2,17,8,128]{3,2,1,0:T(8,128)S(1)} %pad_maximum_fusion.14), channel_id=1, source_target_pairs={{0,24},{8,0},{16,8},{24,16},{1,25},{9,1},{17,9},{25,17},{2,26},{10... | collective-permute-start | bytes 417800 | tf_op jit(solution)/shard_map/ppermute | solution.py:31
  16.1 3.3 %collective-permute-done.2 = f32[2,17,8,128]{3,2,1,0:T(8,128)S(1)} collective-permute-done((f32[2,17,8,128]{3,2,1,0:T(8,128)S(1)}, f32[2,17,8,128]{3,2,1,0:T(8,128)S(1)}, u32[]{:S(2)}, u32[]{:S(2)}) %collective-permute-start.2) | collective-permute-done | bytes 139296 | tf_op jit(solution)/shard_map/ppermute | solution.py:31
  19.4 3.6 %collective-permute-done.1 = f32[2,17,8,128]{3,2,1,0:T(8,128)S(1)} collective-permute-done((f32[2,17,8,128]{3,2,1,0:T(8,128)S(1)}, f32[2,17,8,128]{3,2,1,0:T(8,128)S(1)}, u32[]{:S(2)}, u32[]{:S(2)}) %collective-permute-start.1) | collective-permute-done | bytes 139296 | tf_op jit(solution)/shard_map/ppermute | solution.py:31
  24.0 7.9 %collective-permute-done.4.halo_after = f32[6,17,8,128]{3,2,1,0:T(8,128)S(1)} collective-permute-done((f32[6,17,8,128]{3,2,1,0:T(8,128)S(1)}, f32[6,17,8,128]{3,2,1,0:T(8,128)S(1)}, u32[]{:S(2)}, u32[]{:S(2)}) %collective-permute-start.4) | collective-permute-done | bytes 417824 | tf_op jit(solution)/shard_map/ppermute | solution.py:31
  31.9 3.2 %collective-permute-done.3.halo_before = f32[6,17,8,128]{3,2,1,0:T(8,128)S(1)} collective-permute-done((f32[6,17,8,128]{3,2,1,0:T(8,128)S(1)}, f32[6,17,8,128]{3,2,1,0:T(8,128)S(1)}, u32[]{:S(2)}, u32[]{:S(2)}) %collective-permute-start.3) | collective-permute-done | bytes 417824 | tf_op jit(solution)/shard_map/ppermute | solution.py:31
  35.1 24.9 %shard_map.395 = (f32[8,256]{1,0:T(8,128)}, f32[240,512]{1,0:T(8,128)}, f32[8,256]{1,0:T(8,128)}, f32[240,512]{1,0:T(8,128)S(1)}, f32[8,256]{1,0:T(8,128)S(1)}, ...) custom-call(f32[6,17,8,128]{3,2,1,0:T(8,128)S(1)} %collective-permut, ...), custom_call_target="tpu_custom_call" | custom-call | flops 29899999232 | bytes 1024 | tf_op jit(solution)/shard_map/pallas_call | solution.py:760
  60.1 1.5 copy-done.7
  61.7 0.9 shard_map.396
  64.3 1.7 dynamic-slice_add_fusion.1
  66.0 1.6 collective-permute-start.7
  67.5 1.3 dynamic-slice_add_fusion.3
  69.4 5.8 %shard_map.397 = (f32[6,16,8,128]{3,2,1,0:T(8,128)S(1)}, f32[6,16,8,128]{3,2,1,0:T(8,128)S(1)}, f32[6,16,8,128]{3,2,1,0:T(8,128)S(1)}, f32[16,16,128]{2,1,0:T(8,128)S(1)}) custom-call(f32[30,8,8,128]{3,2,1,0:T(8,128)S(1)} %copy-done.12, f32[240,2048]{1,0:T(8,128)S(1)} %copy-done.9, f32[240,256]{1,0:T(8,128)S(1)} %copy-done.16, ...), custom_call_target="tpu_custom_call" | custom-call | flops 14949999616 | bytes 1024 | tf_op jit(solution)/shard_map/pallas_call | solution.py:760
  75.2 0.8 collective-permute-start.9
  76.0 1.3 dynamic-slice_add_fusion.2
  77.3 1.4 dynamic-slice_add_fusion
  78.7 9.8 %collective-permute-done.7 = f32[448,512]{1,0:T(8,128)S(1)} collective-permute-done((f32[448,512]{1,0:T(8,128)S(1)}, f32[448,512]{1,0:T(8,128)S(1)}, u32[]{:S(2)}, u32[]{:S(2)}) %collective-permute-start.7) | collective-permute-done | bytes 917536 | tf_op jit(solution)/shard_map/ppermute | solution.py:55
  89.4 1.4 collective-permute-start.12
  90.9 4.9 %collective-permute-done.9 = f32[6,16,8,128]{3,2,1,0:T(8,128)S(1)} collective-permute-done((f32[6,16,8,128]{3,2,1,0:T(8,128)S(1)}, f32[6,16,8,128]{3,2,1,0:T(8,128)S(1)}, u32[]{:S(2)}, u32[]{:S(2)}) %collective-permute-start.9) | collective-permute-done | bytes 393248 | tf_op jit(solution)/shard_map/ppermute | solution.py:31
  96.3 3.4 %collective-permute-start.13 = (f32[2,16,8,128]{3,2,1,0:T(8,128)S(1)}, f32[2,16,8,128]{3,2,1,0:T(8,128)S(1)}, u32[]{:S(2)}, u32[]{:S(2)}) collective-permute-start(f32[2,16,8,128]{3,2,1,0:T(8,128)S(1)} %get-tuple-element.344), channel_id=1, source_target_pairs={{0,24},{8,0},{16,8},{24,16},{1,25},{9,1},{17,9},{25,17},{2,26},{10... | collective-permute-start | bytes 393224 | tf_op jit(solution)/shard_map/ppermute | solution.py:31
  99.8 6.7 %collective-permute-done.11 = f32[224,512]{1,0:T(8,128)S(1)} collective-permute-done((f32[224,512]{1,0:T(8,128)S(1)}, f32[224,512]{1,0:T(8,128)S(1)}, u32[]{:S(2)}, u32[]{:S(2)}) %collective-permute-start.11) | collective-permute-done | bytes 458784 | tf_op jit(solution)/shard_map/ppermute | solution.py:55
  106.8 0.9 collective-permute-start.15
  108.1 3.0 %collective-permute-done.15 = f32[16,8,128]{2,1,0:T(8,128)S(1)} collective-permute-done((f32[16,8,128]{2,1,0:T(8,128)S(1)}, f32[16,8,128]{2,1,0:T(8,128)S(1)}, u32[]{:S(2)}, u32[]{:S(2)}) %collective-permute-start.15) | collective-permute-done | bytes 65568 | tf_op jit(solution)/shard_map/ppermute | solution.py:885
  111.8 6.8 %shard_map.398 = (f32[8,256]{1,0:T(8,128)}, f32[240,512]{1,0:T(8,128)}, f32[384,512]{1,0:T(8,128)}, f32[384,512]{1,0:T(8,128)}, f32[384,512]{1,0:T(8,128)}, /*index=5*/f32[384,512]{1,0:T(8,128)}) custom-call(f32[16,16,128]{2,1,0:T(8,128)} %copy-done.14, f32[16,8,128]{2,1,0:T(8,128)} %bitcast_add_fusion.returned, f32[240,512]{1,0:T(8,128)} %copy-done.8, ...), custom_call_target="tpu_custom_call" | custom-call | flops 8049999872 | bytes 1024 | tf_op jit(solution)/shard_map/pallas_call | solution.py:760
  119.3 1.2 collective-permute-start.19
  120.5 1.1 collective-permute-done.17
  121.6 1.8 dynamic-slice_add_fusion.11
  123.4 0.8 collective-permute-start.20
  124.3 1.8 dynamic-slice_add_fusion.10
  126.0 0.9 collective-permute-start.21
  127.0 4.8 %collective-permute-done.19 = f32[104,512]{1,0:T(8,128)S(1)} collective-permute-done((f32[104,512]{1,0:T(8,128)S(1)}, f32[104,512]{1,0:T(8,128)S(1)}, u32[]{:S(2)}, u32[]{:S(2)}) %collective-permute-start.19) | collective-permute-done | bytes 213024 | tf_op jit(solution)/shard_map/ppermute | solution.py:55
  132.0 1.1 dynamic-slice_add_fusion.8
  133.0 1.7 collective-permute-done.20
  135.4 2.1 collective-permute-done.21
  137.4 1.0 dynamic-slice_add_fusion.20
  138.4 1.6 collective-permute-start.23
  140.0 1.0 dynamic-slice_add_fusion.18
  141.3 2.8 %collective-permute-done.23 = f32[96,512]{1,0:T(8,128)S(1)} collective-permute-done((f32[96,512]{1,0:T(8,128)S(1)}, f32[96,512]{1,0:T(8,128)S(1)}, u32[]{:S(2)}, u32[]{:S(2)}) %collective-permute-start.23) | collective-permute-done | bytes 196640 | tf_op jit(solution)/shard_map/ppermute | solution.py:55
  144.7 1.8 collective-permute-start.26
  146.5 6.7 %collective-permute-done.25 = f32[96,512]{1,0:T(8,128)S(1)} collective-permute-done((f32[96,512]{1,0:T(8,128)S(1)}, f32[96,512]{1,0:T(8,128)S(1)}, u32[]{:S(2)}, u32[]{:S(2)}) %collective-permute-start.25) | collective-permute-done | bytes 196640 | tf_op jit(solution)/shard_map/ppermute | solution.py:55
  153.7 6.6 %collective-permute-done.26 = f32[208,512]{1,0:T(8,128)S(1)} collective-permute-done((f32[208,512]{1,0:T(8,128)S(1)}, f32[208,512]{1,0:T(8,128)S(1)}, u32[]{:S(2)}, u32[]{:S(2)}) %collective-permute-start.26) | collective-permute-done | bytes 426016 | tf_op jit(solution)/shard_map/ppermute | solution.py:55
  161.6 1.1 collective-permute-start.30
  162.8 1.1 collective-permute-start.27
  163.9 4.0 %collective-permute-done.30 = f32[48,512]{1,0:T(8,128)S(1)} collective-permute-done((f32[48,512]{1,0:T(8,128)S(1)}, f32[48,512]{1,0:T(8,128)S(1)}, u32[]{:S(2)}, u32[]{:S(2)}) %collective-permute-start.30) | collective-permute-done | bytes 98336 | tf_op jit(solution)/shard_map/ppermute | solution.py:55
  167.9 1.4 collective-permute-start.31
  169.4 0.9 collective-permute-start.28
  170.3 3.4 %collective-permute-done.31 = f32[96,512]{1,0:T(8,128)S(1)} collective-permute-done((f32[96,512]{1,0:T(8,128)S(1)}, f32[96,512]{1,0:T(8,128)S(1)}, u32[]{:S(2)}, u32[]{:S(2)}) %collective-permute-start.31) | collective-permute-done | bytes 196640 | tf_op jit(solution)/shard_map/ppermute | solution.py:55
  173.7 1.6 collective-permute-start.33
  175.6 1.1 collective-permute-start.34
  176.7 4.7 %collective-permute-done.28 = f32[192,512]{1,0:T(8,128)S(1)} collective-permute-done((f32[192,512]{1,0:T(8,128)S(1)}, f32[192,512]{1,0:T(8,128)S(1)}, u32[]{:S(2)}, u32[]{:S(2)}) %collective-permute-start.28) | collective-permute-done | bytes 393248 | tf_op jit(solution)/shard_map/ppermute | solution.py:55
  181.5 1.5 collective-permute-start.35
  183.2 2.4 %collective-permute-done.33 = f32[96,512]{1,0:T(8,128)S(1)} collective-permute-done((f32[96,512]{1,0:T(8,128)S(1)}, f32[96,512]{1,0:T(8,128)S(1)}, u32[]{:S(2)}, u32[]{:S(2)}) %collective-permute-start.33) | collective-permute-done | bytes 196640 | tf_op jit(solution)/shard_map/ppermute | solution.py:55
  185.6 13.4 %collective-permute-done.34 = f32[448,512]{1,0:T(8,128)S(1)} collective-permute-done((f32[448,512]{1,0:T(8,128)S(1)}, f32[448,512]{1,0:T(8,128)S(1)}, u32[]{:S(2)}, u32[]{:S(2)}) %collective-permute-start.34) | collective-permute-done | bytes 917536 | tf_op jit(solution)/shard_map/ppermute | solution.py:55
  202.7 0.9 collective-permute-start.38
  203.6 1.6 collective-permute-start.39
  205.2 1.5 collective-permute-done.37.b_other
  206.7 3.1 %shard_map.399 = (f32[2,512,512]{2,1,0:T(8,128)}, f32[2,256,512]{2,1,0:T(8,128)}, f32[64,1024]{1,0:T(8,128)}, f32[64,512]{1,0:T(8,128)}, f32[32,1024]{1,0:T(8,12...) custom-call(f32[896,512]{1,0:T(8,128)S(1)} %maximum_add_fusion.a_mine, ...), custom_call_target="tpu_custom_call" | custom-call | bytes 1024 | tf_op jit(solution)/shard_map/pallas_call | solution.py:760
  209.8 4.0 %collective-permute-done.38 = f32[192,512]{1,0:T(8,128)S(1)} collective-permute-done((f32[192,512]{1,0:T(8,128)S(1)}, f32[192,512]{1,0:T(8,128)S(1)}, u32[]{:S(2)}, u32[]{:S(2)}) %collective-permute-start.38) | collective-permute-done | bytes 393248 | tf_op jit(solution)/shard_map/ppermute | solution.py:55
  215.1 1.8 collective-permute-done.41.d_other
  216.9 1.1 collective-permute-done.40.c_other
  218.0 3.4 %shard_map.400 = (f32[2,512,512]{2,1,0:T(8,128)}, f32[5,128,512]{2,1,0:T(8,128)}, f32[64,512]{1,0:T(8,128)}, f32[32,512]{1,0:T(8,128)}, f32[3,256]{1,0:T(4,128)}) custom-call(f32[384,512]{1,0:T(8,128)S(1)} %pad_maximum_fusion.5.c_mine, f32[384,512]{1,0:T(8,128)S(1)} %collective-permute-done.40.c_other, f32[384,512]{1,0:T(8,128)S(1)} %pad_maximum_fusion.6.d_mine, ...), custom_call_target="tpu_custom_call" | custom-call | flops 3449999872 | bytes 1024 | tf_op jit(solution)/shard_map/pallas_call | solution.py:760
  (166 shorter events, 14.3 us)
Async XLA Ops:
  0.7 7.8 %copy-start.26 = (s32[240]{0:T(256)S(1)}, s32[240]{0:T(256)}, u32[]{:S(2)}) copy-start(s32[240]{0:T(256)} %param.32) | copy-start | bytes 2884
  0.7 7.9 %copy-start.22 = (s32[240,8]{0,1:T(8,128)S(1)}, s32[240,8]{0,1:T(8,128)}, u32[]{:S(2)}) copy-start(s32[240,8]{0,1:T(8,128)} %param.33) | copy-start | bytes 23044
  0.7 7.9 %copy-start.24 = (s32[240,8]{0,1:T(8,128)S(1)}, s32[240,8]{0,1:T(8,128)}, u32[]{:S(2)}) copy-start(s32[240,8]{0,1:T(8,128)} %param.35) | copy-start | bytes 23044
  0.7 22.9 %copy-start.23 = (s32[240,8]{0,1:T(8,128)S(1)}, s32[240,8]{0,1:T(8,128)}, u32[]{:S(2)}) copy-start(s32[240,8]{0,1:T(8,128)} %param.34) | copy-start | bytes 23044
  0.7 22.9 %copy-start.25 = (s32[240,8]{0,1:T(8,128)S(1)}, s32[240,8]{0,1:T(8,128)}, u32[]{:S(2)}) copy-start(s32[240,8]{0,1:T(8,128)} %param.36) | copy-start | bytes 23044
  5.4 29.7 %copy-start = (f32[240,512]{1,0:T(8,128)S(1)}, f32[240,512]{1,0:T(8,128)}, u32[]{:S(2)}) copy-start(f32[240,512]{1,0:T(8,128)} %edge.5) | copy-start | bytes 1474564
  5.4 29.7 %copy-start.1 = (bf16[1024,64]{0,1:T(8,128)(2,1)S(1)}, bf16[1024,64]{0,1:T(8,128)(2,1)}, u32[]{:S(2)}) copy-start(bf16[1024,64]{0,1:T(8,128)(2,1)} %param.41) | copy-start | bytes 393220
  5.4 29.7 %copy-start.2 = (bf16[64,512]{1,0:T(8,128)(2,1)S(1)}, bf16[64,512]{1,0:T(8,128)(2,1)}, u32[]{:S(2)}) copy-start(bf16[64,512]{1,0:T(8,128)(2,1)} %trip_up.1) | copy-start | bytes 196612
  5.4 29.7 %copy-start.3 = (bf16[1024,32]{0,1:T(8,128)(2,1)S(1)}, bf16[1024,32]{0,1:T(8,128)(2,1)}, u32[]{:S(2)}) copy-start(bf16[1024,32]{0,1:T(8,128)(2,1)} %param.44) | copy-start | bytes 196612
  5.4 29.7 %copy-start.4 = (bf16[32,512]{1,0:T(8,128)(2,1)S(1)}, bf16[32,512]{1,0:T(8,128)(2,1)}, u32[]{:S(2)}) copy-start(bf16[32,512]{1,0:T(8,128)(2,1)} %quad_up.1) | copy-start | bytes 98308
  5.4 29.7 %copy-start.5 = (f32[8,256]{1,0:T(8,128)S(1)}, f32[8,256]{1,0:T(8,128)}, u32[]{:S(2)}) copy-start(f32[8,256]{1,0:T(8,128)} %cot_atoms.1) | copy-start | bytes 24580
  5.4 29.7 %copy-start.6 = (f32[8,256]{1,0:T(8,128)S(1)}, f32[8,256]{1,0:T(8,128)}, u32[]{:S(2)}) copy-start(f32[8,256]{1,0:T(8,128)} %cot_energy.1) | copy-start | bytes 24580
  5.4 29.7 %copy-start.10 = (f32[240,128]{1,0:T(8,128)S(1)}, f32[240,128]{1,0:T(8,128)}, u32[]{:S(2)}) copy-start(f32[240,128]{1,0:T(8,128)} %get-tuple-element.173.radial) | copy-start | bytes 368644
  5.5 29.7 %copy-start.11 = (f32[17,16,128]{2,1,0:T(8,128)S(1)}, f32[17,16,128]{2,1,0:T(8,128)}, u32[]{:S(2)}) copy-start(f32[17,16,128]{2,1,0:T(8,128)} %get-tuple-element.169.local) | copy-start | bytes 417796
  5.5 29.7 %copy-start.13 = (f32[240,128]{1,0:T(8,128)S(1)}, f32[240,128]{1,0:T(8,128)}, u32[]{:S(2)}) copy-start(f32[240,128]{1,0:T(8,128)} %get-tuple-element.171.columns) | copy-start | bytes 368644
  5.5 29.7 %copy-start.17 = (f32[8,256]{1,0:T(8,128)S(1)}, f32[8,256]{1,0:T(8,128)}, u32[]{:S(2)}) copy-start(f32[8,256]{1,0:T(8,128)} %get-tuple-element.170.tagged) | copy-start | bytes 24580
  5.5 5.5 %collective-permute-start = (f32[17,8,128]{2,1,0:T(8,128)}, f32[17,8,128]{2,1,0:T(8,128)S(1)}, u32[]{:S(2)}, u32[]{:S(2)}) collective-permute-start(f32[17,8,128]{2,1,0:T(8,128)} %get-tuple-element.168), channel_id=1, source_target_pairs={{0,1},{1,0},{2,3},{3,2},{4,5},{5,4},{6,7},{7,6},{8,9},{9,8},{10,11... | collective-permute-start | bytes 208904 | tf_op jit(solution)/shard_map/ppermute | solution.py:36
  11.9 7.5 %collective-permute-start.2 = (f32[2,17,8,128]{3,2,1,0:T(8,128)S(1)}, f32[2,17,8,128]{3,2,1,0:T(8,128)S(1)}, u32[]{:S(2)}, u32[]{:S(2)}) collective-permute-start(f32[2,17,8,128]{3,2,1,0:T(8,128)S(1)} %pad_maximum_fusion.14), channel_id=1, source_target_pairs={{0,24},{8,0},{16,8},{24,16},{1,25},{9,1},{17,9},{25,17},{2,26},{10... | collective-permute-start | bytes 417800 | tf_op jit(solution)/shard_map/ppermute | solution.py:31
  16.1 6.9 %collective-permute-start.1 = (f32[2,17,8,128]{3,2,1,0:T(8,128)S(1)}, f32[2,17,8,128]{3,2,1,0:T(8,128)S(1)}, u32[]{:S(2)}, u32[]{:S(2)}) collective-permute-start(f32[2,17,8,128]{3,2,1,0:T(8,128)S(1)} %pad_maximum_fusion.14), channel_id=1, source_target_pairs={{0,8},{8,16},{16,24},{24,0},{1,9},{9,17},{17,25},{25,1},{2,10},{10... | collective-permute-start | bytes 417800 | tf_op jit(solution)/shard_map/ppermute | solution.py:31
  23.0 8.9 %collective-permute-start.4 = (f32[6,17,8,128]{3,2,1,0:T(8,128)S(1)}, f32[6,17,8,128]{3,2,1,0:T(8,128)S(1)}, u32[]{:S(2)}, u32[]{:S(2)}) collective-permute-start(f32[6,17,8,128]{3,2,1,0:T(8,128)S(1)} %pad_maximum_fusion.8.halo_here), channel_id=1, source_target_pairs={{0,6},{2,0},{4,2},{6,4},{1,7},{3,1},{5,3},{7,5},{8,14},{10,8},{12,... | collective-permute-start | bytes 1253384 | tf_op jit(solution)/shard_map/ppermute | solution.py:31
  23.0 12.0 %collective-permute-start.3 = (f32[6,17,8,128]{3,2,1,0:T(8,128)S(1)}, f32[6,17,8,128]{3,2,1,0:T(8,128)S(1)}, u32[]{:S(2)}, u32[]{:S(2)}) collective-permute-start(f32[6,17,8,128]{3,2,1,0:T(8,128)S(1)} %pad_maximum_fusion.8.halo_here), channel_id=1, source_target_pairs={{0,2},{2,4},{4,6},{6,0},{1,3},{3,5},{5,7},{7,1},{8,10},{10,12},{12... | collective-permute-start | bytes 1253384 | tf_op jit(solution)/shard_map/ppermute | solution.py:31
  60.1 4.2 %collective-permute-start.5 = (f32[896,512]{1,0:T(8,128)}, f32[896,512]{1,0:T(8,128)}, u32[]{:S(2)}, u32[]{:S(2)}) collective-permute-start(f32[896,512]{1,0:T(8,128)} %get-tuple-element.179), channel_id=1, source_target_pairs={{0,2},{2,0},{1,3},{3,1},{4,6},{6,4},{5,7},{7,5},{8,10},{10,8},{9,1... | collective-permute-start | bytes 5505032 | tf_op jit(solution)/shard_map/ppermute | solution.py:55
  62.6 4.9 %collective-permute-start.6 = (f32[768,512]{1,0:T(8,128)S(1)}, f32[768,512]{1,0:T(8,128)}, u32[]{:S(2)}, u32[]{:S(2)}) collective-permute-start(f32[768,512]{1,0:T(8,128)S(1)} %get-tuple-element.184), channel_id=1, source_target_pairs={{0,2},{2,0},{1,3},{3,1},{4,6},{6,4},{5,7},{7,5},{8,10},{10,8},{9,1... | collective-permute-start | bytes 4718600 | tf_op jit(solution)/shard_map/ppermute | solution.py:55
  64.2 5.2 %copy-start.12 = (f32[30,8,8,128]{3,2,1,0:T(8,128)S(1)}, f32[30,8,8,128]{3,2,1,0:T(8,128)}, u32[]{:S(2)}) copy-start(f32[30,8,8,128]{3,2,1,0:T(8,128)} %get-tuple-element.177.cosines) | copy-start | bytes 2949124
  66.0 3.4 %copy-start.9 = (f32[240,2048]{1,0:T(8,128)S(1)}, f32[240,2048]{1,0:T(8,128)}, u32[]{:S(2)}) copy-start(f32[240,2048]{1,0:T(8,128)} %get-tuple-element.188.sums) | copy-start | bytes 5898244
  66.0 3.4 %copy-start.16 = (f32[240,256]{1,0:T(8,128)S(1)}, f32[240,256]{1,0:T(8,128)}, u32[]{:S(2)}) copy-start(f32[240,256]{1,0:T(8,128)} %copy-done.15) | copy-start | bytes 737284
  66.0 22.5 %collective-permute-start.7 = (f32[448,512]{1,0:T(8,128)S(1)}, f32[448,512]{1,0:T(8,128)S(1)}, u32[]{:S(2)}, u32[]{:S(2)}) collective-permute-start(f32[448,512]{1,0:T(8,128)S(1)} %dynamic-slice_add_fusion.1), channel_id=1, source_target_pairs={{0,1},{1,0},{2,3},{3,2},{4,5},{5,4},{6,7},{7,6},{8,9},{9,8},{10,11... | collective-permute-start | bytes 2752520 | tf_op jit(solution)/shard_map/ppermute | solution.py:55
  68.8 20.5 %collective-permute-start.8 = (f32[384,512]{1,0:T(8,128)S(1)}, f32[384,512]{1,0:T(8,128)S(1)}, u32[]{:S(2)}, u32[]{:S(2)}) collective-permute-start(f32[384,512]{1,0:T(8,128)S(1)} %dynamic-slice_add_fusion.3), channel_id=1, source_target_pairs={{0,4},{4,0},{1,5},{5,1},{2,6},{6,2},{3,7},{7,3},{8,12},{12,8},{9,1... | collective-permute-start | bytes 2359304 | tf_op jit(solution)/shard_map/ppermute | solution.py:55
  75.2 3.4 %copy-start.14 = (f32[16,16,128]{2,1,0:T(8,128)}, f32[16,16,128]{2,1,0:T(8,128)S(1)}, u32[]{:S(2)}) copy-start(f32[16,16,128]{2,1,0:T(8,128)S(1)} %get-tuple-element.190.back_local) | copy-start | bytes 393220
  75.2 20.5 %collective-permute-start.9 = (f32[6,16,8,128]{3,2,1,0:T(8,128)S(1)}, f32[6,16,8,128]{3,2,1,0:T(8,128)S(1)}, u32[]{:S(2)}, u32[]{:S(2)}) collective-permute-start(f32[6,16,8,128]{3,2,1,0:T(8,128)S(1)} %get-tuple-element.203), channel_id=1, source_target_pairs={{0,6},{2,0},{4,2},{6,4},{1,7},{3,1},{5,3},{7,5},{8,14},{10,8},{12,... | collective-permute-start | bytes 1179656 | tf_op jit(solution)/shard_map/ppermute | solution.py:31
  76.0 19.8 %collective-permute-start.10 = (f32[6,16,8,128]{3,2,1,0:T(8,128)S(1)}, f32[6,16,8,128]{3,2,1,0:T(8,128)S(1)}, u32[]{:S(2)}, u32[]{:S(2)}) collective-permute-start(f32[6,16,8,128]{3,2,1,0:T(8,128)S(1)} %get-tuple-element.204), channel_id=1, source_target_pairs={{0,2},{2,4},{4,6},{6,0},{1,3},{3,5},{5,7},{7,1},{8,10},{10,12},{12... | collective-permute-start | bytes 1179656 | tf_op jit(solution)/shard_map/ppermute | solution.py:31
  88.5 17.9 %collective-permute-start.11 = (f32[224,512]{1,0:T(8,128)S(1)}, f32[224,512]{1,0:T(8,128)S(1)}, u32[]{:S(2)}, u32[]{:S(2)}) collective-permute-start(f32[224,512]{1,0:T(8,128)S(1)} %dynamic-slice_add_fusion.5), channel_id=1, source_target_pairs={{0,4},{4,0},{1,5},{5,1},{2,6},{6,2},{3,7},{7,3},{8,12},{12,8},{9,1... | collective-permute-start | bytes 1376264 | tf_op jit(solution)/shard_map/ppermute | solution.py:55
  89.4 10.4 %collective-permute-start.12 = (f32[192,512]{1,0:T(8,128)S(1)}, f32[192,512]{1,0:T(8,128)S(1)}, u32[]{:S(2)}, u32[]{:S(2)}) collective-permute-start(f32[192,512]{1,0:T(8,128)S(1)} %dynamic-slice_add_fusion.13), channel_id=1, source_target_pairs={{0,1},{1,0},{2,3},{3,2},{4,5},{5,4},{6,7},{7,6},{8,9},{9,8},{10,11... | collective-permute-start | bytes 1179656 | tf_op jit(solution)/shard_map/ppermute | solution.py:55
  95.9 10.8 %collective-permute-start.14 = (f32[2,16,8,128]{3,2,1,0:T(8,128)S(1)}, f32[2,16,8,128]{3,2,1,0:T(8,128)S(1)}, u32[]{:S(2)}, u32[]{:S(2)}) collective-permute-start(f32[2,16,8,128]{3,2,1,0:T(8,128)S(1)} %get-tuple-element.343), channel_id=1, source_target_pairs={{0,8},{8,16},{16,24},{24,0},{1,9},{9,17},{17,25},{25,1},{2,10},{10... | collective-permute-start | bytes 393224 | tf_op jit(solution)/shard_map/ppermute | solution.py:31
  96.3 10.4 %collective-permute-start.13 = (f32[2,16,8,128]{3,2,1,0:T(8,128)S(1)}, f32[2,16,8,128]{3,2,1,0:T(8,128)S(1)}, u32[]{:S(2)}, u32[]{:S(2)}) collective-permute-start(f32[2,16,8,128]{3,2,1,0:T(8,128)S(1)} %get-tuple-element.344), channel_id=1, source_target_pairs={{0,24},{8,0},{16,8},{24,16},{1,25},{9,1},{17,9},{25,17},{2,26},{10... | collective-permute-start | bytes 393224 | tf_op jit(solution)/shard_map/ppermute | solution.py:31
  106.8 4.3 %collective-permute-start.15 = (f32[16,8,128]{2,1,0:T(8,128)S(1)}, f32[16,8,128]{2,1,0:T(8,128)S(1)}, u32[]{:S(2)}, u32[]{:S(2)}) collective-permute-start(f32[16,8,128]{2,1,0:T(8,128)S(1)} %select_bitcast_fusion.2), channel_id=1, source_target_pairs={{0,1},{1,0},{2,3},{3,2},{4,5},{5,4},{6,7},{7,6},{8,9},{9,8},{10,11... | collective-permute-start | bytes 196616 | tf_op jit(solution)/shard_map/ppermute | solution.py:885
  107.7 10.9 %collective-permute-start.16 = (f32[208,512]{1,0:T(8,128)S(1)}, f32[208,512]{1,0:T(8,128)S(1)}, u32[]{:S(2)}, u32[]{:S(2)}) collective-permute-start(f32[208,512]{1,0:T(8,128)S(1)} %dynamic-slice_add_fusion.7), channel_id=1, source_target_pairs={{0,8},{8,0},{16,24},{24,16},{1,9},{9,1},{17,25},{25,17},{2,10},{10... | collective-permute-start | bytes 1277960 | tf_op jit(solution)/shard_map/ppermute | solution.py:55
  118.6 5.7 %copy-start.20 = (f32[384,512]{1,0:T(8,128)S(1)}, f32[384,512]{1,0:T(8,128)}, u32[]{:S(2)}) copy-start(f32[384,512]{1,0:T(8,128)} %get-tuple-element.247) | copy-start | bytes 2359300
  118.6 13.3 %copy-start.21 = (f32[384,512]{1,0:T(8,128)S(1)}, f32[384,512]{1,0:T(8,128)}, u32[]{:S(2)}) copy-start(f32[384,512]{1,0:T(8,128)} %get-tuple-element.243) | copy-start | bytes 2359300
  118.7 2.9 %collective-permute-start.17 = (f32[384,512]{1,0:T(8,128)}, f32[384,512]{1,0:T(8,128)S(1)}, u32[]{:S(2)}, u32[]{:S(2)}) collective-permute-start(f32[384,512]{1,0:T(8,128)} %get-tuple-element.234), channel_id=1, source_target_pairs={{0,2},{2,0},{1,3},{3,1},{4,6},{6,4},{5,7},{7,5},{8,10},{10,8},{9,1... | collective-permute-start | bytes 2359304 | tf_op jit(solution)/shard_map/ppermute | solution.py:55
  118.8 5.5 %collective-permute-start.18 = (f32[384,512]{1,0:T(8,128)}, f32[384,512]{1,0:T(8,128)}, u32[]{:S(2)}, u32[]{:S(2)}) collective-permute-start(f32[384,512]{1,0:T(8,128)} %get-tuple-element.238), channel_id=1, source_target_pairs={{0,2},{2,0},{1,3},{3,1},{4,6},{6,4},{5,7},{7,5},{8,10},{10,8},{9,1... | collective-permute-start | bytes 2359304 | tf_op jit(solution)/shard_map/ppermute | solution.py:55
  119.3 12.5 %collective-permute-start.19 = (f32[104,512]{1,0:T(8,128)S(1)}, f32[104,512]{1,0:T(8,128)S(1)}, u32[]{:S(2)}, u32[]{:S(2)}) collective-permute-start(f32[104,512]{1,0:T(8,128)S(1)} %dynamic-slice_add_fusion.15), channel_id=1, source_target_pairs={{0,16},{8,24},{16,0},{24,8},{1,17},{9,25},{17,1},{25,9},{2,18},{10... | collective-permute-start | bytes 638984 | tf_op jit(solution)/shard_map/ppermute | solution.py:55
  123.4 11.4 %collective-permute-start.20 = (f32[192,512]{1,0:T(8,128)}, f32[192,512]{1,0:T(8,128)S(1)}, u32[]{:S(2)}, u32[]{:S(2)}) collective-permute-start(f32[192,512]{1,0:T(8,128)} %dynamic-slice_add_fusion.11), channel_id=1, source_target_pairs={{0,1},{1,0},{2,3},{3,2},{4,5},{5,4},{6,7},{7,6},{8,9},{9,8},{10,11... | collective-permute-start | bytes 1179656 | tf_op jit(solution)/shard_map/ppermute | solution.py:55
  126.0 11.4 %collective-permute-start.21 = (f32[192,512]{1,0:T(8,128)}, f32[192,512]{1,0:T(8,128)}, u32[]{:S(2)}, u32[]{:S(2)}) collective-permute-start(f32[192,512]{1,0:T(8,128)} %dynamic-slice_add_fusion.10), channel_id=1, source_target_pairs={{0,4},{4,0},{1,5},{5,1},{2,6},{6,2},{3,7},{7,3},{8,12},{12,8},{9,1... | collective-permute-start | bytes 1179656 | tf_op jit(solution)/shard_map/ppermute | solution.py:55
  131.8 12.8 %collective-permute-start.24 = (f32[104,512]{1,0:T(8,128)S(1)}, f32[104,512]{1,0:T(8,128)S(1)}, u32[]{:S(2)}, u32[]{:S(2)}) collective-permute-start(f32[104,512]{1,0:T(8,128)S(1)} %add.320), channel_id=1, source_target_pairs={{0,16},{8,24},{16,0},{24,8},{1,17},{9,25},{17,1},{25,9},{2,18},{10... | collective-permute-start | bytes 638984 | tf_op jit(solution)/shard_map/ppermute | solution.py:55
  134.8 6.6 %collective-permute-start.22 = (f32[96,512]{1,0:T(8,128)S(1)}, f32[96,512]{1,0:T(8,128)S(1)}, u32[]{:S(2)}, u32[]{:S(2)}) collective-permute-start(f32[96,512]{1,0:T(8,128)S(1)} %dynamic-slice_add_fusion.21), channel_id=1, source_target_pairs={{0,4},{4,0},{1,5},{5,1},{2,6},{6,2},{3,7},{7,3},{8,12},{12,8},{9,1... | collective-permute-start | bytes 589832 | tf_op jit(solution)/shard_map/ppermute | solution.py:55
  138.4 5.7 %collective-permute-start.23 = (f32[96,512]{1,0:T(8,128)S(1)}, f32[96,512]{1,0:T(8,128)S(1)}, u32[]{:S(2)}, u32[]{:S(2)}) collective-permute-start(f32[96,512]{1,0:T(8,128)S(1)} %dynamic-slice_add_fusion.20), channel_id=1, source_target_pairs={{0,1},{1,0},{2,3},{3,2},{4,5},{5,4},{6,7},{7,6},{8,9},{9,8},{10,11... | collective-permute-start | bytes 589832 | tf_op jit(solution)/shard_map/ppermute | solution.py:55
  144.2 9.0 %collective-permute-start.25 = (f32[96,512]{1,0:T(8,128)S(1)}, f32[96,512]{1,0:T(8,128)S(1)}, u32[]{:S(2)}, u32[]{:S(2)}) collective-permute-start(f32[96,512]{1,0:T(8,128)S(1)} %dynamic-slice_add_fusion.17), channel_id=1, source_target_pairs={{0,8},{8,0},{16,24},{24,16},{1,9},{9,1},{17,25},{25,17},{2,10},{10... | collective-permute-start | bytes 589832 | tf_op jit(solution)/shard_map/ppermute | solution.py:55
  144.7 15.6 %collective-permute-start.26 = (f32[208,512]{1,0:T(8,128)S(1)}, f32[208,512]{1,0:T(8,128)S(1)}, u32[]{:S(2)}, u32[]{:S(2)}) collective-permute-start(f32[208,512]{1,0:T(8,128)S(1)} %pad_maximum_fusion.7), channel_id=1, source_target_pairs={{0,8},{8,0},{16,24},{24,16},{1,9},{9,1},{17,25},{25,17},{2,10},{10... | collective-permute-start | bytes 1277960 | tf_op jit(solution)/shard_map/ppermute | solution.py:55
  153.2 7.2 %collective-permute-start.29 = (f32[48,512]{1,0:T(8,128)S(1)}, f32[48,512]{1,0:T(8,128)S(1)}, u32[]{:S(2)}, u32[]{:S(2)}) collective-permute-start(f32[48,512]{1,0:T(8,128)S(1)} %dynamic-slice_add_fusion.23), channel_id=1, source_target_pairs={{0,16},{8,24},{16,0},{24,8},{1,17},{9,25},{17,1},{25,9},{2,18},{10... | collective-permute-start | bytes 294920 | tf_op jit(solution)/shard_map/ppermute | solution.py:55
  161.6 6.2 %collective-permute-start.30 = (f32[48,512]{1,0:T(8,128)S(1)}, f32[48,512]{1,0:T(8,128)S(1)}, u32[]{:S(2)}, u32[]{:S(2)}) collective-permute-start(f32[48,512]{1,0:T(8,128)S(1)} %add_add_fusion.2), channel_id=1, source_target_pairs={{0,16},{8,24},{16,0},{24,8},{1,17},{9,25},{17,1},{25,9},{2,18},{10... | collective-permute-start | bytes 294920 | tf_op jit(solution)/shard_map/ppermute | solution.py:55
  162.8 12.6 %collective-permute-start.27 = (f32[224,512]{1,0:T(8,128)S(1)}, f32[224,512]{1,0:T(8,128)S(1)}, u32[]{:S(2)}, u32[]{:S(2)}) collective-permute-start(f32[224,512]{1,0:T(8,128)S(1)} %fusion), channel_id=1, source_target_pairs={{0,4},{4,0},{1,5},{5,1},{2,6},{6,2},{3,7},{7,3},{8,12},{12,8},{9,1... | collective-permute-start | bytes 1376264 | tf_op jit(solution)/shard_map/ppermute | solution.py:55
  167.9 5.7 %collective-permute-start.31 = (f32[96,512]{1,0:T(8,128)S(1)}, f32[96,512]{1,0:T(8,128)S(1)}, u32[]{:S(2)}, u32[]{:S(2)}) collective-permute-start(f32[96,512]{1,0:T(8,128)S(1)} %pad_maximum_fusion.13), channel_id=1, source_target_pairs={{0,8},{8,0},{16,24},{24,16},{1,9},{9,1},{17,25},{25,17},{2,10},{10... | collective-permute-start | bytes 589832 | tf_op jit(solution)/shard_map/ppermute | solution.py:55
  169.4 12.0 %collective-permute-start.28 = (f32[192,512]{1,0:T(8,128)S(1)}, f32[192,512]{1,0:T(8,128)S(1)}, u32[]{:S(2)}, u32[]{:S(2)}) collective-permute-start(f32[192,512]{1,0:T(8,128)S(1)} %slice.49), channel_id=1, source_target_pairs={{0,1},{1,0},{2,3},{3,2},{4,5},{5,4},{6,7},{7,6},{8,9},{9,8},{10,11... | collective-permute-start | bytes 1179656 | tf_op jit(solution)/shard_map/ppermute | solution.py:55
  173.7 11.9 %collective-permute-start.33 = (f32[96,512]{1,0:T(8,128)S(1)}, f32[96,512]{1,0:T(8,128)S(1)}, u32[]{:S(2)}, u32[]{:S(2)}) collective-permute-start(f32[96,512]{1,0:T(8,128)S(1)} %get-tuple-element.285), channel_id=1, source_target_pairs={{0,1},{1,0},{2,3},{3,2},{4,5},{5,4},{6,7},{7,6},{8,9},{9,8},{10,11... | collective-permute-start | bytes 589832 | tf_op jit(solution)/shard_map/ppermute | solution.py:55
  175.2 7.8 %collective-permute-start.32 = (f32[96,512]{1,0:T(8,128)S(1)}, f32[96,512]{1,0:T(8,128)S(1)}, u32[]{:S(2)}, u32[]{:S(2)}) collective-permute-start(f32[96,512]{1,0:T(8,128)S(1)} %get-tuple-element.283), channel_id=1, source_target_pairs={{0,4},{4,0},{1,5},{5,1},{2,6},{6,2},{3,7},{7,3},{8,12},{12,8},{9,1... | collective-permute-start | bytes 589832 | tf_op jit(solution)/shard_map/ppermute | solution.py:55
  175.6 23.4 %collective-permute-start.34 = (f32[448,512]{1,0:T(8,128)S(1)}, f32[448,512]{1,0:T(8,128)S(1)}, u32[]{:S(2)}, u32[]{:S(2)}) collective-permute-start(f32[448,512]{1,0:T(8,128)S(1)} %pad_maximum_fusion.1), channel_id=1, source_target_pairs={{0,1},{1,0},{2,3},{3,2},{4,5},{5,4},{6,7},{7,6},{8,9},{9,8},{10,11... | collective-permute-start | bytes 2752520 | tf_op jit(solution)/shard_map/ppermute | solution.py:55
  181.5 19.2 %collective-permute-start.35 = (f32[384,512]{1,0:T(8,128)S(1)}, f32[384,512]{1,0:T(8,128)S(1)}, u32[]{:S(2)}, u32[]{:S(2)}) collective-permute-start(f32[384,512]{1,0:T(8,128)S(1)} %pad_maximum_fusion.4), channel_id=1, source_target_pairs={{0,4},{4,0},{1,5},{5,1},{2,6},{6,2},{3,7},{7,3},{8,12},{12,8},{9,1... | collective-permute-start | bytes 2359304 | tf_op jit(solution)/shard_map/ppermute | solution.py:55
  200.6 6.1 %collective-permute-start.36 = (f32[896,512]{1,0:T(8,128)S(1)}, f32[896,512]{1,0:T(8,128)S(1)}, u32[]{:S(2)}, u32[]{:S(2)}) collective-permute-start(f32[896,512]{1,0:T(8,128)S(1)} %maximum_add_fusion.a_mine), channel_id=1, source_target_pairs={{0,2},{2,0},{1,3},{3,1},{4,6},{6,4},{5,7},{7,5},{8,10},{10,8},{9,1... | collective-permute-start | bytes 5505032 | tf_op jit(solution)/shard_map/ppermute | solution.py:55
  202.2 4.5 %collective-permute-start.37 = (f32[768,512]{1,0:T(8,128)S(1)}, f32[768,512]{1,0:T(8,128)S(1)}, u32[]{:S(2)}, u32[]{:S(2)}) collective-permute-start(f32[768,512]{1,0:T(8,128)S(1)} %maximum_add_fusion.1.b_mine), channel_id=1, source_target_pairs={{0,2},{2,0},{1,3},{3,1},{4,6},{6,4},{5,7},{7,5},{8,10},{10,8},{9,1... | collective-permute-start | bytes 4718600 | tf_op jit(solution)/shard_map/ppermute | solution.py:55
  202.7 11.1 %collective-permute-start.38 = (f32[192,512]{1,0:T(8,128)S(1)}, f32[192,512]{1,0:T(8,128)S(1)}, u32[]{:S(2)}, u32[]{:S(2)}) collective-permute-start(f32[192,512]{1,0:T(8,128)S(1)} %pad_maximum_fusion.11), channel_id=1, source_target_pairs={{0,1},{1,0},{2,3},{3,2},{4,5},{5,4},{6,7},{7,6},{8,9},{9,8},{10,11... | collective-permute-start | bytes 1179656 | tf_op jit(solution)/shard_map/ppermute | solution.py:55
  203.6 10.8 %collective-permute-start.39 = (f32[192,512]{1,0:T(8,128)S(1)}, f32[192,512]{1,0:T(8,128)S(1)}, u32[]{:S(2)}, u32[]{:S(2)}) collective-permute-start(f32[192,512]{1,0:T(8,128)S(1)} %pad_maximum_fusion.12), channel_id=1, source_target_pairs={{0,4},{4,0},{1,5},{5,1},{2,6},{6,2},{3,7},{7,3},{8,12},{12,8},{9,1... | collective-permute-start | bytes 1179656 | tf_op jit(solution)/shard_map/ppermute | solution.py:55
  214.5 2.4 %collective-permute-start.41 = (f32[384,512]{1,0:T(8,128)S(1)}, f32[384,512]{1,0:T(8,128)S(1)}, u32[]{:S(2)}, u32[]{:S(2)}) collective-permute-start(f32[384,512]{1,0:T(8,128)S(1)} %pad_maximum_fusion.6.d_mine), channel_id=1, source_target_pairs={{0,2},{2,0},{1,3},{3,1},{4,6},{6,4},{5,7},{7,5},{8,10},{10,8},{9,1... | collective-permute-start | bytes 2359304 | tf_op jit(solution)/shard_map/ppermute | solution.py:55
  214.6 3.4 %collective-permute-start.40 = (f32[384,512]{1,0:T(8,128)S(1)}, f32[384,512]{1,0:T(8,128)S(1)}, u32[]{:S(2)}, u32[]{:S(2)}) collective-permute-start(f32[384,512]{1,0:T(8,128)S(1)} %pad_maximum_fusion.5.c_mine), channel_id=1, source_target_pairs={{0,2},{2,0},{1,3},{3,1},{4,6},{6,4},{5,7},{7,5},{8,10},{10,8},{9,1... | collective-permute-start | bytes 2359304 | tf_op jit(solution)/shard_map/ppermute | solution.py:55
  (5 other events, 11.3 us)

commit v11 on v10

--- a/solution.py
+++ b/solution.py
@@ -295,9 +295,9 @@
     tags = to_column(tag_row[...])
     radial = radial_of(to_column(length))
     radial_out[...] = radial
-    split = stacked(radial)
+    split = side_by_side(radial)
     for k in range(5):
-        rads[k] = folded(dot(split, w_rad[k]))
+        rads[k] = dot(split, jnp.concatenate([w_rad[k], w_rad[k]], axis=0))
     split = stacked(edge[...])
     pre[0] = folded(dot(split, w_in[0]))
     pre[1] = folded(dot(split, w_in[1]))
@@ -548,7 +548,8 @@
         [gathered, summary, updated, a0_act, new_atoms, e_act, d_a0, d_a1, d_e, d_out, d_gate], axis=1
     )
     split_cores(core, first, keep, send)
-    grad_sums[...] = times(d_down, weight[...])
+    twice = jnp.concatenate([weight[...], weight[...]], axis=0)
+    grad_sums[...] = dot(side_by_side(d_down), twice)
 
 
 def late_kernel(grad_rads, radial, atom_rows, quad_up_grad, core, keep, send, second):

time: 222 us -> 222 us (level)
  no operation moved by 1% of the time
where the time goes in v11:
time: 222 us; the launch traced here: 221 us
  waiting for transfers between devices  109 us (49%)
  Pallas kernels  49.4 us (22%)
  starting transfers between devices  38.8 us (17%)
  other arithmetic  16.6 us (7%)
  local copies, waits for them, and re-layouts  4.19 us (2%)
  between operations  3.7 us (2%)
    ppermute x32, waiting for transfers between devices, swap(): return lax.ppermute(value, axis, [(i, i ^ 1 << bit) for i in range(count)])  80.5 us
    pallas_call x7, Pallas kernels, call(): pl.pallas_call(kernel, out_shape=[jax.ShapeDtypeStruct(shape, F32) for sh...  49.4 us
    ppermute x32, starting transfers between devices, swap(): return lax.ppermute(value, axis, [(i, i ^ 1 << bit) for i in range(count)])  25.5 us
    ppermute x8, waiting for transfers between devices, shifted(): return lax.ppermute(value, axis, pairs)  22.9 us
    add x24, other arithmetic, part(): total = total + lax.dynamic_slice_in_dim(x, at, size)  12.9 us
    ppermute x8, starting transfers between devices, shifted(): return lax.ppermute(value, axis, pairs)  9.38 us
  transfers between devices with their start and end apart: 42, of which 30 were waited for; matrix products, arithmetic and copies ran while one was open for 8% of the time, Pallas kernels for 8%

profile of v11, /device:TPU:0, one launch (start us, length us, event | category | flops | bytes accessed | tf_op | source)
XLA Modules:
  0.0 221.4 jit_solution(1649402385313345790)
XLA Ops:
  0.7 4.4 %shard_map.394 = (f32[17,8,128]{2,1,0:T(8,128)}, f32[17,16,128]{2,1,0:T(8,128)}, f32[8,256]{1,0:T(8,128)}, f32[2,240,512]{2,1,0:T(8,128)}, f32[240,128]{1,0:T(8,...) custom-call(f32[240,512]{1,0:T(8,128)} %edge.5, f32[3,240]{1,0:T(4,128)} %vec.1, ...), custom_call_target="tpu_custom_call" | custom-call | flops 5750000128 | bytes 1024 | tf_op jit(solution)/shard_map/pallas_call | solution.py:761
  5.2 3.0 %collective-permute-start = (f32[17,8,128]{2,1,0:T(8,128)}, f32[17,8,128]{2,1,0:T(8,128)S(1)}, u32[]{:S(2)}, u32[]{:S(2)}) collective-permute-start(f32[17,8,128]{2,1,0:T(8,128)} %get-tuple-element.168), channel_id=1, source_target_pairs={{0,1},{1,0},{2,3},{3,2},{4,5},{5,4},{6,7},{7,6},{8,9},{9,8},{10,11... | collective-permute-start | bytes 208904 | tf_op jit(solution)/shard_map/ppermute | solution.py:36
  8.4 2.3 %collective-permute-done = f32[17,8,128]{2,1,0:T(8,128)S(1)} collective-permute-done((f32[17,8,128]{2,1,0:T(8,128)}, f32[17,8,128]{2,1,0:T(8,128)S(1)}, u32[]{:S(2)}, u32[]{:S(2)}) %collective-permute-start) | collective-permute-done | bytes 69664 | tf_op jit(solution)/shard_map/ppermute | solution.py:36
  10.7 0.9 select_bitcast_fusion.1
  11.6 4.2 %collective-permute-start.2 = (f32[2,17,8,128]{3,2,1,0:T(8,128)S(1)}, f32[2,17,8,128]{3,2,1,0:T(8,128)S(1)}, u32[]{:S(2)}, u32[]{:S(2)}) collective-permute-start(f32[2,17,8,128]{3,2,1,0:T(8,128)S(1)} %pad_maximum_fusion.14), channel_id=1, source_target_pairs={{0,24},{8,0},{16,8},{24,16},{1,25},{9,1},{17,9},{25,17},{2,26},{10... | collective-permute-start | bytes 417800 | tf_op jit(solution)/shard_map/ppermute | solution.py:31
  15.8 3.3 %collective-permute-done.2 = f32[2,17,8,128]{3,2,1,0:T(8,128)S(1)} collective-permute-done((f32[2,17,8,128]{3,2,1,0:T(8,128)S(1)}, f32[2,17,8,128]{3,2,1,0:T(8,128)S(1)}, u32[]{:S(2)}, u32[]{:S(2)}) %collective-permute-start.2) | collective-permute-done | bytes 139296 | tf_op jit(solution)/shard_map/ppermute | solution.py:31
  19.1 3.6 %collective-permute-done.1 = f32[2,17,8,128]{3,2,1,0:T(8,128)S(1)} collective-permute-done((f32[2,17,8,128]{3,2,1,0:T(8,128)S(1)}, f32[2,17,8,128]{3,2,1,0:T(8,128)S(1)}, u32[]{:S(2)}, u32[]{:S(2)}) %collective-permute-start.1) | collective-permute-done | bytes 139296 | tf_op jit(solution)/shard_map/ppermute | solution.py:31
  23.7 7.9 %collective-permute-done.4.halo_after = f32[6,17,8,128]{3,2,1,0:T(8,128)S(1)} collective-permute-done((f32[6,17,8,128]{3,2,1,0:T(8,128)S(1)}, f32[6,17,8,128]{3,2,1,0:T(8,128)S(1)}, u32[]{:S(2)}, u32[]{:S(2)}) %collective-permute-start.4) | collective-permute-done | bytes 417824 | tf_op jit(solution)/shard_map/ppermute | solution.py:31
  31.6 3.2 %collective-permute-done.3.halo_before = f32[6,17,8,128]{3,2,1,0:T(8,128)S(1)} collective-permute-done((f32[6,17,8,128]{3,2,1,0:T(8,128)S(1)}, f32[6,17,8,128]{3,2,1,0:T(8,128)S(1)}, u32[]{:S(2)}, u32[]{:S(2)}) %collective-permute-start.3) | collective-permute-done | bytes 417824 | tf_op jit(solution)/shard_map/ppermute | solution.py:31
  34.9 24.9 %shard_map.395 = (f32[8,256]{1,0:T(8,128)}, f32[240,512]{1,0:T(8,128)}, f32[8,256]{1,0:T(8,128)}, f32[240,512]{1,0:T(8,128)S(1)}, f32[8,256]{1,0:T(8,128)S(1)}, ...) custom-call(f32[6,17,8,128]{3,2,1,0:T(8,128)S(1)} %collective-permut, ...), custom_call_target="tpu_custom_call" | custom-call | flops 29899999232 | bytes 1024 | tf_op jit(solution)/shard_map/pallas_call | solution.py:761
  59.9 1.5 copy-done.7
  61.4 0.9 shard_map.396
  64.0 1.7 dynamic-slice_add_fusion.1
  65.7 1.6 collective-permute-start.7
  67.3 1.3 dynamic-slice_add_fusion.3
  69.1 5.8 %shard_map.397 = (f32[6,16,8,128]{3,2,1,0:T(8,128)S(1)}, f32[6,16,8,128]{3,2,1,0:T(8,128)S(1)}, f32[6,16,8,128]{3,2,1,0:T(8,128)S(1)}, f32[16,16,128]{2,1,0:T(8,128)S(1)}) custom-call(f32[30,8,8,128]{3,2,1,0:T(8,128)S(1)} %copy-done.12, f32[240,2048]{1,0:T(8,128)S(1)} %copy-done.9, f32[240,256]{1,0:T(8,128)S(1)} %copy-done.16, ...), custom_call_target="tpu_custom_call" | custom-call | flops 14949999616 | bytes 1024 | tf_op jit(solution)/shard_map/pallas_call | solution.py:761
  75.0 0.8 collective-permute-start.9
  75.7 1.3 dynamic-slice_add_fusion.2
  77.0 1.4 dynamic-slice_add_fusion
  78.4 9.8 %collective-permute-done.7 = f32[448,512]{1,0:T(8,128)S(1)} collective-permute-done((f32[448,512]{1,0:T(8,128)S(1)}, f32[448,512]{1,0:T(8,128)S(1)}, u32[]{:S(2)}, u32[]{:S(2)}) %collective-permute-start.7) | collective-permute-done | bytes 917536 | tf_op jit(solution)/shard_map/ppermute | solution.py:55
  89.1 1.4 collective-permute-start.12
  90.6 4.9 %collective-permute-done.9 = f32[6,16,8,128]{3,2,1,0:T(8,128)S(1)} collective-permute-done((f32[6,16,8,128]{3,2,1,0:T(8,128)S(1)}, f32[6,16,8,128]{3,2,1,0:T(8,128)S(1)}, u32[]{:S(2)}, u32[]{:S(2)}) %collective-permute-start.9) | collective-permute-done | bytes 393248 | tf_op jit(solution)/shard_map/ppermute | solution.py:31
  96.0 3.4 %collective-permute-start.13 = (f32[2,16,8,128]{3,2,1,0:T(8,128)S(1)}, f32[2,16,8,128]{3,2,1,0:T(8,128)S(1)}, u32[]{:S(2)}, u32[]{:S(2)}) collective-permute-start(f32[2,16,8,128]{3,2,1,0:T(8,128)S(1)} %get-tuple-element.344), channel_id=1, source_target_pairs={{0,24},{8,0},{16,8},{24,16},{1,25},{9,1},{17,9},{25,17},{2,26},{10... | collective-permute-start | bytes 393224 | tf_op jit(solution)/shard_map/ppermute | solution.py:31
  99.5 6.7 %collective-permute-done.11 = f32[224,512]{1,0:T(8,128)S(1)} collective-permute-done((f32[224,512]{1,0:T(8,128)S(1)}, f32[224,512]{1,0:T(8,128)S(1)}, u32[]{:S(2)}, u32[]{:S(2)}) %collective-permute-start.11) | collective-permute-done | bytes 458784 | tf_op jit(solution)/shard_map/ppermute | solution.py:55
  106.5 0.9 collective-permute-start.15
  107.8 3.0 %collective-permute-done.15 = f32[16,8,128]{2,1,0:T(8,128)S(1)} collective-permute-done((f32[16,8,128]{2,1,0:T(8,128)S(1)}, f32[16,8,128]{2,1,0:T(8,128)S(1)}, u32[]{:S(2)}, u32[]{:S(2)}) %collective-permute-start.15) | collective-permute-done | bytes 65568 | tf_op jit(solution)/shard_map/ppermute | solution.py:886
  111.5 6.8 %shard_map.398 = (f32[8,256]{1,0:T(8,128)}, f32[240,512]{1,0:T(8,128)}, f32[384,512]{1,0:T(8,128)}, f32[384,512]{1,0:T(8,128)}, f32[384,512]{1,0:T(8,128)}, /*index=5*/f32[384,512]{1,0:T(8,128)}) custom-call(f32[16,16,128]{2,1,0:T(8,128)} %copy-done.14, f32[16,8,128]{2,1,0:T(8,128)} %bitcast_add_fusion.returned, f32[240,512]{1,0:T(8,128)} %copy-done.8, ...), custom_call_target="tpu_custom_call" | custom-call | flops 8049999872 | bytes 1024 | tf_op jit(solution)/shard_map/pallas_call | solution.py:761
  119.0 1.2 collective-permute-start.19
  120.2 1.1 collective-permute-done.17
  121.3 1.8 dynamic-slice_add_fusion.11
  123.1 0.8 collective-permute-start.20
  124.0 1.8 dynamic-slice_add_fusion.10
  125.8 0.9 collective-permute-start.21
  126.7 4.9 %collective-permute-done.19 = f32[104,512]{1,0:T(8,128)S(1)} collective-permute-done((f32[104,512]{1,0:T(8,128)S(1)}, f32[104,512]{1,0:T(8,128)S(1)}, u32[]{:S(2)}, u32[]{:S(2)}) %collective-permute-start.19) | collective-permute-done | bytes 213024 | tf_op jit(solution)/shard_map/ppermute | solution.py:55
  131.7 1.1 dynamic-slice_add_fusion.8
  132.8 1.7 collective-permute-done.20
  135.1 2.1 collective-permute-done.21
  137.2 1.0 dynamic-slice_add_fusion.20
  138.1 1.6 collective-permute-start.23
  139.7 1.0 dynamic-slice_add_fusion.18
  141.1 2.8 %collective-permute-done.23 = f32[96,512]{1,0:T(8,128)S(1)} collective-permute-done((f32[96,512]{1,0:T(8,128)S(1)}, f32[96,512]{1,0:T(8,128)S(1)}, u32[]{:S(2)}, u32[]{:S(2)}) %collective-permute-start.23) | collective-permute-done | bytes 196640 | tf_op jit(solution)/shard_map/ppermute | solution.py:55
  144.4 1.8 collective-permute-start.26
  146.2 6.7 %collective-permute-done.25 = f32[96,512]{1,0:T(8,128)S(1)} collective-permute-done((f32[96,512]{1,0:T(8,128)S(1)}, f32[96,512]{1,0:T(8,128)S(1)}, u32[]{:S(2)}, u32[]{:S(2)}) %collective-permute-start.25) | collective-permute-done | bytes 196640 | tf_op jit(solution)/shard_map/ppermute | solution.py:55
  153.4 6.6 %collective-permute-done.26 = f32[208,512]{1,0:T(8,128)S(1)} collective-permute-done((f32[208,512]{1,0:T(8,128)S(1)}, f32[208,512]{1,0:T(8,128)S(1)}, u32[]{:S(2)}, u32[]{:S(2)}) %collective-permute-start.26) | collective-permute-done | bytes 426016 | tf_op jit(solution)/shard_map/ppermute | solution.py:55
  161.4 1.1 collective-permute-start.30
  162.5 1.1 collective-permute-start.27
  163.5 4.1 %collective-permute-done.30 = f32[48,512]{1,0:T(8,128)S(1)} collective-permute-done((f32[48,512]{1,0:T(8,128)S(1)}, f32[48,512]{1,0:T(8,128)S(1)}, u32[]{:S(2)}, u32[]{:S(2)}) %collective-permute-start.30) | collective-permute-done | bytes 98336 | tf_op jit(solution)/shard_map/ppermute | solution.py:55
  167.6 1.4 collective-permute-start.31
  169.1 0.9 collective-permute-start.28
  170.0 3.4 %collective-permute-done.31 = f32[96,512]{1,0:T(8,128)S(1)} collective-permute-done((f32[96,512]{1,0:T(8,128)S(1)}, f32[96,512]{1,0:T(8,128)S(1)}, u32[]{:S(2)}, u32[]{:S(2)}) %collective-permute-start.31) | collective-permute-done | bytes 196640 | tf_op jit(solution)/shard_map/ppermute | solution.py:55
  173.4 1.6 collective-permute-start.33
  175.3 1.1 collective-permute-start.34
  176.3 4.7 %collective-permute-done.28 = f32[192,512]{1,0:T(8,128)S(1)} collective-permute-done((f32[192,512]{1,0:T(8,128)S(1)}, f32[192,512]{1,0:T(8,128)S(1)}, u32[]{:S(2)}, u32[]{:S(2)}) %collective-permute-start.28) | collective-permute-done | bytes 393248 | tf_op jit(solution)/shard_map/ppermute | solution.py:55
  181.2 1.4 collective-permute-start.35
  182.9 2.4 %collective-permute-done.33 = f32[96,512]{1,0:T(8,128)S(1)} collective-permute-done((f32[96,512]{1,0:T(8,128)S(1)}, f32[96,512]{1,0:T(8,128)S(1)}, u32[]{:S(2)}, u32[]{:S(2)}) %collective-permute-start.33) | collective-permute-done | bytes 196640 | tf_op jit(solution)/shard_map/ppermute | solution.py:55
  185.4 13.3 %collective-permute-done.34 = f32[448,512]{1,0:T(8,128)S(1)} collective-permute-done((f32[448,512]{1,0:T(8,128)S(1)}, f32[448,512]{1,0:T(8,128)S(1)}, u32[]{:S(2)}, u32[]{:S(2)}) %collective-permute-start.34) | collective-permute-done | bytes 917536 | tf_op jit(solution)/shard_map/ppermute | solution.py:55
  202.4 0.9 collective-permute-start.38
  203.3 1.6 collective-permute-start.39
  204.9 1.5 collective-permute-done.37.b_other
  206.4 3.1 %shard_map.399 = (f32[2,512,512]{2,1,0:T(8,128)}, f32[2,256,512]{2,1,0:T(8,128)}, f32[64,1024]{1,0:T(8,128)}, f32[64,512]{1,0:T(8,128)}, f32[32,1024]{1,0:T(8,12...) custom-call(f32[896,512]{1,0:T(8,128)S(1)} %maximum_add_fusion.a_mine, ...), custom_call_target="tpu_custom_call" | custom-call | bytes 1024 | tf_op jit(solution)/shard_map/pallas_call | solution.py:761
  209.5 4.0 %collective-permute-done.38 = f32[192,512]{1,0:T(8,128)S(1)} collective-permute-done((f32[192,512]{1,0:T(8,128)S(1)}, f32[192,512]{1,0:T(8,128)S(1)}, u32[]{:S(2)}, u32[]{:S(2)}) %collective-permute-start.38) | collective-permute-done | bytes 393248 | tf_op jit(solution)/shard_map/ppermute | solution.py:55
  214.8 1.8 collective-permute-done.41.d_other
  216.6 1.1 collective-permute-done.40.c_other
  217.7 3.4 %shard_map.400 = (f32[2,512,512]{2,1,0:T(8,128)}, f32[5,128,512]{2,1,0:T(8,128)}, f32[64,512]{1,0:T(8,128)}, f32[32,512]{1,0:T(8,128)}, f32[3,256]{1,0:T(4,128)}) custom-call(f32[384,512]{1,0:T(8,128)S(1)} %pad_maximum_fusion.5.c_mine, f32[384,512]{1,0:T(8,128)S(1)} %collective-permute-done.40.c_other, f32[384,512]{1,0:T(8,128)S(1)} %pad_maximum_fusion.6.d_mine, ...), custom_call_target="tpu_custom_call" | custom-call | flops 3449999872 | bytes 1024 | tf_op jit(solution)/shard_map/pallas_call | solution.py:761
  (166 shorter events, 14.3 us)
Async XLA Ops:
  0.7 7.6 %copy-start.26 = (s32[240]{0:T(256)S(1)}, s32[240]{0:T(256)}, u32[]{:S(2)}) copy-start(s32[240]{0:T(256)} %param.32) | copy-start | bytes 2884
  0.7 7.6 %copy-start.22 = (s32[240,8]{0,1:T(8,128)S(1)}, s32[240,8]{0,1:T(8,128)}, u32[]{:S(2)}) copy-start(s32[240,8]{0,1:T(8,128)} %param.33) | copy-start | bytes 23044
  0.7 7.6 %copy-start.24 = (s32[240,8]{0,1:T(8,128)S(1)}, s32[240,8]{0,1:T(8,128)}, u32[]{:S(2)}) copy-start(s32[240,8]{0,1:T(8,128)} %param.35) | copy-start | bytes 23044
  0.7 22.6 %copy-start.23 = (s32[240,8]{0,1:T(8,128)S(1)}, s32[240,8]{0,1:T(8,128)}, u32[]{:S(2)}) copy-start(s32[240,8]{0,1:T(8,128)} %param.34) | copy-start | bytes 23044
  0.7 22.6 %copy-start.25 = (s32[240,8]{0,1:T(8,128)S(1)}, s32[240,8]{0,1:T(8,128)}, u32[]{:S(2)}) copy-start(s32[240,8]{0,1:T(8,128)} %param.36) | copy-start | bytes 23044
  5.1 29.7 %copy-start = (f32[240,512]{1,0:T(8,128)S(1)}, f32[240,512]{1,0:T(8,128)}, u32[]{:S(2)}) copy-start(f32[240,512]{1,0:T(8,128)} %edge.5) | copy-start | bytes 1474564
  5.1 29.7 %copy-start.1 = (bf16[1024,64]{0,1:T(8,128)(2,1)S(1)}, bf16[1024,64]{0,1:T(8,128)(2,1)}, u32[]{:S(2)}) copy-start(bf16[1024,64]{0,1:T(8,128)(2,1)} %param.41) | copy-start | bytes 393220
  5.1 29.7 %copy-start.2 = (bf16[64,512]{1,0:T(8,128)(2,1)S(1)}, bf16[64,512]{1,0:T(8,128)(2,1)}, u32[]{:S(2)}) copy-start(bf16[64,512]{1,0:T(8,128)(2,1)} %trip_up.1) | copy-start | bytes 196612
  5.1 29.7 %copy-start.3 = (bf16[1024,32]{0,1:T(8,128)(2,1)S(1)}, bf16[1024,32]{0,1:T(8,128)(2,1)}, u32[]{:S(2)}) copy-start(bf16[1024,32]{0,1:T(8,128)(2,1)} %param.44) | copy-start | bytes 196612
  5.1 29.7 %copy-start.4 = (bf16[32,512]{1,0:T(8,128)(2,1)S(1)}, bf16[32,512]{1,0:T(8,128)(2,1)}, u32[]{:S(2)}) copy-start(bf16[32,512]{1,0:T(8,128)(2,1)} %quad_up.1) | copy-start | bytes 98308
  5.1 29.7 %copy-start.5 = (f32[8,256]{1,0:T(8,128)S(1)}, f32[8,256]{1,0:T(8,128)}, u32[]{:S(2)}) copy-start(f32[8,256]{1,0:T(8,128)} %cot_atoms.1) | copy-start | bytes 24580
  5.2 29.7 %copy-start.6 = (f32[8,256]{1,0:T(8,128)S(1)}, f32[8,256]{1,0:T(8,128)}, u32[]{:S(2)}) copy-start(f32[8,256]{1,0:T(8,128)} %cot_energy.1) | copy-start | bytes 24580
  5.2 29.7 %copy-start.10 = (f32[240,128]{1,0:T(8,128)S(1)}, f32[240,128]{1,0:T(8,128)}, u32[]{:S(2)}) copy-start(f32[240,128]{1,0:T(8,128)} %get-tuple-element.173.radial) | copy-start | bytes 368644
  5.2 29.7 %copy-start.11 = (f32[17,16,128]{2,1,0:T(8,128)S(1)}, f32[17,16,128]{2,1,0:T(8,128)}, u32[]{:S(2)}) copy-start(f32[17,16,128]{2,1,0:T(8,128)} %get-tuple-element.169.local) | copy-start | bytes 417796
  5.2 29.7 %copy-start.13 = (f32[240,128]{1,0:T(8,128)S(1)}, f32[240,128]{1,0:T(8,128)}, u32[]{:S(2)}) copy-start(f32[240,128]{1,0:T(8,128)} %get-tuple-element.171.columns) | copy-start | bytes 368644
  5.2 29.7 %copy-start.17 = (f32[8,256]{1,0:T(8,128)S(1)}, f32[8,256]{1,0:T(8,128)}, u32[]{:S(2)}) copy-start(f32[8,256]{1,0:T(8,128)} %get-tuple-element.170.tagged) | copy-start | bytes 24580
  5.2 5.5 %collective-permute-start = (f32[17,8,128]{2,1,0:T(8,128)}, f32[17,8,128]{2,1,0:T(8,128)S(1)}, u32[]{:S(2)}, u32[]{:S(2)}) collective-permute-start(f32[17,8,128]{2,1,0:T(8,128)} %get-tuple-element.168), channel_id=1, source_target_pairs={{0,1},{1,0},{2,3},{3,2},{4,5},{5,4},{6,7},{7,6},{8,9},{9,8},{10,11... | collective-permute-start | bytes 208904 | tf_op jit(solution)/shard_map/ppermute | solution.py:36
  11.6 7.5 %collective-permute-start.2 = (f32[2,17,8,128]{3,2,1,0:T(8,128)S(1)}, f32[2,17,8,128]{3,2,1,0:T(8,128)S(1)}, u32[]{:S(2)}, u32[]{:S(2)}) collective-permute-start(f32[2,17,8,128]{3,2,1,0:T(8,128)S(1)} %pad_maximum_fusion.14), channel_id=1, source_target_pairs={{0,24},{8,0},{16,8},{24,16},{1,25},{9,1},{17,9},{25,17},{2,26},{10... | collective-permute-start | bytes 417800 | tf_op jit(solution)/shard_map/ppermute | solution.py:31
  15.8 6.9 %collective-permute-start.1 = (f32[2,17,8,128]{3,2,1,0:T(8,128)S(1)}, f32[2,17,8,128]{3,2,1,0:T(8,128)S(1)}, u32[]{:S(2)}, u32[]{:S(2)}) collective-permute-start(f32[2,17,8,128]{3,2,1,0:T(8,128)S(1)} %pad_maximum_fusion.14), channel_id=1, source_target_pairs={{0,8},{8,16},{16,24},{24,0},{1,9},{9,17},{17,25},{25,1},{2,10},{10... | collective-permute-start | bytes 417800 | tf_op jit(solution)/shard_map/ppermute | solution.py:31
  22.7 8.9 %collective-permute-start.4 = (f32[6,17,8,128]{3,2,1,0:T(8,128)S(1)}, f32[6,17,8,128]{3,2,1,0:T(8,128)S(1)}, u32[]{:S(2)}, u32[]{:S(2)}) collective-permute-start(f32[6,17,8,128]{3,2,1,0:T(8,128)S(1)} %pad_maximum_fusion.8.halo_here), channel_id=1, source_target_pairs={{0,6},{2,0},{4,2},{6,4},{1,7},{3,1},{5,3},{7,5},{8,14},{10,8},{12,... | collective-permute-start | bytes 1253384 | tf_op jit(solution)/shard_map/ppermute | solution.py:31
  22.8 12.0 %collective-permute-start.3 = (f32[6,17,8,128]{3,2,1,0:T(8,128)S(1)}, f32[6,17,8,128]{3,2,1,0:T(8,128)S(1)}, u32[]{:S(2)}, u32[]{:S(2)}) collective-permute-start(f32[6,17,8,128]{3,2,1,0:T(8,128)S(1)} %pad_maximum_fusion.8.halo_here), channel_id=1, source_target_pairs={{0,2},{2,4},{4,6},{6,0},{1,3},{3,5},{5,7},{7,1},{8,10},{10,12},{12... | collective-permute-start | bytes 1253384 | tf_op jit(solution)/shard_map/ppermute | solution.py:31
  59.8 4.2 %collective-permute-start.5 = (f32[896,512]{1,0:T(8,128)}, f32[896,512]{1,0:T(8,128)}, u32[]{:S(2)}, u32[]{:S(2)}) collective-permute-start(f32[896,512]{1,0:T(8,128)} %get-tuple-element.179), channel_id=1, source_target_pairs={{0,2},{2,0},{1,3},{3,1},{4,6},{6,4},{5,7},{7,5},{8,10},{10,8},{9,1... | collective-permute-start | bytes 5505032 | tf_op jit(solution)/shard_map/ppermute | solution.py:55
  62.4 4.9 %collective-permute-start.6 = (f32[768,512]{1,0:T(8,128)S(1)}, f32[768,512]{1,0:T(8,128)}, u32[]{:S(2)}, u32[]{:S(2)}) collective-permute-start(f32[768,512]{1,0:T(8,128)S(1)} %get-tuple-element.184), channel_id=1, source_target_pairs={{0,2},{2,0},{1,3},{3,1},{4,6},{6,4},{5,7},{7,5},{8,10},{10,8},{9,1... | collective-permute-start | bytes 4718600 | tf_op jit(solution)/shard_map/ppermute | solution.py:55
  64.0 5.1 %copy-start.12 = (f32[30,8,8,128]{3,2,1,0:T(8,128)S(1)}, f32[30,8,8,128]{3,2,1,0:T(8,128)}, u32[]{:S(2)}) copy-start(f32[30,8,8,128]{3,2,1,0:T(8,128)} %get-tuple-element.177.cosines) | copy-start | bytes 2949124
  65.7 3.4 %copy-start.9 = (f32[240,2048]{1,0:T(8,128)S(1)}, f32[240,2048]{1,0:T(8,128)}, u32[]{:S(2)}) copy-start(f32[240,2048]{1,0:T(8,128)} %get-tuple-element.188.sums) | copy-start | bytes 5898244
  65.7 3.4 %copy-start.16 = (f32[240,256]{1,0:T(8,128)S(1)}, f32[240,256]{1,0:T(8,128)}, u32[]{:S(2)}) copy-start(f32[240,256]{1,0:T(8,128)} %copy-done.15) | copy-start | bytes 737284
  65.7 22.5 %collective-permute-start.7 = (f32[448,512]{1,0:T(8,128)S(1)}, f32[448,512]{1,0:T(8,128)S(1)}, u32[]{:S(2)}, u32[]{:S(2)}) collective-permute-start(f32[448,512]{1,0:T(8,128)S(1)} %dynamic-slice_add_fusion.1), channel_id=1, source_target_pairs={{0,1},{1,0},{2,3},{3,2},{4,5},{5,4},{6,7},{7,6},{8,9},{9,8},{10,11... | collective-permute-start | bytes 2752520 | tf_op jit(solution)/shard_map/ppermute | solution.py:55
  68.5 20.5 %collective-permute-start.8 = (f32[384,512]{1,0:T(8,128)S(1)}, f32[384,512]{1,0:T(8,128)S(1)}, u32[]{:S(2)}, u32[]{:S(2)}) collective-permute-start(f32[384,512]{1,0:T(8,128)S(1)} %dynamic-slice_add_fusion.3), channel_id=1, source_target_pairs={{0,4},{4,0},{1,5},{5,1},{2,6},{6,2},{3,7},{7,3},{8,12},{12,8},{9,1... | collective-permute-start | bytes 2359304 | tf_op jit(solution)/shard_map/ppermute | solution.py:55
  74.9 3.4 %copy-start.14 = (f32[16,16,128]{2,1,0:T(8,128)}, f32[16,16,128]{2,1,0:T(8,128)S(1)}, u32[]{:S(2)}) copy-start(f32[16,16,128]{2,1,0:T(8,128)S(1)} %get-tuple-element.190.back_local) | copy-start | bytes 393220
  75.0 20.5 %collective-permute-start.9 = (f32[6,16,8,128]{3,2,1,0:T(8,128)S(1)}, f32[6,16,8,128]{3,2,1,0:T(8,128)S(1)}, u32[]{:S(2)}, u32[]{:S(2)}) collective-permute-start(f32[6,16,8,128]{3,2,1,0:T(8,128)S(1)} %get-tuple-element.203), channel_id=1, source_target_pairs={{0,6},{2,0},{4,2},{6,4},{1,7},{3,1},{5,3},{7,5},{8,14},{10,8},{12,... | collective-permute-start | bytes 1179656 | tf_op jit(solution)/shard_map/ppermute | solution.py:31
  75.7 19.8 %collective-permute-start.10 = (f32[6,16,8,128]{3,2,1,0:T(8,128)S(1)}, f32[6,16,8,128]{3,2,1,0:T(8,128)S(1)}, u32[]{:S(2)}, u32[]{:S(2)}) collective-permute-start(f32[6,16,8,128]{3,2,1,0:T(8,128)S(1)} %get-tuple-element.204), channel_id=1, source_target_pairs={{0,2},{2,4},{4,6},{6,0},{1,3},{3,5},{5,7},{7,1},{8,10},{10,12},{12... | collective-permute-start | bytes 1179656 | tf_op jit(solution)/shard_map/ppermute | solution.py:31
  88.2 17.9 %collective-permute-start.11 = (f32[224,512]{1,0:T(8,128)S(1)}, f32[224,512]{1,0:T(8,128)S(1)}, u32[]{:S(2)}, u32[]{:S(2)}) collective-permute-start(f32[224,512]{1,0:T(8,128)S(1)} %dynamic-slice_add_fusion.5), channel_id=1, source_target_pairs={{0,4},{4,0},{1,5},{5,1},{2,6},{6,2},{3,7},{7,3},{8,12},{12,8},{9,1... | collective-permute-start | bytes 1376264 | tf_op jit(solution)/shard_map/ppermute | solution.py:55
  89.1 10.4 %collective-permute-start.12 = (f32[192,512]{1,0:T(8,128)S(1)}, f32[192,512]{1,0:T(8,128)S(1)}, u32[]{:S(2)}, u32[]{:S(2)}) collective-permute-start(f32[192,512]{1,0:T(8,128)S(1)} %dynamic-slice_add_fusion.13), channel_id=1, source_target_pairs={{0,1},{1,0},{2,3},{3,2},{4,5},{5,4},{6,7},{7,6},{8,9},{9,8},{10,11... | collective-permute-start | bytes 1179656 | tf_op jit(solution)/shard_map/ppermute | solution.py:55
  95.6 10.9 %collective-permute-start.14 = (f32[2,16,8,128]{3,2,1,0:T(8,128)S(1)}, f32[2,16,8,128]{3,2,1,0:T(8,128)S(1)}, u32[]{:S(2)}, u32[]{:S(2)}) collective-permute-start(f32[2,16,8,128]{3,2,1,0:T(8,128)S(1)} %get-tuple-element.343), channel_id=1, source_target_pairs={{0,8},{8,16},{16,24},{24,0},{1,9},{9,17},{17,25},{25,1},{2,10},{10... | collective-permute-start | bytes 393224 | tf_op jit(solution)/shard_map/ppermute | solution.py:31
  96.0 10.4 %collective-permute-start.13 = (f32[2,16,8,128]{3,2,1,0:T(8,128)S(1)}, f32[2,16,8,128]{3,2,1,0:T(8,128)S(1)}, u32[]{:S(2)}, u32[]{:S(2)}) collective-permute-start(f32[2,16,8,128]{3,2,1,0:T(8,128)S(1)} %get-tuple-element.344), channel_id=1, source_target_pairs={{0,24},{8,0},{16,8},{24,16},{1,25},{9,1},{17,9},{25,17},{2,26},{10... | collective-permute-start | bytes 393224 | tf_op jit(solution)/shard_map/ppermute | solution.py:31
  106.5 4.3 %collective-permute-start.15 = (f32[16,8,128]{2,1,0:T(8,128)S(1)}, f32[16,8,128]{2,1,0:T(8,128)S(1)}, u32[]{:S(2)}, u32[]{:S(2)}) collective-permute-start(f32[16,8,128]{2,1,0:T(8,128)S(1)} %select_bitcast_fusion.2), channel_id=1, source_target_pairs={{0,1},{1,0},{2,3},{3,2},{4,5},{5,4},{6,7},{7,6},{8,9},{9,8},{10,11... | collective-permute-start | bytes 196616 | tf_op jit(solution)/shard_map/ppermute | solution.py:886
  107.4 10.9 %collective-permute-start.16 = (f32[208,512]{1,0:T(8,128)S(1)}, f32[208,512]{1,0:T(8,128)S(1)}, u32[]{:S(2)}, u32[]{:S(2)}) collective-permute-start(f32[208,512]{1,0:T(8,128)S(1)} %dynamic-slice_add_fusion.7), channel_id=1, source_target_pairs={{0,8},{8,0},{16,24},{24,16},{1,9},{9,1},{17,25},{25,17},{2,10},{10... | collective-permute-start | bytes 1277960 | tf_op jit(solution)/shard_map/ppermute | solution.py:55
  118.3 5.7 %copy-start.20 = (f32[384,512]{1,0:T(8,128)S(1)}, f32[384,512]{1,0:T(8,128)}, u32[]{:S(2)}) copy-start(f32[384,512]{1,0:T(8,128)} %get-tuple-element.247) | copy-start | bytes 2359300
  118.4 13.3 %copy-start.21 = (f32[384,512]{1,0:T(8,128)S(1)}, f32[384,512]{1,0:T(8,128)}, u32[]{:S(2)}) copy-start(f32[384,512]{1,0:T(8,128)} %get-tuple-element.243) | copy-start | bytes 2359300
  118.4 2.9 %collective-permute-start.17 = (f32[384,512]{1,0:T(8,128)}, f32[384,512]{1,0:T(8,128)S(1)}, u32[]{:S(2)}, u32[]{:S(2)}) collective-permute-start(f32[384,512]{1,0:T(8,128)} %get-tuple-element.234), channel_id=1, source_target_pairs={{0,2},{2,0},{1,3},{3,1},{4,6},{6,4},{5,7},{7,5},{8,10},{10,8},{9,1... | collective-permute-start | bytes 2359304 | tf_op jit(solution)/shard_map/ppermute | solution.py:55
  118.5 5.5 %collective-permute-start.18 = (f32[384,512]{1,0:T(8,128)}, f32[384,512]{1,0:T(8,128)}, u32[]{:S(2)}, u32[]{:S(2)}) collective-permute-start(f32[384,512]{1,0:T(8,128)} %get-tuple-element.238), channel_id=1, source_target_pairs={{0,2},{2,0},{1,3},{3,1},{4,6},{6,4},{5,7},{7,5},{8,10},{10,8},{9,1... | collective-permute-start | bytes 2359304 | tf_op jit(solution)/shard_map/ppermute | solution.py:55
  119.0 12.5 %collective-permute-start.19 = (f32[104,512]{1,0:T(8,128)S(1)}, f32[104,512]{1,0:T(8,128)S(1)}, u32[]{:S(2)}, u32[]{:S(2)}) collective-permute-start(f32[104,512]{1,0:T(8,128)S(1)} %dynamic-slice_add_fusion.15), channel_id=1, source_target_pairs={{0,16},{8,24},{16,0},{24,8},{1,17},{9,25},{17,1},{25,9},{2,18},{10... | collective-permute-start | bytes 638984 | tf_op jit(solution)/shard_map/ppermute | solution.py:55
  123.1 11.4 %collective-permute-start.20 = (f32[192,512]{1,0:T(8,128)}, f32[192,512]{1,0:T(8,128)S(1)}, u32[]{:S(2)}, u32[]{:S(2)}) collective-permute-start(f32[192,512]{1,0:T(8,128)} %dynamic-slice_add_fusion.11), channel_id=1, source_target_pairs={{0,1},{1,0},{2,3},{3,2},{4,5},{5,4},{6,7},{7,6},{8,9},{9,8},{10,11... | collective-permute-start | bytes 1179656 | tf_op jit(solution)/shard_map/ppermute | solution.py:55
  125.8 11.4 %collective-permute-start.21 = (f32[192,512]{1,0:T(8,128)}, f32[192,512]{1,0:T(8,128)}, u32[]{:S(2)}, u32[]{:S(2)}) collective-permute-start(f32[192,512]{1,0:T(8,128)} %dynamic-slice_add_fusion.10), channel_id=1, source_target_pairs={{0,4},{4,0},{1,5},{5,1},{2,6},{6,2},{3,7},{7,3},{8,12},{12,8},{9,1... | collective-permute-start | bytes 1179656 | tf_op jit(solution)/shard_map/ppermute | solution.py:55
  131.6 12.8 %collective-permute-start.24 = (f32[104,512]{1,0:T(8,128)S(1)}, f32[104,512]{1,0:T(8,128)S(1)}, u32[]{:S(2)}, u32[]{:S(2)}) collective-permute-start(f32[104,512]{1,0:T(8,128)S(1)} %add.320), channel_id=1, source_target_pairs={{0,16},{8,24},{16,0},{24,8},{1,17},{9,25},{17,1},{25,9},{2,18},{10... | collective-permute-start | bytes 638984 | tf_op jit(solution)/shard_map/ppermute | solution.py:55
  134.5 6.6 %collective-permute-start.22 = (f32[96,512]{1,0:T(8,128)S(1)}, f32[96,512]{1,0:T(8,128)S(1)}, u32[]{:S(2)}, u32[]{:S(2)}) collective-permute-start(f32[96,512]{1,0:T(8,128)S(1)} %dynamic-slice_add_fusion.21), channel_id=1, source_target_pairs={{0,4},{4,0},{1,5},{5,1},{2,6},{6,2},{3,7},{7,3},{8,12},{12,8},{9,1... | collective-permute-start | bytes 589832 | tf_op jit(solution)/shard_map/ppermute | solution.py:55
  138.1 5.7 %collective-permute-start.23 = (f32[96,512]{1,0:T(8,128)S(1)}, f32[96,512]{1,0:T(8,128)S(1)}, u32[]{:S(2)}, u32[]{:S(2)}) collective-permute-start(f32[96,512]{1,0:T(8,128)S(1)} %dynamic-slice_add_fusion.20), channel_id=1, source_target_pairs={{0,1},{1,0},{2,3},{3,2},{4,5},{5,4},{6,7},{7,6},{8,9},{9,8},{10,11... | collective-permute-start | bytes 589832 | tf_op jit(solution)/shard_map/ppermute | solution.py:55
  144.0 9.0 %collective-permute-start.25 = (f32[96,512]{1,0:T(8,128)S(1)}, f32[96,512]{1,0:T(8,128)S(1)}, u32[]{:S(2)}, u32[]{:S(2)}) collective-permute-start(f32[96,512]{1,0:T(8,128)S(1)} %dynamic-slice_add_fusion.17), channel_id=1, source_target_pairs={{0,8},{8,0},{16,24},{24,16},{1,9},{9,1},{17,25},{25,17},{2,10},{10... | collective-permute-start | bytes 589832 | tf_op jit(solution)/shard_map/ppermute | solution.py:55
  144.4 15.6 %collective-permute-start.26 = (f32[208,512]{1,0:T(8,128)S(1)}, f32[208,512]{1,0:T(8,128)S(1)}, u32[]{:S(2)}, u32[]{:S(2)}) collective-permute-start(f32[208,512]{1,0:T(8,128)S(1)} %pad_maximum_fusion.7), channel_id=1, source_target_pairs={{0,8},{8,0},{16,24},{24,16},{1,9},{9,1},{17,25},{25,17},{2,10},{10... | collective-permute-start | bytes 1277960 | tf_op jit(solution)/shard_map/ppermute | solution.py:55
  152.9 7.2 %collective-permute-start.29 = (f32[48,512]{1,0:T(8,128)S(1)}, f32[48,512]{1,0:T(8,128)S(1)}, u32[]{:S(2)}, u32[]{:S(2)}) collective-permute-start(f32[48,512]{1,0:T(8,128)S(1)} %dynamic-slice_add_fusion.23), channel_id=1, source_target_pairs={{0,16},{8,24},{16,0},{24,8},{1,17},{9,25},{17,1},{25,9},{2,18},{10... | collective-permute-start | bytes 294920 | tf_op jit(solution)/shard_map/ppermute | solution.py:55
  161.4 6.2 %collective-permute-start.30 = (f32[48,512]{1,0:T(8,128)S(1)}, f32[48,512]{1,0:T(8,128)S(1)}, u32[]{:S(2)}, u32[]{:S(2)}) collective-permute-start(f32[48,512]{1,0:T(8,128)S(1)} %add_add_fusion.2), channel_id=1, source_target_pairs={{0,16},{8,24},{16,0},{24,8},{1,17},{9,25},{17,1},{25,9},{2,18},{10... | collective-permute-start | bytes 294920 | tf_op jit(solution)/shard_map/ppermute | solution.py:55
  162.5 12.6 %collective-permute-start.27 = (f32[224,512]{1,0:T(8,128)S(1)}, f32[224,512]{1,0:T(8,128)S(1)}, u32[]{:S(2)}, u32[]{:S(2)}) collective-permute-start(f32[224,512]{1,0:T(8,128)S(1)} %fusion), channel_id=1, source_target_pairs={{0,4},{4,0},{1,5},{5,1},{2,6},{6,2},{3,7},{7,3},{8,12},{12,8},{9,1... | collective-permute-start | bytes 1376264 | tf_op jit(solution)/shard_map/ppermute | solution.py:55
  167.6 5.7 %collective-permute-start.31 = (f32[96,512]{1,0:T(8,128)S(1)}, f32[96,512]{1,0:T(8,128)S(1)}, u32[]{:S(2)}, u32[]{:S(2)}) collective-permute-start(f32[96,512]{1,0:T(8,128)S(1)} %pad_maximum_fusion.13), channel_id=1, source_target_pairs={{0,8},{8,0},{16,24},{24,16},{1,9},{9,1},{17,25},{25,17},{2,10},{10... | collective-permute-start | bytes 589832 | tf_op jit(solution)/shard_map/ppermute | solution.py:55
  169.1 12.0 %collective-permute-start.28 = (f32[192,512]{1,0:T(8,128)S(1)}, f32[192,512]{1,0:T(8,128)S(1)}, u32[]{:S(2)}, u32[]{:S(2)}) collective-permute-start(f32[192,512]{1,0:T(8,128)S(1)} %slice.49), channel_id=1, source_target_pairs={{0,1},{1,0},{2,3},{3,2},{4,5},{5,4},{6,7},{7,6},{8,9},{9,8},{10,11... | collective-permute-start | bytes 1179656 | tf_op jit(solution)/shard_map/ppermute | solution.py:55
  173.4 11.9 %collective-permute-start.33 = (f32[96,512]{1,0:T(8,128)S(1)}, f32[96,512]{1,0:T(8,128)S(1)}, u32[]{:S(2)}, u32[]{:S(2)}) collective-permute-start(f32[96,512]{1,0:T(8,128)S(1)} %get-tuple-element.285), channel_id=1, source_target_pairs={{0,1},{1,0},{2,3},{3,2},{4,5},{5,4},{6,7},{7,6},{8,9},{9,8},{10,11... | collective-permute-start | bytes 589832 | tf_op jit(solution)/shard_map/ppermute | solution.py:55
  175.0 7.8 %collective-permute-start.32 = (f32[96,512]{1,0:T(8,128)S(1)}, f32[96,512]{1,0:T(8,128)S(1)}, u32[]{:S(2)}, u32[]{:S(2)}) collective-permute-start(f32[96,512]{1,0:T(8,128)S(1)} %get-tuple-element.283), channel_id=1, source_target_pairs={{0,4},{4,0},{1,5},{5,1},{2,6},{6,2},{3,7},{7,3},{8,12},{12,8},{9,1... | collective-permute-start | bytes 589832 | tf_op jit(solution)/shard_map/ppermute | solution.py:55
  175.3 23.4 %collective-permute-start.34 = (f32[448,512]{1,0:T(8,128)S(1)}, f32[448,512]{1,0:T(8,128)S(1)}, u32[]{:S(2)}, u32[]{:S(2)}) collective-permute-start(f32[448,512]{1,0:T(8,128)S(1)} %pad_maximum_fusion.1), channel_id=1, source_target_pairs={{0,1},{1,0},{2,3},{3,2},{4,5},{5,4},{6,7},{7,6},{8,9},{9,8},{10,11... | collective-permute-start | bytes 2752520 | tf_op jit(solution)/shard_map/ppermute | solution.py:55
  181.2 19.1 %collective-permute-start.35 = (f32[384,512]{1,0:T(8,128)S(1)}, f32[384,512]{1,0:T(8,128)S(1)}, u32[]{:S(2)}, u32[]{:S(2)}) collective-permute-start(f32[384,512]{1,0:T(8,128)S(1)} %pad_maximum_fusion.4), channel_id=1, source_target_pairs={{0,4},{4,0},{1,5},{5,1},{2,6},{6,2},{3,7},{7,3},{8,12},{12,8},{9,1... | collective-permute-start | bytes 2359304 | tf_op jit(solution)/shard_map/ppermute | solution.py:55
  200.3 6.1 %collective-permute-start.36 = (f32[896,512]{1,0:T(8,128)S(1)}, f32[896,512]{1,0:T(8,128)S(1)}, u32[]{:S(2)}, u32[]{:S(2)}) collective-permute-start(f32[896,512]{1,0:T(8,128)S(1)} %maximum_add_fusion.a_mine), channel_id=1, source_target_pairs={{0,2},{2,0},{1,3},{3,1},{4,6},{6,4},{5,7},{7,5},{8,10},{10,8},{9,1... | collective-permute-start | bytes 5505032 | tf_op jit(solution)/shard_map/ppermute | solution.py:55
  201.9 4.5 %collective-permute-start.37 = (f32[768,512]{1,0:T(8,128)S(1)}, f32[768,512]{1,0:T(8,128)S(1)}, u32[]{:S(2)}, u32[]{:S(2)}) collective-permute-start(f32[768,512]{1,0:T(8,128)S(1)} %maximum_add_fusion.1.b_mine), channel_id=1, source_target_pairs={{0,2},{2,0},{1,3},{3,1},{4,6},{6,4},{5,7},{7,5},{8,10},{10,8},{9,1... | collective-permute-start | bytes 4718600 | tf_op jit(solution)/shard_map/ppermute | solution.py:55
  202.4 11.1 %collective-permute-start.38 = (f32[192,512]{1,0:T(8,128)S(1)}, f32[192,512]{1,0:T(8,128)S(1)}, u32[]{:S(2)}, u32[]{:S(2)}) collective-permute-start(f32[192,512]{1,0:T(8,128)S(1)} %pad_maximum_fusion.11), channel_id=1, source_target_pairs={{0,1},{1,0},{2,3},{3,2},{4,5},{5,4},{6,7},{7,6},{8,9},{9,8},{10,11... | collective-permute-start | bytes 1179656 | tf_op jit(solution)/shard_map/ppermute | solution.py:55
  203.3 10.8 %collective-permute-start.39 = (f32[192,512]{1,0:T(8,128)S(1)}, f32[192,512]{1,0:T(8,128)S(1)}, u32[]{:S(2)}, u32[]{:S(2)}) collective-permute-start(f32[192,512]{1,0:T(8,128)S(1)} %pad_maximum_fusion.12), channel_id=1, source_target_pairs={{0,4},{4,0},{1,5},{5,1},{2,6},{6,2},{3,7},{7,3},{8,12},{12,8},{9,1... | collective-permute-start | bytes 1179656 | tf_op jit(solution)/shard_map/ppermute | solution.py:55
  214.3 2.4 %collective-permute-start.41 = (f32[384,512]{1,0:T(8,128)S(1)}, f32[384,512]{1,0:T(8,128)S(1)}, u32[]{:S(2)}, u32[]{:S(2)}) collective-permute-start(f32[384,512]{1,0:T(8,128)S(1)} %pad_maximum_fusion.6.d_mine), channel_id=1, source_target_pairs={{0,2},{2,0},{1,3},{3,1},{4,6},{6,4},{5,7},{7,5},{8,10},{10,8},{9,1... | collective-permute-start | bytes 2359304 | tf_op jit(solution)/shard_map/ppermute | solution.py:55
  214.4 3.4 %collective-permute-start.40 = (f32[384,512]{1,0:T(8,128)S(1)}, f32[384,512]{1,0:T(8,128)S(1)}, u32[]{:S(2)}, u32[]{:S(2)}) collective-permute-start(f32[384,512]{1,0:T(8,128)S(1)} %pad_maximum_fusion.5.c_mine), channel_id=1, source_target_pairs={{0,2},{2,0},{1,3},{3,1},{4,6},{6,4},{5,7},{7,5},{8,10},{10,8},{9,1... | collective-permute-start | bytes 2359304 | tf_op jit(solution)/shard_map/ppermute | solution.py:55
  (5 other events, 11.3 us)

commit v12 on v11

--- a/solution.py
+++ b/solution.py
@@ -114,7 +114,7 @@
     sizes = [x[0].shape[0] for x in lanes]
     joint = [jnp.concatenate(pair) for pair in zip(*chain.after(lanes))]
     for axis, bit in bits_of("gx"):
-        joint = halved(chain, joint, axis, bit, tight)
+        joint = halved(chain, joint, axis, bit, tight and bit == 0)
         yield
     joint = chain.after(joint)
     value = sum(joint[1:], joint[0])

time: 222 us -> 222 us (level)
  waiting for transfers between devices: 109 us -> 113 us
  other arithmetic: 16.6 us -> 13.2 us
    ppermute x32, waiting for transfers between devices: 80.5 us -> 84.6 us  [swap(): return lax.ppermute(value, axis, [(i, i ^ 1 << bit) for i in range(count)])]
    add x24, other arithmetic: 12.9 us -> 9.52 us  [part(): total = total + lax.dynamic_slice_in_dim(x, at, size)]
  transfers between devices with their start and end apart: 42 -> 42, of which waited for: 30 -> 31; matrix products, arithmetic and copies ran while one was open for 8% -> 6% of each run, Pallas kernels for 8% -> 8%
where the time goes in v12:
time: 222 us
  waiting for transfers between devices  113 us (51%)
  Pallas kernels  49.4 us (22%)
  starting transfers between devices  38.5 us (17%)
  other arithmetic  13.2 us (6%)
  local copies, waits for them, and re-layouts  4.19 us (2%)
  between operations  3.7 us (2%)
    ppermute x32, waiting for transfers between devices, swap(): return lax.ppermute(value, axis, [(i, i ^ 1 << bit) for i in range(count)])  84.6 us
    pallas_call x7, Pallas kernels, call(): pl.pallas_call(kernel, out_shape=[jax.ShapeDtypeStruct(shape, F32) for sh...  49.4 us
    ppermute x32, starting transfers between devices, swap(): return lax.ppermute(value, axis, [(i, i ^ 1 << bit) for i in range(count)])  25.2 us
    ppermute x8, waiting for transfers between devices, shifted(): return lax.ppermute(value, axis, pairs)  22.8 us
    add x24, other arithmetic, part(): total = total + lax.dynamic_slice_in_dim(x, at, size)  9.52 us
    ppermute x8, starting transfers between devices, shifted(): return lax.ppermute(value, axis, pairs)  9.38 us
  transfers between devices with their start and end apart: 42, of which 31 were waited for; matrix products, arithmetic and copies ran while one was open for 6% of the time, Pallas kernels for 8%

profile of v12, /device:TPU:0, one launch (start us, length us, event | category | flops | bytes accessed | tf_op | source)
XLA Modules:
  0.0 221.8 jit_solution(7503672873759292211)
XLA Ops:
  0.7 4.4 %shard_map.394 = (f32[17,8,128]{2,1,0:T(8,128)}, f32[17,16,128]{2,1,0:T(8,128)}, f32[8,256]{1,0:T(8,128)}, f32[2,240,512]{2,1,0:T(8,128)}, f32[240,128]{1,0:T(8,...) custom-call(f32[240,512]{1,0:T(8,128)} %edge.5, f32[3,240]{1,0:T(4,128)} %vec.1, ...), custom_call_target="tpu_custom_call" | custom-call | flops 5750000128 | bytes 1024 | tf_op jit(solution)/shard_map/pallas_call | solution.py:761
  5.2 3.0 %collective-permute-start = (f32[17,8,128]{2,1,0:T(8,128)}, f32[17,8,128]{2,1,0:T(8,128)S(1)}, u32[]{:S(2)}, u32[]{:S(2)}) collective-permute-start(f32[17,8,128]{2,1,0:T(8,128)} %get-tuple-element.168), channel_id=1, source_target_pairs={{0,1},{1,0},{2,3},{3,2},{4,5},{5,4},{6,7},{7,6},{8,9},{9,8},{10,11... | collective-permute-start | bytes 208904 | tf_op jit(solution)/shard_map/ppermute | solution.py:36
  8.4 2.3 %collective-permute-done = f32[17,8,128]{2,1,0:T(8,128)S(1)} collective-permute-done((f32[17,8,128]{2,1,0:T(8,128)}, f32[17,8,128]{2,1,0:T(8,128)S(1)}, u32[]{:S(2)}, u32[]{:S(2)}) %collective-permute-start) | collective-permute-done | bytes 69664 | tf_op jit(solution)/shard_map/ppermute | solution.py:36
  10.7 0.9 select_bitcast_fusion.1
  11.6 4.2 %collective-permute-start.2 = (f32[2,17,8,128]{3,2,1,0:T(8,128)S(1)}, f32[2,17,8,128]{3,2,1,0:T(8,128)S(1)}, u32[]{:S(2)}, u32[]{:S(2)}) collective-permute-start(f32[2,17,8,128]{3,2,1,0:T(8,128)S(1)} %pad_maximum_fusion.14), channel_id=1, source_target_pairs={{0,24},{8,0},{16,8},{24,16},{1,25},{9,1},{17,9},{25,17},{2,26},{10... | collective-permute-start | bytes 417800 | tf_op jit(solution)/shard_map/ppermute | solution.py:31
  15.8 3.3 %collective-permute-done.2 = f32[2,17,8,128]{3,2,1,0:T(8,128)S(1)} collective-permute-done((f32[2,17,8,128]{3,2,1,0:T(8,128)S(1)}, f32[2,17,8,128]{3,2,1,0:T(8,128)S(1)}, u32[]{:S(2)}, u32[]{:S(2)}) %collective-permute-start.2) | collective-permute-done | bytes 139296 | tf_op jit(solution)/shard_map/ppermute | solution.py:31
  19.1 3.6 %collective-permute-done.1 = f32[2,17,8,128]{3,2,1,0:T(8,128)S(1)} collective-permute-done((f32[2,17,8,128]{3,2,1,0:T(8,128)S(1)}, f32[2,17,8,128]{3,2,1,0:T(8,128)S(1)}, u32[]{:S(2)}, u32[]{:S(2)}) %collective-permute-start.1) | collective-permute-done | bytes 139296 | tf_op jit(solution)/shard_map/ppermute | solution.py:31
  23.7 7.9 %collective-permute-done.4.halo_after = f32[6,17,8,128]{3,2,1,0:T(8,128)S(1)} collective-permute-done((f32[6,17,8,128]{3,2,1,0:T(8,128)S(1)}, f32[6,17,8,128]{3,2,1,0:T(8,128)S(1)}, u32[]{:S(2)}, u32[]{:S(2)}) %collective-permute-start.4) | collective-permute-done | bytes 417824 | tf_op jit(solution)/shard_map/ppermute | solution.py:31
  31.6 3.2 %collective-permute-done.3.halo_before = f32[6,17,8,128]{3,2,1,0:T(8,128)S(1)} collective-permute-done((f32[6,17,8,128]{3,2,1,0:T(8,128)S(1)}, f32[6,17,8,128]{3,2,1,0:T(8,128)S(1)}, u32[]{:S(2)}, u32[]{:S(2)}) %collective-permute-start.3) | collective-permute-done | bytes 417824 | tf_op jit(solution)/shard_map/ppermute | solution.py:31
  34.9 24.9 %shard_map.395 = (f32[8,256]{1,0:T(8,128)}, f32[240,512]{1,0:T(8,128)}, f32[8,256]{1,0:T(8,128)}, f32[240,512]{1,0:T(8,128)S(1)}, f32[8,256]{1,0:T(8,128)S(1)}, ...) custom-call(f32[6,17,8,128]{3,2,1,0:T(8,128)S(1)} %collective-permut, ...), custom_call_target="tpu_custom_call" | custom-call | flops 29899999232 | bytes 1024 | tf_op jit(solution)/shard_map/pallas_call | solution.py:761
  59.9 1.5 copy-done.7
  61.4 0.9 shard_map.396
  64.0 1.7 dynamic-slice_add_fusion.1
  65.7 1.6 collective-permute-start.7
  67.3 1.3 dynamic-slice_add_fusion.3
  69.1 5.8 %shard_map.397 = (f32[6,16,8,128]{3,2,1,0:T(8,128)S(1)}, f32[6,16,8,128]{3,2,1,0:T(8,128)S(1)}, f32[6,16,8,128]{3,2,1,0:T(8,128)S(1)}, f32[16,16,128]{2,1,0:T(8,128)S(1)}) custom-call(f32[30,8,8,128]{3,2,1,0:T(8,128)S(1)} %copy-done.12, f32[240,2048]{1,0:T(8,128)S(1)} %copy-done.9, f32[240,256]{1,0:T(8,128)S(1)} %copy-done.16, ...), custom_call_target="tpu_custom_call" | custom-call | flops 14949999616 | bytes 1024 | tf_op jit(solution)/shard_map/pallas_call | solution.py:761
  75.0 0.8 collective-permute-start.9
  75.7 1.3 dynamic-slice_add_fusion.2
  77.0 1.4 dynamic-slice_add_fusion
  78.4 9.8 %collective-permute-done.7 = f32[448,512]{1,0:T(8,128)S(1)} collective-permute-done((f32[448,512]{1,0:T(8,128)S(1)}, f32[448,512]{1,0:T(8,128)S(1)}, u32[]{:S(2)}, u32[]{:S(2)}) %collective-permute-start.7) | collective-permute-done | bytes 917536 | tf_op jit(solution)/shard_map/ppermute | solution.py:55
  89.1 1.4 collective-permute-start.12
  90.6 4.9 %collective-permute-done.9 = f32[6,16,8,128]{3,2,1,0:T(8,128)S(1)} collective-permute-done((f32[6,16,8,128]{3,2,1,0:T(8,128)S(1)}, f32[6,16,8,128]{3,2,1,0:T(8,128)S(1)}, u32[]{:S(2)}, u32[]{:S(2)}) %collective-permute-start.9) | collective-permute-done | bytes 393248 | tf_op jit(solution)/shard_map/ppermute | solution.py:31
  96.0 3.4 %collective-permute-start.13 = (f32[2,16,8,128]{3,2,1,0:T(8,128)S(1)}, f32[2,16,8,128]{3,2,1,0:T(8,128)S(1)}, u32[]{:S(2)}, u32[]{:S(2)}) collective-permute-start(f32[2,16,8,128]{3,2,1,0:T(8,128)S(1)} %get-tuple-element.344), channel_id=1, source_target_pairs={{0,24},{8,0},{16,8},{24,16},{1,25},{9,1},{17,9},{25,17},{2,26},{10... | collective-permute-start | bytes 393224 | tf_op jit(solution)/shard_map/ppermute | solution.py:31
  99.5 6.7 %collective-permute-done.11 = f32[224,512]{1,0:T(8,128)S(1)} collective-permute-done((f32[224,512]{1,0:T(8,128)S(1)}, f32[224,512]{1,0:T(8,128)S(1)}, u32[]{:S(2)}, u32[]{:S(2)}) %collective-permute-start.11) | collective-permute-done | bytes 458784 | tf_op jit(solution)/shard_map/ppermute | solution.py:55
  106.5 0.9 collective-permute-start.15
  107.8 3.0 %collective-permute-done.15 = f32[16,8,128]{2,1,0:T(8,128)S(1)} collective-permute-done((f32[16,8,128]{2,1,0:T(8,128)S(1)}, f32[16,8,128]{2,1,0:T(8,128)S(1)}, u32[]{:S(2)}, u32[]{:S(2)}) %collective-permute-start.15) | collective-permute-done | bytes 65568 | tf_op jit(solution)/shard_map/ppermute | solution.py:886
  111.5 6.8 %shard_map.398 = (f32[8,256]{1,0:T(8,128)}, f32[240,512]{1,0:T(8,128)}, f32[384,512]{1,0:T(8,128)}, f32[384,512]{1,0:T(8,128)}, f32[384,512]{1,0:T(8,128)}, /*index=5*/f32[384,512]{1,0:T(8,128)}) custom-call(f32[16,16,128]{2,1,0:T(8,128)} %copy-done.14, f32[16,8,128]{2,1,0:T(8,128)} %bitcast_add_fusion.returned, f32[240,512]{1,0:T(8,128)} %copy-done.8, ...), custom_call_target="tpu_custom_call" | custom-call | flops 8049999872 | bytes 1024 | tf_op jit(solution)/shard_map/pallas_call | solution.py:761
  118.9 1.2 collective-permute-start.19
  120.1 1.1 collective-permute-done.17
  121.3 1.1 dynamic-slice_add_fusion.11
  122.3 0.9 collective-permute-start.20
  123.2 1.1 dynamic-slice_add_fusion.10
  124.3 1.0 collective-permute-start.21
  125.3 6.2 %collective-permute-done.19 = f32[104,512]{1,0:T(8,128)S(1)} collective-permute-done((f32[104,512]{1,0:T(8,128)S(1)}, f32[104,512]{1,0:T(8,128)S(1)}, u32[]{:S(2)}, u32[]{:S(2)}) %collective-permute-start.19) | collective-permute-done | bytes 213024 | tf_op jit(solution)/shard_map/ppermute | solution.py:55
  131.7 1.1 dynamic-slice_add_fusion.8
  132.7 0.8 collective-permute-done.20
  134.1 1.1 collective-permute-done.21
  135.3 1.2 collective-permute-start.23
  136.6 3.2 %collective-permute-done.22 = f32[96,512]{1,0:T(8,128)S(1)} collective-permute-done((f32[96,512]{1,0:T(8,128)S(1)}, f32[96,512]{1,0:T(8,128)S(1)}, u32[]{:S(2)}, u32[]{:S(2)}) %collective-permute-start.22) | collective-permute-done | bytes 196640 | tf_op jit(solution)/shard_map/ppermute | solution.py:55
  139.8 1.4 collective-permute-done.23
  141.2 1.0 collective-permute-start.25
  143.5 5.1 %collective-permute-done.25 = f32[96,512]{1,0:T(8,128)S(1)} collective-permute-done((f32[96,512]{1,0:T(8,128)S(1)}, f32[96,512]{1,0:T(8,128)S(1)}, u32[]{:S(2)}, u32[]{:S(2)}) %collective-permute-start.25) | collective-permute-done | bytes 196640 | tf_op jit(solution)/shard_map/ppermute | solution.py:55
  148.6 1.5 collective-permute-start.29
  150.1 8.2 %collective-permute-done.26 = f32[208,512]{1,0:T(8,128)S(1)} collective-permute-done((f32[208,512]{1,0:T(8,128)S(1)}, f32[208,512]{1,0:T(8,128)S(1)}, u32[]{:S(2)}, u32[]{:S(2)}) %collective-permute-start.26) | collective-permute-done | bytes 426016 | tf_op jit(solution)/shard_map/ppermute | solution.py:55
  159.7 1.6 collective-permute-start.30
  161.3 1.1 collective-permute-start.27
  162.4 3.9 %collective-permute-done.30 = f32[48,512]{1,0:T(8,128)S(1)} collective-permute-done((f32[48,512]{1,0:T(8,128)S(1)}, f32[48,512]{1,0:T(8,128)S(1)}, u32[]{:S(2)}, u32[]{:S(2)}) %collective-permute-start.30) | collective-permute-done | bytes 98336 | tf_op jit(solution)/shard_map/ppermute | solution.py:55
  166.7 1.4 collective-permute-start.28
  168.1 4.0 %collective-permute-done.31 = f32[96,512]{1,0:T(8,128)S(1)} collective-permute-done((f32[96,512]{1,0:T(8,128)S(1)}, f32[96,512]{1,0:T(8,128)S(1)}, u32[]{:S(2)}, u32[]{:S(2)}) %collective-permute-start.31) | collective-permute-done | bytes 196640 | tf_op jit(solution)/shard_map/ppermute | solution.py:55
  172.1 1.2 collective-permute-start.33
  173.3 1.2 collective-permute-start.32
  175.4 3.2 %collective-permute-done.28 = f32[192,512]{1,0:T(8,128)S(1)} collective-permute-done((f32[192,512]{1,0:T(8,128)S(1)}, f32[192,512]{1,0:T(8,128)S(1)}, u32[]{:S(2)}, u32[]{:S(2)}) %collective-permute-start.28) | collective-permute-done | bytes 393248 | tf_op jit(solution)/shard_map/ppermute | solution.py:55
  178.8 1.0 collective-permute-start.35
  179.8 1.4 collective-permute-done.32
  181.2 1.6 collective-permute-done.33
  182.9 16.0 %collective-permute-done.34 = f32[448,512]{1,0:T(8,128)S(1)} collective-permute-done((f32[448,512]{1,0:T(8,128)S(1)}, f32[448,512]{1,0:T(8,128)S(1)}, u32[]{:S(2)}, u32[]{:S(2)}) %collective-permute-start.34) | collective-permute-done | bytes 917536 | tf_op jit(solution)/shard_map/ppermute | solution.py:55
  202.6 1.1 collective-permute-start.38
  203.7 1.1 collective-permute-start.39
  204.8 1.8 collective-permute-done.37.b_other
  206.6 3.1 %shard_map.399 = (f32[2,512,512]{2,1,0:T(8,128)}, f32[2,256,512]{2,1,0:T(8,128)}, f32[64,1024]{1,0:T(8,128)}, f32[64,512]{1,0:T(8,128)}, f32[32,1024]{1,0:T(8,12...) custom-call(f32[896,512]{1,0:T(8,128)S(1)} %maximum_add_fusion.a_mine, ...), custom_call_target="tpu_custom_call" | custom-call | bytes 1024 | tf_op jit(solution)/shard_map/pallas_call | solution.py:761
  209.7 4.0 %collective-permute-done.38 = f32[192,512]{1,0:T(8,128)S(1)} collective-permute-done((f32[192,512]{1,0:T(8,128)S(1)}, f32[192,512]{1,0:T(8,128)S(1)}, u32[]{:S(2)}, u32[]{:S(2)}) %collective-permute-start.38) | collective-permute-done | bytes 393248 | tf_op jit(solution)/shard_map/ppermute | solution.py:55
  215.3 1.8 collective-permute-done.41.d_other
  217.0 1.1 collective-permute-done.40.c_other
  218.2 3.4 %shard_map.400 = (f32[2,512,512]{2,1,0:T(8,128)}, f32[5,128,512]{2,1,0:T(8,128)}, f32[64,512]{1,0:T(8,128)}, f32[32,512]{1,0:T(8,128)}, f32[3,256]{1,0:T(4,128)}) custom-call(f32[384,512]{1,0:T(8,128)S(1)} %pad_maximum_fusion.5.c_mine, f32[384,512]{1,0:T(8,128)S(1)} %collective-permute-done.40.c_other, f32[384,512]{1,0:T(8,128)S(1)} %pad_maximum_fusion.6.d_mine, ...), custom_call_target="tpu_custom_call" | custom-call | flops 3449999872 | bytes 1024 | tf_op jit(solution)/shard_map/pallas_call | solution.py:761
  (166 shorter events, 15.4 us)
Async XLA Ops:
  0.7 7.6 %copy-start.26 = (s32[240]{0:T(256)S(1)}, s32[240]{0:T(256)}, u32[]{:S(2)}) copy-start(s32[240]{0:T(256)} %param.32) | copy-start | bytes 2884
  0.7 7.6 %copy-start.22 = (s32[240,8]{0,1:T(8,128)S(1)}, s32[240,8]{0,1:T(8,128)}, u32[]{:S(2)}) copy-start(s32[240,8]{0,1:T(8,128)} %param.33) | copy-start | bytes 23044
  0.7 7.6 %copy-start.24 = (s32[240,8]{0,1:T(8,128)S(1)}, s32[240,8]{0,1:T(8,128)}, u32[]{:S(2)}) copy-start(s32[240,8]{0,1:T(8,128)} %param.35) | copy-start | bytes 23044
  0.7 22.6 %copy-start.23 = (s32[240,8]{0,1:T(8,128)S(1)}, s32[240,8]{0,1:T(8,128)}, u32[]{:S(2)}) copy-start(s32[240,8]{0,1:T(8,128)} %param.34) | copy-start | bytes 23044
  0.7 22.6 %copy-start.25 = (s32[240,8]{0,1:T(8,128)S(1)}, s32[240,8]{0,1:T(8,128)}, u32[]{:S(2)}) copy-start(s32[240,8]{0,1:T(8,128)} %param.36) | copy-start | bytes 23044
  5.1 29.7 %copy-start = (f32[240,512]{1,0:T(8,128)S(1)}, f32[240,512]{1,0:T(8,128)}, u32[]{:S(2)}) copy-start(f32[240,512]{1,0:T(8,128)} %edge.5) | copy-start | bytes 1474564
  5.1 29.7 %copy-start.1 = (bf16[1024,64]{0,1:T(8,128)(2,1)S(1)}, bf16[1024,64]{0,1:T(8,128)(2,1)}, u32[]{:S(2)}) copy-start(bf16[1024,64]{0,1:T(8,128)(2,1)} %param.41) | copy-start | bytes 393220
  5.1 29.7 %copy-start.2 = (bf16[64,512]{1,0:T(8,128)(2,1)S(1)}, bf16[64,512]{1,0:T(8,128)(2,1)}, u32[]{:S(2)}) copy-start(bf16[64,512]{1,0:T(8,128)(2,1)} %trip_up.1) | copy-start | bytes 196612
  5.1 29.7 %copy-start.3 = (bf16[1024,32]{0,1:T(8,128)(2,1)S(1)}, bf16[1024,32]{0,1:T(8,128)(2,1)}, u32[]{:S(2)}) copy-start(bf16[1024,32]{0,1:T(8,128)(2,1)} %param.44) | copy-start | bytes 196612
  5.1 29.7 %copy-start.4 = (bf16[32,512]{1,0:T(8,128)(2,1)S(1)}, bf16[32,512]{1,0:T(8,128)(2,1)}, u32[]{:S(2)}) copy-start(bf16[32,512]{1,0:T(8,128)(2,1)} %quad_up.1) | copy-start | bytes 98308
  5.1 29.7 %copy-start.5 = (f32[8,256]{1,0:T(8,128)S(1)}, f32[8,256]{1,0:T(8,128)}, u32[]{:S(2)}) copy-start(f32[8,256]{1,0:T(8,128)} %cot_atoms.1) | copy-start | bytes 24580
  5.2 29.7 %copy-start.6 = (f32[8,256]{1,0:T(8,128)S(1)}, f32[8,256]{1,0:T(8,128)}, u32[]{:S(2)}) copy-start(f32[8,256]{1,0:T(8,128)} %cot_energy.1) | copy-start | bytes 24580
  5.2 29.7 %copy-start.10 = (f32[240,128]{1,0:T(8,128)S(1)}, f32[240,128]{1,0:T(8,128)}, u32[]{:S(2)}) copy-start(f32[240,128]{1,0:T(8,128)} %get-tuple-element.173.radial) | copy-start | bytes 368644
  5.2 29.7 %copy-start.11 = (f32[17,16,128]{2,1,0:T(8,128)S(1)}, f32[17,16,128]{2,1,0:T(8,128)}, u32[]{:S(2)}) copy-start(f32[17,16,128]{2,1,0:T(8,128)} %get-tuple-element.169.local) | copy-start | bytes 417796
  5.2 29.7 %copy-start.13 = (f32[240,128]{1,0:T(8,128)S(1)}, f32[240,128]{1,0:T(8,128)}, u32[]{:S(2)}) copy-start(f32[240,128]{1,0:T(8,128)} %get-tuple-element.171.columns) | copy-start | bytes 368644
  5.2 29.7 %copy-start.17 = (f32[8,256]{1,0:T(8,128)S(1)}, f32[8,256]{1,0:T(8,128)}, u32[]{:S(2)}) copy-start(f32[8,256]{1,0:T(8,128)} %get-tuple-element.170.tagged) | copy-start | bytes 24580
  5.2 5.5 %collective-permute-start = (f32[17,8,128]{2,1,0:T(8,128)}, f32[17,8,128]{2,1,0:T(8,128)S(1)}, u32[]{:S(2)}, u32[]{:S(2)}) collective-permute-start(f32[17,8,128]{2,1,0:T(8,128)} %get-tuple-element.168), channel_id=1, source_target_pairs={{0,1},{1,0},{2,3},{3,2},{4,5},{5,4},{6,7},{7,6},{8,9},{9,8},{10,11... | collective-permute-start | bytes 208904 | tf_op jit(solution)/shard_map/ppermute | solution.py:36
  11.6 7.5 %collective-permute-start.2 = (f32[2,17,8,128]{3,2,1,0:T(8,128)S(1)}, f32[2,17,8,128]{3,2,1,0:T(8,128)S(1)}, u32[]{:S(2)}, u32[]{:S(2)}) collective-permute-start(f32[2,17,8,128]{3,2,1,0:T(8,128)S(1)} %pad_maximum_fusion.14), channel_id=1, source_target_pairs={{0,24},{8,0},{16,8},{24,16},{1,25},{9,1},{17,9},{25,17},{2,26},{10... | collective-permute-start | bytes 417800 | tf_op jit(solution)/shard_map/ppermute | solution.py:31
  15.8 6.9 %collective-permute-start.1 = (f32[2,17,8,128]{3,2,1,0:T(8,128)S(1)}, f32[2,17,8,128]{3,2,1,0:T(8,128)S(1)}, u32[]{:S(2)}, u32[]{:S(2)}) collective-permute-start(f32[2,17,8,128]{3,2,1,0:T(8,128)S(1)} %pad_maximum_fusion.14), channel_id=1, source_target_pairs={{0,8},{8,16},{16,24},{24,0},{1,9},{9,17},{17,25},{25,1},{2,10},{10... | collective-permute-start | bytes 417800 | tf_op jit(solution)/shard_map/ppermute | solution.py:31
  22.7 8.9 %collective-permute-start.4 = (f32[6,17,8,128]{3,2,1,0:T(8,128)S(1)}, f32[6,17,8,128]{3,2,1,0:T(8,128)S(1)}, u32[]{:S(2)}, u32[]{:S(2)}) collective-permute-start(f32[6,17,8,128]{3,2,1,0:T(8,128)S(1)} %pad_maximum_fusion.8.halo_here), channel_id=1, source_target_pairs={{0,6},{2,0},{4,2},{6,4},{1,7},{3,1},{5,3},{7,5},{8,14},{10,8},{12,... | collective-permute-start | bytes 1253384 | tf_op jit(solution)/shard_map/ppermute | solution.py:31
  22.8 12.0 %collective-permute-start.3 = (f32[6,17,8,128]{3,2,1,0:T(8,128)S(1)}, f32[6,17,8,128]{3,2,1,0:T(8,128)S(1)}, u32[]{:S(2)}, u32[]{:S(2)}) collective-permute-start(f32[6,17,8,128]{3,2,1,0:T(8,128)S(1)} %pad_maximum_fusion.8.halo_here), channel_id=1, source_target_pairs={{0,2},{2,4},{4,6},{6,0},{1,3},{3,5},{5,7},{7,1},{8,10},{10,12},{12... | collective-permute-start | bytes 1253384 | tf_op jit(solution)/shard_map/ppermute | solution.py:31
  59.8 4.2 %collective-permute-start.5 = (f32[896,512]{1,0:T(8,128)}, f32[896,512]{1,0:T(8,128)}, u32[]{:S(2)}, u32[]{:S(2)}) collective-permute-start(f32[896,512]{1,0:T(8,128)} %get-tuple-element.179), channel_id=1, source_target_pairs={{0,2},{2,0},{1,3},{3,1},{4,6},{6,4},{5,7},{7,5},{8,10},{10,8},{9,1... | collective-permute-start | bytes 5505032 | tf_op jit(solution)/shard_map/ppermute | solution.py:55
  62.4 4.9 %collective-permute-start.6 = (f32[768,512]{1,0:T(8,128)S(1)}, f32[768,512]{1,0:T(8,128)}, u32[]{:S(2)}, u32[]{:S(2)}) collective-permute-start(f32[768,512]{1,0:T(8,128)S(1)} %get-tuple-element.184), channel_id=1, source_target_pairs={{0,2},{2,0},{1,3},{3,1},{4,6},{6,4},{5,7},{7,5},{8,10},{10,8},{9,1... | collective-permute-start | bytes 4718600 | tf_op jit(solution)/shard_map/ppermute | solution.py:55
  64.0 5.1 %copy-start.12 = (f32[30,8,8,128]{3,2,1,0:T(8,128)S(1)}, f32[30,8,8,128]{3,2,1,0:T(8,128)}, u32[]{:S(2)}) copy-start(f32[30,8,8,128]{3,2,1,0:T(8,128)} %get-tuple-element.177.cosines) | copy-start | bytes 2949124
  65.7 3.4 %copy-start.9 = (f32[240,2048]{1,0:T(8,128)S(1)}, f32[240,2048]{1,0:T(8,128)}, u32[]{:S(2)}) copy-start(f32[240,2048]{1,0:T(8,128)} %get-tuple-element.188.sums) | copy-start | bytes 5898244
  65.7 3.4 %copy-start.16 = (f32[240,256]{1,0:T(8,128)S(1)}, f32[240,256]{1,0:T(8,128)}, u32[]{:S(2)}) copy-start(f32[240,256]{1,0:T(8,128)} %copy-done.15) | copy-start | bytes 737284
  65.7 22.5 %collective-permute-start.7 = (f32[448,512]{1,0:T(8,128)S(1)}, f32[448,512]{1,0:T(8,128)S(1)}, u32[]{:S(2)}, u32[]{:S(2)}) collective-permute-start(f32[448,512]{1,0:T(8,128)S(1)} %dynamic-slice_add_fusion.1), channel_id=1, source_target_pairs={{0,1},{1,0},{2,3},{3,2},{4,5},{5,4},{6,7},{7,6},{8,9},{9,8},{10,11... | collective-permute-start | bytes 2752520 | tf_op jit(solution)/shard_map/ppermute | solution.py:55
  68.5 20.5 %collective-permute-start.8 = (f32[384,512]{1,0:T(8,128)S(1)}, f32[384,512]{1,0:T(8,128)S(1)}, u32[]{:S(2)}, u32[]{:S(2)}) collective-permute-start(f32[384,512]{1,0:T(8,128)S(1)} %dynamic-slice_add_fusion.3), channel_id=1, source_target_pairs={{0,4},{4,0},{1,5},{5,1},{2,6},{6,2},{3,7},{7,3},{8,12},{12,8},{9,1... | collective-permute-start | bytes 2359304 | tf_op jit(solution)/shard_map/ppermute | solution.py:55
  74.9 3.4 %copy-start.14 = (f32[16,16,128]{2,1,0:T(8,128)}, f32[16,16,128]{2,1,0:T(8,128)S(1)}, u32[]{:S(2)}) copy-start(f32[16,16,128]{2,1,0:T(8,128)S(1)} %get-tuple-element.190.back_local) | copy-start | bytes 393220
  75.0 20.5 %collective-permute-start.9 = (f32[6,16,8,128]{3,2,1,0:T(8,128)S(1)}, f32[6,16,8,128]{3,2,1,0:T(8,128)S(1)}, u32[]{:S(2)}, u32[]{:S(2)}) collective-permute-start(f32[6,16,8,128]{3,2,1,0:T(8,128)S(1)} %get-tuple-element.203), channel_id=1, source_target_pairs={{0,6},{2,0},{4,2},{6,4},{1,7},{3,1},{5,3},{7,5},{8,14},{10,8},{12,... | collective-permute-start | bytes 1179656 | tf_op jit(solution)/shard_map/ppermute | solution.py:31
  75.7 19.8 %collective-permute-start.10 = (f32[6,16,8,128]{3,2,1,0:T(8,128)S(1)}, f32[6,16,8,128]{3,2,1,0:T(8,128)S(1)}, u32[]{:S(2)}, u32[]{:S(2)}) collective-permute-start(f32[6,16,8,128]{3,2,1,0:T(8,128)S(1)} %get-tuple-element.204), channel_id=1, source_target_pairs={{0,2},{2,4},{4,6},{6,0},{1,3},{3,5},{5,7},{7,1},{8,10},{10,12},{12... | collective-permute-start | bytes 1179656 | tf_op jit(solution)/shard_map/ppermute | solution.py:31
  88.2 17.9 %collective-permute-start.11 = (f32[224,512]{1,0:T(8,128)S(1)}, f32[224,512]{1,0:T(8,128)S(1)}, u32[]{:S(2)}, u32[]{:S(2)}) collective-permute-start(f32[224,512]{1,0:T(8,128)S(1)} %dynamic-slice_add_fusion.5), channel_id=1, source_target_pairs={{0,4},{4,0},{1,5},{5,1},{2,6},{6,2},{3,7},{7,3},{8,12},{12,8},{9,1... | collective-permute-start | bytes 1376264 | tf_op jit(solution)/shard_map/ppermute | solution.py:55
  89.1 10.4 %collective-permute-start.12 = (f32[192,512]{1,0:T(8,128)S(1)}, f32[192,512]{1,0:T(8,128)S(1)}, u32[]{:S(2)}, u32[]{:S(2)}) collective-permute-start(f32[192,512]{1,0:T(8,128)S(1)} %dynamic-slice_add_fusion.13), channel_id=1, source_target_pairs={{0,1},{1,0},{2,3},{3,2},{4,5},{5,4},{6,7},{7,6},{8,9},{9,8},{10,11... | collective-permute-start | bytes 1179656 | tf_op jit(solution)/shard_map/ppermute | solution.py:55
  95.6 10.9 %collective-permute-start.14 = (f32[2,16,8,128]{3,2,1,0:T(8,128)S(1)}, f32[2,16,8,128]{3,2,1,0:T(8,128)S(1)}, u32[]{:S(2)}, u32[]{:S(2)}) collective-permute-start(f32[2,16,8,128]{3,2,1,0:T(8,128)S(1)} %get-tuple-element.343), channel_id=1, source_target_pairs={{0,8},{8,16},{16,24},{24,0},{1,9},{9,17},{17,25},{25,1},{2,10},{10... | collective-permute-start | bytes 393224 | tf_op jit(solution)/shard_map/ppermute | solution.py:31
  96.0 10.4 %collective-permute-start.13 = (f32[2,16,8,128]{3,2,1,0:T(8,128)S(1)}, f32[2,16,8,128]{3,2,1,0:T(8,128)S(1)}, u32[]{:S(2)}, u32[]{:S(2)}) collective-permute-start(f32[2,16,8,128]{3,2,1,0:T(8,128)S(1)} %get-tuple-element.344), channel_id=1, source_target_pairs={{0,24},{8,0},{16,8},{24,16},{1,25},{9,1},{17,9},{25,17},{2,26},{10... | collective-permute-start | bytes 393224 | tf_op jit(solution)/shard_map/ppermute | solution.py:31
  106.5 4.3 %collective-permute-start.15 = (f32[16,8,128]{2,1,0:T(8,128)S(1)}, f32[16,8,128]{2,1,0:T(8,128)S(1)}, u32[]{:S(2)}, u32[]{:S(2)}) collective-permute-start(f32[16,8,128]{2,1,0:T(8,128)S(1)} %select_bitcast_fusion.2), channel_id=1, source_target_pairs={{0,1},{1,0},{2,3},{3,2},{4,5},{5,4},{6,7},{7,6},{8,9},{9,8},{10,11... | collective-permute-start | bytes 196616 | tf_op jit(solution)/shard_map/ppermute | solution.py:886
  107.4 10.9 %collective-permute-start.16 = (f32[208,512]{1,0:T(8,128)S(1)}, f32[208,512]{1,0:T(8,128)S(1)}, u32[]{:S(2)}, u32[]{:S(2)}) collective-permute-start(f32[208,512]{1,0:T(8,128)S(1)} %dynamic-slice_add_fusion.7), channel_id=1, source_target_pairs={{0,8},{8,0},{16,24},{24,16},{1,9},{9,1},{17,25},{25,17},{2,10},{10... | collective-permute-start | bytes 1277960 | tf_op jit(solution)/shard_map/ppermute | solution.py:55
  118.3 4.9 %copy-start.20 = (f32[384,512]{1,0:T(8,128)S(1)}, f32[384,512]{1,0:T(8,128)}, u32[]{:S(2)}) copy-start(f32[384,512]{1,0:T(8,128)} %get-tuple-element.247) | copy-start | bytes 2359300
  118.4 2.9 %collective-permute-start.17 = (f32[384,512]{1,0:T(8,128)}, f32[384,512]{1,0:T(8,128)S(1)}, u32[]{:S(2)}, u32[]{:S(2)}) collective-permute-start(f32[384,512]{1,0:T(8,128)} %get-tuple-element.232), channel_id=1, source_target_pairs={{0,2},{2,0},{1,3},{3,1},{4,6},{6,4},{5,7},{7,5},{8,10},{10,8},{9,1... | collective-permute-start | bytes 2359304 | tf_op jit(solution)/shard_map/ppermute | solution.py:55
  118.4 4.8 %collective-permute-start.18 = (f32[384,512]{1,0:T(8,128)}, f32[384,512]{1,0:T(8,128)}, u32[]{:S(2)}, u32[]{:S(2)}) collective-permute-start(f32[384,512]{1,0:T(8,128)} %get-tuple-element.236), channel_id=1, source_target_pairs={{0,2},{2,0},{1,3},{3,1},{4,6},{6,4},{5,7},{7,5},{8,10},{10,8},{9,1... | collective-permute-start | bytes 2359304 | tf_op jit(solution)/shard_map/ppermute | solution.py:55
  118.9 12.7 %copy-start.21 = (f32[384,512]{1,0:T(8,128)S(1)}, f32[384,512]{1,0:T(8,128)}, u32[]{:S(2)}) copy-start(f32[384,512]{1,0:T(8,128)} %get-tuple-element.243) | copy-start | bytes 2359300
  118.9 12.5 %collective-permute-start.19 = (f32[104,512]{1,0:T(8,128)S(1)}, f32[104,512]{1,0:T(8,128)S(1)}, u32[]{:S(2)}, u32[]{:S(2)}) collective-permute-start(f32[104,512]{1,0:T(8,128)S(1)} %dynamic-slice_add_fusion.15), channel_id=1, source_target_pairs={{0,16},{8,24},{16,0},{24,8},{1,17},{9,25},{17,1},{25,9},{2,18},{10... | collective-permute-start | bytes 638984 | tf_op jit(solution)/shard_map/ppermute | solution.py:55
  122.3 11.2 %collective-permute-start.20 = (f32[192,512]{1,0:T(8,128)S(1)}, f32[192,512]{1,0:T(8,128)S(1)}, u32[]{:S(2)}, u32[]{:S(2)}) collective-permute-start(f32[192,512]{1,0:T(8,128)S(1)} %dynamic-slice_add_fusion.11), channel_id=1, source_target_pairs={{0,1},{1,0},{2,3},{3,2},{4,5},{5,4},{6,7},{7,6},{8,9},{9,8},{10,11... | collective-permute-start | bytes 1179656 | tf_op jit(solution)/shard_map/ppermute | solution.py:55
  124.3 10.9 %collective-permute-start.21 = (f32[192,512]{1,0:T(8,128)S(1)}, f32[192,512]{1,0:T(8,128)S(1)}, u32[]{:S(2)}, u32[]{:S(2)}) collective-permute-start(f32[192,512]{1,0:T(8,128)S(1)} %dynamic-slice_add_fusion.10), channel_id=1, source_target_pairs={{0,4},{4,0},{1,5},{5,1},{2,6},{6,2},{3,7},{7,3},{8,12},{12,8},{9,1... | collective-permute-start | bytes 1179656 | tf_op jit(solution)/shard_map/ppermute | solution.py:55
  131.5 11.4 %collective-permute-start.24 = (f32[104,512]{1,0:T(8,128)S(1)}, f32[104,512]{1,0:T(8,128)S(1)}, u32[]{:S(2)}, u32[]{:S(2)}) collective-permute-start(f32[104,512]{1,0:T(8,128)S(1)} %add.320), channel_id=1, source_target_pairs={{0,16},{8,24},{16,0},{24,8},{1,17},{9,25},{17,1},{25,9},{2,18},{10... | collective-permute-start | bytes 638984 | tf_op jit(solution)/shard_map/ppermute | solution.py:55
  133.6 6.2 %collective-permute-start.22 = (f32[96,512]{1,0:T(8,128)S(1)}, f32[96,512]{1,0:T(8,128)S(1)}, u32[]{:S(2)}, u32[]{:S(2)}) collective-permute-start(f32[96,512]{1,0:T(8,128)S(1)} %dynamic-slice_add_fusion.21), channel_id=1, source_target_pairs={{0,4},{4,0},{1,5},{5,1},{2,6},{6,2},{3,7},{7,3},{8,12},{12,8},{9,1... | collective-permute-start | bytes 589832 | tf_op jit(solution)/shard_map/ppermute | solution.py:55
  135.3 5.9 %collective-permute-start.23 = (f32[96,512]{1,0:T(8,128)S(1)}, f32[96,512]{1,0:T(8,128)S(1)}, u32[]{:S(2)}, u32[]{:S(2)}) collective-permute-start(f32[96,512]{1,0:T(8,128)S(1)} %dynamic-slice_add_fusion.20), channel_id=1, source_target_pairs={{0,1},{1,0},{2,3},{3,2},{4,5},{5,4},{6,7},{7,6},{8,9},{9,8},{10,11... | collective-permute-start | bytes 589832 | tf_op jit(solution)/shard_map/ppermute | solution.py:55
  141.2 7.3 %collective-permute-start.25 = (f32[96,512]{1,0:T(8,128)S(1)}, f32[96,512]{1,0:T(8,128)S(1)}, u32[]{:S(2)}, u32[]{:S(2)}) collective-permute-start(f32[96,512]{1,0:T(8,128)S(1)} %dynamic-slice_add_fusion.17), channel_id=1, source_target_pairs={{0,8},{8,0},{16,24},{24,16},{1,9},{9,1},{17,25},{25,17},{2,10},{10... | collective-permute-start | bytes 589832 | tf_op jit(solution)/shard_map/ppermute | solution.py:55
  143.0 15.3 %collective-permute-start.26 = (f32[208,512]{1,0:T(8,128)S(1)}, f32[208,512]{1,0:T(8,128)S(1)}, u32[]{:S(2)}, u32[]{:S(2)}) collective-permute-start(f32[208,512]{1,0:T(8,128)S(1)} %pad_maximum_fusion.7), channel_id=1, source_target_pairs={{0,8},{8,0},{16,24},{24,16},{1,9},{9,1},{17,25},{25,17},{2,10},{10... | collective-permute-start | bytes 1277960 | tf_op jit(solution)/shard_map/ppermute | solution.py:55
  148.6 9.9 %collective-permute-start.29 = (f32[48,512]{1,0:T(8,128)S(1)}, f32[48,512]{1,0:T(8,128)S(1)}, u32[]{:S(2)}, u32[]{:S(2)}) collective-permute-start(f32[48,512]{1,0:T(8,128)S(1)} %dynamic-slice_add_fusion.23), channel_id=1, source_target_pairs={{0,16},{8,24},{16,0},{24,8},{1,17},{9,25},{17,1},{25,9},{2,18},{10... | collective-permute-start | bytes 294920 | tf_op jit(solution)/shard_map/ppermute | solution.py:55
  159.7 6.6 %collective-permute-start.30 = (f32[48,512]{1,0:T(8,128)S(1)}, f32[48,512]{1,0:T(8,128)S(1)}, u32[]{:S(2)}, u32[]{:S(2)}) collective-permute-start(f32[48,512]{1,0:T(8,128)S(1)} %add_add_fusion.2), channel_id=1, source_target_pairs={{0,16},{8,24},{16,0},{24,8},{1,17},{9,25},{17,1},{25,9},{2,18},{10... | collective-permute-start | bytes 294920 | tf_op jit(solution)/shard_map/ppermute | solution.py:55
  161.3 13.2 %collective-permute-start.27 = (f32[224,512]{1,0:T(8,128)S(1)}, f32[224,512]{1,0:T(8,128)S(1)}, u32[]{:S(2)}, u32[]{:S(2)}) collective-permute-start(f32[224,512]{1,0:T(8,128)S(1)} %fusion), channel_id=1, source_target_pairs={{0,4},{4,0},{1,5},{5,1},{2,6},{6,2},{3,7},{7,3},{8,12},{12,8},{9,1... | collective-permute-start | bytes 1376264 | tf_op jit(solution)/shard_map/ppermute | solution.py:55
  166.3 5.7 %collective-permute-start.31 = (f32[96,512]{1,0:T(8,128)S(1)}, f32[96,512]{1,0:T(8,128)S(1)}, u32[]{:S(2)}, u32[]{:S(2)}) collective-permute-start(f32[96,512]{1,0:T(8,128)S(1)} %pad_maximum_fusion.13), channel_id=1, source_target_pairs={{0,8},{8,0},{16,24},{24,16},{1,9},{9,1},{17,25},{25,17},{2,10},{10... | collective-permute-start | bytes 589832 | tf_op jit(solution)/shard_map/ppermute | solution.py:55
  166.7 11.9 %collective-permute-start.28 = (f32[192,512]{1,0:T(8,128)S(1)}, f32[192,512]{1,0:T(8,128)S(1)}, u32[]{:S(2)}, u32[]{:S(2)}) collective-permute-start(f32[192,512]{1,0:T(8,128)S(1)} %slice.49), channel_id=1, source_target_pairs={{0,1},{1,0},{2,3},{3,2},{4,5},{5,4},{6,7},{7,6},{8,9},{9,8},{10,11... | collective-permute-start | bytes 1179656 | tf_op jit(solution)/shard_map/ppermute | solution.py:55
  172.1 10.7 %collective-permute-start.33 = (f32[96,512]{1,0:T(8,128)S(1)}, f32[96,512]{1,0:T(8,128)S(1)}, u32[]{:S(2)}, u32[]{:S(2)}) collective-permute-start(f32[96,512]{1,0:T(8,128)S(1)} %get-tuple-element.285), channel_id=1, source_target_pairs={{0,1},{1,0},{2,3},{3,2},{4,5},{5,4},{6,7},{7,6},{8,9},{9,8},{10,11... | collective-permute-start | bytes 589832 | tf_op jit(solution)/shard_map/ppermute | solution.py:55
  173.3 7.8 %collective-permute-start.32 = (f32[96,512]{1,0:T(8,128)S(1)}, f32[96,512]{1,0:T(8,128)S(1)}, u32[]{:S(2)}, u32[]{:S(2)}) collective-permute-start(f32[96,512]{1,0:T(8,128)S(1)} %get-tuple-element.283), channel_id=1, source_target_pairs={{0,4},{4,0},{1,5},{5,1},{2,6},{6,2},{3,7},{7,3},{8,12},{12,8},{9,1... | collective-permute-start | bytes 589832 | tf_op jit(solution)/shard_map/ppermute | solution.py:55
  174.7 24.2 %collective-permute-start.34 = (f32[448,512]{1,0:T(8,128)S(1)}, f32[448,512]{1,0:T(8,128)S(1)}, u32[]{:S(2)}, u32[]{:S(2)}) collective-permute-start(f32[448,512]{1,0:T(8,128)S(1)} %pad_maximum_fusion.1), channel_id=1, source_target_pairs={{0,1},{1,0},{2,3},{3,2},{4,5},{5,4},{6,7},{7,6},{8,9},{9,8},{10,11... | collective-permute-start | bytes 2752520 | tf_op jit(solution)/shard_map/ppermute | solution.py:55
  178.8 21.8 %collective-permute-start.35 = (f32[384,512]{1,0:T(8,128)S(1)}, f32[384,512]{1,0:T(8,128)S(1)}, u32[]{:S(2)}, u32[]{:S(2)}) collective-permute-start(f32[384,512]{1,0:T(8,128)S(1)} %pad_maximum_fusion.4), channel_id=1, source_target_pairs={{0,4},{4,0},{1,5},{5,1},{2,6},{6,2},{3,7},{7,3},{8,12},{12,8},{9,1... | collective-permute-start | bytes 2359304 | tf_op jit(solution)/shard_map/ppermute | solution.py:55
  200.4 6.1 %collective-permute-start.36 = (f32[896,512]{1,0:T(8,128)S(1)}, f32[896,512]{1,0:T(8,128)S(1)}, u32[]{:S(2)}, u32[]{:S(2)}) collective-permute-start(f32[896,512]{1,0:T(8,128)S(1)} %maximum_add_fusion.a_mine), channel_id=1, source_target_pairs={{0,2},{2,0},{1,3},{3,1},{4,6},{6,4},{5,7},{7,5},{8,10},{10,8},{9,1... | collective-permute-start | bytes 5505032 | tf_op jit(solution)/shard_map/ppermute | solution.py:55
  202.1 4.5 %collective-permute-start.37 = (f32[768,512]{1,0:T(8,128)S(1)}, f32[768,512]{1,0:T(8,128)S(1)}, u32[]{:S(2)}, u32[]{:S(2)}) collective-permute-start(f32[768,512]{1,0:T(8,128)S(1)} %maximum_add_fusion.1.b_mine), channel_id=1, source_target_pairs={{0,2},{2,0},{1,3},{3,1},{4,6},{6,4},{5,7},{7,5},{8,10},{10,8},{9,1... | collective-permute-start | bytes 4718600 | tf_op jit(solution)/shard_map/ppermute | solution.py:55
  202.6 11.1 %collective-permute-start.38 = (f32[192,512]{1,0:T(8,128)S(1)}, f32[192,512]{1,0:T(8,128)S(1)}, u32[]{:S(2)}, u32[]{:S(2)}) collective-permute-start(f32[192,512]{1,0:T(8,128)S(1)} %pad_maximum_fusion.11), channel_id=1, source_target_pairs={{0,1},{1,0},{2,3},{3,2},{4,5},{5,4},{6,7},{7,6},{8,9},{9,8},{10,11... | collective-permute-start | bytes 1179656 | tf_op jit(solution)/shard_map/ppermute | solution.py:55
  203.7 10.8 %collective-permute-start.39 = (f32[192,512]{1,0:T(8,128)S(1)}, f32[192,512]{1,0:T(8,128)S(1)}, u32[]{:S(2)}, u32[]{:S(2)}) collective-permute-start(f32[192,512]{1,0:T(8,128)S(1)} %pad_maximum_fusion.12), channel_id=1, source_target_pairs={{0,4},{4,0},{1,5},{5,1},{2,6},{6,2},{3,7},{7,3},{8,12},{12,8},{9,1... | collective-permute-start | bytes 1179656 | tf_op jit(solution)/shard_map/ppermute | solution.py:55
  214.7 2.4 %collective-permute-start.41 = (f32[384,512]{1,0:T(8,128)S(1)}, f32[384,512]{1,0:T(8,128)S(1)}, u32[]{:S(2)}, u32[]{:S(2)}) collective-permute-start(f32[384,512]{1,0:T(8,128)S(1)} %pad_maximum_fusion.6.d_mine), channel_id=1, source_target_pairs={{0,2},{2,0},{1,3},{3,1},{4,6},{6,4},{5,7},{7,5},{8,10},{10,8},{9,1... | collective-permute-start | bytes 2359304 | tf_op jit(solution)/shard_map/ppermute | solution.py:55
  214.8 3.4 %collective-permute-start.40 = (f32[384,512]{1,0:T(8,128)S(1)}, f32[384,512]{1,0:T(8,128)S(1)}, u32[]{:S(2)}, u32[]{:S(2)}) collective-permute-start(f32[384,512]{1,0:T(8,128)S(1)} %pad_maximum_fusion.5.c_mine), channel_id=1, source_target_pairs={{0,2},{2,0},{1,3},{3,1},{4,6},{6,4},{5,7},{7,5},{8,10},{10,8},{9,1... | collective-permute-start | bytes 2359304 | tf_op jit(solution)/shard_map/ppermute | solution.py:55
  (5 other events, 11.3 us)
